TPU v7x, 32 devices: a whole 2x2x4 slice. The times are simulated.
32 devices in a mesh: scen: 8 (over z, core), inst: 4 (over y, x).
Axes of the slice: x: 2, y: 2, z: 4, core: 2. Of those that a mesh axis runs over, the one named last changes fastest.
Arguments:
- shocks: bfloat16 [4096, 2048], P('scen', 'inst'), may hold values from -6 to 6
- loadings: bfloat16 [2048, 16384], P(None, 'inst'), may hold values from -0.125 to 0.125
- delta: float32 [16384], P('inst'), may hold values from -6 to 6
- gamma: float32 [16384], P('inst'), may hold values from -3 to 3
- kappa: float32 [16384], P('inst'), may hold values from -1.2 to 1.2
- book_of: int32 [16384], P('inst'), may hold values from 0 to 255
- bracket_low: int32 [256], replicated, may hold values from -48 to -25
- bracket_high: int32 [256], replicated, may hold values from -24 to 8
- rank: int32 [256], replicated, may hold values from 32 to 64
Outputs:
- contribution: float32 [256, 16384], P('scen', 'inst')
- quantile: float32 [256], P('inst')
Inputs may be any that keep to these rules, and one draw needn't show every extreme that they name: `book_of`: each instrument's book.
All inputs are finite; a program needn't handle non-finite values.
Results may differ from a plain program's by a relative error of at most 0.002.
Values may be sent and summed in bfloat16 or wider, within the bound.
No kernel may reach another device: no remote copies, remote signals or barrier semaphores. Data moves between devices by JAX's collectives and lax.ppermute only.
A program may use at most 128 MiB of HBM per device.

v0:
```python
import jax
import jax.numpy as jnp
from jax import lax
from jax.sharding import PartitionSpec as P

PIVOTS = 64
ROUNDS = 3


tail_width = 0.5
bracket_unit = 0.125


def revalue(moves, delta, gamma, kappa):
    return (moves * (delta + moves * (gamma + moves * kappa))).astype(jnp.bfloat16)


def count_below(book_pnl, pivots):
    group = min(book_pnl.shape[1], 32)
    blocks = book_pnl.T.reshape(-1, group, book_pnl.shape[0])
    pivot_blocks = pivots.reshape(-1, group, pivots.shape[1])

    def one_block(pair):
        values, marks = pair
        return jnp.sum((values[:, :, None] <= marks[:, None, :]).astype(jnp.int32), axis=1)

    return lax.map(one_block, (blocks, pivot_blocks)).reshape(pivots.shape)


def locate(book_pnl, bracket_low, bracket_high, rank, total):
    lower = bracket_low.astype(jnp.float32) * bracket_unit
    upper = bracket_high.astype(jnp.float32) * bracket_unit
    marks = jnp.arange(PIVOTS, dtype=jnp.int32)
    levels = marks.astype(jnp.float32)
    for sweep_index in range(ROUNDS):
        spacing = (upper - lower) / (PIVOTS - 1)
        pivots = lower[:, None] + levels[None, :] * spacing[:, None]
        counts = total(count_below(book_pnl, pivots))
        below = jnp.sum((counts < rank[:, None]).astype(jnp.int32), axis=1)
        chosen = jnp.clip(below, 1, PIVOTS - 1)
        lower = jnp.sum(jnp.where(marks[None, :] == (chosen - 1)[:, None], pivots, 0.0), axis=1)
        upper = jnp.sum(jnp.where(marks[None, :] == chosen[:, None], pivots, 0.0), axis=1)
    return (lower + upper) * 0.5


def body(shocks, loadings, delta, gamma, kappa, book_of, bracket_low, bracket_high, rank):
    inst_cols = loadings.shape[1]
    book_count = bracket_low.shape[0]
    inst_devices = lax.axis_size("inst")
    scale = (book_count / (inst_cols * inst_devices)) ** 0.5
    moves = jnp.dot(
        lax.all_gather(shocks, "inst", axis=1, tiled=True),
        loadings,
        preferred_element_type=jnp.float32,
    )
    profit = revalue(moves, delta, gamma, kappa)
    books = jnp.arange(book_count, dtype=jnp.int32)
    onehot = (book_of[:, None] == books[None, :]).astype(jnp.bfloat16)
    partial_sums = jnp.dot(profit, onehot, preferred_element_type=jnp.float32) * scale
    share = book_count // inst_devices
    share_start = lax.axis_index("inst") * share
    own_low = lax.dynamic_slice_in_dim(bracket_low, share_start, share, 0)
    own_high = lax.dynamic_slice_in_dim(bracket_high, share_start, share, 0)
    own_rank = lax.dynamic_slice_in_dim(rank, share_start, share, 0)
    own_pnl = lax.psum_scatter(partial_sums, "inst", scatter_dimension=1, tiled=True)
    every_pnl = lax.all_gather(own_pnl, "scen", axis=0, tiled=True)
    quantile = locate(every_pnl, own_low, own_high, own_rank, lambda counts: counts)
    own_weights = jax.nn.sigmoid((quantile[None, :] - own_pnl) / tail_width).astype(jnp.bfloat16)
    weights = lax.all_gather(own_weights, "inst", axis=1, tiled=True)
    mass = lax.psum(jnp.sum(weights.astype(jnp.float32), axis=0), "scen")
    rows_here = book_count // lax.axis_size("scen")
    summed = lax.psum_scatter(
        lax.dot_general(
            weights, profit, (((0,), (0,)), ((), ())), preferred_element_type=jnp.float32
        ),
        "scen",
        scatter_dimension=0,
        tiled=True,
    )
    own_mass = lax.dynamic_slice_in_dim(mass, lax.axis_index("scen") * rows_here, rows_here, 0)
    contribution = summed / own_mass[:, None]
    return (contribution, quantile)


def solution(mesh):
    placed = (
        P("scen", "inst"),
        P(None, "inst"),
        P("inst"),
        P("inst"),
        P("inst"),
        P("inst"),
        P(),
        P(),
        P(),
    )
    return jax.shard_map(
        body, mesh=mesh, in_specs=placed, out_specs=(P("scen", "inst"), P("inst")), check_vma=False
    )
```

profile of v0, /device:TPU:0, one launch (start us, length us, event | category | flops | bytes accessed | tf_op | source)
XLA Modules:
  0.0 220.1 jit_solution(2846894398038148799)
XLA Ops:
  7.2 0.7 all-gather.3.cloned.1.call-update
  8.0 39.7 %all-gather.3.cloned.1.call-done = bf16[512,2048]{1,0:T(8,128)(2,1)} async-done(((bf16[512,512]{1,0:T(8,128)(2,1)}), bf16[512,2048]{1,0:T(8,128)(2,1)}) %all-gather.3.cloned.1.call-update) | async-done | bytes 2097168 | tf_op jit(solution)/shard_map/all_gather | solution.py:52
  47.7 12.3 %fusion.4 = f32[512,4096]{1,0:T(8,128)S(1)} fusion(bf16[512,2048]{1,0:T(8,128)(2,1)} %all-gather.3.cloned.1.call-done, bf16[2048,4096]{1,0:T(8,128)(2,1)} %param.16), kind=kOutput, calls=%fused_computation.56 | convolution fusion | flops 8589934592 | bytes 27262976 | tf_op jit(solution)/shard_map/dot_general | solution.py:51
  60.0 3.2 %copy-done.9 = f32[512,4096]{1,0:T(8,128)} copy-done((f32[512,4096]{1,0:T(8,128)}, f32[512,4096]{1,0:T(8,128)S(1)}, u32[]{:S(2)}) %copy-start.9) | copy-done | bytes 8388632
  63.3 3.7 %fusion.2 = f32[512,256]{0,1:T(8,128)} fusion(s32[4096]{0:T(1024)S(1)} %copy-done.4, f32[512,4096]{1,0:T(8,128)S(1)} %fusion.4, f32[4096]{0:T(1024)S(1)} %copy-done.5, f32[4096]{0:T(1024)S(1)} %copy-done.6, f32[4096]{0:T(1024)S(1)} %copy-done.7), kind=kOutput, calls=%fused_computation.16 | convolution fusion | flops 1087504384 | bytes 8978432 | tf_op jit(solution)/shard_map/dot_general | solution.py:59
  67.1 24.9 %reduce-scatter.3.cloned.1.call-done = f32[512,64]{0,1:T(8,128)} async-done(((f32[512,256]{0,1:T(8,128)}), f32[512,64]{0,1:T(8,128)}) %reduce-scatter.3.cloned.1.call-update) | async-done | bytes 131088 | tf_op jit(solution)/shard_map/reduce_scatter | solution.py:65
  92.0 0.2 reduce-scatter.5.cloned.1.call-start
  92.8 23.0 %all-gather.5.cloned.1.call-done = f32[4096,64]{0,1:T(8,128)} async-done(((f32[512,64]{0,1:T(8,128)}), f32[4096,64]{0,1:T(8,128)}) %all-gather.5.cloned.1.call-update) | async-done | bytes 1048592 | tf_op jit(solution)/shard_map/all_gather | solution.py:66
  115.8 9.4 %while.30 = (s32[]{:T(128)}, s32[2,32,64]{2,1,0:T(8,128)S(1)}, f32[2,32,4096]{2,1,0:T(8,128)}, f32[2,32,64]{2,1,0:T(8,128)S(1)}, s32[]{:T(128)}) while((s32[]{:T(128)}, s32[2,32,64]{2,1,0:T(8,128)S(1)}, f32[2,32,4096]{2,1,0:T(8,128)}, f32[2,32,64]{2,1,0:T(8,128)S(1)}, s32[]{:T(128)}) %tuple.69), condition=%wide.region_3.4_spmd, body=%wide.region_1.3_spmd.sunk | while | flops 25163776 | bytes 1638481 | solution.py:27
  115.8 1.1 dynamic-slice_bitcast_fusion.13
  116.9 3.6 %convert_reduce_fusion.10 = s32[32,64]{1,0:T(8,128)S(1)} fusion(f32[32,64]{1,0:T(8,128)S(1)} %dynamic-slice_bitcast_fusion.12, f32[32,4096]{1,0:T(8,128)S(1)} %dynamic-slice_bitcast_fusion.13), kind=kLoop, calls=%fused_computation.clone.1 | loop fusion | flops 25163776 | bytes 540672 | tf_op jit(solution)/shard_map/while/body/eval_jaxpr/reduce_sum | solution.py:25
  120.5 1.1 dynamic-slice_bitcast_fusion.13
  121.6 3.6 %convert_reduce_fusion.10 = s32[32,64]{1,0:T(8,128)S(1)} fusion(f32[32,64]{1,0:T(8,128)S(1)} %dynamic-slice_bitcast_fusion.12, f32[32,4096]{1,0:T(8,128)S(1)} %dynamic-slice_bitcast_fusion.13), kind=kLoop, calls=%fused_computation.clone.1 | loop fusion | flops 25163776 | bytes 540672 | tf_op jit(solution)/shard_map/while/body/eval_jaxpr/reduce_sum | solution.py:25
  125.5 0.2 select_reduce_fusion.5
  126.0 9.4 %while.31 = (s32[]{:T(128)}, s32[2,32,64]{2,1,0:T(8,128)S(1)}, f32[2,32,4096]{2,1,0:T(8,128)}, f32[2,32,64]{2,1,0:T(8,128)S(1)}, s32[]{:T(128)}) while((s32[]{:T(128)}, s32[2,32,64]{2,1,0:T(8,128)S(1)}, f32[2,32,4096]{2,1,0:T(8,128)}, f32[2,32,64]{2,1,0:T(8,128)S(1)}, s32[]{:T(128)}) %tuple.70), condition=%wide.region_9.10_spmd, body=%wide.region_7.9_spmd.sunk | while | flops 25163776 | bytes 1638481 | solution.py:27
  126.0 1.1 dynamic-slice_bitcast_fusion.15
  127.1 3.6 %convert_reduce_fusion.11 = s32[32,64]{1,0:T(8,128)S(1)} fusion(f32[32,64]{1,0:T(8,128)S(1)} %dynamic-slice_bitcast_fusion.14, f32[32,4096]{1,0:T(8,128)S(1)} %dynamic-slice_bitcast_fusion.15), kind=kLoop, calls=%fused_computation.4.clone.1 | loop fusion | flops 25163776 | bytes 540672 | tf_op jit(solution)/shard_map/while/body/eval_jaxpr/reduce_sum | solution.py:25
  130.7 1.1 dynamic-slice_bitcast_fusion.15
  131.8 3.6 %convert_reduce_fusion.11 = s32[32,64]{1,0:T(8,128)S(1)} fusion(f32[32,64]{1,0:T(8,128)S(1)} %dynamic-slice_bitcast_fusion.14, f32[32,4096]{1,0:T(8,128)S(1)} %dynamic-slice_bitcast_fusion.15), kind=kLoop, calls=%fused_computation.4.clone.1 | loop fusion | flops 25163776 | bytes 540672 | tf_op jit(solution)/shard_map/while/body/eval_jaxpr/reduce_sum | solution.py:25
  135.4 0.2 convert_reduce_fusion.5
  135.7 0.2 select_reduce_fusion.3
  136.2 9.4 %while.32 = (s32[]{:T(128)}, s32[2,32,64]{2,1,0:T(8,128)S(1)}, f32[2,32,4096]{2,1,0:T(8,128)}, f32[2,32,64]{2,1,0:T(8,128)S(1)}, s32[]{:T(128)}) while((s32[]{:T(128)}, s32[2,32,64]{2,1,0:T(8,128)S(1)}, f32[2,32,4096]{2,1,0:T(8,128)}, f32[2,32,64]{2,1,0:T(8,128)S(1)}, s32[]{:T(128)}) %tuple.71), condition=%wide.region_15.16_spmd, body=%wide.region_13.15_spmd.sunk | while | flops 25163776 | bytes 1638481 | solution.py:27
  136.2 1.1 dynamic-slice_bitcast_fusion.17
  137.3 3.6 %convert_reduce_fusion.12 = s32[32,64]{1,0:T(8,128)S(1)} fusion(f32[32,64]{1,0:T(8,128)S(1)} %dynamic-slice_bitcast_fusion.16, f32[32,4096]{1,0:T(8,128)S(1)} %dynamic-slice_bitcast_fusion.17), kind=kLoop, calls=%fused_computation.8.clone.1 | loop fusion | flops 25163776 | bytes 540672 | tf_op jit(solution)/shard_map/while/body/eval_jaxpr/reduce_sum | solution.py:25
  140.9 1.1 dynamic-slice_bitcast_fusion.17
  142.0 3.6 %convert_reduce_fusion.12 = s32[32,64]{1,0:T(8,128)S(1)} fusion(f32[32,64]{1,0:T(8,128)S(1)} %dynamic-slice_bitcast_fusion.16, f32[32,4096]{1,0:T(8,128)S(1)} %dynamic-slice_bitcast_fusion.17), kind=kLoop, calls=%fused_computation.8.clone.1 | loop fusion | flops 25163776 | bytes 540672 | tf_op jit(solution)/shard_map/while/body/eval_jaxpr/reduce_sum | solution.py:25
  145.9 0.2 select_reduce_fusion
  146.2 8.9 %all_gather.11 = bf16[512,256]{0,1:T(8,128)(2,1)S(1)} all-gather(bf16[512,64]{0,1:T(8,128)(2,1)S(1)} %divide_convert_fusion), channel_id=1, replica_groups=mesh['scen'=8,'inst'=4] {'inst'}, dimensions={1}, use_global_device_ids=true | all-gather | bytes 327680 | tf_op jit(solution)/shard_map/all_gather | solution.py:69
  155.2 7.4 %fusion.3 = f32[256,4096]{1,0:T(8,128)} fusion(bf16[512,256]{0,1:T(8,128)(2,1)S(1)} %all_gather.11, f32[512,4096]{1,0:T(8,128)} %copy-done.9, f32[4096]{0:T(1024)S(1)} %copy-done.5, f32[4096]{0:T(1024)S(1)} %copy-done.6, f32[4096]{0:T(1024)S(1)} %copy-done.7), kind=kOutput, calls=%fused_computation.55 | convolution fusion | flops 1086324736 | bytes 12894208 | tf_op jit(solution)/shard_map/dot_general | solution.py:73
  162.7 13.8 %psum.7 = f32[256]{0:T(256)S(1)} all-reduce(f32[256]{0:T(256)S(1)} %convert_reduce_fusion.3), channel_id=1, replica_groups=mesh['scen'=8,'inst'=4] {'scen'}, use_global_device_ids=true, to_apply=%region_21.22 | all-reduce | flops 256 | bytes 2048 | tf_op jit(solution)/shard_map/psum | solution.py:70
  176.6 35.0 %reduce-scatter.5.cloned.1.call-done = f32[32,4096]{1,0:T(8,128)} async-done(((f32[256,4096]{1,0:T(8,128)}), f32[32,4096]{1,0:T(8,128)}) %reduce-scatter.5.cloned.1.call-update) | async-done | bytes 524304 | tf_op jit(solution)/shard_map/reduce_scatter | solution.py:72
  211.6 1.9 broadcast_divide_fusion
  (72 shorter events, 2.3 us)
Async XLA Ops:
  7.2 40.6 %all-gather.3.cloned.1.call-start = ((), (), s32[]{:S(2)}) async-start(), calls=%async_computation.2 | async-start | bytes 2621440 | tf_op jit(solution)/shard_map/all_gather | solution.py:52
  7.9 55.3 %copy-start.4 = (s32[4096]{0:T(1024)S(1)}, s32[4096]{0:T(1024)}, u32[]{:S(2)}) copy-start(s32[4096]{0:T(1024)} %param.20) | copy-start | bytes 49156
  7.9 55.3 %copy-start.5 = (f32[4096]{0:T(1024)S(1)}, f32[4096]{0:T(1024)}, u32[]{:S(2)}) copy-start(f32[4096]{0:T(1024)} %param.19) | copy-start | bytes 49156
  7.9 55.3 %copy-start.6 = (f32[4096]{0:T(1024)S(1)}, f32[4096]{0:T(1024)}, u32[]{:S(2)}) copy-start(f32[4096]{0:T(1024)} %param.18) | copy-start | bytes 49156
  7.9 55.3 %copy-start.7 = (f32[4096]{0:T(1024)S(1)}, f32[4096]{0:T(1024)}, u32[]{:S(2)}) copy-start(f32[4096]{0:T(1024)} %param.17) | copy-start | bytes 49156
  7.9 84.1 %reduce-scatter.3.cloned.1.call-start = ((), (), s32[]{:S(2)}) async-start(), calls=%async_computation.3 | async-start | bytes 655360 | tf_op jit(solution)/shard_map/reduce_scatter | solution.py:65
  60.0 3.2 %copy-start.9 = (f32[512,4096]{1,0:T(8,128)}, f32[512,4096]{1,0:T(8,128)S(1)}, u32[]{:S(2)}) copy-start(f32[512,4096]{1,0:T(8,128)S(1)} %fusion.4) | copy-start | bytes 25165828
  63.2 29.0 %copy-start.8 = (s32[256]{0:T(256)S(1)}, s32[256]{0:T(256)}, u32[]{:S(2)}) copy-start(s32[256]{0:T(256)} %param.23) | copy-start | bytes 3076
  63.2 29.2 %copy-start.2 = (s32[256]{0:T(256)S(1)}, s32[256]{0:T(256)}, u32[]{:S(2)}) copy-start(s32[256]{0:T(256)} %param.21) | copy-start | bytes 3076
  63.3 29.2 %copy-start.3 = (s32[256]{0:T(256)S(1)}, s32[256]{0:T(256)}, u32[]{:S(2)}) copy-start(s32[256]{0:T(256)} %param.22) | copy-start | bytes 3076
  67.0 48.8 %all-gather.5.cloned.1.call-start = ((), (), s32[]{:S(2)}) async-start(), calls=%async_computation.4 | async-start | bytes 1179648 | tf_op jit(solution)/shard_map/all_gather | solution.py:66
  92.0 119.6 %reduce-scatter.5.cloned.1.call-start = ((), (), s32[]{:S(2)}) async-start(), calls=%async_computation.5 | async-start | bytes 4718592 | tf_op jit(solution)/shard_map/reduce_scatter | solution.py:72
  126.0 20.1 %copy-start = (f32[512,64]{0,1:T(8,128)S(1)}, f32[512,64]{0,1:T(8,128)}, u32[]{:S(2)}) copy-start(f32[512,64]{0,1:T(8,128)} %reduce-scatter.3.cloned.1.call-done) | copy-start | bytes 393220
  146.1 16.5 %copy-start.1 = (f32[64]{0:T(128)}, f32[64]{0:T(128)S(1)}, u32[]{:S(2)}) copy-start(f32[64]{0:T(128)S(1)} %add_multiply_fusion) | copy-start | bytes 772
Sparse Core Ops, SparseCore 0:
  9.8 37.8 all-gather.2
  67.2 24.7 reduce-scatter.2
  93.7 22.0 all-gather.4
  162.7 48.8 reduce-scatter.4
where the time goes:
time: 221 us; the launch traced here: 220 us
  waiting for transfers between devices  123 us (56%)
  other arithmetic  25.1 us (11%)
  matrix products  23.4 us (11%)
  blocking collectives  22.8 us (10%)
  between operations  14 us (6%)
  local copies, waits for them, and re-layouts  10.9 us (5%)
    all_gather x1, waiting for transfers between devices, body(): lax.all_gather(shocks, 'inst', axis=1, tiled=True)  39.7 us
    reduce_scatter x1, waiting for transfers between devices, body(): lax.psum_scatter(lax.dot_general(weights, profit, (((0,), (0,)), ((), ())...  35 us
    reduce_scatter x1, waiting for transfers between devices, body(): lax.psum_scatter(partial_sums, 'inst', scatter_dimension=1, tiled=True)  24.9 us
    all_gather x1, waiting for transfers between devices, body(): every_pnl = lax.all_gather(own_pnl, 'scen', axis=0, tiled=True)  23 us
    reduce_sum x6, other arithmetic, one_block(): jnp.sum((values[:, :, None] <= marks[:, None, :]).astype(jnp.int32), axis=1)  21.4 us
    psum x1, blocking collectives, body(): mass = lax.psum(jnp.sum(weights.astype(jnp.float32), axis=0), 'scen')  13.8 us
    dot_general x1, matrix products, body(): jnp.dot(lax.all_gather(shocks, 'inst', axis=1, tiled=True), loadings, pre...  12.3 us
    all_gather x1, blocking collectives, body(): weights = lax.all_gather(own_weights, 'inst', axis=1, tiled=True)  8.94 us
  transfers between devices with their start and end apart: 4, of which 4 were waited for; matrix products, arithmetic and copies ran while one was open for 0% of the time, Pallas kernels for 0%

commit v1 on v0

v1 whole, which is shorter than its diff:
```python
import functools

import jax
import jax.numpy as jnp
from jax import lax
from jax.experimental import pallas as pl
from jax.experimental.pallas import tpu as pltpu
from jax.sharding import PartitionSpec as P

PIVOTS = 64
ROUNDS = 3
CORES = 2
LANES = 128

tail_width = 0.5
bracket_unit = 0.125
code_top = 65535.0
code_mid = 32768.0
top16 = 32600.0
octave = 0.6931471805599453
finest = 8.0
half_word = 16384.0

BF16 = jnp.bfloat16
F32 = jnp.float32


def params(megabytes):
    return pltpu.CompilerParams(vmem_limit_bytes=megabytes * 2**20)


def dot(a, b):
    return jnp.dot(a, b, preferred_element_type=F32)


def dot_nt(a, b):
    return lax.dot_general(a, b, (((1,), (1,)), ((), ())), preferred_element_type=F32)


def swap(value, axis, flip):
    n = lax.axis_size(axis)
    return lax.ppermute(value, axis, [(k, k ^ flip) for k in range(n)])


def first_moves_kernel(count, where_ref, *refs):
    shock_refs, load_refs, out_ref = refs[:count], refs[count : 2 * count], refs[2 * count]
    total = dot(shock_refs[0][...], load_refs[0][...])
    for shock_ref, load_ref in zip(shock_refs[1:], load_refs[1:]):
        total = total + dot(shock_ref[...], load_ref[...])
    out_ref[...] = total


def first_moves(where, shocks, flips, loadings, tile):
    rows, depth = shocks[0].shape
    cols = loadings.shape[1]
    count = len(shocks)
    steps = cols // tile
    col_of = functools.partial(column_tile, steps)
    specs = [pl.BlockSpec((rows, depth), lambda n, w: (0, 0)) for _ in shocks]
    specs += [
        pl.BlockSpec((depth, tile), lambda n, w, f=f: (w[0] ^ f, col_of(n, w))) for f in flips
    ]
    return pl.pallas_call(
        functools.partial(first_moves_kernel, count),
        out_shape=jax.ShapeDtypeStruct((rows, cols), F32),
        grid_spec=pltpu.PrefetchScalarGridSpec(
            num_scalar_prefetch=1,
            grid=(steps,),
            in_specs=specs,
            out_specs=pl.BlockSpec((rows, tile), lambda n, w: (0, n)),
        ),
        compiler_params=params(48),
        cost_estimate=pl.CostEstimate(
            flops=2 * rows * depth * cols * count,
            bytes_accessed=2 * depth * cols * count + 4 * rows * cols,
            transcendentals=0,
        ),
        name="first_moves",
    )(where, *shocks, *([loadings] * count))


def column_tile(steps, n, where_ref):
    return lax.rem(n + (1 - where_ref[1]) * (steps // CORES), steps)


def profit_kernel(count, slots, where_ref, *refs):
    top_refs, low_refs, load_refs = refs[:count], refs[count : 2 * count], refs[2 * count : 3 * count]
    first_ref, delta_ref, gamma_ref, kappa_ref, book_ref = refs[3 * count : 3 * count + 5]
    mine_ref, theirs_ref = refs[3 * count + 5 : 3 * count + 7]
    sum_refs = refs[3 * count + 7 :]
    step = pl.program_id(0)
    share = sum_refs[0].shape[0]
    half = top_refs[0].shape[0]
    tile = first_ref.shape[1]

    @pl.when(step == 0)
    def _():
        for sum_ref in sum_refs:
            sum_ref[...] = jnp.zeros_like(sum_ref)

    parts = []
    for at, shock_refs in ((0, top_refs), (half, low_refs)):
        moves = first_ref[at : at + half, :]
        for shock_ref, load_ref in zip(shock_refs, load_refs):
            moves = moves + dot(shock_ref[...], load_ref[...])
        value = moves * (delta_ref[...] + moves * (gamma_ref[...] + moves * kappa_ref[...]))
        parts.append(value.astype(BF16))
    profit = jnp.concatenate(parts, axis=0)

    @pl.when(step < pl.num_programs(0) // CORES)
    def _():
        theirs_ref[...] = profit

    @pl.when(step >= pl.num_programs(0) // CORES)
    def _():
        mine_ref[...] = profit

    row = lax.broadcasted_iota(jnp.int32, (share, tile), 0)
    for slot in range(slots):
        start = (where_ref[0] ^ slot) * share
        onehot = jnp.where(row + start == book_ref[...], 1.0, 0.0).astype(BF16)
        sum_refs[slot][...] += dot_nt(onehot, profit)


def profits(where, tops, lows, flips, loadings, first, delta, gamma, kappa, book_of, slots, books, tile):
    half, depth = tops[0].shape
    rows, cols = first.shape
    count = len(tops)
    steps = cols // tile
    col_of = functools.partial(column_tile, steps)
    share = books // slots
    line = pl.BlockSpec((1, tile), lambda n, w: (0, col_of(n, w)))
    specs = [pl.BlockSpec((half, depth), lambda n, w: (0, 0)) for _ in range(2 * count)]
    specs += [
        pl.BlockSpec((depth, tile), lambda n, w, f=f: (w[0] ^ f, col_of(n, w))) for f in flips
    ]
    specs += [pl.BlockSpec((rows, tile), lambda n, w: (0, n)), line, line, line, line]
    part = steps // CORES
    out_specs = [
        pl.BlockSpec((rows, tile), lambda n, w: (0, jnp.maximum(n - part, 0))),
        pl.BlockSpec((rows, tile), lambda n, w: (0, jnp.minimum(n, part - 1))),
    ]
    out_specs += [pl.BlockSpec((share, rows), lambda n, w: (0, 0)) for _ in range(slots)]
    out_shape = [jax.ShapeDtypeStruct((rows, cols // CORES), BF16)] * 2
    out_shape += [jax.ShapeDtypeStruct((share, rows), F32)] * slots
    return pl.pallas_call(
        functools.partial(profit_kernel, count, slots),
        out_shape=out_shape,
        grid_spec=pltpu.PrefetchScalarGridSpec(
            num_scalar_prefetch=1, grid=(steps,), in_specs=specs, out_specs=out_specs
        ),
        compiler_params=params(48),
        cost_estimate=pl.CostEstimate(
            flops=2 * rows * cols * (depth * count + books),
            bytes_accessed=2 * depth * cols * count + 6 * rows * cols,
            transcendentals=0,
        ),
        name="profits",
    )(where, *tops, *lows, *([loadings] * count), first, delta, gamma, kappa, book_of)


def gather_and_revalue(where, shocks, loadings, delta, gamma, kappa, book_of, books):
    slots = lax.axis_size("inst")
    inner = 1
    while inner * inner * 4 <= slots:
        inner *= 2
    outer = slots // inner
    rows = shocks.shape[0]
    half = rows // 2
    along = [f for f in range(1, inner)]
    across = [f * inner for f in range(1, outer)]
    near = {f: swap(shocks, "inst", f) for f in along + across}
    corners = [(a, b) for a in along for b in across]
    tops = [swap(near[a][:half], "inst", b) for a, b in corners]
    lows = [swap(near[b][half:], "inst", a) for a, b in corners]
    flips = [0] + along + across
    first = first_moves(where, [shocks] + [near[f] for f in along + across], flips, loadings, 512)
    return profits(
        where, tops, lows, [a ^ b for a, b in corners], loadings, first, delta, gamma, kappa, book_of, slots, books, 512
    )


def book_value_kernel(scale, low_ref, high_ref, *refs):
    part_refs, (value_ref, code_ref) = refs[:-2], refs[-2:]
    value = part_refs[0][...]
    for part_ref in part_refs[1:]:
        value = value + part_ref[...]
    value = value * scale
    value_ref[...] = value
    low = low_ref[...].astype(F32) * bracket_unit
    high = high_ref[...].astype(F32) * bracket_unit
    code = (value - low) * (code_top / (high - low))
    code = jnp.minimum(jnp.maximum(code, 0.0), code_top)
    code_ref[...] = (jnp.round(code) - code_mid).astype(jnp.int32).astype(jnp.int16)


def book_values(scale, low, high, parts):
    share, rows = parts[0].shape
    return pl.pallas_call(
        functools.partial(book_value_kernel, scale),
        out_shape=[
            jax.ShapeDtypeStruct((share, rows), F32),
            jax.ShapeDtypeStruct((share, rows), jnp.int16),
        ],
        compiler_params=params(16),
        name="book_values",
    )(low, high, *parts)


def quantile_kernel(low_ref, high_ref, rank_ref, value_ref, *refs):
    code_refs, (weight_ref, quantile_ref, held) = refs[:-3], refs[-3:]
    share, rows = value_ref.shape
    for at, code_ref in enumerate(code_refs):
        held[:, at * rows : (at + 1) * rows] = code_ref[...].astype(F32)
    width = held.shape[1]
    low = low_ref[...].astype(F32) * bracket_unit
    high = high_ref[...].astype(F32) * bracket_unit
    rank = rank_ref[...].astype(F32)
    per_unit = code_top / (high - low)
    lower, upper = low, high
    for _ in range(ROUNDS):
        spacing = (upper - lower) / (PIVOTS - 1)
        below = jnp.zeros_like(low)
        stride = PIVOTS // 2
        while stride:
            pivot = lower + (below + (stride - 1)) * spacing
            mark = jnp.floor((pivot - low) * per_unit) - code_mid
            mark = jnp.broadcast_to(mark, (share, LANES))
            count = jnp.zeros((share, LANES), F32)
            for at in range(0, width, LANES):
                count = count + jnp.where(held[:, at : at + LANES] <= mark, 1.0, 0.0)
            count = jnp.sum(count, axis=1, keepdims=True)
            below = below + jnp.where(count < rank, float(stride), 0.0)
            stride //= 2
        chosen = jnp.clip(below, 1.0, float(PIVOTS - 1))
        lower, upper = lower + (chosen - 1.0) * spacing, lower + chosen * spacing
    quantile = (lower + upper) * 0.5
    quantile_ref[...] = quantile
    weight_ref[...] = jax.nn.sigmoid((quantile - value_ref[...]) / tail_width).astype(BF16)


def quantiles(low, high, rank, value, codes):
    share, rows = value.shape
    return pl.pallas_call(
        quantile_kernel,
        out_shape=[
            jax.ShapeDtypeStruct((share, rows), BF16),
            jax.ShapeDtypeStruct((share, 1), F32),
        ],
        scratch_shapes=[pltpu.VMEM((share, rows * len(codes)), F32)],
        compiler_params=params(16),
        name="quantiles",
    )(low, high, rank, value, *codes)


def encode(total, mass):
    top = jnp.maximum(jnp.max(jnp.abs(total), axis=1, keepdims=True), 1e-30)
    level = jnp.ceil(jnp.log(top * (1.0 / top16)) * (finest / octave))
    words = jnp.round(total * jnp.exp(level * (-octave / finest)))
    mass = jnp.maximum(mass, 1e-30)
    power = jnp.ceil(jnp.log(mass) * (1.0 / octave))
    scaled = mass * jnp.exp(power * -octave) * half_word
    upper = jnp.floor(scaled)
    lower = jnp.round((scaled - upper) * half_word)
    column = lax.broadcasted_iota(jnp.int32, (total.shape[0], LANES), 1)
    side = jnp.where(column == 0, level, 0.0)
    side = jnp.where(column == 1, power, side)
    side = jnp.where(column == 2, upper, side)
    side = jnp.where(column == 3, lower, side)
    return words.astype(jnp.int32).astype(jnp.int16), side.astype(jnp.int32).astype(jnp.int16)


def put_words(ref, total, mass):
    words, side = encode(total, mass)
    cols = total.shape[1]
    ref[:, :cols] = words
    ref[:, cols:] = side


def get_words(ref):
    cols = ref.shape[1] - LANES
    side = ref[:, cols:].astype(F32)
    level, power, upper, lower = (side[:, k : k + 1] for k in range(4))
    mass = (upper + lower * (1.0 / half_word)) * (1.0 / half_word) * jnp.exp(power * octave)
    total = ref[:, :cols].astype(F32) * jnp.exp(level * (octave / finest))
    return total, mass


def put_plain(ref, total, mass):
    cols = total.shape[1]
    ref[:, :cols] = total
    ref[:, cols:] = jnp.broadcast_to(mass, (total.shape[0], LANES))


def get_plain(ref):
    cols = ref.shape[1] - LANES
    return ref[:, :cols], ref[:, cols : cols + 1]


def tail_kernel(slots, lines, where_ref, *refs):
    count = CORES * slots
    weight_refs = refs[:count]
    profit_refs = refs[count : count + CORES]
    away_ref, partner_ref, handled_ref, own_ref, held, total = refs[count + CORES :]
    step = pl.program_id(0)
    share, rows = weight_refs[0].shape
    books = share * slots
    block = books // lines
    piece = min(share, block)
    tile = profit_refs[0].shape[1]

    @pl.when(step == 0)
    def _():
        for core in range(CORES):
            for slot in range(slots):
                ref = weight_refs[core * slots + slot]
                for at in range(0, share, piece):
                    start = (where_ref[0] ^ slot) * share + at
                    line = start // block
                    to = (where_ref[2] ^ line) * block + (start - line * block)
                    to = pl.multiple_of(to, piece)
                    held[pl.ds(to, piece), core * rows : (core + 1) * rows] = ref[at : at + piece, :]

    spot = pl.multiple_of(step * tile, tile)
    result = dot(held[:, :rows], profit_refs[0][...])
    total[:, pl.ds(spot, tile)] = result + dot(held[:, rows:], profit_refs[1][...])

    @pl.when(step == pl.num_programs(0) - 1)
    def _():
        for line in range(lines):
            at = line * block
            value = total[at : at + block, :]
            mass = jnp.sum(held[at : at + block, :].astype(F32), axis=1, keepdims=True)
            to = (line // 2 - 1) * block
            if line == 0:
                put_plain(own_ref, value, mass)
            elif line == 1:
                put_words(partner_ref, value, mass)
            elif line % 2 == 0:
                put_words(away_ref.at[to : to + block], value, mass)
            else:
                put_plain(handled_ref.at[to : to + block], value, mass)


def tail_sums(where, weights, profit_pair, slots, lines, tile):
    share, rows = weights[0].shape
    cols = profit_pair[0].shape[1]
    books = share * slots
    block = books // lines
    others = lines // 2 - 1
    wide = cols + LANES
    specs = [pl.BlockSpec((share, rows), lambda n, w: (0, 0)) for _ in weights]
    specs += [pl.BlockSpec((rows, tile), lambda n, w: (0, n)) for _ in profit_pair]
    shapes = [
        ((others * block, wide), jnp.int16),
        ((block, wide), jnp.int16),
        ((others * block, wide), F32),
        ((block, wide), F32),
    ]
    return pl.pallas_call(
        functools.partial(tail_kernel, slots, lines),
        out_shape=[jax.ShapeDtypeStruct(*shape) for shape in shapes],
        grid_spec=pltpu.PrefetchScalarGridSpec(
            num_scalar_prefetch=1,
            grid=(cols // tile,),
            in_specs=specs,
            out_specs=[pl.BlockSpec(shape, lambda n, w: (0, 0)) for shape, _ in shapes],
            scratch_shapes=[
                pltpu.VMEM((books, CORES * rows), BF16),
                pltpu.VMEM((books, cols), F32),
            ],
        ),
        compiler_params=params(48),
        name="tail_sums",
    )(where, *weights, *profit_pair)


def relay_kernel(words_ref, plain_ref, out_ref):
    total, mass = get_words(words_ref)
    own_total, own_mass = get_plain(plain_ref)
    put_words(out_ref, total + own_total, mass + own_mass)


def relay(words, plain):
    return pl.pallas_call(
        relay_kernel,
        out_shape=jax.ShapeDtypeStruct(words.shape, jnp.int16),
        compiler_params=params(16),
        name="relay",
    )(words, plain)


def finish_kernel(where_ref, plain_ref, *refs):
    words_refs, (keep_ref, give_ref, held) = refs[:-3], refs[-3:]
    total, mass = get_plain(plain_ref)
    for words_ref in words_refs:
        more, more_mass = get_words(words_ref)
        total, mass = total + more, mass + more_mass
    held[...] = total / mass
    rows = keep_ref.shape[0]
    keep_ref[...] = held[pl.ds(pl.multiple_of(where_ref[1] * rows, rows), rows), :]
    give_ref[...] = held[pl.ds(pl.multiple_of((1 - where_ref[1]) * rows, rows), rows), :]


def finish(where, plain, words):
    block, wide = plain.shape
    cols = wide - LANES
    vmem = pl.BlockSpec(memory_space=pltpu.VMEM)
    return pl.pallas_call(
        finish_kernel,
        out_shape=[jax.ShapeDtypeStruct((block // CORES, cols), F32)] * 2,
        in_specs=[pl.BlockSpec(memory_space=pltpu.SMEM)] + [vmem] * (1 + len(words)),
        out_specs=[vmem] * 2,
        scratch_shapes=[pltpu.VMEM((block, cols), F32)],
        compiler_params=params(16),
        name="finish",
    )(where, plain, *words)


def body(shocks, loadings, delta, gamma, kappa, book_of, bracket_low, bracket_high, rank):
    inst_cols = loadings.shape[1]
    books = bracket_low.shape[0]
    slots = lax.axis_size("inst")
    lines = lax.axis_size("scen") // CORES
    share = books // slots
    scale = (books / (inst_cols * slots)) ** 0.5
    inst = lax.axis_index("inst")
    scen = lax.axis_index("scen")
    core, line = scen % CORES, scen // CORES
    where = jnp.stack([inst, core, line]).astype(jnp.int32)

    mine, theirs, *sums = gather_and_revalue(
        where,
        shocks,
        loadings,
        delta[None, :],
        gamma[None, :],
        kappa[None, :],
        book_of[None, :],
        books,
    )
    got = swap(theirs, "scen", 1)

    own = lambda v: lax.dynamic_slice_in_dim(v, inst * share, share, 0)[:, None]
    low, high, own_rank = own(bracket_low), own(bracket_high), own(rank)
    parts = [sums[0]] + [swap(sums[slot], "inst", slot) for slot in range(1, slots)]
    value, code = book_values(scale, low, high, parts)
    codes = [code] + [swap(code, "scen", CORES * k) for k in range(1, lines)]
    codes = codes + [swap(c, "scen", 1) for c in codes]
    weight, quantile = quantiles(low, high, own_rank, value, codes)
    weights = [weight] + [swap(weight, "inst", slot) for slot in range(1, slots)]
    others = [swap(w, "scen", 1) for w in weights]

    away, partner, handled, plain = tail_sums(where, weights + others, [mine, got], slots, lines, 512)
    passed = swap(away, "scen", CORES)
    from_partner = swap(partner, "scen", CORES)
    sent = relay(passed, handled)
    block = books // lines
    words = [from_partner]
    for k in range(1, lines // 2):
        words.append(swap(sent[(k - 1) * block : k * block], "scen", CORES * (2 * k + 1)))
    keep, give = finish(where, plain, words)
    taken = swap(give, "scen", 1)
    left = jnp.where(core == 0, keep, taken)
    right = jnp.where(core == 0, taken, keep)
    return jnp.concatenate([left, right], axis=1), quantile[:, 0]


def solution(mesh):
    placed = (
        P("scen", "inst"),
        P(None, "inst"),
        P("inst"),
        P("inst"),
        P("inst"),
        P("inst"),
        P(),
        P(),
        P(),
    )
    return jax.shard_map(
        body, mesh=mesh, in_specs=placed, out_specs=(P("scen", "inst"), P("inst")), check_vma=False
    )
```

time: 221 us -> 111 us (0.50)
  waiting for transfers between devices: 123 us -> 45.4 us
  Pallas kernels: 0 us -> 37.3 us
  other arithmetic: 25.1 us -> 1.57 us
  matrix products: 23.4 us -> 0 us
  starting transfers between devices: 0.34 us -> 23.5 us
  blocking collectives: 22.8 us -> 0 us
  between operations: 14 us -> 0.81 us
  local copies, waits for them, and re-layouts: 10.9 us -> 1.55 us
    all_gather x2 -> x0, waiting for transfers between devices: 62.8 us -> none  [the longest x1 39.7 us: body(): lax.all_gather(shocks, 'inst', axis=1, tiled=True)]
    reduce_scatter x2 -> x0, waiting for transfers between devices: 59.9 us -> none  [the longest x1 35 us: body(): lax.psum_scatter(lax.dot_general(weights, profit, (((0,), (0,)), ((), ())...]
    ppermute x0 -> x26, waiting for transfers between devices: none -> 45.4 us  [swap(): return lax.ppermute(value, axis, [(k, k ^ flip) for k in range(n)])]
    pallas_call x0 -> x7, Pallas kernels: none -> 37.3 us  [the longest x1 14.3 us: profits(): pl.pallas_call(functools.partial(profit_kernel, count, slots), out_shape=...]
    ppermute x0 -> x26, starting transfers between devices: none -> 23.5 us  [swap(): return lax.ppermute(value, axis, [(k, k ^ flip) for k in range(n)])]
    dot_general x3 -> x0, matrix products: 23.4 us -> none  [the longest x1 12.3 us: body(): jnp.dot(lax.all_gather(shocks, 'inst', axis=1, tiled=True), loadings, pre...]
    reduce_sum x13 -> x0, other arithmetic: 22.6 us -> none  [the longest x6 21.4 us: one_block(): jnp.sum((values[:, :, None] <= marks[:, None, :]).astype(jnp.int32), axis=1)]
    psum x1 -> x0, blocking collectives: 13.8 us -> none  [body(): mass = lax.psum(jnp.sum(weights.astype(jnp.float32), axis=0), 'scen')]
  transfers between devices with their start and end apart: 4 -> 26, of which waited for: 4 -> 15; matrix products, arithmetic and copies ran while one was open for 0% -> 1% of each run, Pallas kernels for 0% -> 16%
where the time goes in v1:
time: 111 us; the launch traced here: 110 us
  waiting for transfers between devices  45.4 us (41%)
  Pallas kernels  37.3 us (34%)
  starting transfers between devices  23.5 us (21%)
  other arithmetic  1.57 us (1%)
  local copies, waits for them, and re-layouts  1.55 us (1%)
    ppermute x26, waiting for transfers between devices, swap(): return lax.ppermute(value, axis, [(k, k ^ flip) for k in range(n)])  45.4 us
    ppermute x26, starting transfers between devices, swap(): return lax.ppermute(value, axis, [(k, k ^ flip) for k in range(n)])  23.5 us
    pallas_call x1, Pallas kernels, profits(): pl.pallas_call(functools.partial(profit_kernel, count, slots), out_shape=...  14.3 us
    pallas_call x1, Pallas kernels, first_moves(): pl.pallas_call(functools.partial(first_moves_kernel, count), out_shape=ja...  13.6 us
    pallas_call x1, Pallas kernels, tail_sums(): pl.pallas_call(functools.partial(tail_kernel, slots, lines), out_shape=[j...  4.51 us
    pallas_call x1, Pallas kernels, quantiles(): pl.pallas_call(quantile_kernel, out_shape=[jax.ShapeDtypeStruct((share, r...  3.71 us
  transfers between devices with their start and end apart: 26, of which 15 were waited for; matrix products, arithmetic and copies ran while one was open for 1% of the time, Pallas kernels for 16%

profile of v1, /device:TPU:0, one launch (start us, length us, event | category | flops | bytes accessed | tf_op | source)
XLA Modules:
  0.0 110.2 jit_solution(15959461084193285976)
XLA Ops:
  0.6 3.0 %collective-permute-start = (bf16[512,512]{1,0:T(8,128)(2,1)}, bf16[512,512]{1,0:T(8,128)(2,1)S(1)}, u32[]{:S(2)}, u32[]{:S(2)}) collective-permute-start(bf16[512,512]{1,0:T(8,128)(2,1)} %refs_0_.1), channel_id=1, source_target_pairs={{0,1},{1,0},{2,3},{3,2},{4,5},{5,4},{6,7},{7,6},{8,9},{9,8},{10,11... | collective-permute-start | bytes 1572872 | tf_op jit(solution)/shard_map/ppermute | solution.py:42
  3.6 1.5 %collective-permute-start.2 = (bf16[512,512]{1,0:T(8,128)(2,1)}, bf16[512,512]{1,0:T(8,128)(2,1)S(1)}, u32[]{:S(2)}, u32[]{:S(2)}) collective-permute-start(bf16[512,512]{1,0:T(8,128)(2,1)} %refs_0_.1), channel_id=1, source_target_pairs={{0,2},{1,3},{2,0},{3,1},{4,6},{5,7},{6,4},{7,5},{8,10},{9,11},{10,... | collective-permute-start | bytes 1572872 | tf_op jit(solution)/shard_map/ppermute | solution.py:42
  5.2 10.5 %collective-permute-done.refs_1_ = bf16[512,512]{1,0:T(8,128)(2,1)S(1)} collective-permute-done((bf16[512,512]{1,0:T(8,128)(2,1)}, bf16[512,512]{1,0:T(8,128)(2,1)S(1)}, u32[]{:S(2)}, u32[]{:S(2)}) %collective-permute-start) | collective-permute-done | bytes 524320 | tf_op jit(solution)/shard_map/ppermute | solution.py:42
  15.8 1.8 %collective-permute-start.1 = (bf16[256,512]{1,0:T(8,128)(2,1)S(1)}, bf16[256,512]{1,0:T(8,128)(2,1)S(1)}, u32[]{:S(2)}, u32[]{:S(2)}) collective-permute-start(bf16[256,512]{1,0:T(8,128)(2,1)S(1)} %slice.8), channel_id=1, source_target_pairs={{0,2},{1,3},{2,0},{3,1},{4,6},{5,7},{6,4},{7,5},{8,10},{9,11},{10,... | collective-permute-start | bytes 786440 | tf_op jit(solution)/shard_map/ppermute | solution.py:42
  17.7 1.6 %collective-permute-start.3 = (bf16[256,512]{1,0:T(8,128)(2,1)S(1)}, bf16[256,512]{1,0:T(8,128)(2,1)S(1)}, u32[]{:S(2)}, u32[]{:S(2)}) collective-permute-start(bf16[256,512]{1,0:T(8,128)(2,1)S(1)} %slice.9), channel_id=1, source_target_pairs={{0,1},{1,0},{2,3},{3,2},{4,5},{5,4},{6,7},{7,6},{8,9},{9,8},{10,11... | collective-permute-start | bytes 786440 | tf_op jit(solution)/shard_map/ppermute | solution.py:42
  19.2 1.0 copy-done.1
  20.3 13.6 %first_moves.1.refs_3_ = f32[512,4096]{1,0:T(8,128)} custom-call(s32[3]{0:T(128)S(1)} %pad_add_fusion.where_ref, bf16[512,512]{1,0:T(8,128)(2,1)S(1)} %copy-done.1, bf16[512,512]{1,0:T(8,128)(2,1)S(1)} %collective-permute-done.refs_1_, bf16[512,512]{1,0:T(8,128)(2,1)S(1)} %collective-permute-done.2.refs_2_, bf16[2048,4096]{1,0:T(8,128)(2,1)} %refs_2_.1, ...), custom_call_target="tpu_custom_call" | custom-call | flops 6442450944 | bytes 20971520 | tf_op jit(solution)/shard_map/first_moves/pallas_call | solution.py:63
  33.9 14.3 %profits.1 = (bf16[512,2048]{1,0:T(8,128)(2,1)S(1)}, bf16[512,2048]{1,0:T(8,128)(2,1)}, f32[64,512]{1,0:T(8,128)S(1)}, f32[64,512]{1,0:T(8,128)S(1)}, f32[64,512]{1,0:T(8,128)S(1)}, /*index=5*/f32[64,512]{1,0:T(8,128)S(1)}) custom-call(s32[3]{0:T(128)S(1)} %pad_add_fusion.where_ref, bf16[256,512]{1,0:T(8,128)(2,1)S(1)} %collective-permute-done.1.refs_0_, ...), custom_call_target="tpu_custom_call" | custom-call | flops 3221225472 | bytes 16777216 | tf_op jit(solution)/shard_map/profits/pallas_call | solution.py:146
  48.7 1.1 %collective-permute-start.5 = (f32[64,512]{1,0:T(8,128)S(1)}, f32[64,512]{1,0:T(8,128)S(1)}, u32[]{:S(2)}, u32[]{:S(2)}) collective-permute-start(f32[64,512]{1,0:T(8,128)S(1)} %get-tuple-element.20), channel_id=1, source_target_pairs={{0,2},{1,3},{2,0},{3,1},{4,6},{5,7},{6,4},{7,5},{8,10},{9,11},{10,... | collective-permute-start | bytes 393224 | tf_op jit(solution)/shard_map/ppermute | solution.py:42
  49.9 1.8 %collective-permute-start.6 = (f32[64,512]{1,0:T(8,128)S(1)}, f32[64,512]{1,0:T(8,128)S(1)}, u32[]{:S(2)}, u32[]{:S(2)}) collective-permute-start(f32[64,512]{1,0:T(8,128)S(1)} %get-tuple-element.21), channel_id=1, source_target_pairs={{0,3},{1,2},{2,1},{3,0},{4,7},{5,6},{6,5},{7,4},{8,11},{9,10},{10,... | collective-permute-start | bytes 393224 | tf_op jit(solution)/shard_map/ppermute | solution.py:42
  52.0 2.5 %collective-permute-done.4.refs_1_ = f32[64,512]{1,0:T(8,128)S(1)} collective-permute-done((f32[64,512]{1,0:T(8,128)S(1)}, f32[64,512]{1,0:T(8,128)S(1)}, u32[]{:S(2)}, u32[]{:S(2)}) %collective-permute-start.4) | collective-permute-done | bytes 131104 | tf_op jit(solution)/shard_map/ppermute | solution.py:42
  54.5 2.7 %collective-permute-done.5.refs_2_ = f32[64,512]{1,0:T(8,128)S(1)} collective-permute-done((f32[64,512]{1,0:T(8,128)S(1)}, f32[64,512]{1,0:T(8,128)S(1)}, u32[]{:S(2)}, u32[]{:S(2)}) %collective-permute-start.5) | collective-permute-done | bytes 131104 | tf_op jit(solution)/shard_map/ppermute | solution.py:42
  57.3 1.6 %collective-permute-start.7 = (s16[64,512]{1,0:T(8,128)(2,1)S(1)}, s16[64,512]{1,0:T(8,128)(2,1)S(1)}, u32[]{:S(2)}, u32[]{:S(2)}) collective-permute-start(s16[64,512]{1,0:T(8,128)(2,1)S(1)} %get-tuple-element.23.refs_0_), channel_id=1, source_target_pairs={{0,8},{4,12},{8,0},{12,4},{16,24},{20,28},{24,16},{28,20},{1,9},{5... | collective-permute-start | bytes 196616 | tf_op jit(solution)/shard_map/ppermute | solution.py:42
  58.9 2.6 %collective-permute-start.8 = (s16[64,512]{1,0:T(8,128)(2,1)S(1)}, s16[64,512]{1,0:T(8,128)(2,1)S(1)}, u32[]{:S(2)}, u32[]{:S(2)}) collective-permute-start(s16[64,512]{1,0:T(8,128)(2,1)S(1)} %get-tuple-element.23.refs_0_), channel_id=1, source_target_pairs={{0,16},{4,20},{8,24},{12,28},{16,0},{20,4},{24,8},{28,12},{1,17},{... | collective-permute-start | bytes 196616 | tf_op jit(solution)/shard_map/ppermute | solution.py:42
  62.3 3.6 %collective-permute-done.8.refs_2_ = s16[64,512]{1,0:T(8,128)(2,1)S(1)} collective-permute-done((s16[64,512]{1,0:T(8,128)(2,1)S(1)}, s16[64,512]{1,0:T(8,128)(2,1)S(1)}, u32[]{:S(2)}, u32[]{:S(2)}) %collective-permute-start.8) | collective-permute-done | bytes 65568 | tf_op jit(solution)/shard_map/ppermute | solution.py:42
  65.8 1.8 %collective-permute-done.9.refs_3_ = s16[64,512]{1,0:T(8,128)(2,1)S(1)} collective-permute-done((s16[64,512]{1,0:T(8,128)(2,1)S(1)}, s16[64,512]{1,0:T(8,128)(2,1)S(1)}, u32[]{:S(2)}, u32[]{:S(2)}) %collective-permute-start.9) | collective-permute-done | bytes 65568 | tf_op jit(solution)/shard_map/ppermute | solution.py:42
  67.8 1.1 collective-permute-done.13.refs_7_
  68.8 3.7 %quantiles.1 = (bf16[64,512]{1,0:T(8,128)(2,1)S(1)}, f32[64,1]{1,0:T(8,128)S(1)}) custom-call(s32[64,1]{1,0:T(8,128)S(1)} %copy.18.low_ref, s32[64,1]{1,0:T(8,128)S(1)} %copy.19.high_ref, s32[64,1]{1,0:T(8,128)S(1)} %copy.20.rank_ref, f32[64,512]{1,0:T(8,128)S(1)} %get-tuple-element.22.value_ref, s16[64,512]{1,0:T(8,128)(2,1)S(1)} %get-tuple-element.23.refs_0_, ...), custom_call_target="tpu_custom_call" | custom-call | tf_op jit(solution)/shard_map/quantiles/pallas_call | solution.py:244
  72.6 1.6 %collective-permute-start.14 = (bf16[64,512]{1,0:T(8,128)(2,1)S(1)}, bf16[64,512]{1,0:T(8,128)(2,1)S(1)}, u32[]{:S(2)}, u32[]{:S(2)}) collective-permute-start(bf16[64,512]{1,0:T(8,128)(2,1)S(1)} %get-tuple-element.24.refs_0_), channel_id=1, source_target_pairs={{0,1},{1,0},{2,3},{3,2},{4,5},{5,4},{6,7},{7,6},{8,9},{9,8},{10,11... | collective-permute-start | bytes 196616 | tf_op jit(solution)/shard_map/ppermute | solution.py:42
  74.6 1.5 %collective-permute-start.16 = (bf16[64,512]{1,0:T(8,128)(2,1)S(1)}, bf16[64,512]{1,0:T(8,128)(2,1)S(1)}, u32[]{:S(2)}, u32[]{:S(2)}) collective-permute-start(bf16[64,512]{1,0:T(8,128)(2,1)S(1)} %get-tuple-element.24.refs_0_), channel_id=1, source_target_pairs={{0,3},{1,2},{2,1},{3,0},{4,7},{5,6},{6,5},{7,4},{8,11},{9,10},{10,... | collective-permute-start | bytes 196616 | tf_op jit(solution)/shard_map/ppermute | solution.py:42
  76.1 0.8 collective-permute-done.14.refs_1_
  76.9 2.2 %collective-permute-done.15.refs_2_ = bf16[64,512]{1,0:T(8,128)(2,1)S(1)} collective-permute-done((bf16[64,512]{1,0:T(8,128)(2,1)S(1)}, bf16[64,512]{1,0:T(8,128)(2,1)S(1)}, u32[]{:S(2)}, u32[]{:S(2)}) %collective-permute-start.15) | collective-permute-done | bytes 65568 | tf_op jit(solution)/shard_map/ppermute | solution.py:42
  80.3 0.7 collective-permute-done.20.refs_7_
  81.1 4.5 %tail_sums.1 = (s16[64,2176]{1,0:T(8,128)(2,1)S(1)}, s16[64,2176]{1,0:T(8,128)(2,1)S(1)}, f32[64,2176]{1,0:T(8,128)S(1)}, f32[64,2176]{1,0:T(8,128)S(1)}) custom-call(s32[3]{0:T(128)S(1)} %pad_add_fusion.where_ref, bf16[64,512]{1,0:T(8,128)(2,1)S(1)} %get-tuple-element.24.refs_0_, bf16[64,512]{1,0:T(8,128)(2,1)S(1)} %collective-permute-done.14.refs_1_, ...), custom_call_target="tpu_custom_call" | custom-call | tf_op jit(solution)/shard_map/tail_sums/pallas_call | solution.py:360
  85.6 2.0 %collective-permute-start.22 = (s16[64,2176]{1,0:T(8,128)(2,1)S(1)}, s16[64,2176]{1,0:T(8,128)(2,1)S(1)}, u32[]{:S(2)}, u32[]{:S(2)}) collective-permute-start(s16[64,2176]{1,0:T(8,128)(2,1)S(1)} %get-tuple-element.28), channel_id=1, source_target_pairs={{0,8},{4,12},{8,0},{12,4},{16,24},{20,28},{24,16},{28,20},{1,9},{5... | collective-permute-start | bytes 835592 | tf_op jit(solution)/shard_map/ppermute | solution.py:42
  87.7 7.5 %collective-permute-done.23.words_ref = s16[64,2176]{1,0:T(8,128)(2,1)S(1)} collective-permute-done((s16[64,2176]{1,0:T(8,128)(2,1)S(1)}, s16[64,2176]{1,0:T(8,128)(2,1)S(1)}, u32[]{:S(2)}, u32[]{:S(2)}) %collective-permute-start.23) | collective-permute-done | bytes 278560 | tf_op jit(solution)/shard_map/ppermute | solution.py:42
  95.4 1.4 %collective-permute-start.24 = (s16[64,2176]{1,0:T(8,128)(2,1)S(1)}, s16[64,2176]{1,0:T(8,128)(2,1)S(1)}, u32[]{:S(2)}, u32[]{:S(2)}) collective-permute-start(s16[64,2176]{1,0:T(8,128)(2,1)S(1)} %relay.1), channel_id=1, source_target_pairs={{0,24},{4,28},{8,16},{12,20},{16,8},{20,12},{24,0},{28,4},{1,25},{... | collective-permute-start | bytes 835592 | tf_op jit(solution)/shard_map/ppermute | solution.py:42
  96.8 3.9 %collective-permute-done.22.refs_0_ = s16[64,2176]{1,0:T(8,128)(2,1)S(1)} collective-permute-done((s16[64,2176]{1,0:T(8,128)(2,1)S(1)}, s16[64,2176]{1,0:T(8,128)(2,1)S(1)}, u32[]{:S(2)}, u32[]{:S(2)}) %collective-permute-start.22) | collective-permute-done | bytes 278560 | tf_op jit(solution)/shard_map/ppermute | solution.py:42
  100.7 6.1 %collective-permute-done.24.refs_1_ = s16[64,2176]{1,0:T(8,128)(2,1)S(1)} collective-permute-done((s16[64,2176]{1,0:T(8,128)(2,1)S(1)}, s16[64,2176]{1,0:T(8,128)(2,1)S(1)}, u32[]{:S(2)}, u32[]{:S(2)}) %collective-permute-start.24) | collective-permute-done | bytes 278560 | tf_op jit(solution)/shard_map/ppermute | solution.py:42
  106.8 0.9 finish.1
  108.4 0.9 collective-permute-done.25
  109.4 0.8 pad_maximum_fusion
  (54 shorter events, 4.9 us)
Async XLA Ops:
  0.6 67.0 %copy-start = (s32[256]{0:T(256)S(1)}, s32[256]{0:T(256)}, u32[]{:S(2)}) copy-start(s32[256]{0:T(256)} %param.17) | copy-start | bytes 3076
  0.6 15.1 %collective-permute-start = (bf16[512,512]{1,0:T(8,128)(2,1)}, bf16[512,512]{1,0:T(8,128)(2,1)S(1)}, u32[]{:S(2)}, u32[]{:S(2)}) collective-permute-start(bf16[512,512]{1,0:T(8,128)(2,1)} %refs_0_.1), channel_id=1, source_target_pairs={{0,1},{1,0},{2,3},{3,2},{4,5},{5,4},{6,7},{7,6},{8,9},{9,8},{10,11... | collective-permute-start | bytes 1572872 | tf_op jit(solution)/shard_map/ppermute | solution.py:42
  3.6 14.0 %collective-permute-start.2 = (bf16[512,512]{1,0:T(8,128)(2,1)}, bf16[512,512]{1,0:T(8,128)(2,1)S(1)}, u32[]{:S(2)}, u32[]{:S(2)}) collective-permute-start(bf16[512,512]{1,0:T(8,128)(2,1)} %refs_0_.1), channel_id=1, source_target_pairs={{0,2},{1,3},{2,0},{3,1},{4,6},{5,7},{6,4},{7,5},{8,10},{9,11},{10,... | collective-permute-start | bytes 1572872 | tf_op jit(solution)/shard_map/ppermute | solution.py:42
  15.8 18.0 %collective-permute-start.1 = (bf16[256,512]{1,0:T(8,128)(2,1)S(1)}, bf16[256,512]{1,0:T(8,128)(2,1)S(1)}, u32[]{:S(2)}, u32[]{:S(2)}) collective-permute-start(bf16[256,512]{1,0:T(8,128)(2,1)S(1)} %slice.8), channel_id=1, source_target_pairs={{0,2},{1,3},{2,0},{3,1},{4,6},{5,7},{6,4},{7,5},{8,10},{9,11},{10,... | collective-permute-start | bytes 786440 | tf_op jit(solution)/shard_map/ppermute | solution.py:42
  17.7 16.2 %collective-permute-start.3 = (bf16[256,512]{1,0:T(8,128)(2,1)S(1)}, bf16[256,512]{1,0:T(8,128)(2,1)S(1)}, u32[]{:S(2)}, u32[]{:S(2)}) collective-permute-start(bf16[256,512]{1,0:T(8,128)(2,1)S(1)} %slice.9), channel_id=1, source_target_pairs={{0,1},{1,0},{2,3},{3,2},{4,5},{5,4},{6,7},{7,6},{8,9},{9,8},{10,11... | collective-permute-start | bytes 786440 | tf_op jit(solution)/shard_map/ppermute | solution.py:42
  20.3 13.6 %copy-start.3 = (f32[4096]{0:T(1024)S(1)}, f32[4096]{0:T(1024)}, u32[]{:S(2)}) copy-start(f32[4096]{0:T(1024)} %param.12) | copy-start | bytes 49156
  20.3 13.6 %copy-start.4 = (f32[4096]{0:T(1024)S(1)}, f32[4096]{0:T(1024)}, u32[]{:S(2)}) copy-start(f32[4096]{0:T(1024)} %param.13) | copy-start | bytes 49156
  20.3 13.6 %copy-start.5 = (s32[4096]{0:T(1024)S(1)}, s32[4096]{0:T(1024)}, u32[]{:S(2)}) copy-start(s32[4096]{0:T(1024)} %param.14) | copy-start | bytes 49156
  33.9 17.8 %copy-start.6 = (s32[256]{0:T(256)S(1)}, s32[256]{0:T(256)}, u32[]{:S(2)}) copy-start(s32[256]{0:T(256)} %param.16) | copy-start | bytes 3076
  33.9 17.8 %copy-start.7 = (s32[256]{0:T(256)S(1)}, s32[256]{0:T(256)}, u32[]{:S(2)}) copy-start(s32[256]{0:T(256)} %param.15) | copy-start | bytes 3076
  48.2 32.9 %collective-permute-start.21 = (bf16[512,2048]{1,0:T(8,128)(2,1)}, bf16[512,2048]{1,0:T(8,128)(2,1)}, u32[]{:S(2)}, u32[]{:S(2)}) collective-permute-start(bf16[512,2048]{1,0:T(8,128)(2,1)} %get-tuple-element.26), channel_id=1, source_target_pairs={{0,4},{4,0},{8,12},{12,8},{16,20},{20,16},{24,28},{28,24},{1,5},{5... | collective-permute-start | bytes 6291464 | tf_op jit(solution)/shard_map/ppermute | solution.py:42
  48.2 6.3 %collective-permute-start.4 = (f32[64,512]{1,0:T(8,128)S(1)}, f32[64,512]{1,0:T(8,128)S(1)}, u32[]{:S(2)}, u32[]{:S(2)}) collective-permute-start(f32[64,512]{1,0:T(8,128)S(1)} %get-tuple-element.19), channel_id=1, source_target_pairs={{0,1},{1,0},{2,3},{3,2},{4,5},{5,4},{6,7},{7,6},{8,9},{9,8},{10,11... | collective-permute-start | bytes 393224 | tf_op jit(solution)/shard_map/ppermute | solution.py:42
  48.7 8.4 %collective-permute-start.5 = (f32[64,512]{1,0:T(8,128)S(1)}, f32[64,512]{1,0:T(8,128)S(1)}, u32[]{:S(2)}, u32[]{:S(2)}) collective-permute-start(f32[64,512]{1,0:T(8,128)S(1)} %get-tuple-element.20), channel_id=1, source_target_pairs={{0,2},{1,3},{2,0},{3,1},{4,6},{5,7},{6,4},{7,5},{8,10},{9,11},{10,... | collective-permute-start | bytes 393224 | tf_op jit(solution)/shard_map/ppermute | solution.py:42
  49.9 7.3 %collective-permute-start.6 = (f32[64,512]{1,0:T(8,128)S(1)}, f32[64,512]{1,0:T(8,128)S(1)}, u32[]{:S(2)}, u32[]{:S(2)}) collective-permute-start(f32[64,512]{1,0:T(8,128)S(1)} %get-tuple-element.21), channel_id=1, source_target_pairs={{0,3},{1,2},{2,1},{3,0},{4,7},{5,6},{6,5},{7,4},{8,11},{9,10},{10,... | collective-permute-start | bytes 393224 | tf_op jit(solution)/shard_map/ppermute | solution.py:42
  57.3 4.5 %collective-permute-start.7 = (s16[64,512]{1,0:T(8,128)(2,1)S(1)}, s16[64,512]{1,0:T(8,128)(2,1)S(1)}, u32[]{:S(2)}, u32[]{:S(2)}) collective-permute-start(s16[64,512]{1,0:T(8,128)(2,1)S(1)} %get-tuple-element.23.refs_0_), channel_id=1, source_target_pairs={{0,8},{4,12},{8,0},{12,4},{16,24},{20,28},{24,16},{28,20},{1,9},{5... | collective-permute-start | bytes 196616 | tf_op jit(solution)/shard_map/ppermute | solution.py:42
  58.9 6.9 %collective-permute-start.8 = (s16[64,512]{1,0:T(8,128)(2,1)S(1)}, s16[64,512]{1,0:T(8,128)(2,1)S(1)}, u32[]{:S(2)}, u32[]{:S(2)}) collective-permute-start(s16[64,512]{1,0:T(8,128)(2,1)S(1)} %get-tuple-element.23.refs_0_), channel_id=1, source_target_pairs={{0,16},{4,20},{8,24},{12,28},{16,0},{20,4},{24,8},{28,12},{1,17},{... | collective-permute-start | bytes 196616 | tf_op jit(solution)/shard_map/ppermute | solution.py:42
  61.5 6.1 %collective-permute-start.9 = (s16[64,512]{1,0:T(8,128)(2,1)S(1)}, s16[64,512]{1,0:T(8,128)(2,1)S(1)}, u32[]{:S(2)}, u32[]{:S(2)}) collective-permute-start(s16[64,512]{1,0:T(8,128)(2,1)S(1)} %get-tuple-element.23.refs_0_), channel_id=1, source_target_pairs={{0,24},{4,28},{8,16},{12,20},{16,8},{20,12},{24,0},{28,4},{1,25},{... | collective-permute-start | bytes 196616 | tf_op jit(solution)/shard_map/ppermute | solution.py:42
  61.7 6.0 %collective-permute-start.10 = (s16[64,512]{1,0:T(8,128)(2,1)S(1)}, s16[64,512]{1,0:T(8,128)(2,1)S(1)}, u32[]{:S(2)}, u32[]{:S(2)}) collective-permute-start(s16[64,512]{1,0:T(8,128)(2,1)S(1)} %get-tuple-element.23.refs_0_), channel_id=1, source_target_pairs={{0,4},{4,0},{8,12},{12,8},{16,20},{20,16},{24,28},{28,24},{1,5},{5... | collective-permute-start | bytes 196616 | tf_op jit(solution)/shard_map/ppermute | solution.py:42
  61.8 6.0 %collective-permute-start.11 = (s16[64,512]{1,0:T(8,128)(2,1)S(1)}, s16[64,512]{1,0:T(8,128)(2,1)S(1)}, u32[]{:S(2)}, u32[]{:S(2)}) collective-permute-start(s16[64,512]{1,0:T(8,128)(2,1)S(1)} %collective-permute-done.7.refs_1_), channel_id=1, source_target_pairs={{0,4},{4,0},{8,12},{12,8},{16,20},{20,16},{24,28},{28,24},{1,5},{5... | collective-permute-start | bytes 196616 | tf_op jit(solution)/shard_map/ppermute | solution.py:42
  65.8 2.0 %collective-permute-start.12 = (s16[64,512]{1,0:T(8,128)(2,1)S(1)}, s16[64,512]{1,0:T(8,128)(2,1)S(1)}, u32[]{:S(2)}, u32[]{:S(2)}) collective-permute-start(s16[64,512]{1,0:T(8,128)(2,1)S(1)} %collective-permute-done.8.refs_2_), channel_id=1, source_target_pairs={{0,4},{4,0},{8,12},{12,8},{16,20},{20,16},{24,28},{28,24},{1,5},{5... | collective-permute-start | bytes 196616 | tf_op jit(solution)/shard_map/ppermute | solution.py:42
  67.6 1.3 %collective-permute-start.13 = (s16[64,512]{1,0:T(8,128)(2,1)S(1)}, s16[64,512]{1,0:T(8,128)(2,1)S(1)}, u32[]{:S(2)}, u32[]{:S(2)}) collective-permute-start(s16[64,512]{1,0:T(8,128)(2,1)S(1)} %collective-permute-done.9.refs_3_), channel_id=1, source_target_pairs={{0,4},{4,0},{8,12},{12,8},{16,20},{20,16},{24,28},{28,24},{1,5},{5... | collective-permute-start | bytes 196616 | tf_op jit(solution)/shard_map/ppermute | solution.py:42
  72.6 4.3 %collective-permute-start.14 = (bf16[64,512]{1,0:T(8,128)(2,1)S(1)}, bf16[64,512]{1,0:T(8,128)(2,1)S(1)}, u32[]{:S(2)}, u32[]{:S(2)}) collective-permute-start(bf16[64,512]{1,0:T(8,128)(2,1)S(1)} %get-tuple-element.24.refs_0_), channel_id=1, source_target_pairs={{0,1},{1,0},{2,3},{3,2},{4,5},{5,4},{6,7},{7,6},{8,9},{9,8},{10,11... | collective-permute-start | bytes 196616 | tf_op jit(solution)/shard_map/ppermute | solution.py:42
  74.1 5.0 %collective-permute-start.15 = (bf16[64,512]{1,0:T(8,128)(2,1)S(1)}, bf16[64,512]{1,0:T(8,128)(2,1)S(1)}, u32[]{:S(2)}, u32[]{:S(2)}) collective-permute-start(bf16[64,512]{1,0:T(8,128)(2,1)S(1)} %get-tuple-element.24.refs_0_), channel_id=1, source_target_pairs={{0,2},{1,3},{2,0},{3,1},{4,6},{5,7},{6,4},{7,5},{8,10},{9,11},{10,... | collective-permute-start | bytes 196616 | tf_op jit(solution)/shard_map/ppermute | solution.py:42
  74.6 5.2 %collective-permute-start.16 = (bf16[64,512]{1,0:T(8,128)(2,1)S(1)}, bf16[64,512]{1,0:T(8,128)(2,1)S(1)}, u32[]{:S(2)}, u32[]{:S(2)}) collective-permute-start(bf16[64,512]{1,0:T(8,128)(2,1)S(1)} %get-tuple-element.24.refs_0_), channel_id=1, source_target_pairs={{0,3},{1,2},{2,1},{3,0},{4,7},{5,6},{6,5},{7,4},{8,11},{9,10},{10,... | collective-permute-start | bytes 196616 | tf_op jit(solution)/shard_map/ppermute | solution.py:42
  76.1 3.7 %collective-permute-start.17 = (bf16[64,512]{1,0:T(8,128)(2,1)S(1)}, bf16[64,512]{1,0:T(8,128)(2,1)S(1)}, u32[]{:S(2)}, u32[]{:S(2)}) collective-permute-start(bf16[64,512]{1,0:T(8,128)(2,1)S(1)} %get-tuple-element.24.refs_0_), channel_id=1, source_target_pairs={{0,4},{4,0},{8,12},{12,8},{16,20},{20,16},{24,28},{28,24},{1,5},{5... | collective-permute-start | bytes 196616 | tf_op jit(solution)/shard_map/ppermute | solution.py:42
  76.9 2.9 %collective-permute-start.18 = (bf16[64,512]{1,0:T(8,128)(2,1)S(1)}, bf16[64,512]{1,0:T(8,128)(2,1)S(1)}, u32[]{:S(2)}, u32[]{:S(2)}) collective-permute-start(bf16[64,512]{1,0:T(8,128)(2,1)S(1)} %collective-permute-done.14.refs_1_), channel_id=1, source_target_pairs={{0,4},{4,0},{8,12},{12,8},{16,20},{20,16},{24,28},{28,24},{1,5},{5... | collective-permute-start | bytes 196616 | tf_op jit(solution)/shard_map/ppermute | solution.py:42
  79.1 1.3 %collective-permute-start.19 = (bf16[64,512]{1,0:T(8,128)(2,1)S(1)}, bf16[64,512]{1,0:T(8,128)(2,1)S(1)}, u32[]{:S(2)}, u32[]{:S(2)}) collective-permute-start(bf16[64,512]{1,0:T(8,128)(2,1)S(1)} %collective-permute-done.15.refs_2_), channel_id=1, source_target_pairs={{0,4},{4,0},{8,12},{12,8},{16,20},{20,16},{24,28},{28,24},{1,5},{5... | collective-permute-start | bytes 196616 | tf_op jit(solution)/shard_map/ppermute | solution.py:42
  79.8 1.3 %collective-permute-start.20 = (bf16[64,512]{1,0:T(8,128)(2,1)S(1)}, bf16[64,512]{1,0:T(8,128)(2,1)S(1)}, u32[]{:S(2)}, u32[]{:S(2)}) collective-permute-start(bf16[64,512]{1,0:T(8,128)(2,1)S(1)} %collective-permute-done.16.refs_3_), channel_id=1, source_target_pairs={{0,4},{4,0},{8,12},{12,8},{16,20},{20,16},{24,28},{28,24},{1,5},{5... | collective-permute-start | bytes 196616 | tf_op jit(solution)/shard_map/ppermute | solution.py:42
  85.6 9.6 %collective-permute-start.23 = (s16[64,2176]{1,0:T(8,128)(2,1)S(1)}, s16[64,2176]{1,0:T(8,128)(2,1)S(1)}, u32[]{:S(2)}, u32[]{:S(2)}) collective-permute-start(s16[64,2176]{1,0:T(8,128)(2,1)S(1)} %get-tuple-element.29), channel_id=1, source_target_pairs={{0,8},{4,12},{8,0},{12,4},{16,24},{20,28},{24,16},{28,20},{1,9},{5... | collective-permute-start | bytes 835592 | tf_op jit(solution)/shard_map/ppermute | solution.py:42
  85.6 15.0 %collective-permute-start.22 = (s16[64,2176]{1,0:T(8,128)(2,1)S(1)}, s16[64,2176]{1,0:T(8,128)(2,1)S(1)}, u32[]{:S(2)}, u32[]{:S(2)}) collective-permute-start(s16[64,2176]{1,0:T(8,128)(2,1)S(1)} %get-tuple-element.28), channel_id=1, source_target_pairs={{0,8},{4,12},{8,0},{12,4},{16,24},{20,28},{24,16},{28,20},{1,9},{5... | collective-permute-start | bytes 835592 | tf_op jit(solution)/shard_map/ppermute | solution.py:42
  95.4 11.4 %collective-permute-start.24 = (s16[64,2176]{1,0:T(8,128)(2,1)S(1)}, s16[64,2176]{1,0:T(8,128)(2,1)S(1)}, u32[]{:S(2)}, u32[]{:S(2)}) collective-permute-start(s16[64,2176]{1,0:T(8,128)(2,1)S(1)} %relay.1), channel_id=1, source_target_pairs={{0,24},{4,28},{8,16},{12,20},{16,8},{20,12},{24,0},{28,4},{1,25},{... | collective-permute-start | bytes 835592 | tf_op jit(solution)/shard_map/ppermute | solution.py:42
  107.7 1.6 %collective-permute-start.25 = (f32[32,2048]{1,0:T(8,128)S(1)}, f32[32,2048]{1,0:T(8,128)S(1)}, u32[]{:S(2)}, u32[]{:S(2)}) collective-permute-start(f32[32,2048]{1,0:T(8,128)S(1)} %get-tuple-element.32), channel_id=1, source_target_pairs={{0,4},{4,0},{8,12},{12,8},{16,20},{20,16},{24,28},{28,24},{1,5},{5... | collective-permute-start | bytes 786440 | tf_op jit(solution)/shard_map/ppermute | solution.py:42
  (2 other events, 14.6 us)

commit v2 on v1

--- a/solution.py
+++ b/solution.py
@@ -42,121 +42,145 @@
     return lax.ppermute(value, axis, [(k, k ^ flip) for k in range(n)])
 
 
-def first_moves_kernel(count, where_ref, *refs):
-    shock_refs, load_refs, out_ref = refs[:count], refs[count : 2 * count], refs[2 * count]
-    total = dot(shock_refs[0][...], load_refs[0][...])
-    for shock_ref, load_ref in zip(shock_refs[1:], load_refs[1:]):
-        total = total + dot(shock_ref[...], load_ref[...])
-    out_ref[...] = total
-
-
-def first_moves(where, shocks, flips, loadings, tile):
-    rows, depth = shocks[0].shape
+def tiles(width, tile):
+    return [slice(at, at + tile) for at in range(0, width, tile)]
+
+
+def stage_kernel(slots, near, far, where_ref, shocks_ref, book_ref, loadings_ref, first_ref, near_ref, far_ref, onehot_ref, own, sems):
+    depth = shocks_ref.shape[1]
+    books, cols = onehot_ref.shape
+    share = books // slots
+    rows_of = lambda flip: pl.ds(pl.multiple_of((where_ref[0] ^ flip) * depth, depth), depth)
+    parts = tiles(cols, cols // 4)
+    own_copies = [
+        pltpu.make_async_copy(loadings_ref.at[rows_of(0), part], own.at[:, part], sems.at[k])
+        for k, part in enumerate(parts)
+    ]
+    rest_copies = [
+        pltpu.make_async_copy(
+            loadings_ref.at[rows_of(flip), :],
+            ref.at[k * depth : (k + 1) * depth, :],
+            sems.at[len(parts) + flip - 1],
+        )
+        for ref, flips in ((near_ref, near), (far_ref, far))
+        for k, flip in enumerate(flips)
+    ]
+    for copy in own_copies + rest_copies:
+        copy.start()
+    tile = cols // 8
+    row = lax.broadcasted_iota(jnp.int32, (books, tile), 0)
+    row = ((row // share) ^ where_ref[0]) * share + row % share
+    for part in tiles(cols, tile):
+        onehot_ref[:, part] = jnp.where(row == book_ref[:, part], 1.0, 0.0).astype(BF16)
+    for copy, part in zip(own_copies, parts):
+        copy.wait()
+        first_ref[:, part] = dot(shocks_ref[...], own[:, part])
+    for copy in rest_copies:
+        copy.wait()
+
+
+def stage(where, shocks, book_of, loadings, slots, near, far, books):
+    rows, depth = shocks.shape
     cols = loadings.shape[1]
-    count = len(shocks)
-    steps = cols // tile
-    col_of = functools.partial(column_tile, steps)
-    specs = [pl.BlockSpec((rows, depth), lambda n, w: (0, 0)) for _ in shocks]
-    specs += [
-        pl.BlockSpec((depth, tile), lambda n, w, f=f: (w[0] ^ f, col_of(n, w))) for f in flips
-    ]
-    return pl.pallas_call(
-        functools.partial(first_moves_kernel, count),
+    vmem = pl.BlockSpec(memory_space=pltpu.VMEM)
+    return pl.pallas_call(
+        functools.partial(stage_kernel, slots, near, far),
+        out_shape=[
+            jax.ShapeDtypeStruct((rows, cols), F32),
+            jax.ShapeDtypeStruct((len(near) * depth, cols), BF16),
+            jax.ShapeDtypeStruct((len(far) * depth, cols), BF16),
+            jax.ShapeDtypeStruct((books, cols), BF16),
+        ],
+        in_specs=[pl.BlockSpec(memory_space=pltpu.SMEM), vmem, vmem, pl.BlockSpec(memory_space=pltpu.HBM)],
+        out_specs=[vmem] * 4,
+        scratch_shapes=[pltpu.VMEM((depth, cols), BF16), pltpu.SemaphoreType.DMA((3 + slots,))],
+        compiler_params=params(16),
+        cost_estimate=pl.CostEstimate(
+            flops=2 * rows * depth * cols, bytes_accessed=2 * loadings.size, transcendentals=0
+        ),
+        name="stage",
+    )(where, shocks, book_of, loadings)
+
+
+def add_moves_kernel(*refs):
+    shock_refs, (rest_ref, before_ref, after_ref) = refs[:-3], refs[-3:]
+    depth = shock_refs[0].shape[1]
+    cols = after_ref.shape[1]
+    for part in tiles(cols, cols // 8):
+        total = before_ref[:, part]
+        for k, shock_ref in enumerate(shock_refs):
+            total = total + dot(shock_ref[...], rest_ref[k * depth : (k + 1) * depth, part])
+        after_ref[:, part] = total
+
+
+def add_moves(shocks, rest, before):
+    vmem = pl.BlockSpec(memory_space=pltpu.VMEM)
+    rows, cols = before.shape
+    depth = shocks[0].shape[1]
+    return pl.pallas_call(
+        add_moves_kernel,
         out_shape=jax.ShapeDtypeStruct((rows, cols), F32),
-        grid_spec=pltpu.PrefetchScalarGridSpec(
-            num_scalar_prefetch=1,
-            grid=(steps,),
-            in_specs=specs,
-            out_specs=pl.BlockSpec((rows, tile), lambda n, w: (0, n)),
+        in_specs=[vmem] * (len(shocks) + 2),
+        out_specs=vmem,
+        input_output_aliases={len(shocks) + 1: 0},
+        compiler_params=params(16),
+        cost_estimate=pl.CostEstimate(
+            flops=2 * rows * depth * cols * len(shocks), bytes_accessed=8 * rows * cols, transcendentals=0
         ),
-        compiler_params=params(48),
+        name="add_moves",
+    )(*shocks, rest, before)
+
+
+def profit_kernel(count, where_ref, *refs):
+    top_refs, low_refs = refs[:count], refs[count : 2 * count]
+    rest_ref, first_ref, delta_ref, gamma_ref, kappa_ref, onehot_ref = refs[2 * count : 2 * count + 6]
+    mine_ref, theirs_ref = refs[2 * count + 6 : 2 * count + 8]
+    sum_refs, total = refs[2 * count + 8 : -1], refs[-1]
+    half, depth = top_refs[0].shape
+    part_cols = mine_ref.shape[1]
+    tile = part_cols // 4
+    share = sum_refs[0].shape[0]
+    fresh = True
+    for side, out_ref in ((1 - where_ref[1], theirs_ref), (where_ref[1], mine_ref)):
+        for spot in tiles(part_cols, tile):
+            part = pl.ds(pl.multiple_of(side * part_cols + spot.start, tile), tile)
+            pieces = []
+            for at, shock_refs in ((0, top_refs), (half, low_refs)):
+                moves = first_ref[at : at + half, part]
+                for k, shock_ref in enumerate(shock_refs):
+                    moves = moves + dot(shock_ref[...], rest_ref[k * depth : (k + 1) * depth, part])
+                value = moves * (delta_ref[:, part] + moves * (gamma_ref[:, part] + moves * kappa_ref[:, part]))
+                pieces.append(value.astype(BF16))
+            profit = jnp.concatenate(pieces, axis=0)
+            out_ref[:, spot] = profit
+            sums = dot_nt(onehot_ref[:, part], profit)
+            total[...] = sums if fresh else total[...] + sums
+            fresh = False
+    for slot, sum_ref in enumerate(sum_refs):
+        sum_ref[...] = total[slot * share : (slot + 1) * share, :]
+
+
+def profits(where, tops, lows, rest, first, delta, gamma, kappa, onehot, slots):
+    rows, cols = first.shape
+    books = onehot.shape[0]
+    depth = tops[0].shape[1]
+    vmem = pl.BlockSpec(memory_space=pltpu.VMEM)
+    out_shape = [jax.ShapeDtypeStruct((rows, cols // CORES), BF16)] * 2
+    out_shape += [jax.ShapeDtypeStruct((books // slots, rows), F32)] * slots
+    return pl.pallas_call(
+        functools.partial(profit_kernel, len(tops)),
+        out_shape=out_shape,
+        in_specs=[pl.BlockSpec(memory_space=pltpu.SMEM)] + [vmem] * (2 * len(tops) + 6),
+        out_specs=[vmem] * len(out_shape),
+        scratch_shapes=[pltpu.VMEM((books, rows), F32)],
+        compiler_params=params(16),
         cost_estimate=pl.CostEstimate(
-            flops=2 * rows * depth * cols * count,
-            bytes_accessed=2 * depth * cols * count + 4 * rows * cols,
-            transcendentals=0,
-        ),
-        name="first_moves",
-    )(where, *shocks, *([loadings] * count))
-
-
-def column_tile(steps, n, where_ref):
-    return lax.rem(n + (1 - where_ref[1]) * (steps // CORES), steps)
-
-
-def profit_kernel(count, slots, where_ref, *refs):
-    top_refs, low_refs, load_refs = refs[:count], refs[count : 2 * count], refs[2 * count : 3 * count]
-    first_ref, delta_ref, gamma_ref, kappa_ref, book_ref = refs[3 * count : 3 * count + 5]
-    mine_ref, theirs_ref = refs[3 * count + 5 : 3 * count + 7]
-    sum_refs = refs[3 * count + 7 :]
-    step = pl.program_id(0)
-    share = sum_refs[0].shape[0]
-    half = top_refs[0].shape[0]
-    tile = first_ref.shape[1]
-
-    @pl.when(step == 0)
-    def _():
-        for sum_ref in sum_refs:
-            sum_ref[...] = jnp.zeros_like(sum_ref)
-
-    parts = []
-    for at, shock_refs in ((0, top_refs), (half, low_refs)):
-        moves = first_ref[at : at + half, :]
-        for shock_ref, load_ref in zip(shock_refs, load_refs):
-            moves = moves + dot(shock_ref[...], load_ref[...])
-        value = moves * (delta_ref[...] + moves * (gamma_ref[...] + moves * kappa_ref[...]))
-        parts.append(value.astype(BF16))
-    profit = jnp.concatenate(parts, axis=0)
-
-    @pl.when(step < pl.num_programs(0) // CORES)
-    def _():
-        theirs_ref[...] = profit
-
-    @pl.when(step >= pl.num_programs(0) // CORES)
-    def _():
-        mine_ref[...] = profit
-
-    row = lax.broadcasted_iota(jnp.int32, (share, tile), 0)
-    for slot in range(slots):
-        start = (where_ref[0] ^ slot) * share
-        onehot = jnp.where(row + start == book_ref[...], 1.0, 0.0).astype(BF16)
-        sum_refs[slot][...] += dot_nt(onehot, profit)
-
-
-def profits(where, tops, lows, flips, loadings, first, delta, gamma, kappa, book_of, slots, books, tile):
-    half, depth = tops[0].shape
-    rows, cols = first.shape
-    count = len(tops)
-    steps = cols // tile
-    col_of = functools.partial(column_tile, steps)
-    share = books // slots
-    line = pl.BlockSpec((1, tile), lambda n, w: (0, col_of(n, w)))
-    specs = [pl.BlockSpec((half, depth), lambda n, w: (0, 0)) for _ in range(2 * count)]
-    specs += [
-        pl.BlockSpec((depth, tile), lambda n, w, f=f: (w[0] ^ f, col_of(n, w))) for f in flips
-    ]
-    specs += [pl.BlockSpec((rows, tile), lambda n, w: (0, n)), line, line, line, line]
-    part = steps // CORES
-    out_specs = [
-        pl.BlockSpec((rows, tile), lambda n, w: (0, jnp.maximum(n - part, 0))),
-        pl.BlockSpec((rows, tile), lambda n, w: (0, jnp.minimum(n, part - 1))),
-    ]
-    out_specs += [pl.BlockSpec((share, rows), lambda n, w: (0, 0)) for _ in range(slots)]
-    out_shape = [jax.ShapeDtypeStruct((rows, cols // CORES), BF16)] * 2
-    out_shape += [jax.ShapeDtypeStruct((share, rows), F32)] * slots
-    return pl.pallas_call(
-        functools.partial(profit_kernel, count, slots),
-        out_shape=out_shape,
-        grid_spec=pltpu.PrefetchScalarGridSpec(
-            num_scalar_prefetch=1, grid=(steps,), in_specs=specs, out_specs=out_specs
-        ),
-        compiler_params=params(48),
-        cost_estimate=pl.CostEstimate(
-            flops=2 * rows * cols * (depth * count + books),
-            bytes_accessed=2 * depth * cols * count + 6 * rows * cols,
+            flops=2 * rows * cols * (depth * len(tops) + books),
+            bytes_accessed=6 * rows * cols,
             transcendentals=0,
         ),
         name="profits",
-    )(where, *tops, *lows, *([loadings] * count), first, delta, gamma, kappa, book_of)
+    )(where, *tops, *lows, rest, first, delta, gamma, kappa, onehot)
 
 
 def gather_and_revalue(where, shocks, loadings, delta, gamma, kappa, book_of, books):
@@ -165,19 +189,18 @@
     while inner * inner * 4 <= slots:
         inner *= 2
     outer = slots // inner
-    rows = shocks.shape[0]
-    half = rows // 2
+    half = shocks.shape[0] // 2
     along = [f for f in range(1, inner)]
     across = [f * inner for f in range(1, outer)]
+    corners = [(a, b) for a in along for b in across]
     near = {f: swap(shocks, "inst", f) for f in along + across}
-    corners = [(a, b) for a in along for b in across]
+    first, near_loads, far_loads, onehot = stage(
+        where, shocks, book_of, loadings, slots, along + across, [a ^ b for a, b in corners], books
+    )
     tops = [swap(near[a][:half], "inst", b) for a, b in corners]
     lows = [swap(near[b][half:], "inst", a) for a, b in corners]
-    flips = [0] + along + across
-    first = first_moves(where, [shocks] + [near[f] for f in along + across], flips, loadings, 512)
-    return profits(
-        where, tops, lows, [a ^ b for a, b in corners], loadings, first, delta, gamma, kappa, book_of, slots, books, 512
-    )
+    first = add_moves([near[f] for f in along + across], near_loads, first)
+    return profits(where, tops, lows, far_loads, first, delta, gamma, kappa, onehot, slots)
 
 
 def book_value_kernel(scale, low_ref, high_ref, *refs):

time: 111 us -> 94.3 us (0.85)
  Pallas kernels: 37.3 us -> 27.1 us
  waiting for transfers between devices: 45.4 us -> 38.7 us
    pallas_call x2 -> x3, Pallas kernels: 27.8 us -> 17.4 us  [the longest x1 6.48 us: stage(): pl.pallas_call(functools.partial(stage_kernel, slots, near, far), out_sha...]
    ppermute x26, waiting for transfers between devices: 45.4 us -> 38.7 us  [swap(): return lax.ppermute(value, axis, [(k, k ^ flip) for k in range(n)])]
  transfers between devices with their start and end apart: 26 -> 26, of which waited for: 15 -> 16; matrix products, arithmetic and copies ran while one was open for 1% -> 1% of each run, Pallas kernels for 16% -> 17%
where the time goes in v2:
time: 94.3 us; the launch traced here: 94 us
  waiting for transfers between devices  38.7 us (41%)
  Pallas kernels  27.1 us (29%)
  starting transfers between devices  23.6 us (25%)
  local copies, waits for them, and re-layouts  2.27 us (2%)
  other arithmetic  1.57 us (2%)
    ppermute x26, waiting for transfers between devices, swap(): return lax.ppermute(value, axis, [(k, k ^ flip) for k in range(n)])  38.7 us
    ppermute x26, starting transfers between devices, swap(): return lax.ppermute(value, axis, [(k, k ^ flip) for k in range(n)])  23.6 us
    pallas_call x1, Pallas kernels, stage(): pl.pallas_call(functools.partial(stage_kernel, slots, near, far), out_sha...  6.48 us
    pallas_call x1, Pallas kernels, profits(): pl.pallas_call(functools.partial(profit_kernel, len(tops)), out_shape=out...  5.99 us
    pallas_call x1, Pallas kernels, add_moves(): pl.pallas_call(add_moves_kernel, out_shape=jax.ShapeDtypeStruct((rows, co...  4.94 us
    pallas_call x1, Pallas kernels, tail_sums(): pl.pallas_call(functools.partial(tail_kernel, slots, lines), out_shape=[j...  4.51 us
    pallas_call x1, Pallas kernels, quantiles(): pl.pallas_call(quantile_kernel, out_shape=[jax.ShapeDtypeStruct((share, r...  3.89 us
  transfers between devices with their start and end apart: 26, of which 16 were waited for; matrix products, arithmetic and copies ran while one was open for 1% of the time, Pallas kernels for 17%

profile of v2, /device:TPU:0, one launch (start us, length us, event | category | flops | bytes accessed | tf_op | source)
XLA Modules:
  0.0 94.0 jit_solution(6975727378753972415)
XLA Ops:
  0.6 3.0 %collective-permute-start = (bf16[512,512]{1,0:T(8,128)(2,1)}, bf16[512,512]{1,0:T(8,128)(2,1)S(1)}, u32[]{:S(2)}, u32[]{:S(2)}) collective-permute-start(bf16[512,512]{1,0:T(8,128)(2,1)} %shocks_ref.1), channel_id=1, source_target_pairs={{0,1},{1,0},{2,3},{3,2},{4,5},{5,4},{6,7},{7,6},{8,9},{9,8},{10,11... | collective-permute-start | bytes 1572872 | tf_op jit(solution)/shard_map/ppermute | solution.py:42
  3.6 1.5 %collective-permute-start.2 = (bf16[512,512]{1,0:T(8,128)(2,1)}, bf16[512,512]{1,0:T(8,128)(2,1)S(1)}, u32[]{:S(2)}, u32[]{:S(2)}) collective-permute-start(bf16[512,512]{1,0:T(8,128)(2,1)} %shocks_ref.1), channel_id=1, source_target_pairs={{0,2},{1,3},{2,0},{3,1},{4,6},{5,7},{6,4},{7,5},{8,10},{9,11},{10,... | collective-permute-start | bytes 1572872 | tf_op jit(solution)/shard_map/ppermute | solution.py:42
  5.2 1.0 %copy-done.1 = bf16[512,512]{1,0:T(8,128)(2,1)S(1)} copy-done((bf16[512,512]{1,0:T(8,128)(2,1)S(1)}, bf16[512,512]{1,0:T(8,128)(2,1)}, u32[]{:S(2)}) %copy-start.1) | copy-done | bytes 524312
  7.0 6.5 %stage.1 = (f32[512,4096]{1,0:T(8,128)S(1)}, bf16[1024,4096]{1,0:T(8,128)(2,1)S(1)}, bf16[512,4096]{1,0:T(8,128)(2,1)S(1)}, bf16[256,4096]{1,0:T(8,128)(2,1)S(1)}) custom-call(s32[3]{0:T(128)S(1)} %pad_add_fusion.where_ref, bf16[512,512]{1,0:T(8,128)(2,1)S(1)} %copy-done.1, s32[1,4096]{1,0:T(1,128)S(1)} %bitcast.13, bf16[2048,4096]{1,0:T(8,128)(2,1)} %loadings_ref.1), custom_call_target="tpu_custom_call" | custom-call | flops 2147483648 | bytes 16777216 | tf_op jit(solution)/shard_map/stage/pallas_call | solution.py:86
  13.5 2.3 %collective-permute-done.refs_0_ = bf16[512,512]{1,0:T(8,128)(2,1)S(1)} collective-permute-done((bf16[512,512]{1,0:T(8,128)(2,1)}, bf16[512,512]{1,0:T(8,128)(2,1)S(1)}, u32[]{:S(2)}, u32[]{:S(2)}) %collective-permute-start) | collective-permute-done | bytes 524320 | tf_op jit(solution)/shard_map/ppermute | solution.py:42
  15.8 1.8 %collective-permute-start.1 = (bf16[256,512]{1,0:T(8,128)(2,1)S(1)}, bf16[256,512]{1,0:T(8,128)(2,1)S(1)}, u32[]{:S(2)}, u32[]{:S(2)}) collective-permute-start(bf16[256,512]{1,0:T(8,128)(2,1)S(1)} %slice.8), channel_id=1, source_target_pairs={{0,2},{1,3},{2,0},{3,1},{4,6},{5,7},{6,4},{7,5},{8,10},{9,11},{10,... | collective-permute-start | bytes 786440 | tf_op jit(solution)/shard_map/ppermute | solution.py:42
  17.7 1.6 %collective-permute-start.3 = (bf16[256,512]{1,0:T(8,128)(2,1)S(1)}, bf16[256,512]{1,0:T(8,128)(2,1)S(1)}, u32[]{:S(2)}, u32[]{:S(2)}) collective-permute-start(bf16[256,512]{1,0:T(8,128)(2,1)S(1)} %slice.9), channel_id=1, source_target_pairs={{0,1},{1,0},{2,3},{3,2},{4,5},{5,4},{6,7},{7,6},{8,9},{9,8},{10,11... | collective-permute-start | bytes 786440 | tf_op jit(solution)/shard_map/ppermute | solution.py:42
  19.2 4.9 %add_moves.1.refs_3_ = f32[512,4096]{1,0:T(8,128)S(1)} custom-call(bf16[512,512]{1,0:T(8,128)(2,1)S(1)} %collective-permute-done.refs_0_, bf16[512,512]{1,0:T(8,128)(2,1)S(1)} %collective-permute-done.2.refs_1_, bf16[1024,4096]{1,0:T(8,128)(2,1)S(1)} %get-tuple-element.23.refs_2_, ...), custom_call_target="tpu_custom_call", output_to_operand_aliasing={{}: (3, {})} | custom-call | flops 4294967296 | bytes 16777216 | tf_op jit(solution)/shard_map/add_moves/pallas_call | solution.py:120
  24.7 6.0 %profits.1 = (bf16[512,2048]{1,0:T(8,128)(2,1)S(1)}, bf16[512,2048]{1,0:T(8,128)(2,1)}, f32[64,512]{1,0:T(8,128)S(1)}, f32[64,512]{1,0:T(8,128)S(1)}, f32[64,512]{1,0:T(8,128)S(1)}, /*index=5*/f32[64,512]{1,0:T(8,128)S(1)}) custom-call(s32[3]{0:T(128)S(1)} %pad_add_fusion.where_ref, bf16[256,512]{1,0:T(8,128)(2,1)S(1)} %collective-permute-done.1.refs_0_, ...), custom_call_target="tpu_custom_call" | custom-call | flops 3221225472 | bytes 12582912 | tf_op jit(solution)/shard_map/profits/pallas_call | solution.py:170
  30.6 1.5 %collective-permute-start.4 = (f32[64,512]{1,0:T(8,128)S(1)}, f32[64,512]{1,0:T(8,128)S(1)}, u32[]{:S(2)}, u32[]{:S(2)}) collective-permute-start(f32[64,512]{1,0:T(8,128)S(1)} %get-tuple-element.27), channel_id=1, source_target_pairs={{0,1},{1,0},{2,3},{3,2},{4,5},{5,4},{6,7},{7,6},{8,9},{9,8},{10,11... | collective-permute-start | bytes 393224 | tf_op jit(solution)/shard_map/ppermute | solution.py:42
  32.6 1.5 %collective-permute-start.6 = (f32[64,512]{1,0:T(8,128)S(1)}, f32[64,512]{1,0:T(8,128)S(1)}, u32[]{:S(2)}, u32[]{:S(2)}) collective-permute-start(f32[64,512]{1,0:T(8,128)S(1)} %get-tuple-element.29), channel_id=1, source_target_pairs={{0,3},{1,2},{2,1},{3,0},{4,7},{5,6},{6,5},{7,4},{8,11},{9,10},{10,... | collective-permute-start | bytes 393224 | tf_op jit(solution)/shard_map/ppermute | solution.py:42
  34.4 2.5 %collective-permute-done.4.refs_1_ = f32[64,512]{1,0:T(8,128)S(1)} collective-permute-done((f32[64,512]{1,0:T(8,128)S(1)}, f32[64,512]{1,0:T(8,128)S(1)}, u32[]{:S(2)}, u32[]{:S(2)}) %collective-permute-start.4) | collective-permute-done | bytes 131104 | tf_op jit(solution)/shard_map/ppermute | solution.py:42
  36.9 3.6 %collective-permute-done.5.refs_2_ = f32[64,512]{1,0:T(8,128)S(1)} collective-permute-done((f32[64,512]{1,0:T(8,128)S(1)}, f32[64,512]{1,0:T(8,128)S(1)}, u32[]{:S(2)}, u32[]{:S(2)}) %collective-permute-start.5) | collective-permute-done | bytes 131104 | tf_op jit(solution)/shard_map/ppermute | solution.py:42
  40.7 1.6 %collective-permute-start.7 = (s16[64,512]{1,0:T(8,128)(2,1)S(1)}, s16[64,512]{1,0:T(8,128)(2,1)S(1)}, u32[]{:S(2)}, u32[]{:S(2)}) collective-permute-start(s16[64,512]{1,0:T(8,128)(2,1)S(1)} %get-tuple-element.31.refs_0_), channel_id=1, source_target_pairs={{0,8},{4,12},{8,0},{12,4},{16,24},{20,28},{24,16},{28,20},{1,9},{5... | collective-permute-start | bytes 196616 | tf_op jit(solution)/shard_map/ppermute | solution.py:42
  42.3 2.6 %collective-permute-start.8 = (s16[64,512]{1,0:T(8,128)(2,1)S(1)}, s16[64,512]{1,0:T(8,128)(2,1)S(1)}, u32[]{:S(2)}, u32[]{:S(2)}) collective-permute-start(s16[64,512]{1,0:T(8,128)(2,1)S(1)} %get-tuple-element.31.refs_0_), channel_id=1, source_target_pairs={{0,16},{4,20},{8,24},{12,28},{16,0},{20,4},{24,8},{28,12},{1,17},{... | collective-permute-start | bytes 196616 | tf_op jit(solution)/shard_map/ppermute | solution.py:42
  45.7 3.2 %collective-permute-done.8.refs_2_ = s16[64,512]{1,0:T(8,128)(2,1)S(1)} collective-permute-done((s16[64,512]{1,0:T(8,128)(2,1)S(1)}, s16[64,512]{1,0:T(8,128)(2,1)S(1)}, u32[]{:S(2)}, u32[]{:S(2)}) %collective-permute-start.8) | collective-permute-done | bytes 65568 | tf_op jit(solution)/shard_map/ppermute | solution.py:42
  48.9 2.1 %collective-permute-done.9.refs_3_ = s16[64,512]{1,0:T(8,128)(2,1)S(1)} collective-permute-done((s16[64,512]{1,0:T(8,128)(2,1)S(1)}, s16[64,512]{1,0:T(8,128)(2,1)S(1)}, u32[]{:S(2)}, u32[]{:S(2)}) %collective-permute-start.9) | collective-permute-done | bytes 65568 | tf_op jit(solution)/shard_map/ppermute | solution.py:42
  51.2 1.1 %collective-permute-done.13.refs_7_ = s16[64,512]{1,0:T(8,128)(2,1)S(1)} collective-permute-done((s16[64,512]{1,0:T(8,128)(2,1)S(1)}, s16[64,512]{1,0:T(8,128)(2,1)S(1)}, u32[]{:S(2)}, u32[]{:S(2)}) %collective-permute-start.13) | collective-permute-done | bytes 65568 | tf_op jit(solution)/shard_map/ppermute | solution.py:42
  52.3 3.9 %quantiles.1 = (bf16[64,512]{1,0:T(8,128)(2,1)S(1)}, f32[64,1]{1,0:T(8,128)S(1)}) custom-call(s32[64,1]{1,0:T(8,128)S(1)} %copy.19.low_ref, s32[64,1]{1,0:T(8,128)S(1)} %copy.20.high_ref, s32[64,1]{1,0:T(8,128)S(1)} %copy.21.rank_ref, f32[64,512]{1,0:T(8,128)S(1)} %get-tuple-element.30.value_ref, s16[64,512]{1,0:T(8,128)(2,1)S(1)} %get-tuple-element.31.refs_0_, ...), custom_call_target="tpu_custom_call" | custom-call | tf_op jit(solution)/shard_map/quantiles/pallas_call | solution.py:267
  56.7 1.2 %collective-permute-start.15 = (bf16[64,512]{1,0:T(8,128)(2,1)S(1)}, bf16[64,512]{1,0:T(8,128)(2,1)S(1)}, u32[]{:S(2)}, u32[]{:S(2)}) collective-permute-start(bf16[64,512]{1,0:T(8,128)(2,1)S(1)} %get-tuple-element.32.refs_0_), channel_id=1, source_target_pairs={{0,2},{1,3},{2,0},{3,1},{4,6},{5,7},{6,4},{7,5},{8,10},{9,11},{10,... | collective-permute-start | bytes 196616 | tf_op jit(solution)/shard_map/ppermute | solution.py:42
  58.0 1.8 %collective-permute-start.16 = (bf16[64,512]{1,0:T(8,128)(2,1)S(1)}, bf16[64,512]{1,0:T(8,128)(2,1)S(1)}, u32[]{:S(2)}, u32[]{:S(2)}) collective-permute-start(bf16[64,512]{1,0:T(8,128)(2,1)S(1)} %get-tuple-element.32.refs_0_), channel_id=1, source_target_pairs={{0,3},{1,2},{2,1},{3,0},{4,7},{5,6},{6,5},{7,4},{8,11},{9,10},{10,... | collective-permute-start | bytes 196616 | tf_op jit(solution)/shard_map/ppermute | solution.py:42
  59.7 0.9 collective-permute-done.14.refs_1_
  61.1 2.0 %collective-permute-done.16.refs_3_ = bf16[64,512]{1,0:T(8,128)(2,1)S(1)} collective-permute-done((bf16[64,512]{1,0:T(8,128)(2,1)S(1)}, bf16[64,512]{1,0:T(8,128)(2,1)S(1)}, u32[]{:S(2)}, u32[]{:S(2)}) %collective-permute-start.16) | collective-permute-done | bytes 65568 | tf_op jit(solution)/shard_map/ppermute | solution.py:42
  63.1 1.2 %collective-permute-done.20.refs_7_ = bf16[64,512]{1,0:T(8,128)(2,1)S(1)} collective-permute-done((bf16[64,512]{1,0:T(8,128)(2,1)S(1)}, bf16[64,512]{1,0:T(8,128)(2,1)S(1)}, u32[]{:S(2)}, u32[]{:S(2)}) %collective-permute-start.20) | collective-permute-done | bytes 65568 | tf_op jit(solution)/shard_map/ppermute | solution.py:42
  64.4 4.5 %tail_sums.1 = (s16[64,2176]{1,0:T(8,128)(2,1)S(1)}, s16[64,2176]{1,0:T(8,128)(2,1)S(1)}, f32[64,2176]{1,0:T(8,128)S(1)}, f32[64,2176]{1,0:T(8,128)S(1)}) custom-call(s32[3]{0:T(128)S(1)} %pad_add_fusion.where_ref, bf16[64,512]{1,0:T(8,128)(2,1)S(1)} %get-tuple-element.32.refs_0_, bf16[64,512]{1,0:T(8,128)(2,1)S(1)} %collective-permute-done.14.refs_1_, ...), custom_call_target="tpu_custom_call" | custom-call | tf_op jit(solution)/shard_map/tail_sums/pallas_call | solution.py:383
  69.0 2.0 %collective-permute-start.22 = (s16[64,2176]{1,0:T(8,128)(2,1)S(1)}, s16[64,2176]{1,0:T(8,128)(2,1)S(1)}, u32[]{:S(2)}, u32[]{:S(2)}) collective-permute-start(s16[64,2176]{1,0:T(8,128)(2,1)S(1)} %get-tuple-element.36), channel_id=1, source_target_pairs={{0,8},{4,12},{8,0},{12,4},{16,24},{20,28},{24,16},{28,20},{1,9},{5... | collective-permute-start | bytes 835592 | tf_op jit(solution)/shard_map/ppermute | solution.py:42
  71.0 7.5 %collective-permute-done.23.words_ref = s16[64,2176]{1,0:T(8,128)(2,1)S(1)} collective-permute-done((s16[64,2176]{1,0:T(8,128)(2,1)S(1)}, s16[64,2176]{1,0:T(8,128)(2,1)S(1)}, u32[]{:S(2)}, u32[]{:S(2)}) %collective-permute-start.23) | collective-permute-done | bytes 278560 | tf_op jit(solution)/shard_map/ppermute | solution.py:42
  78.7 1.9 %collective-permute-start.24 = (s16[64,2176]{1,0:T(8,128)(2,1)S(1)}, s16[64,2176]{1,0:T(8,128)(2,1)S(1)}, u32[]{:S(2)}, u32[]{:S(2)}) collective-permute-start(s16[64,2176]{1,0:T(8,128)(2,1)S(1)} %relay.1), channel_id=1, source_target_pairs={{0,24},{4,28},{8,16},{12,20},{16,8},{20,12},{24,0},{28,4},{1,25},{... | collective-permute-start | bytes 835592 | tf_op jit(solution)/shard_map/ppermute | solution.py:42
  80.6 3.0 %collective-permute-done.22.refs_0_ = s16[64,2176]{1,0:T(8,128)(2,1)S(1)} collective-permute-done((s16[64,2176]{1,0:T(8,128)(2,1)S(1)}, s16[64,2176]{1,0:T(8,128)(2,1)S(1)}, u32[]{:S(2)}, u32[]{:S(2)}) %collective-permute-start.22) | collective-permute-done | bytes 278560 | tf_op jit(solution)/shard_map/ppermute | solution.py:42
  83.7 7.0 %collective-permute-done.24.refs_1_ = s16[64,2176]{1,0:T(8,128)(2,1)S(1)} collective-permute-done((s16[64,2176]{1,0:T(8,128)(2,1)S(1)}, s16[64,2176]{1,0:T(8,128)(2,1)S(1)}, u32[]{:S(2)}, u32[]{:S(2)}) %collective-permute-start.24) | collective-permute-done | bytes 278560 | tf_op jit(solution)/shard_map/ppermute | solution.py:42
  90.6 0.9 finish.1
  92.2 0.9 collective-permute-done.25
  (55 shorter events, 6.2 us)
Async XLA Ops:
  0.6 50.4 %copy-start = (s32[256]{0:T(256)S(1)}, s32[256]{0:T(256)}, u32[]{:S(2)}) copy-start(s32[256]{0:T(256)} %param.17) | copy-start | bytes 3076
  0.6 15.1 %collective-permute-start = (bf16[512,512]{1,0:T(8,128)(2,1)}, bf16[512,512]{1,0:T(8,128)(2,1)S(1)}, u32[]{:S(2)}, u32[]{:S(2)}) collective-permute-start(bf16[512,512]{1,0:T(8,128)(2,1)} %shocks_ref.1), channel_id=1, source_target_pairs={{0,1},{1,0},{2,3},{3,2},{4,5},{5,4},{6,7},{7,6},{8,9},{9,8},{10,11... | collective-permute-start | bytes 1572872 | tf_op jit(solution)/shard_map/ppermute | solution.py:42
  3.6 14.0 %collective-permute-start.2 = (bf16[512,512]{1,0:T(8,128)(2,1)}, bf16[512,512]{1,0:T(8,128)(2,1)S(1)}, u32[]{:S(2)}, u32[]{:S(2)}) collective-permute-start(bf16[512,512]{1,0:T(8,128)(2,1)} %shocks_ref.1), channel_id=1, source_target_pairs={{0,2},{1,3},{2,0},{3,1},{4,6},{5,7},{6,4},{7,5},{8,10},{9,11},{10,... | collective-permute-start | bytes 1572872 | tf_op jit(solution)/shard_map/ppermute | solution.py:42
  15.8 8.4 %collective-permute-start.1 = (bf16[256,512]{1,0:T(8,128)(2,1)S(1)}, bf16[256,512]{1,0:T(8,128)(2,1)S(1)}, u32[]{:S(2)}, u32[]{:S(2)}) collective-permute-start(bf16[256,512]{1,0:T(8,128)(2,1)S(1)} %slice.8), channel_id=1, source_target_pairs={{0,2},{1,3},{2,0},{3,1},{4,6},{5,7},{6,4},{7,5},{8,10},{9,11},{10,... | collective-permute-start | bytes 786440 | tf_op jit(solution)/shard_map/ppermute | solution.py:42
  17.7 7.0 %collective-permute-start.3 = (bf16[256,512]{1,0:T(8,128)(2,1)S(1)}, bf16[256,512]{1,0:T(8,128)(2,1)S(1)}, u32[]{:S(2)}, u32[]{:S(2)}) collective-permute-start(bf16[256,512]{1,0:T(8,128)(2,1)S(1)} %slice.9), channel_id=1, source_target_pairs={{0,1},{1,0},{2,3},{3,2},{4,5},{5,4},{6,7},{7,6},{8,9},{9,8},{10,11... | collective-permute-start | bytes 786440 | tf_op jit(solution)/shard_map/ppermute | solution.py:42
  19.2 5.4 %copy-start.3 = (f32[4096]{0:T(1024)S(1)}, f32[4096]{0:T(1024)}, u32[]{:S(2)}) copy-start(f32[4096]{0:T(1024)} %param.11) | copy-start | bytes 49156
  19.2 5.4 %copy-start.4 = (f32[4096]{0:T(1024)S(1)}, f32[4096]{0:T(1024)}, u32[]{:S(2)}) copy-start(f32[4096]{0:T(1024)} %param.12) | copy-start | bytes 49156
  19.2 5.4 %copy-start.5 = (f32[4096]{0:T(1024)S(1)}, f32[4096]{0:T(1024)}, u32[]{:S(2)}) copy-start(f32[4096]{0:T(1024)} %param.13) | copy-start | bytes 49156
  24.6 9.5 %copy-start.6 = (s32[256]{0:T(256)S(1)}, s32[256]{0:T(256)}, u32[]{:S(2)}) copy-start(s32[256]{0:T(256)} %param.16) | copy-start | bytes 3076
  24.6 9.5 %copy-start.7 = (s32[256]{0:T(256)S(1)}, s32[256]{0:T(256)}, u32[]{:S(2)}) copy-start(s32[256]{0:T(256)} %param.15) | copy-start | bytes 3076
  30.6 33.7 %collective-permute-start.21 = (bf16[512,2048]{1,0:T(8,128)(2,1)}, bf16[512,2048]{1,0:T(8,128)(2,1)}, u32[]{:S(2)}, u32[]{:S(2)}) collective-permute-start(bf16[512,2048]{1,0:T(8,128)(2,1)} %get-tuple-element.34), channel_id=1, source_target_pairs={{0,4},{4,0},{8,12},{12,8},{16,20},{20,16},{24,28},{28,24},{1,5},{5... | collective-permute-start | bytes 6291464 | tf_op jit(solution)/shard_map/ppermute | solution.py:42
  30.6 6.3 %collective-permute-start.4 = (f32[64,512]{1,0:T(8,128)S(1)}, f32[64,512]{1,0:T(8,128)S(1)}, u32[]{:S(2)}, u32[]{:S(2)}) collective-permute-start(f32[64,512]{1,0:T(8,128)S(1)} %get-tuple-element.27), channel_id=1, source_target_pairs={{0,1},{1,0},{2,3},{3,2},{4,5},{5,4},{6,7},{7,6},{8,9},{9,8},{10,11... | collective-permute-start | bytes 393224 | tf_op jit(solution)/shard_map/ppermute | solution.py:42
  32.1 8.4 %collective-permute-start.5 = (f32[64,512]{1,0:T(8,128)S(1)}, f32[64,512]{1,0:T(8,128)S(1)}, u32[]{:S(2)}, u32[]{:S(2)}) collective-permute-start(f32[64,512]{1,0:T(8,128)S(1)} %get-tuple-element.28), channel_id=1, source_target_pairs={{0,2},{1,3},{2,0},{3,1},{4,6},{5,7},{6,4},{7,5},{8,10},{9,11},{10,... | collective-permute-start | bytes 393224 | tf_op jit(solution)/shard_map/ppermute | solution.py:42
  32.6 7.9 %collective-permute-start.6 = (f32[64,512]{1,0:T(8,128)S(1)}, f32[64,512]{1,0:T(8,128)S(1)}, u32[]{:S(2)}, u32[]{:S(2)}) collective-permute-start(f32[64,512]{1,0:T(8,128)S(1)} %get-tuple-element.29), channel_id=1, source_target_pairs={{0,3},{1,2},{2,1},{3,0},{4,7},{5,6},{6,5},{7,4},{8,11},{9,10},{10,... | collective-permute-start | bytes 393224 | tf_op jit(solution)/shard_map/ppermute | solution.py:42
  40.7 5.0 %collective-permute-start.7 = (s16[64,512]{1,0:T(8,128)(2,1)S(1)}, s16[64,512]{1,0:T(8,128)(2,1)S(1)}, u32[]{:S(2)}, u32[]{:S(2)}) collective-permute-start(s16[64,512]{1,0:T(8,128)(2,1)S(1)} %get-tuple-element.31.refs_0_), channel_id=1, source_target_pairs={{0,8},{4,12},{8,0},{12,4},{16,24},{20,28},{24,16},{28,20},{1,9},{5... | collective-permute-start | bytes 196616 | tf_op jit(solution)/shard_map/ppermute | solution.py:42
  42.3 6.6 %collective-permute-start.8 = (s16[64,512]{1,0:T(8,128)(2,1)S(1)}, s16[64,512]{1,0:T(8,128)(2,1)S(1)}, u32[]{:S(2)}, u32[]{:S(2)}) collective-permute-start(s16[64,512]{1,0:T(8,128)(2,1)S(1)} %get-tuple-element.31.refs_0_), channel_id=1, source_target_pairs={{0,16},{4,20},{8,24},{12,28},{16,0},{20,4},{24,8},{28,12},{1,17},{... | collective-permute-start | bytes 196616 | tf_op jit(solution)/shard_map/ppermute | solution.py:42
  44.9 6.1 %collective-permute-start.9 = (s16[64,512]{1,0:T(8,128)(2,1)S(1)}, s16[64,512]{1,0:T(8,128)(2,1)S(1)}, u32[]{:S(2)}, u32[]{:S(2)}) collective-permute-start(s16[64,512]{1,0:T(8,128)(2,1)S(1)} %get-tuple-element.31.refs_0_), channel_id=1, source_target_pairs={{0,24},{4,28},{8,16},{12,20},{16,8},{20,12},{24,0},{28,4},{1,25},{... | collective-permute-start | bytes 196616 | tf_op jit(solution)/shard_map/ppermute | solution.py:42
  45.2 6.0 %collective-permute-start.10 = (s16[64,512]{1,0:T(8,128)(2,1)S(1)}, s16[64,512]{1,0:T(8,128)(2,1)S(1)}, u32[]{:S(2)}, u32[]{:S(2)}) collective-permute-start(s16[64,512]{1,0:T(8,128)(2,1)S(1)} %get-tuple-element.31.refs_0_), channel_id=1, source_target_pairs={{0,4},{4,0},{8,12},{12,8},{16,20},{20,16},{24,28},{28,24},{1,5},{5... | collective-permute-start | bytes 196616 | tf_op jit(solution)/shard_map/ppermute | solution.py:42
  45.7 5.5 %collective-permute-start.11 = (s16[64,512]{1,0:T(8,128)(2,1)S(1)}, s16[64,512]{1,0:T(8,128)(2,1)S(1)}, u32[]{:S(2)}, u32[]{:S(2)}) collective-permute-start(s16[64,512]{1,0:T(8,128)(2,1)S(1)} %collective-permute-done.7.refs_1_), channel_id=1, source_target_pairs={{0,4},{4,0},{8,12},{12,8},{16,20},{20,16},{24,28},{28,24},{1,5},{5... | collective-permute-start | bytes 196616 | tf_op jit(solution)/shard_map/ppermute | solution.py:42
  48.9 2.3 %collective-permute-start.12 = (s16[64,512]{1,0:T(8,128)(2,1)S(1)}, s16[64,512]{1,0:T(8,128)(2,1)S(1)}, u32[]{:S(2)}, u32[]{:S(2)}) collective-permute-start(s16[64,512]{1,0:T(8,128)(2,1)S(1)} %collective-permute-done.8.refs_2_), channel_id=1, source_target_pairs={{0,4},{4,0},{8,12},{12,8},{16,20},{20,16},{24,28},{28,24},{1,5},{5... | collective-permute-start | bytes 196616 | tf_op jit(solution)/shard_map/ppermute | solution.py:42
  51.0 1.3 %collective-permute-start.13 = (s16[64,512]{1,0:T(8,128)(2,1)S(1)}, s16[64,512]{1,0:T(8,128)(2,1)S(1)}, u32[]{:S(2)}, u32[]{:S(2)}) collective-permute-start(s16[64,512]{1,0:T(8,128)(2,1)S(1)} %collective-permute-done.9.refs_3_), channel_id=1, source_target_pairs={{0,4},{4,0},{8,12},{12,8},{16,20},{20,16},{24,28},{28,24},{1,5},{5... | collective-permute-start | bytes 196616 | tf_op jit(solution)/shard_map/ppermute | solution.py:42
  56.1 4.5 %collective-permute-start.14 = (bf16[64,512]{1,0:T(8,128)(2,1)S(1)}, bf16[64,512]{1,0:T(8,128)(2,1)S(1)}, u32[]{:S(2)}, u32[]{:S(2)}) collective-permute-start(bf16[64,512]{1,0:T(8,128)(2,1)S(1)} %get-tuple-element.32.refs_0_), channel_id=1, source_target_pairs={{0,1},{1,0},{2,3},{3,2},{4,5},{5,4},{6,7},{7,6},{8,9},{9,8},{10,11... | collective-permute-start | bytes 196616 | tf_op jit(solution)/shard_map/ppermute | solution.py:42
  56.7 4.3 %collective-permute-start.15 = (bf16[64,512]{1,0:T(8,128)(2,1)S(1)}, bf16[64,512]{1,0:T(8,128)(2,1)S(1)}, u32[]{:S(2)}, u32[]{:S(2)}) collective-permute-start(bf16[64,512]{1,0:T(8,128)(2,1)S(1)} %get-tuple-element.32.refs_0_), channel_id=1, source_target_pairs={{0,2},{1,3},{2,0},{3,1},{4,6},{5,7},{6,4},{7,5},{8,10},{9,11},{10,... | collective-permute-start | bytes 196616 | tf_op jit(solution)/shard_map/ppermute | solution.py:42
  58.0 5.2 %collective-permute-start.16 = (bf16[64,512]{1,0:T(8,128)(2,1)S(1)}, bf16[64,512]{1,0:T(8,128)(2,1)S(1)}, u32[]{:S(2)}, u32[]{:S(2)}) collective-permute-start(bf16[64,512]{1,0:T(8,128)(2,1)S(1)} %get-tuple-element.32.refs_0_), channel_id=1, source_target_pairs={{0,3},{1,2},{2,1},{3,0},{4,7},{5,6},{6,5},{7,4},{8,11},{9,10},{10,... | collective-permute-start | bytes 196616 | tf_op jit(solution)/shard_map/ppermute | solution.py:42
  59.7 3.4 %collective-permute-start.17 = (bf16[64,512]{1,0:T(8,128)(2,1)S(1)}, bf16[64,512]{1,0:T(8,128)(2,1)S(1)}, u32[]{:S(2)}, u32[]{:S(2)}) collective-permute-start(bf16[64,512]{1,0:T(8,128)(2,1)S(1)} %get-tuple-element.32.refs_0_), channel_id=1, source_target_pairs={{0,4},{4,0},{8,12},{12,8},{16,20},{20,16},{24,28},{28,24},{1,5},{5... | collective-permute-start | bytes 196616 | tf_op jit(solution)/shard_map/ppermute | solution.py:42
  60.6 2.5 %collective-permute-start.18 = (bf16[64,512]{1,0:T(8,128)(2,1)S(1)}, bf16[64,512]{1,0:T(8,128)(2,1)S(1)}, u32[]{:S(2)}, u32[]{:S(2)}) collective-permute-start(bf16[64,512]{1,0:T(8,128)(2,1)S(1)} %collective-permute-done.14.refs_1_), channel_id=1, source_target_pairs={{0,4},{4,0},{8,12},{12,8},{16,20},{20,16},{24,28},{28,24},{1,5},{5... | collective-permute-start | bytes 196616 | tf_op jit(solution)/shard_map/ppermute | solution.py:42
  61.0 2.1 %collective-permute-start.19 = (bf16[64,512]{1,0:T(8,128)(2,1)S(1)}, bf16[64,512]{1,0:T(8,128)(2,1)S(1)}, u32[]{:S(2)}, u32[]{:S(2)}) collective-permute-start(bf16[64,512]{1,0:T(8,128)(2,1)S(1)} %collective-permute-done.15.refs_2_), channel_id=1, source_target_pairs={{0,4},{4,0},{8,12},{12,8},{16,20},{20,16},{24,28},{28,24},{1,5},{5... | collective-permute-start | bytes 196616 | tf_op jit(solution)/shard_map/ppermute | solution.py:42
  63.1 1.3 %collective-permute-start.20 = (bf16[64,512]{1,0:T(8,128)(2,1)S(1)}, bf16[64,512]{1,0:T(8,128)(2,1)S(1)}, u32[]{:S(2)}, u32[]{:S(2)}) collective-permute-start(bf16[64,512]{1,0:T(8,128)(2,1)S(1)} %collective-permute-done.16.refs_3_), channel_id=1, source_target_pairs={{0,4},{4,0},{8,12},{12,8},{16,20},{20,16},{24,28},{28,24},{1,5},{5... | collective-permute-start | bytes 196616 | tf_op jit(solution)/shard_map/ppermute | solution.py:42
  68.9 9.6 %collective-permute-start.23 = (s16[64,2176]{1,0:T(8,128)(2,1)S(1)}, s16[64,2176]{1,0:T(8,128)(2,1)S(1)}, u32[]{:S(2)}, u32[]{:S(2)}) collective-permute-start(s16[64,2176]{1,0:T(8,128)(2,1)S(1)} %get-tuple-element.37), channel_id=1, source_target_pairs={{0,8},{4,12},{8,0},{12,4},{16,24},{20,28},{24,16},{28,20},{1,9},{5... | collective-permute-start | bytes 835592 | tf_op jit(solution)/shard_map/ppermute | solution.py:42
  69.0 14.7 %collective-permute-start.22 = (s16[64,2176]{1,0:T(8,128)(2,1)S(1)}, s16[64,2176]{1,0:T(8,128)(2,1)S(1)}, u32[]{:S(2)}, u32[]{:S(2)}) collective-permute-start(s16[64,2176]{1,0:T(8,128)(2,1)S(1)} %get-tuple-element.36), channel_id=1, source_target_pairs={{0,8},{4,12},{8,0},{12,4},{16,24},{20,28},{24,16},{28,20},{1,9},{5... | collective-permute-start | bytes 835592 | tf_op jit(solution)/shard_map/ppermute | solution.py:42
  78.7 11.9 %collective-permute-start.24 = (s16[64,2176]{1,0:T(8,128)(2,1)S(1)}, s16[64,2176]{1,0:T(8,128)(2,1)S(1)}, u32[]{:S(2)}, u32[]{:S(2)}) collective-permute-start(s16[64,2176]{1,0:T(8,128)(2,1)S(1)} %relay.1), channel_id=1, source_target_pairs={{0,24},{4,28},{8,16},{12,20},{16,8},{20,12},{24,0},{28,4},{1,25},{... | collective-permute-start | bytes 835592 | tf_op jit(solution)/shard_map/ppermute | solution.py:42
  91.5 1.6 %collective-permute-start.25 = (f32[32,2048]{1,0:T(8,128)S(1)}, f32[32,2048]{1,0:T(8,128)S(1)}, u32[]{:S(2)}, u32[]{:S(2)}) collective-permute-start(f32[32,2048]{1,0:T(8,128)S(1)} %get-tuple-element.40), channel_id=1, source_target_pairs={{0,4},{4,0},{8,12},{12,8},{16,20},{20,16},{24,28},{28,24},{1,5},{5... | collective-permute-start | bytes 786440 | tf_op jit(solution)/shard_map/ppermute | solution.py:42
  (2 other events, 1.8 us)

commit v3 on v2

--- a/solution.py
+++ b/solution.py
@@ -232,7 +232,7 @@
 
 def quantile_kernel(low_ref, high_ref, rank_ref, value_ref, *refs):
     code_refs, (weight_ref, quantile_ref, held) = refs[:-3], refs[-3:]
-    share, rows = value_ref.shape
+    share, rows = code_refs[0].shape
     for at, code_ref in enumerate(code_refs):
         held[:, at * rows : (at + 1) * rows] = code_ref[...].astype(F32)
     width = held.shape[1]
@@ -258,17 +258,19 @@
         chosen = jnp.clip(below, 1.0, float(PIVOTS - 1))
         lower, upper = lower + (chosen - 1.0) * spacing, lower + chosen * spacing
     quantile = (lower + upper) * 0.5
-    quantile_ref[...] = quantile
     weight_ref[...] = jax.nn.sigmoid((quantile - value_ref[...]) / tail_width).astype(BF16)
+    quantile = jnp.broadcast_to(quantile, (share, LANES))
+    square = jnp.concatenate([quantile, jnp.zeros((LANES - share, LANES), F32)], axis=0)
+    quantile_ref[...] = square.T[: quantile_ref.shape[0], :]
 
 
 def quantiles(low, high, rank, value, codes):
-    share, rows = value.shape
+    share, rows = codes[0].shape
     return pl.pallas_call(
         quantile_kernel,
         out_shape=[
             jax.ShapeDtypeStruct((share, rows), BF16),
-            jax.ShapeDtypeStruct((share, 1), F32),
+            jax.ShapeDtypeStruct((8, LANES), F32),
         ],
         scratch_shapes=[pltpu.VMEM((share, rows * len(codes)), F32)],
         compiler_params=params(16),
@@ -309,12 +311,6 @@
     return total, mass
 
 
-def put_plain(ref, total, mass):
-    cols = total.shape[1]
-    ref[:, :cols] = total
-    ref[:, cols:] = jnp.broadcast_to(mass, (total.shape[0], LANES))
-
-
 def get_plain(ref):
     cols = ref.shape[1] - LANES
     return ref[:, :cols], ref[:, cols : cols + 1]
@@ -322,80 +318,64 @@
 
 def tail_kernel(slots, lines, where_ref, *refs):
     count = CORES * slots
-    weight_refs = refs[:count]
-    profit_refs = refs[count : count + CORES]
-    away_ref, partner_ref, handled_ref, own_ref, held, total = refs[count + CORES :]
-    step = pl.program_id(0)
+    weight_refs, profit_refs = refs[:count], refs[count : count + CORES]
+    out_refs, (held, total) = refs[count + CORES : -2], refs[-2:]
+    away_refs, partner_refs, handled_refs, own_refs = (out_refs[k : k + 2] for k in range(0, 8, 2))
     share, rows = weight_refs[0].shape
     books = share * slots
     block = books // lines
     piece = min(share, block)
-    tile = profit_refs[0].shape[1]
-
-    @pl.when(step == 0)
-    def _():
+    for slot in range(slots):
         for core in range(CORES):
-            for slot in range(slots):
-                ref = weight_refs[core * slots + slot]
-                for at in range(0, share, piece):
-                    start = (where_ref[0] ^ slot) * share + at
-                    line = start // block
-                    to = (where_ref[2] ^ line) * block + (start - line * block)
-                    to = pl.multiple_of(to, piece)
-                    held[pl.ds(to, piece), core * rows : (core + 1) * rows] = ref[at : at + piece, :]
-
-    spot = pl.multiple_of(step * tile, tile)
-    result = dot(held[:, :rows], profit_refs[0][...])
-    total[:, pl.ds(spot, tile)] = result + dot(held[:, rows:], profit_refs[1][...])
-
-    @pl.when(step == pl.num_programs(0) - 1)
-    def _():
-        for line in range(lines):
-            at = line * block
-            value = total[at : at + block, :]
-            mass = jnp.sum(held[at : at + block, :].astype(F32), axis=1, keepdims=True)
-            to = (line // 2 - 1) * block
+            ref = weight_refs[core * slots + slot]
+            for at in range(0, share, piece):
+                start = (where_ref[0] ^ slot) * share + at
+                line = start // block
+                to = (where_ref[2] ^ line) * block + (start - line * block)
+                to = pl.multiple_of(to, piece)
+                held[pl.ds(to, piece), core * rows : (core + 1) * rows] = ref[at : at + piece, :]
+    cols = total.shape[1] - LANES
+    for part in tiles(cols, cols // 4):
+        result = dot(held[:, :rows], profit_refs[0][:, part])
+        total[:, part] = result + dot(held[:, rows:], profit_refs[1][:, part])
+    mass = jnp.sum(held[...].astype(F32), axis=1, keepdims=True)
+    total[:, cols:] = jnp.broadcast_to(mass, (books, LANES))
+    half = block // CORES
+    for side in range(CORES):
+        core = where_ref[1] if side == 0 else 1 - where_ref[1]
+        for line in [*range(2, lines, 2), 1, *range(3, lines, 2), 0]:
+            spot = pl.ds(pl.multiple_of(line * block + core * half, half), half)
+            value = total[spot, :]
+            to = slice((line // 2 - 1) * half, line // 2 * half)
             if line == 0:
-                put_plain(own_ref, value, mass)
+                own_refs[side][...] = value
             elif line == 1:
-                put_words(partner_ref, value, mass)
+                put_words(partner_refs[side], value[:, :cols], value[:, cols : cols + 1])
             elif line % 2 == 0:
-                put_words(away_ref.at[to : to + block], value, mass)
+                put_words(away_refs[side].at[to, :], value[:, :cols], value[:, cols : cols + 1])
             else:
-                put_plain(handled_ref.at[to : to + block], value, mass)
-
-
-def tail_sums(where, weights, profit_pair, slots, lines, tile):
+                handled_refs[side][to, :] = value
+
+
+def tail_sums(where, weights, profit_pair, slots, lines):
     share, rows = weights[0].shape
     cols = profit_pair[0].shape[1]
     books = share * slots
-    block = books // lines
+    half = books // lines // CORES
     others = lines // 2 - 1
     wide = cols + LANES
-    specs = [pl.BlockSpec((share, rows), lambda n, w: (0, 0)) for _ in weights]
-    specs += [pl.BlockSpec((rows, tile), lambda n, w: (0, n)) for _ in profit_pair]
-    shapes = [
-        ((others * block, wide), jnp.int16),
-        ((block, wide), jnp.int16),
-        ((others * block, wide), F32),
-        ((block, wide), F32),
-    ]
+    kinds = [(others * half, jnp.int16), (half, jnp.int16), (others * half, F32), (half, F32)]
+    vmem = pl.BlockSpec(memory_space=pltpu.VMEM)
+    inputs = [*weights, *profit_pair]
     return pl.pallas_call(
         functools.partial(tail_kernel, slots, lines),
-        out_shape=[jax.ShapeDtypeStruct(*shape) for shape in shapes],
-        grid_spec=pltpu.PrefetchScalarGridSpec(
-            num_scalar_prefetch=1,
-            grid=(cols // tile,),
-            in_specs=specs,
-            out_specs=[pl.BlockSpec(shape, lambda n, w: (0, 0)) for shape, _ in shapes],
-            scratch_shapes=[
-                pltpu.VMEM((books, CORES * rows), BF16),
-                pltpu.VMEM((books, cols), F32),
-            ],
-        ),
-        compiler_params=params(48),
+        out_shape=[jax.ShapeDtypeStruct((n, wide), kind) for n, kind in kinds for _ in range(CORES)],
+        in_specs=[pl.BlockSpec(memory_space=pltpu.SMEM)] + [vmem] * len(inputs),
+        out_specs=[vmem] * (len(kinds) * CORES),
+        scratch_shapes=[pltpu.VMEM((books, CORES * rows), BF16), pltpu.VMEM((books, wide), F32)],
+        compiler_params=params(24),
         name="tail_sums",
-    )(where, *weights, *profit_pair)
+    )(where, *inputs)
 
 
 def relay_kernel(words_ref, plain_ref, out_ref):
@@ -413,31 +393,30 @@
     )(words, plain)
 
 
-def finish_kernel(where_ref, plain_ref, *refs):
-    words_refs, (keep_ref, give_ref, held) = refs[:-3], refs[-3:]
-    total, mass = get_plain(plain_ref)
-    for words_ref in words_refs:
-        more, more_mass = get_words(words_ref)
-        total, mass = total + more, mass + more_mass
-    held[...] = total / mass
-    rows = keep_ref.shape[0]
-    keep_ref[...] = held[pl.ds(pl.multiple_of(where_ref[1] * rows, rows), rows), :]
-    give_ref[...] = held[pl.ds(pl.multiple_of((1 - where_ref[1]) * rows, rows), rows), :]
-
-
-def finish(where, plain, words):
-    block, wide = plain.shape
-    cols = wide - LANES
+def finish_kernel(where_ref, *refs):
+    groups, out_ref = (refs[: len(refs) // 2], refs[len(refs) // 2 : -1]), refs[-1]
+    cols = groups[0][0].shape[1] - LANES
+    for side, group in enumerate(groups):
+        total, mass = get_plain(group[0])
+        for words_ref in group[1:]:
+            more, more_mass = get_words(words_ref)
+            total, mass = total + more, mass + more_mass
+        core = where_ref[1] if side == 0 else 1 - where_ref[1]
+        out_ref[:, pl.ds(pl.multiple_of(core * cols, cols), cols)] = total * (1.0 / mass)
+
+
+def finish(where, groups):
+    half, wide = groups[0][0].shape
+    inputs = [*groups[0], *groups[1]]
     vmem = pl.BlockSpec(memory_space=pltpu.VMEM)
     return pl.pallas_call(
         finish_kernel,
-        out_shape=[jax.ShapeDtypeStruct((block // CORES, cols), F32)] * 2,
-        in_specs=[pl.BlockSpec(memory_space=pltpu.SMEM)] + [vmem] * (1 + len(words)),
-        out_specs=[vmem] * 2,
-        scratch_shapes=[pltpu.VMEM((block, cols), F32)],
+        out_shape=jax.ShapeDtypeStruct((half, (wide - LANES) * CORES), F32),
+        in_specs=[pl.BlockSpec(memory_space=pltpu.SMEM)] + [vmem] * len(inputs),
+        out_specs=vmem,
         compiler_params=params(16),
         name="finish",
-    )(where, plain, *words)
+    )(where, *inputs)
 
 
 def body(shocks, loadings, delta, gamma, kappa, book_of, bracket_low, bracket_high, rank):
@@ -470,23 +449,24 @@
     value, code = book_values(scale, low, high, parts)
     codes = [code] + [swap(code, "scen", CORES * k) for k in range(1, lines)]
     codes = codes + [swap(c, "scen", 1) for c in codes]
-    weight, quantile = quantiles(low, high, own_rank, value, codes)
+    weight, row = quantiles(low, high, own_rank, value, codes)
     weights = [weight] + [swap(weight, "inst", slot) for slot in range(1, slots)]
-    others = [swap(w, "scen", 1) for w in weights]
-
-    away, partner, handled, plain = tail_sums(where, weights + others, [mine, got], slots, lines, 512)
-    passed = swap(away, "scen", CORES)
-    from_partner = swap(partner, "scen", CORES)
-    sent = relay(passed, handled)
-    block = books // lines
-    words = [from_partner]
-    for k in range(1, lines // 2):
-        words.append(swap(sent[(k - 1) * block : k * block], "scen", CORES * (2 * k + 1)))
-    keep, give = finish(where, plain, words)
-    taken = swap(give, "scen", 1)
-    left = jnp.where(core == 0, keep, taken)
-    right = jnp.where(core == 0, taken, keep)
-    return jnp.concatenate([left, right], axis=1), quantile[:, 0]
+    weights = weights + [swap(w, "scen", 1) for w in weights]
+
+    outs = tail_sums(where, weights, [mine, got], slots, lines)
+    away, partner, handled, plain = (outs[k : k + 2] for k in range(0, 8, 2))
+    half = books // lines // CORES
+    groups = []
+    for side in range(CORES):
+        passed = swap(away[side], "scen", CORES)
+        words = [swap(partner[side], "scen", CORES ^ side)]
+        sent = relay(passed, handled[side])
+        for k in range(1, lines // 2):
+            block = sent[(k - 1) * half : k * half]
+            words.append(swap(block, "scen", (CORES * (2 * k + 1)) ^ side))
+        first = plain[0] if side == 0 else swap(plain[1], "scen", 1)
+        groups.append([first, *words])
+    return finish(where, groups), row[0, :share]
 
 
 def solution(mesh):

time: 94.3 us -> 91.2 us (0.967)
  waiting for transfers between devices: 38.7 us -> 35 us
  starting transfers between devices: 23.6 us -> 25.4 us
  other arithmetic: 1.57 us -> 0.08 us
    ppermute x26 -> x29, waiting for transfers between devices: 38.7 us -> 35 us  [swap(): return lax.ppermute(value, axis, [(k, k ^ flip) for k in range(n)])]
    ppermute x26 -> x29, starting transfers between devices: 23.6 us -> 25.4 us  [swap(): return lax.ppermute(value, axis, [(k, k ^ flip) for k in range(n)])]
    pallas_call x1, Pallas kernels: 4.51 us -> 3.22 us  [tail_sums(): pl.pallas_call(functools.partial(tail_kernel, slots, lines), out_shape=[j...]
  transfers between devices with their start and end apart: 26 -> 29, of which waited for: 16 -> 18; matrix products, arithmetic and copies ran while one was open for 1% -> 1% of each run, Pallas kernels for 17% -> 18%
where the time goes in v3:
time: 91.2 us; the launch traced here: 90.9 us
  waiting for transfers between devices  35 us (38%)
  Pallas kernels  26.8 us (29%)
  starting transfers between devices  25.4 us (28%)
  local copies, waits for them, and re-layouts  2.78 us (3%)
    ppermute x29, waiting for transfers between devices, swap(): return lax.ppermute(value, axis, [(k, k ^ flip) for k in range(n)])  35 us
    ppermute x29, starting transfers between devices, swap(): return lax.ppermute(value, axis, [(k, k ^ flip) for k in range(n)])  25.4 us
    pallas_call x1, Pallas kernels, stage(): pl.pallas_call(functools.partial(stage_kernel, slots, near, far), out_sha...  6.48 us
    pallas_call x1, Pallas kernels, profits(): pl.pallas_call(functools.partial(profit_kernel, len(tops)), out_shape=out...  5.99 us
    pallas_call x1, Pallas kernels, add_moves(): pl.pallas_call(add_moves_kernel, out_shape=jax.ShapeDtypeStruct((rows, co...  4.94 us
    pallas_call x1, Pallas kernels, quantiles(): pl.pallas_call(quantile_kernel, out_shape=[jax.ShapeDtypeStruct((share, r...  3.93 us
    pallas_call x1, Pallas kernels, tail_sums(): pl.pallas_call(functools.partial(tail_kernel, slots, lines), out_shape=[j...  3.22 us
  transfers between devices with their start and end apart: 29, of which 18 were waited for; matrix products, arithmetic and copies ran while one was open for 1% of the time, Pallas kernels for 18%

profile of v3, /device:TPU:0, one launch (start us, length us, event | category | flops | bytes accessed | tf_op | source)
XLA Modules:
  0.0 90.9 jit_solution(15981672708421476373)
XLA Ops:
  0.6 3.0 %collective-permute-start = (bf16[512,512]{1,0:T(8,128)(2,1)}, bf16[512,512]{1,0:T(8,128)(2,1)S(1)}, u32[]{:S(2)}, u32[]{:S(2)}) collective-permute-start(bf16[512,512]{1,0:T(8,128)(2,1)} %shocks_ref.1), channel_id=1, source_target_pairs={{0,1},{1,0},{2,3},{3,2},{4,5},{5,4},{6,7},{7,6},{8,9},{9,8},{10,11... | collective-permute-start | bytes 1572872 | tf_op jit(solution)/shard_map/ppermute | solution.py:42
  3.6 1.5 %collective-permute-start.2 = (bf16[512,512]{1,0:T(8,128)(2,1)}, bf16[512,512]{1,0:T(8,128)(2,1)S(1)}, u32[]{:S(2)}, u32[]{:S(2)}) collective-permute-start(bf16[512,512]{1,0:T(8,128)(2,1)} %shocks_ref.1), channel_id=1, source_target_pairs={{0,2},{1,3},{2,0},{3,1},{4,6},{5,7},{6,4},{7,5},{8,10},{9,11},{10,... | collective-permute-start | bytes 1572872 | tf_op jit(solution)/shard_map/ppermute | solution.py:42
  7.0 6.5 %stage.1 = (f32[512,4096]{1,0:T(8,128)S(1)}, bf16[1024,4096]{1,0:T(8,128)(2,1)S(1)}, bf16[512,4096]{1,0:T(8,128)(2,1)S(1)}, bf16[256,4096]{1,0:T(8,128)(2,1)S(1)}) custom-call(s32[3]{0:T(128)S(1)} %pad_add_fusion.where_ref, bf16[512,512]{1,0:T(8,128)(2,1)S(1)} %copy-done.1, s32[1,4096]{1,0:T(1,128)S(1)} %bitcast.15, bf16[2048,4096]{1,0:T(8,128)(2,1)} %loadings_ref.1), custom_call_target="tpu_custom_call" | custom-call | flops 2147483648 | bytes 16777216 | tf_op jit(solution)/shard_map/stage/pallas_call | solution.py:86
  13.5 2.3 %collective-permute-done.refs_0_ = bf16[512,512]{1,0:T(8,128)(2,1)S(1)} collective-permute-done((bf16[512,512]{1,0:T(8,128)(2,1)}, bf16[512,512]{1,0:T(8,128)(2,1)S(1)}, u32[]{:S(2)}, u32[]{:S(2)}) %collective-permute-start) | collective-permute-done | bytes 524320 | tf_op jit(solution)/shard_map/ppermute | solution.py:42
  15.8 1.8 %collective-permute-start.1 = (bf16[256,512]{1,0:T(8,128)(2,1)S(1)}, bf16[256,512]{1,0:T(8,128)(2,1)S(1)}, u32[]{:S(2)}, u32[]{:S(2)}) collective-permute-start(bf16[256,512]{1,0:T(8,128)(2,1)S(1)} %slice.12), channel_id=1, source_target_pairs={{0,2},{1,3},{2,0},{3,1},{4,6},{5,7},{6,4},{7,5},{8,10},{9,11},{10,... | collective-permute-start | bytes 786440 | tf_op jit(solution)/shard_map/ppermute | solution.py:42
  17.7 1.6 %collective-permute-start.3 = (bf16[256,512]{1,0:T(8,128)(2,1)S(1)}, bf16[256,512]{1,0:T(8,128)(2,1)S(1)}, u32[]{:S(2)}, u32[]{:S(2)}) collective-permute-start(bf16[256,512]{1,0:T(8,128)(2,1)S(1)} %slice.13), channel_id=1, source_target_pairs={{0,1},{1,0},{2,3},{3,2},{4,5},{5,4},{6,7},{7,6},{8,9},{9,8},{10,11... | collective-permute-start | bytes 786440 | tf_op jit(solution)/shard_map/ppermute | solution.py:42
  19.2 4.9 %add_moves.1.refs_3_ = f32[512,4096]{1,0:T(8,128)S(1)} custom-call(bf16[512,512]{1,0:T(8,128)(2,1)S(1)} %collective-permute-done.refs_0_, bf16[512,512]{1,0:T(8,128)(2,1)S(1)} %collective-permute-done.2.refs_1_, bf16[1024,4096]{1,0:T(8,128)(2,1)S(1)} %get-tuple-element.25.refs_2_, ...), custom_call_target="tpu_custom_call", output_to_operand_aliasing={{}: (3, {})} | custom-call | flops 4294967296 | bytes 16777216 | tf_op jit(solution)/shard_map/add_moves/pallas_call | solution.py:120
  24.7 6.0 %profits.1 = (bf16[512,2048]{1,0:T(8,128)(2,1)S(1)}, bf16[512,2048]{1,0:T(8,128)(2,1)}, f32[64,512]{1,0:T(8,128)S(1)}, f32[64,512]{1,0:T(8,128)S(1)}, f32[64,512]{1,0:T(8,128)S(1)}, /*index=5*/f32[64,512]{1,0:T(8,128)S(1)}) custom-call(s32[3]{0:T(128)S(1)} %pad_add_fusion.where_ref, bf16[256,512]{1,0:T(8,128)(2,1)S(1)} %collective-permute-done.1.refs_0_, ...), custom_call_target="tpu_custom_call" | custom-call | flops 3221225472 | bytes 12582912 | tf_op jit(solution)/shard_map/profits/pallas_call | solution.py:170
  30.7 1.5 %collective-permute-start.4 = (f32[64,512]{1,0:T(8,128)S(1)}, f32[64,512]{1,0:T(8,128)S(1)}, u32[]{:S(2)}, u32[]{:S(2)}) collective-permute-start(f32[64,512]{1,0:T(8,128)S(1)} %get-tuple-element.29), channel_id=1, source_target_pairs={{0,1},{1,0},{2,3},{3,2},{4,5},{5,4},{6,7},{7,6},{8,9},{9,8},{10,11... | collective-permute-start | bytes 393224 | tf_op jit(solution)/shard_map/ppermute | solution.py:42
  32.6 1.5 %collective-permute-start.6 = (f32[64,512]{1,0:T(8,128)S(1)}, f32[64,512]{1,0:T(8,128)S(1)}, u32[]{:S(2)}, u32[]{:S(2)}) collective-permute-start(f32[64,512]{1,0:T(8,128)S(1)} %get-tuple-element.31), channel_id=1, source_target_pairs={{0,3},{1,2},{2,1},{3,0},{4,7},{5,6},{6,5},{7,4},{8,11},{9,10},{10,... | collective-permute-start | bytes 393224 | tf_op jit(solution)/shard_map/ppermute | solution.py:42
  34.4 2.5 %collective-permute-done.4.refs_1_ = f32[64,512]{1,0:T(8,128)S(1)} collective-permute-done((f32[64,512]{1,0:T(8,128)S(1)}, f32[64,512]{1,0:T(8,128)S(1)}, u32[]{:S(2)}, u32[]{:S(2)}) %collective-permute-start.4) | collective-permute-done | bytes 131104 | tf_op jit(solution)/shard_map/ppermute | solution.py:42
  36.9 3.6 %collective-permute-done.5.refs_2_ = f32[64,512]{1,0:T(8,128)S(1)} collective-permute-done((f32[64,512]{1,0:T(8,128)S(1)}, f32[64,512]{1,0:T(8,128)S(1)}, u32[]{:S(2)}, u32[]{:S(2)}) %collective-permute-start.5) | collective-permute-done | bytes 131104 | tf_op jit(solution)/shard_map/ppermute | solution.py:42
  40.7 1.6 %collective-permute-start.7 = (s16[64,512]{1,0:T(8,128)(2,1)S(1)}, s16[64,512]{1,0:T(8,128)(2,1)S(1)}, u32[]{:S(2)}, u32[]{:S(2)}) collective-permute-start(s16[64,512]{1,0:T(8,128)(2,1)S(1)} %get-tuple-element.33.refs_0_), channel_id=1, source_target_pairs={{0,8},{4,12},{8,0},{12,4},{16,24},{20,28},{24,16},{28,20},{1,9},{5... | collective-permute-start | bytes 196616 | tf_op jit(solution)/shard_map/ppermute | solution.py:42
  42.3 2.6 %collective-permute-start.8 = (s16[64,512]{1,0:T(8,128)(2,1)S(1)}, s16[64,512]{1,0:T(8,128)(2,1)S(1)}, u32[]{:S(2)}, u32[]{:S(2)}) collective-permute-start(s16[64,512]{1,0:T(8,128)(2,1)S(1)} %get-tuple-element.33.refs_0_), channel_id=1, source_target_pairs={{0,16},{4,20},{8,24},{12,28},{16,0},{20,4},{24,8},{28,12},{1,17},{... | collective-permute-start | bytes 196616 | tf_op jit(solution)/shard_map/ppermute | solution.py:42
  45.7 3.2 %collective-permute-done.8.refs_2_ = s16[64,512]{1,0:T(8,128)(2,1)S(1)} collective-permute-done((s16[64,512]{1,0:T(8,128)(2,1)S(1)}, s16[64,512]{1,0:T(8,128)(2,1)S(1)}, u32[]{:S(2)}, u32[]{:S(2)}) %collective-permute-start.8) | collective-permute-done | bytes 65568 | tf_op jit(solution)/shard_map/ppermute | solution.py:42
  48.9 2.1 %collective-permute-done.9.refs_3_ = s16[64,512]{1,0:T(8,128)(2,1)S(1)} collective-permute-done((s16[64,512]{1,0:T(8,128)(2,1)S(1)}, s16[64,512]{1,0:T(8,128)(2,1)S(1)}, u32[]{:S(2)}, u32[]{:S(2)}) %collective-permute-start.9) | collective-permute-done | bytes 65568 | tf_op jit(solution)/shard_map/ppermute | solution.py:42
  51.2 1.1 %collective-permute-done.13.refs_7_ = s16[64,512]{1,0:T(8,128)(2,1)S(1)} collective-permute-done((s16[64,512]{1,0:T(8,128)(2,1)S(1)}, s16[64,512]{1,0:T(8,128)(2,1)S(1)}, u32[]{:S(2)}, u32[]{:S(2)}) %collective-permute-start.13) | collective-permute-done | bytes 65568 | tf_op jit(solution)/shard_map/ppermute | solution.py:42
  52.3 3.9 %quantiles.1 = (bf16[64,512]{1,0:T(8,128)(2,1)S(1)}, f32[8,128]{1,0:T(8,128)S(1)}) custom-call(s32[64,1]{1,0:T(8,128)S(1)} %copy.14.low_ref, s32[64,1]{1,0:T(8,128)S(1)} %copy.15.high_ref, s32[64,1]{1,0:T(8,128)S(1)} %copy.16.rank_ref, f32[64,512]{1,0:T(8,128)S(1)} %get-tuple-element.32.value_ref, s16[64,512]{1,0:T(8,128)(2,1)S(1)} %get-tuple-element.33.refs_0_, ...), custom_call_target="tpu_custom_call" | custom-call | tf_op jit(solution)/shard_map/quantiles/pallas_call | solution.py:269
  56.7 1.2 %collective-permute-start.15 = (bf16[64,512]{1,0:T(8,128)(2,1)S(1)}, bf16[64,512]{1,0:T(8,128)(2,1)S(1)}, u32[]{:S(2)}, u32[]{:S(2)}) collective-permute-start(bf16[64,512]{1,0:T(8,128)(2,1)S(1)} %get-tuple-element.34.refs_0_), channel_id=1, source_target_pairs={{0,2},{1,3},{2,0},{3,1},{4,6},{5,7},{6,4},{7,5},{8,10},{9,11},{10,... | collective-permute-start | bytes 196616 | tf_op jit(solution)/shard_map/ppermute | solution.py:42
  58.0 1.8 %collective-permute-start.16 = (bf16[64,512]{1,0:T(8,128)(2,1)S(1)}, bf16[64,512]{1,0:T(8,128)(2,1)S(1)}, u32[]{:S(2)}, u32[]{:S(2)}) collective-permute-start(bf16[64,512]{1,0:T(8,128)(2,1)S(1)} %get-tuple-element.34.refs_0_), channel_id=1, source_target_pairs={{0,3},{1,2},{2,1},{3,0},{4,7},{5,6},{6,5},{7,4},{8,11},{9,10},{10,... | collective-permute-start | bytes 196616 | tf_op jit(solution)/shard_map/ppermute | solution.py:42
  61.1 2.0 %collective-permute-done.16.refs_3_ = bf16[64,512]{1,0:T(8,128)(2,1)S(1)} collective-permute-done((bf16[64,512]{1,0:T(8,128)(2,1)S(1)}, bf16[64,512]{1,0:T(8,128)(2,1)S(1)}, u32[]{:S(2)}, u32[]{:S(2)}) %collective-permute-start.16) | collective-permute-done | bytes 65568 | tf_op jit(solution)/shard_map/ppermute | solution.py:42
  63.1 1.2 %collective-permute-done.20.refs_7_ = bf16[64,512]{1,0:T(8,128)(2,1)S(1)} collective-permute-done((bf16[64,512]{1,0:T(8,128)(2,1)S(1)}, bf16[64,512]{1,0:T(8,128)(2,1)S(1)}, u32[]{:S(2)}, u32[]{:S(2)}) %collective-permute-start.20) | collective-permute-done | bytes 65568 | tf_op jit(solution)/shard_map/ppermute | solution.py:42
  64.4 3.2 %tail_sums.1 = (s16[32,2176]{1,0:T(8,128)(2,1)S(1)}, s16[32,2176]{1,0:T(8,128)(2,1)S(1)}, s16[32,2176]{1,0:T(8,128)(2,1)S(1)}, s16[32,2176]{1,0:T(8,128)(2,1)S(1...) custom-call(s32[3]{0:T(128)S(1)} %pad_add_fusion.where_ref, ...), custom_call_target="tpu_custom_call" | custom-call | tf_op jit(solution)/shard_map/tail_sums/pallas_call | solution.py:370
  67.7 2.0 %collective-permute-start.23 = (s16[32,2176]{1,0:T(8,128)(2,1)S(1)}, s16[32,2176]{1,0:T(8,128)(2,1)S(1)}, u32[]{:S(2)}, u32[]{:S(2)}) collective-permute-start(s16[32,2176]{1,0:T(8,128)(2,1)S(1)} %get-tuple-element.39), channel_id=1, source_target_pairs={{0,8},{4,12},{8,0},{12,4},{16,24},{20,28},{24,16},{28,20},{1,9},{5... | collective-permute-start | bytes 417800 | tf_op jit(solution)/shard_map/ppermute | solution.py:42
  69.8 1.8 %collective-permute-start.26 = (s16[32,2176]{1,0:T(8,128)(2,1)S(1)}, s16[32,2176]{1,0:T(8,128)(2,1)S(1)}, u32[]{:S(2)}, u32[]{:S(2)}) collective-permute-start(s16[32,2176]{1,0:T(8,128)(2,1)S(1)} %get-tuple-element.42), channel_id=1, source_target_pairs={{0,12},{4,8},{8,4},{12,0},{16,28},{20,24},{24,20},{28,16},{1,13},{... | collective-permute-start | bytes 417800 | tf_op jit(solution)/shard_map/ppermute | solution.py:42
  71.6 2.6 %collective-permute-done.27.words_ref = s16[32,2176]{1,0:T(8,128)(2,1)S(1)} collective-permute-done((s16[32,2176]{1,0:T(8,128)(2,1)S(1)}, s16[32,2176]{1,0:T(8,128)(2,1)S(1)}, u32[]{:S(2)}, u32[]{:S(2)}) %collective-permute-start.27) | collective-permute-done | bytes 139296 | tf_op jit(solution)/shard_map/ppermute | solution.py:42
  74.5 2.7 %collective-permute-done.23.words_ref = s16[32,2176]{1,0:T(8,128)(2,1)S(1)} collective-permute-done((s16[32,2176]{1,0:T(8,128)(2,1)S(1)}, s16[32,2176]{1,0:T(8,128)(2,1)S(1)}, u32[]{:S(2)}, u32[]{:S(2)}) %collective-permute-start.23) | collective-permute-done | bytes 139296 | tf_op jit(solution)/shard_map/ppermute | solution.py:42
  77.4 1.9 %collective-permute-start.24 = (s16[32,2176]{1,0:T(8,128)(2,1)S(1)}, s16[32,2176]{1,0:T(8,128)(2,1)S(1)}, u32[]{:S(2)}, u32[]{:S(2)}) collective-permute-start(s16[32,2176]{1,0:T(8,128)(2,1)S(1)} %relay.2), channel_id=1, source_target_pairs={{0,24},{4,28},{8,16},{12,20},{16,8},{20,12},{24,0},{28,4},{1,25},{... | collective-permute-start | bytes 417800 | tf_op jit(solution)/shard_map/ppermute | solution.py:42
  80.2 1.4 %collective-permute-done.26.refs_4_ = s16[32,2176]{1,0:T(8,128)(2,1)S(1)} collective-permute-done((s16[32,2176]{1,0:T(8,128)(2,1)S(1)}, s16[32,2176]{1,0:T(8,128)(2,1)S(1)}, u32[]{:S(2)}, u32[]{:S(2)}) %collective-permute-start.26) | collective-permute-done | bytes 139296 | tf_op jit(solution)/shard_map/ppermute | solution.py:42
  81.6 3.9 %collective-permute-done.28.refs_5_ = s16[32,2176]{1,0:T(8,128)(2,1)S(1)} collective-permute-done((s16[32,2176]{1,0:T(8,128)(2,1)S(1)}, s16[32,2176]{1,0:T(8,128)(2,1)S(1)}, u32[]{:S(2)}, u32[]{:S(2)}) %collective-permute-start.28) | collective-permute-done | bytes 139296 | tf_op jit(solution)/shard_map/ppermute | solution.py:42
  85.5 3.8 %collective-permute-done.24.refs_2_ = s16[32,2176]{1,0:T(8,128)(2,1)S(1)} collective-permute-done((s16[32,2176]{1,0:T(8,128)(2,1)S(1)}, s16[32,2176]{1,0:T(8,128)(2,1)S(1)}, u32[]{:S(2)}, u32[]{:S(2)}) %collective-permute-start.24) | collective-permute-done | bytes 139296 | tf_op jit(solution)/shard_map/ppermute | solution.py:42
  89.2 1.7 %finish.1 = f32[32,4096]{1,0:T(8,128)} custom-call(s32[3]{0:T(128)S(1)} %pad_add_fusion.where_ref, f32[32,2176]{1,0:T(8,128)S(1)} %get-tuple-element.37.refs_0_, s16[32,2176]{1,0:T(8,128)(2,1)S(1)} %collective-permute-done.22.refs_1_, s16[32,2176]{1,0:T(8,128)(2,1)S(1)} %collective-permute-done.24.refs_2_, f32[32,2176]{1,0:T(8,128)S(1)} %collective-permute-done.25.refs_3_, ...), custom_call_target="tpu_custom_call" | custom-call | tf_op jit(solution)/shard_map/finish/pallas_call | solution.py:412
  (60 shorter events, 7.7 us)
Async XLA Ops:
  0.6 50.4 %copy-start = (s32[256]{0:T(256)S(1)}, s32[256]{0:T(256)}, u32[]{:S(2)}) copy-start(s32[256]{0:T(256)} %param.17) | copy-start | bytes 3076
  0.6 15.1 %collective-permute-start = (bf16[512,512]{1,0:T(8,128)(2,1)}, bf16[512,512]{1,0:T(8,128)(2,1)S(1)}, u32[]{:S(2)}, u32[]{:S(2)}) collective-permute-start(bf16[512,512]{1,0:T(8,128)(2,1)} %shocks_ref.1), channel_id=1, source_target_pairs={{0,1},{1,0},{2,3},{3,2},{4,5},{5,4},{6,7},{7,6},{8,9},{9,8},{10,11... | collective-permute-start | bytes 1572872 | tf_op jit(solution)/shard_map/ppermute | solution.py:42
  3.6 14.0 %collective-permute-start.2 = (bf16[512,512]{1,0:T(8,128)(2,1)}, bf16[512,512]{1,0:T(8,128)(2,1)S(1)}, u32[]{:S(2)}, u32[]{:S(2)}) collective-permute-start(bf16[512,512]{1,0:T(8,128)(2,1)} %shocks_ref.1), channel_id=1, source_target_pairs={{0,2},{1,3},{2,0},{3,1},{4,6},{5,7},{6,4},{7,5},{8,10},{9,11},{10,... | collective-permute-start | bytes 1572872 | tf_op jit(solution)/shard_map/ppermute | solution.py:42
  15.8 8.4 %collective-permute-start.1 = (bf16[256,512]{1,0:T(8,128)(2,1)S(1)}, bf16[256,512]{1,0:T(8,128)(2,1)S(1)}, u32[]{:S(2)}, u32[]{:S(2)}) collective-permute-start(bf16[256,512]{1,0:T(8,128)(2,1)S(1)} %slice.12), channel_id=1, source_target_pairs={{0,2},{1,3},{2,0},{3,1},{4,6},{5,7},{6,4},{7,5},{8,10},{9,11},{10,... | collective-permute-start | bytes 786440 | tf_op jit(solution)/shard_map/ppermute | solution.py:42
  17.7 7.0 %collective-permute-start.3 = (bf16[256,512]{1,0:T(8,128)(2,1)S(1)}, bf16[256,512]{1,0:T(8,128)(2,1)S(1)}, u32[]{:S(2)}, u32[]{:S(2)}) collective-permute-start(bf16[256,512]{1,0:T(8,128)(2,1)S(1)} %slice.13), channel_id=1, source_target_pairs={{0,1},{1,0},{2,3},{3,2},{4,5},{5,4},{6,7},{7,6},{8,9},{9,8},{10,11... | collective-permute-start | bytes 786440 | tf_op jit(solution)/shard_map/ppermute | solution.py:42
  24.6 9.5 %copy-start.6 = (s32[256]{0:T(256)S(1)}, s32[256]{0:T(256)}, u32[]{:S(2)}) copy-start(s32[256]{0:T(256)} %param.16) | copy-start | bytes 3076
  24.6 9.5 %copy-start.7 = (s32[256]{0:T(256)S(1)}, s32[256]{0:T(256)}, u32[]{:S(2)}) copy-start(s32[256]{0:T(256)} %param.15) | copy-start | bytes 3076
  30.6 33.7 %collective-permute-start.21 = (bf16[512,2048]{1,0:T(8,128)(2,1)}, bf16[512,2048]{1,0:T(8,128)(2,1)}, u32[]{:S(2)}, u32[]{:S(2)}) collective-permute-start(bf16[512,2048]{1,0:T(8,128)(2,1)} %get-tuple-element.36), channel_id=1, source_target_pairs={{0,4},{4,0},{8,12},{12,8},{16,20},{20,16},{24,28},{28,24},{1,5},{5... | collective-permute-start | bytes 6291464 | tf_op jit(solution)/shard_map/ppermute | solution.py:42
  30.7 6.3 %collective-permute-start.4 = (f32[64,512]{1,0:T(8,128)S(1)}, f32[64,512]{1,0:T(8,128)S(1)}, u32[]{:S(2)}, u32[]{:S(2)}) collective-permute-start(f32[64,512]{1,0:T(8,128)S(1)} %get-tuple-element.29), channel_id=1, source_target_pairs={{0,1},{1,0},{2,3},{3,2},{4,5},{5,4},{6,7},{7,6},{8,9},{9,8},{10,11... | collective-permute-start | bytes 393224 | tf_op jit(solution)/shard_map/ppermute | solution.py:42
  32.1 8.4 %collective-permute-start.5 = (f32[64,512]{1,0:T(8,128)S(1)}, f32[64,512]{1,0:T(8,128)S(1)}, u32[]{:S(2)}, u32[]{:S(2)}) collective-permute-start(f32[64,512]{1,0:T(8,128)S(1)} %get-tuple-element.30), channel_id=1, source_target_pairs={{0,2},{1,3},{2,0},{3,1},{4,6},{5,7},{6,4},{7,5},{8,10},{9,11},{10,... | collective-permute-start | bytes 393224 | tf_op jit(solution)/shard_map/ppermute | solution.py:42
  32.6 7.9 %collective-permute-start.6 = (f32[64,512]{1,0:T(8,128)S(1)}, f32[64,512]{1,0:T(8,128)S(1)}, u32[]{:S(2)}, u32[]{:S(2)}) collective-permute-start(f32[64,512]{1,0:T(8,128)S(1)} %get-tuple-element.31), channel_id=1, source_target_pairs={{0,3},{1,2},{2,1},{3,0},{4,7},{5,6},{6,5},{7,4},{8,11},{9,10},{10,... | collective-permute-start | bytes 393224 | tf_op jit(solution)/shard_map/ppermute | solution.py:42
  40.7 5.0 %collective-permute-start.7 = (s16[64,512]{1,0:T(8,128)(2,1)S(1)}, s16[64,512]{1,0:T(8,128)(2,1)S(1)}, u32[]{:S(2)}, u32[]{:S(2)}) collective-permute-start(s16[64,512]{1,0:T(8,128)(2,1)S(1)} %get-tuple-element.33.refs_0_), channel_id=1, source_target_pairs={{0,8},{4,12},{8,0},{12,4},{16,24},{20,28},{24,16},{28,20},{1,9},{5... | collective-permute-start | bytes 196616 | tf_op jit(solution)/shard_map/ppermute | solution.py:42
  42.3 6.6 %collective-permute-start.8 = (s16[64,512]{1,0:T(8,128)(2,1)S(1)}, s16[64,512]{1,0:T(8,128)(2,1)S(1)}, u32[]{:S(2)}, u32[]{:S(2)}) collective-permute-start(s16[64,512]{1,0:T(8,128)(2,1)S(1)} %get-tuple-element.33.refs_0_), channel_id=1, source_target_pairs={{0,16},{4,20},{8,24},{12,28},{16,0},{20,4},{24,8},{28,12},{1,17},{... | collective-permute-start | bytes 196616 | tf_op jit(solution)/shard_map/ppermute | solution.py:42
  44.9 6.1 %collective-permute-start.9 = (s16[64,512]{1,0:T(8,128)(2,1)S(1)}, s16[64,512]{1,0:T(8,128)(2,1)S(1)}, u32[]{:S(2)}, u32[]{:S(2)}) collective-permute-start(s16[64,512]{1,0:T(8,128)(2,1)S(1)} %get-tuple-element.33.refs_0_), channel_id=1, source_target_pairs={{0,24},{4,28},{8,16},{12,20},{16,8},{20,12},{24,0},{28,4},{1,25},{... | collective-permute-start | bytes 196616 | tf_op jit(solution)/shard_map/ppermute | solution.py:42
  45.2 6.0 %collective-permute-start.10 = (s16[64,512]{1,0:T(8,128)(2,1)S(1)}, s16[64,512]{1,0:T(8,128)(2,1)S(1)}, u32[]{:S(2)}, u32[]{:S(2)}) collective-permute-start(s16[64,512]{1,0:T(8,128)(2,1)S(1)} %get-tuple-element.33.refs_0_), channel_id=1, source_target_pairs={{0,4},{4,0},{8,12},{12,8},{16,20},{20,16},{24,28},{28,24},{1,5},{5... | collective-permute-start | bytes 196616 | tf_op jit(solution)/shard_map/ppermute | solution.py:42
  45.7 5.5 %collective-permute-start.11 = (s16[64,512]{1,0:T(8,128)(2,1)S(1)}, s16[64,512]{1,0:T(8,128)(2,1)S(1)}, u32[]{:S(2)}, u32[]{:S(2)}) collective-permute-start(s16[64,512]{1,0:T(8,128)(2,1)S(1)} %collective-permute-done.7.refs_1_), channel_id=1, source_target_pairs={{0,4},{4,0},{8,12},{12,8},{16,20},{20,16},{24,28},{28,24},{1,5},{5... | collective-permute-start | bytes 196616 | tf_op jit(solution)/shard_map/ppermute | solution.py:42
  48.9 2.3 %collective-permute-start.12 = (s16[64,512]{1,0:T(8,128)(2,1)S(1)}, s16[64,512]{1,0:T(8,128)(2,1)S(1)}, u32[]{:S(2)}, u32[]{:S(2)}) collective-permute-start(s16[64,512]{1,0:T(8,128)(2,1)S(1)} %collective-permute-done.8.refs_2_), channel_id=1, source_target_pairs={{0,4},{4,0},{8,12},{12,8},{16,20},{20,16},{24,28},{28,24},{1,5},{5... | collective-permute-start | bytes 196616 | tf_op jit(solution)/shard_map/ppermute | solution.py:42
  51.0 1.3 %collective-permute-start.13 = (s16[64,512]{1,0:T(8,128)(2,1)S(1)}, s16[64,512]{1,0:T(8,128)(2,1)S(1)}, u32[]{:S(2)}, u32[]{:S(2)}) collective-permute-start(s16[64,512]{1,0:T(8,128)(2,1)S(1)} %collective-permute-done.9.refs_3_), channel_id=1, source_target_pairs={{0,4},{4,0},{8,12},{12,8},{16,20},{20,16},{24,28},{28,24},{1,5},{5... | collective-permute-start | bytes 196616 | tf_op jit(solution)/shard_map/ppermute | solution.py:42
  56.2 4.4 %collective-permute-start.14 = (bf16[64,512]{1,0:T(8,128)(2,1)S(1)}, bf16[64,512]{1,0:T(8,128)(2,1)S(1)}, u32[]{:S(2)}, u32[]{:S(2)}) collective-permute-start(bf16[64,512]{1,0:T(8,128)(2,1)S(1)} %get-tuple-element.34.refs_0_), channel_id=1, source_target_pairs={{0,1},{1,0},{2,3},{3,2},{4,5},{5,4},{6,7},{7,6},{8,9},{9,8},{10,11... | collective-permute-start | bytes 196616 | tf_op jit(solution)/shard_map/ppermute | solution.py:42
  56.7 4.3 %collective-permute-start.15 = (bf16[64,512]{1,0:T(8,128)(2,1)S(1)}, bf16[64,512]{1,0:T(8,128)(2,1)S(1)}, u32[]{:S(2)}, u32[]{:S(2)}) collective-permute-start(bf16[64,512]{1,0:T(8,128)(2,1)S(1)} %get-tuple-element.34.refs_0_), channel_id=1, source_target_pairs={{0,2},{1,3},{2,0},{3,1},{4,6},{5,7},{6,4},{7,5},{8,10},{9,11},{10,... | collective-permute-start | bytes 196616 | tf_op jit(solution)/shard_map/ppermute | solution.py:42
  58.0 5.2 %collective-permute-start.16 = (bf16[64,512]{1,0:T(8,128)(2,1)S(1)}, bf16[64,512]{1,0:T(8,128)(2,1)S(1)}, u32[]{:S(2)}, u32[]{:S(2)}) collective-permute-start(bf16[64,512]{1,0:T(8,128)(2,1)S(1)} %get-tuple-element.34.refs_0_), channel_id=1, source_target_pairs={{0,3},{1,2},{2,1},{3,0},{4,7},{5,6},{6,5},{7,4},{8,11},{9,10},{10,... | collective-permute-start | bytes 196616 | tf_op jit(solution)/shard_map/ppermute | solution.py:42
  59.7 3.4 %collective-permute-start.17 = (bf16[64,512]{1,0:T(8,128)(2,1)S(1)}, bf16[64,512]{1,0:T(8,128)(2,1)S(1)}, u32[]{:S(2)}, u32[]{:S(2)}) collective-permute-start(bf16[64,512]{1,0:T(8,128)(2,1)S(1)} %get-tuple-element.34.refs_0_), channel_id=1, source_target_pairs={{0,4},{4,0},{8,12},{12,8},{16,20},{20,16},{24,28},{28,24},{1,5},{5... | collective-permute-start | bytes 196616 | tf_op jit(solution)/shard_map/ppermute | solution.py:42
  60.6 2.5 %collective-permute-start.18 = (bf16[64,512]{1,0:T(8,128)(2,1)S(1)}, bf16[64,512]{1,0:T(8,128)(2,1)S(1)}, u32[]{:S(2)}, u32[]{:S(2)}) collective-permute-start(bf16[64,512]{1,0:T(8,128)(2,1)S(1)} %collective-permute-done.14.refs_1_), channel_id=1, source_target_pairs={{0,4},{4,0},{8,12},{12,8},{16,20},{20,16},{24,28},{28,24},{1,5},{5... | collective-permute-start | bytes 196616 | tf_op jit(solution)/shard_map/ppermute | solution.py:42
  61.0 2.1 %collective-permute-start.19 = (bf16[64,512]{1,0:T(8,128)(2,1)S(1)}, bf16[64,512]{1,0:T(8,128)(2,1)S(1)}, u32[]{:S(2)}, u32[]{:S(2)}) collective-permute-start(bf16[64,512]{1,0:T(8,128)(2,1)S(1)} %collective-permute-done.15.refs_2_), channel_id=1, source_target_pairs={{0,4},{4,0},{8,12},{12,8},{16,20},{20,16},{24,28},{28,24},{1,5},{5... | collective-permute-start | bytes 196616 | tf_op jit(solution)/shard_map/ppermute | solution.py:42
  63.1 1.3 %collective-permute-start.20 = (bf16[64,512]{1,0:T(8,128)(2,1)S(1)}, bf16[64,512]{1,0:T(8,128)(2,1)S(1)}, u32[]{:S(2)}, u32[]{:S(2)}) collective-permute-start(bf16[64,512]{1,0:T(8,128)(2,1)S(1)} %collective-permute-done.16.refs_3_), channel_id=1, source_target_pairs={{0,4},{4,0},{8,12},{12,8},{16,20},{20,16},{24,28},{28,24},{1,5},{5... | collective-permute-start | bytes 196616 | tf_op jit(solution)/shard_map/ppermute | solution.py:42
  67.6 6.6 %collective-permute-start.27 = (s16[32,2176]{1,0:T(8,128)(2,1)S(1)}, s16[32,2176]{1,0:T(8,128)(2,1)S(1)}, u32[]{:S(2)}, u32[]{:S(2)}) collective-permute-start(s16[32,2176]{1,0:T(8,128)(2,1)S(1)} %get-tuple-element.43), channel_id=1, source_target_pairs={{0,8},{4,12},{8,0},{12,4},{16,24},{20,28},{24,16},{28,20},{1,9},{5... | collective-permute-start | bytes 417800 | tf_op jit(solution)/shard_map/ppermute | solution.py:42
  67.7 9.5 %collective-permute-start.23 = (s16[32,2176]{1,0:T(8,128)(2,1)S(1)}, s16[32,2176]{1,0:T(8,128)(2,1)S(1)}, u32[]{:S(2)}, u32[]{:S(2)}) collective-permute-start(s16[32,2176]{1,0:T(8,128)(2,1)S(1)} %get-tuple-element.39), channel_id=1, source_target_pairs={{0,8},{4,12},{8,0},{12,4},{16,24},{20,28},{24,16},{28,20},{1,9},{5... | collective-permute-start | bytes 417800 | tf_op jit(solution)/shard_map/ppermute | solution.py:42
  69.7 19.5 %collective-permute-start.25 = (f32[32,2176]{1,0:T(8,128)S(1)}, f32[32,2176]{1,0:T(8,128)S(1)}, u32[]{:S(2)}, u32[]{:S(2)}) collective-permute-start(f32[32,2176]{1,0:T(8,128)S(1)} %get-tuple-element.41), channel_id=1, source_target_pairs={{0,4},{4,0},{8,12},{12,8},{16,20},{20,16},{24,28},{28,24},{1,5},{5... | collective-permute-start | bytes 835592 | tf_op jit(solution)/shard_map/ppermute | solution.py:42
  69.7 10.5 %collective-permute-start.22 = (s16[32,2176]{1,0:T(8,128)(2,1)S(1)}, s16[32,2176]{1,0:T(8,128)(2,1)S(1)}, u32[]{:S(2)}, u32[]{:S(2)}) collective-permute-start(s16[32,2176]{1,0:T(8,128)(2,1)S(1)} %get-tuple-element.38), channel_id=1, source_target_pairs={{0,8},{4,12},{8,0},{12,4},{16,24},{20,28},{24,16},{28,20},{1,9},{5... | collective-permute-start | bytes 417800 | tf_op jit(solution)/shard_map/ppermute | solution.py:42
  69.8 11.8 %collective-permute-start.26 = (s16[32,2176]{1,0:T(8,128)(2,1)S(1)}, s16[32,2176]{1,0:T(8,128)(2,1)S(1)}, u32[]{:S(2)}, u32[]{:S(2)}) collective-permute-start(s16[32,2176]{1,0:T(8,128)(2,1)S(1)} %get-tuple-element.42), channel_id=1, source_target_pairs={{0,12},{4,8},{8,4},{12,0},{16,28},{20,24},{24,20},{28,16},{1,13},{... | collective-permute-start | bytes 417800 | tf_op jit(solution)/shard_map/ppermute | solution.py:42
  74.4 11.0 %collective-permute-start.28 = (s16[32,2176]{1,0:T(8,128)(2,1)S(1)}, s16[32,2176]{1,0:T(8,128)(2,1)S(1)}, u32[]{:S(2)}, u32[]{:S(2)}) collective-permute-start(s16[32,2176]{1,0:T(8,128)(2,1)S(1)} %relay.3), channel_id=1, source_target_pairs={{0,28},{4,24},{8,20},{12,16},{16,12},{20,8},{24,4},{28,0},{1,29},{... | collective-permute-start | bytes 417800 | tf_op jit(solution)/shard_map/ppermute | solution.py:42
  77.4 11.8 %collective-permute-start.24 = (s16[32,2176]{1,0:T(8,128)(2,1)S(1)}, s16[32,2176]{1,0:T(8,128)(2,1)S(1)}, u32[]{:S(2)}, u32[]{:S(2)}) collective-permute-start(s16[32,2176]{1,0:T(8,128)(2,1)S(1)} %relay.2), channel_id=1, source_target_pairs={{0,24},{4,28},{8,16},{12,20},{16,8},{20,12},{24,0},{28,4},{1,25},{... | collective-permute-start | bytes 417800 | tf_op jit(solution)/shard_map/ppermute | solution.py:42
  (5 other events, 18.0 us)

commit v4 on v3

--- a/solution.py
+++ b/solution.py
@@ -11,11 +11,10 @@
 ROUNDS = 3
 CORES = 2
 LANES = 128
+RANK_PART = 64
 
 tail_width = 0.5
 bracket_unit = 0.125
-code_top = 65535.0
-code_mid = 32768.0
 top16 = 32600.0
 octave = 0.6931471805599453
 finest = 8.0
@@ -135,13 +134,13 @@
     top_refs, low_refs = refs[:count], refs[count : 2 * count]
     rest_ref, first_ref, delta_ref, gamma_ref, kappa_ref, onehot_ref = refs[2 * count : 2 * count + 6]
     mine_ref, theirs_ref = refs[2 * count + 6 : 2 * count + 8]
-    sum_refs, total = refs[2 * count + 8 : -1], refs[-1]
+    sum_refs, (total, held, sems) = refs[2 * count + 8 : -3], refs[-3:]
     half, depth = top_refs[0].shape
     part_cols = mine_ref.shape[1]
     tile = part_cols // 4
     share = sum_refs[0].shape[0]
-    fresh = True
-    for side, out_ref in ((1 - where_ref[1], theirs_ref), (where_ref[1], mine_ref)):
+    fresh, copies = True, []
+    for side, out_ref in ((1 - where_ref[1], held), (where_ref[1], mine_ref)):
         for spot in tiles(part_cols, tile):
             part = pl.ds(pl.multiple_of(side * part_cols + spot.start, tile), tile)
             pieces = []
@@ -153,11 +152,16 @@
                 pieces.append(value.astype(BF16))
             profit = jnp.concatenate(pieces, axis=0)
             out_ref[:, spot] = profit
+            if out_ref is held:
+                copies.append(pltpu.make_async_copy(held.at[:, spot], theirs_ref.at[:, spot], sems.at[len(copies)]))
+                copies[-1].start()
             sums = dot_nt(onehot_ref[:, part], profit)
             total[...] = sums if fresh else total[...] + sums
             fresh = False
     for slot, sum_ref in enumerate(sum_refs):
         sum_ref[...] = total[slot * share : (slot + 1) * share, :]
+    for copy in copies:
+        copy.wait()
 
 
 def profits(where, tops, lows, rest, first, delta, gamma, kappa, onehot, slots):
@@ -171,8 +175,12 @@
         functools.partial(profit_kernel, len(tops)),
         out_shape=out_shape,
         in_specs=[pl.BlockSpec(memory_space=pltpu.SMEM)] + [vmem] * (2 * len(tops) + 6),
-        out_specs=[vmem] * len(out_shape),
-        scratch_shapes=[pltpu.VMEM((books, rows), F32)],
+        out_specs=[vmem, pl.BlockSpec(memory_space=pltpu.HBM)] + [vmem] * slots,
+        scratch_shapes=[
+            pltpu.VMEM((books, rows), F32),
+            pltpu.VMEM((rows, cols // CORES), BF16),
+            pltpu.SemaphoreType.DMA((4,)),
+        ],
         compiler_params=params(16),
         cost_estimate=pl.CostEstimate(
             flops=2 * rows * cols * (depth * len(tops) + books),
@@ -203,79 +211,126 @@
     return profits(where, tops, lows, far_loads, first, delta, gamma, kappa, onehot, slots)
 
 
-def book_value_kernel(scale, low_ref, high_ref, *refs):
-    part_refs, (value_ref, code_ref) = refs[:-2], refs[-2:]
+def sorting_pairs(n):
+    pairs, p = [], 1
+    while p < n:
+        k = p
+        while k:
+            for j in range(k % p, n - k, 2 * k):
+                for i in range(j, j + min(k, n - j - k)):
+                    if i // (2 * p) == (i + k) // (2 * p):
+                        pairs.append((i, i + k))
+            k //= 2
+        p *= 2
+    return pairs
+
+
+def compare(values, pairs):
+    for i, j in pairs:
+        values[i], values[j] = jnp.minimum(values[i], values[j]), jnp.maximum(values[i], values[j])
+    return values
+
+
+def merged(one, other, most):
+    n = len(one)
+    if 2 * n <= most:
+        values = one + other[::-1]
+    else:
+        values = [jnp.minimum(a, b) for a, b in zip(one, other[::-1])]
+    n = len(values)
+    stride = n // 2
+    while stride:
+        compare(values, [(i, i + stride) for i in range(n) if not i & stride])
+        stride //= 2
+    return values
+
+
+def lowest(values, share, most):
+    values = compare(list(values), sorting_pairs(len(values)))
+    for axis, shift in [(0, 4), (0, 2), (0, 1)] + [(1, shift) for shift in doubling(share, LANES)]:
+        values = merged(values, [pltpu.roll(v, shift, axis) for v in values], most)
+    return values
+
+
+def doubling(start, stop):
+    while start < stop:
+        yield start
+        start *= 2
+
+
+def blocks_of(ref):
+    return [ref[at : at + 8, :] for at in range(0, ref.shape[0], 8)]
+
+
+def book_value_kernel(scale, most, *refs):
+    part_refs, (value_ref, list_ref) = refs[:-2], refs[-2:]
     value = part_refs[0][...]
     for part_ref in part_refs[1:]:
         value = value + part_ref[...]
     value = value * scale
     value_ref[...] = value
-    low = low_ref[...].astype(F32) * bracket_unit
-    high = high_ref[...].astype(F32) * bracket_unit
-    code = (value - low) * (code_top / (high - low))
-    code = jnp.minimum(jnp.maximum(code, 0.0), code_top)
-    code_ref[...] = (jnp.round(code) - code_mid).astype(jnp.int32).astype(jnp.int16)
-
-
-def book_values(scale, low, high, parts):
+    share, rows = value.shape
+    groups = LANES // share
+    depth = rows // groups
+    columns = jnp.concatenate([value[:, at : at + depth] for at in range(0, rows, depth)], axis=0).T
+    values = lowest([columns[at : at + 8, :] for at in range(0, depth, 8)], share, most)
+    place = lax.broadcasted_iota(jnp.int32, (8, LANES), 0)
+    place = place + lax.broadcasted_iota(jnp.int32, (8, LANES), 1) // share * 8
+    for at in range(0, most, 8 * groups):
+        block = values[at]
+        for k in range(1, 8 * groups):
+            block = jnp.where(place == k, values[at + k], block)
+        list_ref[at // groups : at // groups + 8, :] = block
+
+
+def book_values(scale, most, parts):
     share, rows = parts[0].shape
     return pl.pallas_call(
-        functools.partial(book_value_kernel, scale),
+        functools.partial(book_value_kernel, scale, most),
         out_shape=[
             jax.ShapeDtypeStruct((share, rows), F32),
-            jax.ShapeDtypeStruct((share, rows), jnp.int16),
+            jax.ShapeDtypeStruct((most * share // LANES, LANES), F32),
         ],
         compiler_params=params(16),
         name="book_values",
-    )(low, high, *parts)
-
-
-def quantile_kernel(low_ref, high_ref, rank_ref, value_ref, *refs):
-    code_refs, (weight_ref, quantile_ref, held) = refs[:-3], refs[-3:]
-    share, rows = code_refs[0].shape
-    for at, code_ref in enumerate(code_refs):
-        held[:, at * rows : (at + 1) * rows] = code_ref[...].astype(F32)
-    width = held.shape[1]
-    low = low_ref[...].astype(F32) * bracket_unit
-    high = high_ref[...].astype(F32) * bracket_unit
-    rank = rank_ref[...].astype(F32)
-    per_unit = code_top / (high - low)
-    lower, upper = low, high
+    )(*parts)
+
+
+def quantile_kernel(most, low_ref, high_ref, rank_ref, value_ref, *refs):
+    list_refs, (weight_ref, quantile_ref) = refs[:-2], refs[-2:]
+    share, rows = value_ref.shape
+    values = lowest([block for ref in list_refs for block in blocks_of(ref)], share, most)
+    rank = jnp.broadcast_to(rank_ref[...], (8, LANES))
+    sought = values[0]
+    for k in range(1, most):
+        sought = jnp.where(rank > k, values[k], sought)
+    sought = sought[:1, :]
+    lower = low_ref[...].astype(F32) * bracket_unit
+    upper = high_ref[...].astype(F32) * bracket_unit
+    levels = lax.broadcasted_iota(jnp.int32, (PIVOTS, LANES), 0).astype(F32)
     for _ in range(ROUNDS):
         spacing = (upper - lower) / (PIVOTS - 1)
-        below = jnp.zeros_like(low)
-        stride = PIVOTS // 2
-        while stride:
-            pivot = lower + (below + (stride - 1)) * spacing
-            mark = jnp.floor((pivot - low) * per_unit) - code_mid
-            mark = jnp.broadcast_to(mark, (share, LANES))
-            count = jnp.zeros((share, LANES), F32)
-            for at in range(0, width, LANES):
-                count = count + jnp.where(held[:, at : at + LANES] <= mark, 1.0, 0.0)
-            count = jnp.sum(count, axis=1, keepdims=True)
-            below = below + jnp.where(count < rank, float(stride), 0.0)
-            stride //= 2
-        chosen = jnp.clip(below, 1.0, float(PIVOTS - 1))
+        below = jnp.where(lower + levels * spacing < sought, 1.0, 0.0)
+        chosen = jnp.clip(jnp.sum(below, axis=0, keepdims=True), 1.0, float(PIVOTS - 1))
         lower, upper = lower + (chosen - 1.0) * spacing, lower + chosen * spacing
     quantile = (lower + upper) * 0.5
-    weight_ref[...] = jax.nn.sigmoid((quantile - value_ref[...]) / tail_width).astype(BF16)
-    quantile = jnp.broadcast_to(quantile, (share, LANES))
-    square = jnp.concatenate([quantile, jnp.zeros((LANES - share, LANES), F32)], axis=0)
-    quantile_ref[...] = square.T[: quantile_ref.shape[0], :]
-
-
-def quantiles(low, high, rank, value, codes):
-    share, rows = codes[0].shape
-    return pl.pallas_call(
-        quantile_kernel,
+    quantile_ref[...] = jnp.broadcast_to(quantile, quantile_ref.shape)
+    column = jnp.broadcast_to(quantile, (LANES, LANES)).T[:share, :]
+    column = jnp.concatenate([column] * (rows // LANES), axis=1)
+    weight_ref[...] = jax.nn.sigmoid((column - value_ref[...]) / tail_width).astype(BF16)
+
+
+def quantiles(most, low, high, rank, value, lists):
+    share, rows = value.shape
+    return pl.pallas_call(
+        functools.partial(quantile_kernel, most),
         out_shape=[
             jax.ShapeDtypeStruct((share, rows), BF16),
             jax.ShapeDtypeStruct((8, LANES), F32),
         ],
-        scratch_shapes=[pltpu.VMEM((share, rows * len(codes)), F32)],
         compiler_params=params(16),
         name="quantiles",
-    )(low, high, rank, value, *codes)
+    )(low, high, rank, value, *lists)
 
 
 def encode(total, mass):
@@ -316,45 +371,82 @@
     return ref[:, :cols], ref[:, cols : cols + 1]
 
 
-def tail_kernel(slots, lines, where_ref, *refs):
+def tail_part(held, profit_refs, total, spot, rows):
+    cols = total.shape[1] - LANES
+    weight = held[spot, :]
+    for part in tiles(cols, cols // 4):
+        result = dot(weight[:, :rows], profit_refs[0][:, part])
+        total[spot, part] = result + dot(weight[:, rows:], profit_refs[1][:, part])
+    mass = jnp.sum(weight.astype(F32), axis=1, keepdims=True)
+    total[spot, cols:] = jnp.broadcast_to(mass, (weight.shape[0], LANES))
+
+
+def halves(where_ref, total, line, block):
+    half = block // CORES
+    for side in range(CORES):
+        core = where_ref[1] if side == 0 else 1 - where_ref[1]
+        value = total[pl.ds(pl.multiple_of(line * block + core * half, half), half), :]
+        yield side, value
+
+
+def away_kernel(slots, lines, where_ref, *refs):
     count = CORES * slots
     weight_refs, profit_refs = refs[:count], refs[count : count + CORES]
-    out_refs, (held, total) = refs[count + CORES : -2], refs[-2:]
-    away_refs, partner_refs, handled_refs, own_refs = (out_refs[k : k + 2] for k in range(0, 8, 2))
+    away_refs, (held, total) = refs[count + CORES : -2], refs[-2:]
     share, rows = weight_refs[0].shape
-    books = share * slots
-    block = books // lines
+    block = share * slots // lines
     piece = min(share, block)
+    cols = total.shape[1] - LANES
+    half = block // CORES
+    away = [line for line in range(2, lines, 2)]
+    order = away + [1] + [line for line in range(3, lines, 2)] + [0]
     for slot in range(slots):
         for core in range(CORES):
             ref = weight_refs[core * slots + slot]
             for at in range(0, share, piece):
                 start = (where_ref[0] ^ slot) * share + at
                 line = start // block
-                to = (where_ref[2] ^ line) * block + (start - line * block)
-                to = pl.multiple_of(to, piece)
+                flip = where_ref[2] ^ line
+                place = 0
+                for k, known in enumerate(order):
+                    place = place + jnp.where(flip == known, k, 0)
+                to = pl.multiple_of(place * block + (start - line * block), piece)
                 held[pl.ds(to, piece), core * rows : (core + 1) * rows] = ref[at : at + piece, :]
+    tail_part(held, profit_refs, total, slice(0, len(away) * block), rows)
+    for k in range(len(away)):
+        for side, value in halves(where_ref, total, k, block):
+            put_words(away_refs[side].at[k * half : (k + 1) * half, :], value[:, :cols], value[:, cols : cols + 1])
+
+
+def home_kernel(lines, where_ref, held, *refs):
+    profit_refs, (partner_refs, handled_refs, own_refs) = refs[:CORES], (refs[k : k + 2] for k in (2, 4, 6))
+    total = refs[-1]
+    rows = held.shape[1] // CORES
+    block = held.shape[0] // lines
+    half = block // CORES
     cols = total.shape[1] - LANES
-    for part in tiles(cols, cols // 4):
-        result = dot(held[:, :rows], profit_refs[0][:, part])
-        total[:, part] = result + dot(held[:, rows:], profit_refs[1][:, part])
-    mass = jnp.sum(held[...].astype(F32), axis=1, keepdims=True)
-    total[:, cols:] = jnp.broadcast_to(mass, (books, LANES))
-    half = block // CORES
-    for side in range(CORES):
-        core = where_ref[1] if side == 0 else 1 - where_ref[1]
-        for line in [*range(2, lines, 2), 1, *range(3, lines, 2), 0]:
-            spot = pl.ds(pl.multiple_of(line * block + core * half, half), half)
-            value = total[spot, :]
-            to = slice((line // 2 - 1) * half, line // 2 * half)
-            if line == 0:
-                own_refs[side][...] = value
-            elif line == 1:
-                put_words(partner_refs[side], value[:, :cols], value[:, cols : cols + 1])
-            elif line % 2 == 0:
-                put_words(away_refs[side].at[to, :], value[:, :cols], value[:, cols : cols + 1])
-            else:
-                handled_refs[side][to, :] = value
+    skip = lines // 2 - 1
+    tail_part(held, profit_refs, total, slice(skip * block, lines * block), rows)
+    for side, value in halves(where_ref, total, skip, block):
+        put_words(partner_refs[side], value[:, :cols], value[:, cols : cols + 1])
+    for k in range(skip):
+        for side, value in halves(where_ref, total, skip + 1 + k, block):
+            handled_refs[side][k * half : (k + 1) * half, :] = value
+    for side, value in halves(where_ref, total, lines - 1, block):
+        own_refs[side][...] = value
+
+
+def tail_call(kernel, name, out_shape, scratch, where, inputs):
+    vmem = pl.BlockSpec(memory_space=pltpu.VMEM)
+    return pl.pallas_call(
+        kernel,
+        out_shape=[jax.ShapeDtypeStruct(shape, kind) for shape, kind in out_shape],
+        in_specs=[pl.BlockSpec(memory_space=pltpu.SMEM)] + [vmem] * len(inputs),
+        out_specs=[vmem] * len(out_shape),
+        scratch_shapes=[pltpu.VMEM(shape, kind) for shape, kind in scratch],
+        compiler_params=params(24),
+        name=name,
+    )(where, *inputs)
 
 
 def tail_sums(where, weights, profit_pair, slots, lines):
@@ -362,20 +454,28 @@
     cols = profit_pair[0].shape[1]
     books = share * slots
     half = books // lines // CORES
-    others = lines // 2 - 1
+    others = (lines // 2 - 1) * half
     wide = cols + LANES
-    kinds = [(others * half, jnp.int16), (half, jnp.int16), (others * half, F32), (half, F32)]
-    vmem = pl.BlockSpec(memory_space=pltpu.VMEM)
-    inputs = [*weights, *profit_pair]
-    return pl.pallas_call(
-        functools.partial(tail_kernel, slots, lines),
-        out_shape=[jax.ShapeDtypeStruct((n, wide), kind) for n, kind in kinds for _ in range(CORES)],
-        in_specs=[pl.BlockSpec(memory_space=pltpu.SMEM)] + [vmem] * len(inputs),
-        out_specs=[vmem] * (len(kinds) * CORES),
-        scratch_shapes=[pltpu.VMEM((books, CORES * rows), BF16), pltpu.VMEM((books, wide), F32)],
-        compiler_params=params(24),
-        name="tail_sums",
-    )(where, *inputs)
+    total = ((books, wide), F32)
+    held_shape = ((books, CORES * rows), BF16)
+    *away, held = tail_call(
+        functools.partial(away_kernel, slots, lines),
+        "away_sums",
+        [((others, wide), jnp.int16)] * CORES + [held_shape],
+        [total],
+        where,
+        [*weights, *profit_pair],
+    )
+    kinds = [(half, jnp.int16), (others, F32), (half, F32)]
+    outs = tail_call(
+        functools.partial(home_kernel, lines),
+        "home_sums",
+        [((n, wide), kind) for n, kind in kinds for _ in range(CORES)],
+        [total],
+        where,
+        [held, *profit_pair],
+    )
+    return away, outs[0:2], outs[2:4], outs[4:6]
 
 
 def relay_kernel(words_ref, plain_ref, out_ref):
@@ -391,6 +491,23 @@
         compiler_params=params(16),
         name="relay",
     )(words, plain)
+
+
+def merge_kernel(plain_ref, words_ref, out_ref):
+    total, mass = get_plain(plain_ref)
+    more, more_mass = get_words(words_ref)
+    cols = total.shape[1]
+    out_ref[:, :cols] = total + more
+    out_ref[:, cols:] = jnp.broadcast_to(mass + more_mass, (total.shape[0], LANES))
+
+
+def merge(plain, words):
+    return pl.pallas_call(
+        merge_kernel,
+        out_shape=jax.ShapeDtypeStruct(plain.shape, F32),
+        compiler_params=params(16),
+        name="merge",
+    )(plain, words)
 
 
 def finish_kernel(where_ref, *refs):
@@ -443,28 +560,30 @@
     )
     got = swap(theirs, "scen", 1)
 
-    own = lambda v: lax.dynamic_slice_in_dim(v, inst * share, share, 0)[:, None]
+    most = shocks.shape[0] * lax.axis_size("scen") // RANK_PART
+    own = lambda v: jnp.tile(lax.dynamic_slice_in_dim(v, inst * share, share, 0), LANES // share)[None, :]
     low, high, own_rank = own(bracket_low), own(bracket_high), own(rank)
-    parts = [sums[0]] + [swap(sums[slot], "inst", slot) for slot in range(1, slots)]
-    value, code = book_values(scale, low, high, parts)
-    codes = [code] + [swap(code, "scen", CORES * k) for k in range(1, lines)]
-    codes = codes + [swap(c, "scen", 1) for c in codes]
-    weight, row = quantiles(low, high, own_rank, value, codes)
-    weights = [weight] + [swap(weight, "inst", slot) for slot in range(1, slots)]
+    parts = [sums[0]] + [swap(sums[slot], "inst", slot) for slot in range(slots - 1, 0, -1)]
+    value, lows = book_values(scale, most, parts)
+    lists = [lows] + [swap(lows, "scen", CORES * k) for k in [*range(1, lines, 2), *range(2, lines, 2)]]
+    lists = lists + [swap(v, "scen", 1) for v in lists]
+    weight, row = quantiles(most, low, high, own_rank, value, lists)
+    far = {slot: swap(weight, "inst", slot) for slot in range(slots - 1, 0, -1)}
+    weights = [weight] + [far[slot] for slot in range(1, slots)]
     weights = weights + [swap(w, "scen", 1) for w in weights]
 
-    outs = tail_sums(where, weights, [mine, got], slots, lines)
-    away, partner, handled, plain = (outs[k : k + 2] for k in range(0, 8, 2))
+    away, partner, handled, plain = tail_sums(where, weights, [mine, got], slots, lines)
     half = books // lines // CORES
     groups = []
     for side in range(CORES):
         passed = swap(away[side], "scen", CORES)
-        words = [swap(partner[side], "scen", CORES ^ side)]
         sent = relay(passed, handled[side])
+        words = []
         for k in range(1, lines // 2):
             block = sent[(k - 1) * half : k * half]
             words.append(swap(block, "scen", (CORES * (2 * k + 1)) ^ side))
         first = plain[0] if side == 0 else swap(plain[1], "scen", 1)
+        first = merge(first, swap(partner[side], "scen", CORES ^ side))
         groups.append([first, *words])
     return finish(where, groups), row[0, :share]
 

time: 91.2 us -> 85.4 us (0.936)
  waiting for transfers between devices: 35 us -> 28.7 us
  starting transfers between devices: 25.4 us -> 26.4 us
    ppermute x29, waiting for transfers between devices: 35 us -> 28.7 us  [swap(): return lax.ppermute(value, axis, [(k, k ^ flip) for k in range(n)])]
    pallas_call x3 -> x6, Pallas kernels: 7.27 us -> 7.21 us  [the longest x2 5.67 us: tail_call(): pl.pallas_call(kernel, out_shape=[jax.ShapeDtypeStruct(shape, kind) for s...]
  transfers between devices with their start and end apart: 29 -> 29, of which waited for: 18 -> 14; matrix products, arithmetic and copies ran while one was open for 1% -> 1% of each run, Pallas kernels for 18% -> 19%
where the time goes in v4:
time: 85.4 us; the launch traced here: 85.2 us
  waiting for transfers between devices  28.7 us (34%)
  starting transfers between devices  26.4 us (31%)
  Pallas kernels  26.4 us (31%)
  local copies, waits for them, and re-layouts  2.83 us (3%)
    ppermute x29, waiting for transfers between devices, swap(): return lax.ppermute(value, axis, [(k, k ^ flip) for k in range(n)])  28.7 us
    ppermute x29, starting transfers between devices, swap(): return lax.ppermute(value, axis, [(k, k ^ flip) for k in range(n)])  26.4 us
    pallas_call x1, Pallas kernels, stage(): pl.pallas_call(functools.partial(stage_kernel, slots, near, far), out_sha...  6.48 us
    pallas_call x2, Pallas kernels, tail_call(): pl.pallas_call(kernel, out_shape=[jax.ShapeDtypeStruct(shape, kind) for s...  5.67 us
    pallas_call x1, Pallas kernels, profits(): pl.pallas_call(functools.partial(profit_kernel, len(tops)), out_shape=out...  5.5 us
    pallas_call x1, Pallas kernels, add_moves(): pl.pallas_call(add_moves_kernel, out_shape=jax.ShapeDtypeStruct((rows, co...  5.11 us
    unnamed x16, local copies, waits for them, and re-layouts  1.79 us
  transfers between devices with their start and end apart: 29, of which 14 were waited for; matrix products, arithmetic and copies ran while one was open for 1% of the time, Pallas kernels for 19%

profile of v4, /device:TPU:0, one launch (start us, length us, event | category | flops | bytes accessed | tf_op | source)
XLA Modules:
  0.0 85.2 jit_solution(4834662425234316546)
XLA Ops:
  0.6 3.0 %collective-permute-start = (bf16[512,512]{1,0:T(8,128)(2,1)}, bf16[512,512]{1,0:T(8,128)(2,1)S(1)}, u32[]{:S(2)}, u32[]{:S(2)}) collective-permute-start(bf16[512,512]{1,0:T(8,128)(2,1)} %shocks_ref.1), channel_id=1, source_target_pairs={{0,1},{1,0},{2,3},{3,2},{4,5},{5,4},{6,7},{7,6},{8,9},{9,8},{10,11... | collective-permute-start | bytes 1572872 | tf_op jit(solution)/shard_map/ppermute | solution.py:41
  3.6 1.5 %collective-permute-start.2 = (bf16[512,512]{1,0:T(8,128)(2,1)}, bf16[512,512]{1,0:T(8,128)(2,1)S(1)}, u32[]{:S(2)}, u32[]{:S(2)}) collective-permute-start(bf16[512,512]{1,0:T(8,128)(2,1)} %shocks_ref.1), channel_id=1, source_target_pairs={{0,2},{1,3},{2,0},{3,1},{4,6},{5,7},{6,4},{7,5},{8,10},{9,11},{10,... | collective-permute-start | bytes 1572872 | tf_op jit(solution)/shard_map/ppermute | solution.py:41
  5.2 1.0 %copy-done = bf16[512,512]{1,0:T(8,128)(2,1)S(1)} copy-done((bf16[512,512]{1,0:T(8,128)(2,1)S(1)}, bf16[512,512]{1,0:T(8,128)(2,1)}, u32[]{:S(2)}) %copy-start) | copy-done | bytes 524312
  7.0 6.5 %stage.1 = (f32[512,4096]{1,0:T(8,128)S(1)}, bf16[1024,4096]{1,0:T(8,128)(2,1)S(1)}, bf16[512,4096]{1,0:T(8,128)(2,1)S(1)}, bf16[256,4096]{1,0:T(8,128)(2,1)S(1)}) custom-call(s32[3]{0:T(128)S(1)} %pad_add_fusion.where_ref, bf16[512,512]{1,0:T(8,128)(2,1)S(1)} %copy-done, s32[1,4096]{1,0:T(1,128)S(1)} %bitcast.9, bf16[2048,4096]{1,0:T(8,128)(2,1)} %loadings_ref.1), custom_call_target="tpu_custom_call" | custom-call | flops 2147483648 | bytes 16777216 | tf_op jit(solution)/shard_map/stage/pallas_call | solution.py:85
  13.5 2.3 %collective-permute-done.refs_0_ = bf16[512,512]{1,0:T(8,128)(2,1)S(1)} collective-permute-done((bf16[512,512]{1,0:T(8,128)(2,1)}, bf16[512,512]{1,0:T(8,128)(2,1)S(1)}, u32[]{:S(2)}, u32[]{:S(2)}) %collective-permute-start) | collective-permute-done | bytes 524320 | tf_op jit(solution)/shard_map/ppermute | solution.py:41
  15.8 1.8 %collective-permute-start.1 = (bf16[256,512]{1,0:T(8,128)(2,1)S(1)}, bf16[256,512]{1,0:T(8,128)(2,1)S(1)}, u32[]{:S(2)}, u32[]{:S(2)}) collective-permute-start(bf16[256,512]{1,0:T(8,128)(2,1)S(1)} %slice.12), channel_id=1, source_target_pairs={{0,2},{1,3},{2,0},{3,1},{4,6},{5,7},{6,4},{7,5},{8,10},{9,11},{10,... | collective-permute-start | bytes 786440 | tf_op jit(solution)/shard_map/ppermute | solution.py:41
  17.6 1.6 %collective-permute-start.3 = (bf16[256,512]{1,0:T(8,128)(2,1)S(1)}, bf16[256,512]{1,0:T(8,128)(2,1)S(1)}, u32[]{:S(2)}, u32[]{:S(2)}) collective-permute-start(bf16[256,512]{1,0:T(8,128)(2,1)S(1)} %slice.13), channel_id=1, source_target_pairs={{0,1},{1,0},{2,3},{3,2},{4,5},{5,4},{6,7},{7,6},{8,9},{9,8},{10,11... | collective-permute-start | bytes 786440 | tf_op jit(solution)/shard_map/ppermute | solution.py:41
  19.2 5.1 %add_moves.1.refs_3_ = f32[512,4096]{1,0:T(8,128)S(1)} custom-call(bf16[512,512]{1,0:T(8,128)(2,1)S(1)} %collective-permute-done.refs_0_, bf16[512,512]{1,0:T(8,128)(2,1)S(1)} %collective-permute-done.2.refs_1_, bf16[1024,4096]{1,0:T(8,128)(2,1)S(1)} %get-tuple-element.26.refs_2_, ...), custom_call_target="tpu_custom_call", output_to_operand_aliasing={{}: (3, {})} | custom-call | flops 4294967296 | bytes 16777216 | tf_op jit(solution)/shard_map/add_moves/pallas_call | solution.py:119
  24.7 5.5 %profits.1 = (bf16[512,2048]{1,0:T(8,128)(2,1)S(1)}, bf16[512,2048]{1,0:T(8,128)(2,1)}, f32[64,512]{1,0:T(8,128)S(1)}, f32[64,512]{1,0:T(8,128)S(1)}, f32[64,512]{1,0:T(8,128)S(1)}, /*index=5*/f32[64,512]{1,0:T(8,128)S(1)}) custom-call(s32[3]{0:T(128)S(1)} %pad_add_fusion.where_ref, bf16[256,512]{1,0:T(8,128)(2,1)S(1)} %collective-permute-done.1.refs_0_, ...), custom_call_target="tpu_custom_call" | custom-call | flops 3221225472 | bytes 12582912 | tf_op jit(solution)/shard_map/profits/pallas_call | solution.py:174
  30.2 1.5 %collective-permute-start.4 = (f32[64,512]{1,0:T(8,128)S(1)}, f32[64,512]{1,0:T(8,128)S(1)}, u32[]{:S(2)}, u32[]{:S(2)}) collective-permute-start(f32[64,512]{1,0:T(8,128)S(1)} %get-tuple-element.30), channel_id=1, source_target_pairs={{0,3},{1,2},{2,1},{3,0},{4,7},{5,6},{6,5},{7,4},{8,11},{9,10},{10,... | collective-permute-start | bytes 393224 | tf_op jit(solution)/shard_map/ppermute | solution.py:41
  31.7 1.5 %collective-permute-start.5 = (f32[64,512]{1,0:T(8,128)S(1)}, f32[64,512]{1,0:T(8,128)S(1)}, u32[]{:S(2)}, u32[]{:S(2)}) collective-permute-start(f32[64,512]{1,0:T(8,128)S(1)} %get-tuple-element.31), channel_id=1, source_target_pairs={{0,2},{1,3},{2,0},{3,1},{4,6},{5,7},{6,4},{7,5},{8,10},{9,11},{10,... | collective-permute-start | bytes 393224 | tf_op jit(solution)/shard_map/ppermute | solution.py:41
  33.8 3.7 %collective-permute-done.4.refs_1_ = f32[64,512]{1,0:T(8,128)S(1)} collective-permute-done((f32[64,512]{1,0:T(8,128)S(1)}, f32[64,512]{1,0:T(8,128)S(1)}, u32[]{:S(2)}, u32[]{:S(2)}) %collective-permute-start.4) | collective-permute-done | bytes 131104 | tf_op jit(solution)/shard_map/ppermute | solution.py:41
  37.6 2.3 %collective-permute-done.5.refs_2_ = f32[64,512]{1,0:T(8,128)S(1)} collective-permute-done((f32[64,512]{1,0:T(8,128)S(1)}, f32[64,512]{1,0:T(8,128)S(1)}, u32[]{:S(2)}, u32[]{:S(2)}) %collective-permute-start.5) | collective-permute-done | bytes 131104 | tf_op jit(solution)/shard_map/ppermute | solution.py:41
  40.4 1.6 %collective-permute-start.7 = (f32[32,128]{1,0:T(8,128)S(1)}, f32[32,128]{1,0:T(8,128)S(1)}, u32[]{:S(2)}, u32[]{:S(2)}) collective-permute-start(f32[32,128]{1,0:T(8,128)S(1)} %get-tuple-element.34.refs_0_), channel_id=1, source_target_pairs={{0,8},{4,12},{8,0},{12,4},{16,24},{20,28},{24,16},{28,20},{1,9},{5... | collective-permute-start | bytes 49160 | tf_op jit(solution)/shard_map/ppermute | solution.py:41
  42.0 2.5 %collective-permute-start.8 = (f32[32,128]{1,0:T(8,128)S(1)}, f32[32,128]{1,0:T(8,128)S(1)}, u32[]{:S(2)}, u32[]{:S(2)}) collective-permute-start(f32[32,128]{1,0:T(8,128)S(1)} %get-tuple-element.34.refs_0_), channel_id=1, source_target_pairs={{0,24},{4,28},{8,16},{12,20},{16,8},{20,12},{24,0},{28,4},{1,25},{... | collective-permute-start | bytes 49160 | tf_op jit(solution)/shard_map/ppermute | solution.py:41
  45.1 2.4 %collective-permute-done.8.refs_2_ = f32[32,128]{1,0:T(8,128)S(1)} collective-permute-done((f32[32,128]{1,0:T(8,128)S(1)}, f32[32,128]{1,0:T(8,128)S(1)}, u32[]{:S(2)}, u32[]{:S(2)}) %collective-permute-start.8) | collective-permute-done | bytes 16416 | tf_op jit(solution)/shard_map/ppermute | solution.py:41
  47.6 1.6 %collective-permute-done.9.refs_3_ = f32[32,128]{1,0:T(8,128)S(1)} collective-permute-done((f32[32,128]{1,0:T(8,128)S(1)}, f32[32,128]{1,0:T(8,128)S(1)}, u32[]{:S(2)}, u32[]{:S(2)}) %collective-permute-start.9) | collective-permute-done | bytes 16416 | tf_op jit(solution)/shard_map/ppermute | solution.py:41
  50.9 1.4 %collective-permute-start.14 = (bf16[64,512]{1,0:T(8,128)(2,1)S(1)}, bf16[64,512]{1,0:T(8,128)(2,1)S(1)}, u32[]{:S(2)}, u32[]{:S(2)}) collective-permute-start(bf16[64,512]{1,0:T(8,128)(2,1)S(1)} %get-tuple-element.35.refs_0_), channel_id=1, source_target_pairs={{0,1},{1,0},{2,3},{3,2},{4,5},{5,4},{6,7},{7,6},{8,9},{9,8},{10,11... | collective-permute-start | bytes 196616 | tf_op jit(solution)/shard_map/ppermute | solution.py:41
  53.1 1.4 %collective-permute-start.16 = (bf16[64,512]{1,0:T(8,128)(2,1)S(1)}, bf16[64,512]{1,0:T(8,128)(2,1)S(1)}, u32[]{:S(2)}, u32[]{:S(2)}) collective-permute-start(bf16[64,512]{1,0:T(8,128)(2,1)S(1)} %get-tuple-element.35.refs_0_), channel_id=1, source_target_pairs={{0,3},{1,2},{2,1},{3,0},{4,7},{5,6},{6,5},{7,4},{8,11},{9,10},{10,... | collective-permute-start | bytes 196616 | tf_op jit(solution)/shard_map/ppermute | solution.py:41
  55.3 2.1 %collective-permute-done.15.refs_2_ = bf16[64,512]{1,0:T(8,128)(2,1)S(1)} collective-permute-done((bf16[64,512]{1,0:T(8,128)(2,1)S(1)}, bf16[64,512]{1,0:T(8,128)(2,1)S(1)}, u32[]{:S(2)}, u32[]{:S(2)}) %collective-permute-start.15) | collective-permute-done | bytes 65568 | tf_op jit(solution)/shard_map/ppermute | solution.py:41
  57.3 0.9 %collective-permute-done.16.refs_3_ = bf16[64,512]{1,0:T(8,128)(2,1)S(1)} collective-permute-done((bf16[64,512]{1,0:T(8,128)(2,1)S(1)}, bf16[64,512]{1,0:T(8,128)(2,1)S(1)}, u32[]{:S(2)}, u32[]{:S(2)}) %collective-permute-start.16) | collective-permute-done | bytes 65568 | tf_op jit(solution)/shard_map/ppermute | solution.py:41
  58.6 0.9 %collective-permute-done.20.refs_7_ = bf16[64,512]{1,0:T(8,128)(2,1)S(1)} collective-permute-done((bf16[64,512]{1,0:T(8,128)(2,1)S(1)}, bf16[64,512]{1,0:T(8,128)(2,1)S(1)}, u32[]{:S(2)}, u32[]{:S(2)}) %collective-permute-start.20) | collective-permute-done | bytes 65568 | tf_op jit(solution)/shard_map/ppermute | solution.py:41
  59.5 2.8 %away_sums.1 = (s16[32,2176]{1,0:T(8,128)(2,1)S(1)}, s16[32,2176]{1,0:T(8,128)(2,1)S(1)}, bf16[256,1024]{1,0:T(8,128)(2,1)S(1)}) custom-call(s32[3]{0:T(128)S(1)} %pad_add_fusion.where_ref, bf16[64,512]{1,0:T(8,128)(2,1)S(1)} %get-tuple-element.35.refs_0_, bf16[64,512]{1,0:T(8,128)(2,1)S(1)} %collective-permute-done.14.refs_1_, ...), custom_call_target="tpu_custom_call" | custom-call | tf_op jit(solution)/shard_map/away_sums/pallas_call | solution.py:441
  63.2 1.3 %collective-permute-start.23 = (s16[32,2176]{1,0:T(8,128)(2,1)S(1)}, s16[32,2176]{1,0:T(8,128)(2,1)S(1)}, u32[]{:S(2)}, u32[]{:S(2)}) collective-permute-start(s16[32,2176]{1,0:T(8,128)(2,1)S(1)} %get-tuple-element.41), channel_id=1, source_target_pairs={{0,8},{4,12},{8,0},{12,4},{16,24},{20,28},{24,16},{28,20},{1,9},{5... | collective-permute-start | bytes 417800 | tf_op jit(solution)/shard_map/ppermute | solution.py:41
  64.5 2.8 %home_sums.1 = (s16[32,2176]{1,0:T(8,128)(2,1)S(1)}, s16[32,2176]{1,0:T(8,128)(2,1)S(1)}, f32[32,2176]{1,0:T(8,128)S(1)}, f32[32,2176]{1,0:T(8,128)S(1)}, f32[32...) custom-call(s32[3]{0:T(128)S(1)} %pad_add_fusion.where_ref, bf16[256,1024]{1,0:T(8,128)(2,1)S(1)} %get-tuple-element.38.held, ...), custom_call_target="tpu_custom_call" | custom-call | tf_op jit(solution)/shard_map/home_sums/pallas_call | solution.py:441
  67.4 0.8 collective-permute-start.26
  68.2 1.3 %collective-permute-start.22 = (s16[32,2176]{1,0:T(8,128)(2,1)S(1)}, s16[32,2176]{1,0:T(8,128)(2,1)S(1)}, u32[]{:S(2)}, u32[]{:S(2)}) collective-permute-start(s16[32,2176]{1,0:T(8,128)(2,1)S(1)} %get-tuple-element.40), channel_id=1, source_target_pairs={{0,8},{4,12},{8,0},{12,4},{16,24},{20,28},{24,16},{28,20},{1,9},{5... | collective-permute-start | bytes 417800 | tf_op jit(solution)/shard_map/ppermute | solution.py:41
  69.8 0.8 collective-permute-start.28
  70.6 1.2 %collective-permute-done.23.words_ref = s16[32,2176]{1,0:T(8,128)(2,1)S(1)} collective-permute-done((s16[32,2176]{1,0:T(8,128)(2,1)S(1)}, s16[32,2176]{1,0:T(8,128)(2,1)S(1)}, u32[]{:S(2)}, u32[]{:S(2)}) %collective-permute-start.23) | collective-permute-done | bytes 139296 | tf_op jit(solution)/shard_map/ppermute | solution.py:41
  72.0 1.4 %collective-permute-start.24 = (s16[32,2176]{1,0:T(8,128)(2,1)S(1)}, s16[32,2176]{1,0:T(8,128)(2,1)S(1)}, u32[]{:S(2)}, u32[]{:S(2)}) collective-permute-start(s16[32,2176]{1,0:T(8,128)(2,1)S(1)} %relay.2), channel_id=1, source_target_pairs={{0,24},{4,28},{8,16},{12,20},{16,8},{20,12},{24,0},{28,4},{1,25},{... | collective-permute-start | bytes 417800 | tf_op jit(solution)/shard_map/ppermute | solution.py:41
  73.9 9.1 %collective-permute-done.22.words_ref = s16[32,2176]{1,0:T(8,128)(2,1)S(1)} collective-permute-done((s16[32,2176]{1,0:T(8,128)(2,1)S(1)}, s16[32,2176]{1,0:T(8,128)(2,1)S(1)}, u32[]{:S(2)}, u32[]{:S(2)}) %collective-permute-start.22) | collective-permute-done | bytes 139296 | tf_op jit(solution)/shard_map/ppermute | solution.py:41
  83.5 1.6 %finish.1 = f32[32,4096]{1,0:T(8,128)} custom-call(s32[3]{0:T(128)S(1)} %pad_add_fusion.where_ref, f32[32,2176]{1,0:T(8,128)S(1)} %merge.2.refs_0_, s16[32,2176]{1,0:T(8,128)(2,1)S(1)} %collective-permute-done.24.refs_1_, f32[32,2176]{1,0:T(8,128)S(1)} %merge.3.refs_2_, s16[32,2176]{1,0:T(8,128)(2,1)S(1)} %collective-permute-done.28.refs_3_), custom_call_target="tpu_custom_call" | custom-call | tf_op jit(solution)/shard_map/finish/pallas_call | solution.py:529
  (67 shorter events, 8.7 us)
Async XLA Ops:
  0.6 15.1 %collective-permute-start = (bf16[512,512]{1,0:T(8,128)(2,1)}, bf16[512,512]{1,0:T(8,128)(2,1)S(1)}, u32[]{:S(2)}, u32[]{:S(2)}) collective-permute-start(bf16[512,512]{1,0:T(8,128)(2,1)} %shocks_ref.1), channel_id=1, source_target_pairs={{0,1},{1,0},{2,3},{3,2},{4,5},{5,4},{6,7},{7,6},{8,9},{9,8},{10,11... | collective-permute-start | bytes 1572872 | tf_op jit(solution)/shard_map/ppermute | solution.py:41
  3.6 14.0 %collective-permute-start.2 = (bf16[512,512]{1,0:T(8,128)(2,1)}, bf16[512,512]{1,0:T(8,128)(2,1)S(1)}, u32[]{:S(2)}, u32[]{:S(2)}) collective-permute-start(bf16[512,512]{1,0:T(8,128)(2,1)} %shocks_ref.1), channel_id=1, source_target_pairs={{0,2},{1,3},{2,0},{3,1},{4,6},{5,7},{6,4},{7,5},{8,10},{9,11},{10,... | collective-permute-start | bytes 1572872 | tf_op jit(solution)/shard_map/ppermute | solution.py:41
  15.8 8.5 %collective-permute-start.1 = (bf16[256,512]{1,0:T(8,128)(2,1)S(1)}, bf16[256,512]{1,0:T(8,128)(2,1)S(1)}, u32[]{:S(2)}, u32[]{:S(2)}) collective-permute-start(bf16[256,512]{1,0:T(8,128)(2,1)S(1)} %slice.12), channel_id=1, source_target_pairs={{0,2},{1,3},{2,0},{3,1},{4,6},{5,7},{6,4},{7,5},{8,10},{9,11},{10,... | collective-permute-start | bytes 786440 | tf_op jit(solution)/shard_map/ppermute | solution.py:41
  17.6 7.0 %collective-permute-start.3 = (bf16[256,512]{1,0:T(8,128)(2,1)S(1)}, bf16[256,512]{1,0:T(8,128)(2,1)S(1)}, u32[]{:S(2)}, u32[]{:S(2)}) collective-permute-start(bf16[256,512]{1,0:T(8,128)(2,1)S(1)} %slice.13), channel_id=1, source_target_pairs={{0,1},{1,0},{2,3},{3,2},{4,5},{5,4},{6,7},{7,6},{8,9},{9,8},{10,11... | collective-permute-start | bytes 786440 | tf_op jit(solution)/shard_map/ppermute | solution.py:41
  24.6 24.5 %copy-start.5 = (s32[256]{0:T(256)S(1)}, s32[256]{0:T(256)}, u32[]{:S(2)}) copy-start(s32[256]{0:T(256)} %param.16) | copy-start | bytes 3076
  24.6 24.7 %copy-start.6 = (s32[256]{0:T(256)S(1)}, s32[256]{0:T(256)}, u32[]{:S(2)}) copy-start(s32[256]{0:T(256)} %param.17) | copy-start | bytes 3076
  24.6 24.9 %copy-start.7 = (s32[256]{0:T(256)S(1)}, s32[256]{0:T(256)}, u32[]{:S(2)}) copy-start(s32[256]{0:T(256)} %param.15) | copy-start | bytes 3076
  30.2 29.4 %collective-permute-start.21 = (bf16[512,2048]{1,0:T(8,128)(2,1)}, bf16[512,2048]{1,0:T(8,128)(2,1)}, u32[]{:S(2)}, u32[]{:S(2)}) collective-permute-start(bf16[512,2048]{1,0:T(8,128)(2,1)} %get-tuple-element.37), channel_id=1, source_target_pairs={{0,4},{4,0},{8,12},{12,8},{16,20},{20,16},{24,28},{28,24},{1,5},{5... | collective-permute-start | bytes 6291464 | tf_op jit(solution)/shard_map/ppermute | solution.py:41
  30.2 7.3 %collective-permute-start.4 = (f32[64,512]{1,0:T(8,128)S(1)}, f32[64,512]{1,0:T(8,128)S(1)}, u32[]{:S(2)}, u32[]{:S(2)}) collective-permute-start(f32[64,512]{1,0:T(8,128)S(1)} %get-tuple-element.30), channel_id=1, source_target_pairs={{0,3},{1,2},{2,1},{3,0},{4,7},{5,6},{6,5},{7,4},{8,11},{9,10},{10,... | collective-permute-start | bytes 393224 | tf_op jit(solution)/shard_map/ppermute | solution.py:41
  31.7 8.1 %collective-permute-start.5 = (f32[64,512]{1,0:T(8,128)S(1)}, f32[64,512]{1,0:T(8,128)S(1)}, u32[]{:S(2)}, u32[]{:S(2)}) collective-permute-start(f32[64,512]{1,0:T(8,128)S(1)} %get-tuple-element.31), channel_id=1, source_target_pairs={{0,2},{1,3},{2,0},{3,1},{4,6},{5,7},{6,4},{7,5},{8,10},{9,11},{10,... | collective-permute-start | bytes 393224 | tf_op jit(solution)/shard_map/ppermute | solution.py:41
  33.3 6.6 %collective-permute-start.6 = (f32[64,512]{1,0:T(8,128)S(1)}, f32[64,512]{1,0:T(8,128)S(1)}, u32[]{:S(2)}, u32[]{:S(2)}) collective-permute-start(f32[64,512]{1,0:T(8,128)S(1)} %get-tuple-element.32), channel_id=1, source_target_pairs={{0,1},{1,0},{2,3},{3,2},{4,5},{5,4},{6,7},{7,6},{8,9},{9,8},{10,11... | collective-permute-start | bytes 393224 | tf_op jit(solution)/shard_map/ppermute | solution.py:41
  40.4 4.2 %collective-permute-start.7 = (f32[32,128]{1,0:T(8,128)S(1)}, f32[32,128]{1,0:T(8,128)S(1)}, u32[]{:S(2)}, u32[]{:S(2)}) collective-permute-start(f32[32,128]{1,0:T(8,128)S(1)} %get-tuple-element.34.refs_0_), channel_id=1, source_target_pairs={{0,8},{4,12},{8,0},{12,4},{16,24},{20,28},{24,16},{28,20},{1,9},{5... | collective-permute-start | bytes 49160 | tf_op jit(solution)/shard_map/ppermute | solution.py:41
  42.0 5.5 %collective-permute-start.8 = (f32[32,128]{1,0:T(8,128)S(1)}, f32[32,128]{1,0:T(8,128)S(1)}, u32[]{:S(2)}, u32[]{:S(2)}) collective-permute-start(f32[32,128]{1,0:T(8,128)S(1)} %get-tuple-element.34.refs_0_), channel_id=1, source_target_pairs={{0,24},{4,28},{8,16},{12,20},{16,8},{20,12},{24,0},{28,4},{1,25},{... | collective-permute-start | bytes 49160 | tf_op jit(solution)/shard_map/ppermute | solution.py:41
  44.5 4.6 %collective-permute-start.9 = (f32[32,128]{1,0:T(8,128)S(1)}, f32[32,128]{1,0:T(8,128)S(1)}, u32[]{:S(2)}, u32[]{:S(2)}) collective-permute-start(f32[32,128]{1,0:T(8,128)S(1)} %get-tuple-element.34.refs_0_), channel_id=1, source_target_pairs={{0,16},{4,20},{8,24},{12,28},{16,0},{20,4},{24,8},{28,12},{1,17},{... | collective-permute-start | bytes 49160 | tf_op jit(solution)/shard_map/ppermute | solution.py:41
  44.6 5.0 %collective-permute-start.10 = (f32[32,128]{1,0:T(8,128)S(1)}, f32[32,128]{1,0:T(8,128)S(1)}, u32[]{:S(2)}, u32[]{:S(2)}) collective-permute-start(f32[32,128]{1,0:T(8,128)S(1)} %get-tuple-element.34.refs_0_), channel_id=1, source_target_pairs={{0,4},{4,0},{8,12},{12,8},{16,20},{20,16},{24,28},{28,24},{1,5},{5... | collective-permute-start | bytes 49160 | tf_op jit(solution)/shard_map/ppermute | solution.py:41
  44.6 5.0 %collective-permute-start.11 = (f32[32,128]{1,0:T(8,128)S(1)}, f32[32,128]{1,0:T(8,128)S(1)}, u32[]{:S(2)}, u32[]{:S(2)}) collective-permute-start(f32[32,128]{1,0:T(8,128)S(1)} %collective-permute-done.7.refs_1_), channel_id=1, source_target_pairs={{0,4},{4,0},{8,12},{12,8},{16,20},{20,16},{24,28},{28,24},{1,5},{5... | collective-permute-start | bytes 49160 | tf_op jit(solution)/shard_map/ppermute | solution.py:41
  47.6 2.1 %collective-permute-start.12 = (f32[32,128]{1,0:T(8,128)S(1)}, f32[32,128]{1,0:T(8,128)S(1)}, u32[]{:S(2)}, u32[]{:S(2)}) collective-permute-start(f32[32,128]{1,0:T(8,128)S(1)} %collective-permute-done.8.refs_2_), channel_id=1, source_target_pairs={{0,4},{4,0},{8,12},{12,8},{16,20},{20,16},{24,28},{28,24},{1,5},{5... | collective-permute-start | bytes 49160 | tf_op jit(solution)/shard_map/ppermute | solution.py:41
  49.2 1.2 %collective-permute-start.13 = (f32[32,128]{1,0:T(8,128)S(1)}, f32[32,128]{1,0:T(8,128)S(1)}, u32[]{:S(2)}, u32[]{:S(2)}) collective-permute-start(f32[32,128]{1,0:T(8,128)S(1)} %collective-permute-done.9.refs_3_), channel_id=1, source_target_pairs={{0,4},{4,0},{8,12},{12,8},{16,20},{20,16},{24,28},{28,24},{1,5},{5... | collective-permute-start | bytes 49160 | tf_op jit(solution)/shard_map/ppermute | solution.py:41
  50.9 4.3 %collective-permute-start.14 = (bf16[64,512]{1,0:T(8,128)(2,1)S(1)}, bf16[64,512]{1,0:T(8,128)(2,1)S(1)}, u32[]{:S(2)}, u32[]{:S(2)}) collective-permute-start(bf16[64,512]{1,0:T(8,128)(2,1)S(1)} %get-tuple-element.35.refs_0_), channel_id=1, source_target_pairs={{0,1},{1,0},{2,3},{3,2},{4,5},{5,4},{6,7},{7,6},{8,9},{9,8},{10,11... | collective-permute-start | bytes 196616 | tf_op jit(solution)/shard_map/ppermute | solution.py:41
  52.4 5.0 %collective-permute-start.15 = (bf16[64,512]{1,0:T(8,128)(2,1)S(1)}, bf16[64,512]{1,0:T(8,128)(2,1)S(1)}, u32[]{:S(2)}, u32[]{:S(2)}) collective-permute-start(bf16[64,512]{1,0:T(8,128)(2,1)S(1)} %get-tuple-element.35.refs_0_), channel_id=1, source_target_pairs={{0,2},{1,3},{2,0},{3,1},{4,6},{5,7},{6,4},{7,5},{8,10},{9,11},{10,... | collective-permute-start | bytes 196616 | tf_op jit(solution)/shard_map/ppermute | solution.py:41
  53.1 5.2 %collective-permute-start.16 = (bf16[64,512]{1,0:T(8,128)(2,1)S(1)}, bf16[64,512]{1,0:T(8,128)(2,1)S(1)}, u32[]{:S(2)}, u32[]{:S(2)}) collective-permute-start(bf16[64,512]{1,0:T(8,128)(2,1)S(1)} %get-tuple-element.35.refs_0_), channel_id=1, source_target_pairs={{0,3},{1,2},{2,1},{3,0},{4,7},{5,6},{6,5},{7,4},{8,11},{9,10},{10,... | collective-permute-start | bytes 196616 | tf_op jit(solution)/shard_map/ppermute | solution.py:41
  54.5 3.8 %collective-permute-start.17 = (bf16[64,512]{1,0:T(8,128)(2,1)S(1)}, bf16[64,512]{1,0:T(8,128)(2,1)S(1)}, u32[]{:S(2)}, u32[]{:S(2)}) collective-permute-start(bf16[64,512]{1,0:T(8,128)(2,1)S(1)} %get-tuple-element.35.refs_0_), channel_id=1, source_target_pairs={{0,4},{4,0},{8,12},{12,8},{16,20},{20,16},{24,28},{28,24},{1,5},{5... | collective-permute-start | bytes 196616 | tf_op jit(solution)/shard_map/ppermute | solution.py:41
  55.3 3.0 %collective-permute-start.18 = (bf16[64,512]{1,0:T(8,128)(2,1)S(1)}, bf16[64,512]{1,0:T(8,128)(2,1)S(1)}, u32[]{:S(2)}, u32[]{:S(2)}) collective-permute-start(bf16[64,512]{1,0:T(8,128)(2,1)S(1)} %collective-permute-done.14.refs_1_), channel_id=1, source_target_pairs={{0,4},{4,0},{8,12},{12,8},{16,20},{20,16},{24,28},{28,24},{1,5},{5... | collective-permute-start | bytes 196616 | tf_op jit(solution)/shard_map/ppermute | solution.py:41
  57.3 1.3 %collective-permute-start.19 = (bf16[64,512]{1,0:T(8,128)(2,1)S(1)}, bf16[64,512]{1,0:T(8,128)(2,1)S(1)}, u32[]{:S(2)}, u32[]{:S(2)}) collective-permute-start(bf16[64,512]{1,0:T(8,128)(2,1)S(1)} %collective-permute-done.15.refs_2_), channel_id=1, source_target_pairs={{0,4},{4,0},{8,12},{12,8},{16,20},{20,16},{24,28},{28,24},{1,5},{5... | collective-permute-start | bytes 196616 | tf_op jit(solution)/shard_map/ppermute | solution.py:41
  58.3 1.3 %collective-permute-start.20 = (bf16[64,512]{1,0:T(8,128)(2,1)S(1)}, bf16[64,512]{1,0:T(8,128)(2,1)S(1)}, u32[]{:S(2)}, u32[]{:S(2)}) collective-permute-start(bf16[64,512]{1,0:T(8,128)(2,1)S(1)} %collective-permute-done.16.refs_3_), channel_id=1, source_target_pairs={{0,4},{4,0},{8,12},{12,8},{16,20},{20,16},{24,28},{28,24},{1,5},{5... | collective-permute-start | bytes 196616 | tf_op jit(solution)/shard_map/ppermute | solution.py:41
  62.4 7.2 %collective-permute-start.27 = (s16[32,2176]{1,0:T(8,128)(2,1)S(1)}, s16[32,2176]{1,0:T(8,128)(2,1)S(1)}, u32[]{:S(2)}, u32[]{:S(2)}) collective-permute-start(s16[32,2176]{1,0:T(8,128)(2,1)S(1)} %get-tuple-element.45), channel_id=1, source_target_pairs={{0,8},{4,12},{8,0},{12,4},{16,24},{20,28},{24,16},{28,20},{1,9},{5... | collective-permute-start | bytes 417800 | tf_op jit(solution)/shard_map/ppermute | solution.py:41
  63.2 8.6 %collective-permute-start.23 = (s16[32,2176]{1,0:T(8,128)(2,1)S(1)}, s16[32,2176]{1,0:T(8,128)(2,1)S(1)}, u32[]{:S(2)}, u32[]{:S(2)}) collective-permute-start(s16[32,2176]{1,0:T(8,128)(2,1)S(1)} %get-tuple-element.41), channel_id=1, source_target_pairs={{0,8},{4,12},{8,0},{12,4},{16,24},{20,28},{24,16},{28,20},{1,9},{5... | collective-permute-start | bytes 417800 | tf_op jit(solution)/shard_map/ppermute | solution.py:41
  67.3 16.0 %collective-permute-start.25 = (f32[32,2176]{1,0:T(8,128)S(1)}, f32[32,2176]{1,0:T(8,128)S(1)}, u32[]{:S(2)}, u32[]{:S(2)}) collective-permute-start(f32[32,2176]{1,0:T(8,128)S(1)} %get-tuple-element.43), channel_id=1, source_target_pairs={{0,4},{4,0},{8,12},{12,8},{16,20},{20,16},{24,28},{28,24},{1,5},{5... | collective-permute-start | bytes 835592 | tf_op jit(solution)/shard_map/ppermute | solution.py:41
  67.4 15.9 %collective-permute-start.26 = (s16[32,2176]{1,0:T(8,128)(2,1)S(1)}, s16[32,2176]{1,0:T(8,128)(2,1)S(1)}, u32[]{:S(2)}, u32[]{:S(2)}) collective-permute-start(s16[32,2176]{1,0:T(8,128)(2,1)S(1)} %get-tuple-element.44), channel_id=1, source_target_pairs={{0,12},{4,8},{8,4},{12,0},{16,28},{20,24},{24,20},{28,16},{1,13},{... | collective-permute-start | bytes 417800 | tf_op jit(solution)/shard_map/ppermute | solution.py:41
  68.2 14.9 %collective-permute-start.22 = (s16[32,2176]{1,0:T(8,128)(2,1)S(1)}, s16[32,2176]{1,0:T(8,128)(2,1)S(1)}, u32[]{:S(2)}, u32[]{:S(2)}) collective-permute-start(s16[32,2176]{1,0:T(8,128)(2,1)S(1)} %get-tuple-element.40), channel_id=1, source_target_pairs={{0,8},{4,12},{8,0},{12,4},{16,24},{20,28},{24,16},{28,20},{1,9},{5... | collective-permute-start | bytes 417800 | tf_op jit(solution)/shard_map/ppermute | solution.py:41
  69.8 13.8 %collective-permute-start.28 = (s16[32,2176]{1,0:T(8,128)(2,1)S(1)}, s16[32,2176]{1,0:T(8,128)(2,1)S(1)}, u32[]{:S(2)}, u32[]{:S(2)}) collective-permute-start(s16[32,2176]{1,0:T(8,128)(2,1)S(1)} %relay.3), channel_id=1, source_target_pairs={{0,28},{4,24},{8,20},{12,16},{16,12},{20,8},{24,4},{28,0},{1,29},{... | collective-permute-start | bytes 417800 | tf_op jit(solution)/shard_map/ppermute | solution.py:41
  72.0 11.5 %collective-permute-start.24 = (s16[32,2176]{1,0:T(8,128)(2,1)S(1)}, s16[32,2176]{1,0:T(8,128)(2,1)S(1)}, u32[]{:S(2)}, u32[]{:S(2)}) collective-permute-start(s16[32,2176]{1,0:T(8,128)(2,1)S(1)} %relay.2), channel_id=1, source_target_pairs={{0,24},{4,28},{8,16},{12,20},{16,8},{20,12},{24,0},{28,4},{1,25},{... | collective-permute-start | bytes 417800 | tf_op jit(solution)/shard_map/ppermute | solution.py:41
  (5 other events, 18.0 us)

commit v5 on v4

--- a/solution.py
+++ b/solution.py
@@ -32,10 +32,6 @@
     return jnp.dot(a, b, preferred_element_type=F32)
 
 
-def dot_nt(a, b):
-    return lax.dot_general(a, b, (((1,), (1,)), ((), ())), preferred_element_type=F32)
-
-
 def swap(value, axis, flip):
     n = lax.axis_size(axis)
     return lax.ppermute(value, axis, [(k, k ^ flip) for k in range(n)])
@@ -47,7 +43,7 @@
 
 def stage_kernel(slots, near, far, where_ref, shocks_ref, book_ref, loadings_ref, first_ref, near_ref, far_ref, onehot_ref, own, sems):
     depth = shocks_ref.shape[1]
-    books, cols = onehot_ref.shape
+    cols, books = onehot_ref.shape
     share = books // slots
     rows_of = lambda flip: pl.ds(pl.multiple_of((where_ref[0] ^ flip) * depth, depth), depth)
     parts = tiles(cols, cols // 4)
@@ -67,10 +63,12 @@
     for copy in own_copies + rest_copies:
         copy.start()
     tile = cols // 8
-    row = lax.broadcasted_iota(jnp.int32, (books, tile), 0)
-    row = ((row // share) ^ where_ref[0]) * share + row % share
+    lane = lax.broadcasted_iota(jnp.int32, (tile, LANES), 1)
     for part in tiles(cols, tile):
-        onehot_ref[:, part] = jnp.where(row == book_ref[:, part], 1.0, 0.0).astype(BF16)
+        book = jnp.broadcast_to(book_ref[:, part], (LANES, tile)).T
+        for at in range(0, books, LANES):
+            known = (((lane + at) // share) ^ where_ref[0]) * share + (lane + at) % share
+            onehot_ref[part, at : at + LANES] = jnp.where(book == known, 1.0, 0.0).astype(BF16)
     for copy, part in zip(own_copies, parts):
         copy.wait()
         first_ref[:, part] = dot(shocks_ref[...], own[:, part])
@@ -88,7 +86,7 @@
             jax.ShapeDtypeStruct((rows, cols), F32),
             jax.ShapeDtypeStruct((len(near) * depth, cols), BF16),
             jax.ShapeDtypeStruct((len(far) * depth, cols), BF16),
-            jax.ShapeDtypeStruct((books, cols), BF16),
+            jax.ShapeDtypeStruct((cols, books), BF16),
         ],
         in_specs=[pl.BlockSpec(memory_space=pltpu.SMEM), vmem, vmem, pl.BlockSpec(memory_space=pltpu.HBM)],
         out_specs=[vmem] * 4,
@@ -155,18 +153,19 @@
             if out_ref is held:
                 copies.append(pltpu.make_async_copy(held.at[:, spot], theirs_ref.at[:, spot], sems.at[len(copies)]))
                 copies[-1].start()
-            sums = dot_nt(onehot_ref[:, part], profit)
+            sums = dot(profit, onehot_ref[part, :])
             total[...] = sums if fresh else total[...] + sums
             fresh = False
+    turned = total[...].T
     for slot, sum_ref in enumerate(sum_refs):
-        sum_ref[...] = total[slot * share : (slot + 1) * share, :]
+        sum_ref[...] = turned[slot * share : (slot + 1) * share, :]
     for copy in copies:
         copy.wait()
 
 
 def profits(where, tops, lows, rest, first, delta, gamma, kappa, onehot, slots):
     rows, cols = first.shape
-    books = onehot.shape[0]
+    books = onehot.shape[1]
     depth = tops[0].shape[1]
     vmem = pl.BlockSpec(memory_space=pltpu.VMEM)
     out_shape = [jax.ShapeDtypeStruct((rows, cols // CORES), BF16)] * 2
@@ -177,7 +176,7 @@
         in_specs=[pl.BlockSpec(memory_space=pltpu.SMEM)] + [vmem] * (2 * len(tops) + 6),
         out_specs=[vmem, pl.BlockSpec(memory_space=pltpu.HBM)] + [vmem] * slots,
         scratch_shapes=[
-            pltpu.VMEM((books, rows), F32),
+            pltpu.VMEM((rows, books), F32),
             pltpu.VMEM((rows, cols // CORES), BF16),
             pltpu.SemaphoreType.DMA((4,)),
         ],
@@ -374,11 +373,11 @@
 def tail_part(held, profit_refs, total, spot, rows):
     cols = total.shape[1] - LANES
     weight = held[spot, :]
+    mass = jnp.sum(weight.astype(F32), axis=1, keepdims=True)
+    total[spot, cols:] = jnp.broadcast_to(mass, (weight.shape[0], LANES))
     for part in tiles(cols, cols // 4):
         result = dot(weight[:, :rows], profit_refs[0][:, part])
         total[spot, part] = result + dot(weight[:, rows:], profit_refs[1][:, part])
-    mass = jnp.sum(weight.astype(F32), axis=1, keepdims=True)
-    total[spot, cols:] = jnp.broadcast_to(mass, (weight.shape[0], LANES))
 
 
 def halves(where_ref, total, line, block):
@@ -436,6 +435,25 @@
         own_refs[side][...] = value
 
 
+def bring_kernel(far_ref, near_ref, sem):
+    copy = pltpu.make_async_copy(far_ref, near_ref, sem)
+    copy.start()
+    copy.wait()
+
+
+def bring(far):
+    return pl.pallas_call(
+        bring_kernel,
+        out_shape=jax.ShapeDtypeStruct(far.shape, far.dtype),
+        in_specs=[pl.BlockSpec(memory_space=pltpu.HBM)],
+        out_specs=pl.BlockSpec(memory_space=pltpu.VMEM),
+        scratch_shapes=[pltpu.SemaphoreType.DMA],
+        compiler_params=params(16),
+        cost_estimate=pl.CostEstimate(flops=0, bytes_accessed=8 * far.size, transcendentals=0),
+        name="bring",
+    )(far)
+
+
 def tail_call(kernel, name, out_shape, scratch, where, inputs):
     vmem = pl.BlockSpec(memory_space=pltpu.VMEM)
     return pl.pallas_call(
@@ -443,7 +461,7 @@
         out_shape=[jax.ShapeDtypeStruct(shape, kind) for shape, kind in out_shape],
         in_specs=[pl.BlockSpec(memory_space=pltpu.SMEM)] + [vmem] * len(inputs),
         out_specs=[vmem] * len(out_shape),
-        scratch_shapes=[pltpu.VMEM(shape, kind) for shape, kind in scratch],
+        scratch_shapes=scratch,
         compiler_params=params(24),
         name=name,
     )(where, *inputs)
@@ -456,12 +474,12 @@
     half = books // lines // CORES
     others = (lines // 2 - 1) * half
     wide = cols + LANES
-    total = ((books, wide), F32)
-    held_shape = ((books, CORES * rows), BF16)
+    total = pltpu.VMEM((books, wide), F32)
+    kept = [((books, CORES * rows), BF16)]
     *away, held = tail_call(
         functools.partial(away_kernel, slots, lines),
         "away_sums",
-        [((others, wide), jnp.int16)] * CORES + [held_shape],
+        [((others, wide), jnp.int16)] * CORES + kept,
         [total],
         where,
         [*weights, *profit_pair],
@@ -493,23 +511,6 @@
     )(words, plain)
 
 
-def merge_kernel(plain_ref, words_ref, out_ref):
-    total, mass = get_plain(plain_ref)
-    more, more_mass = get_words(words_ref)
-    cols = total.shape[1]
-    out_ref[:, :cols] = total + more
-    out_ref[:, cols:] = jnp.broadcast_to(mass + more_mass, (total.shape[0], LANES))
-
-
-def merge(plain, words):
-    return pl.pallas_call(
-        merge_kernel,
-        out_shape=jax.ShapeDtypeStruct(plain.shape, F32),
-        compiler_params=params(16),
-        name="merge",
-    )(plain, words)
-
-
 def finish_kernel(where_ref, *refs):
     groups, out_ref = (refs[: len(refs) // 2], refs[len(refs) // 2 : -1]), refs[-1]
     cols = groups[0][0].shape[1] - LANES
@@ -569,10 +570,11 @@
     lists = lists + [swap(v, "scen", 1) for v in lists]
     weight, row = quantiles(most, low, high, own_rank, value, lists)
     far = {slot: swap(weight, "inst", slot) for slot in range(slots - 1, 0, -1)}
+    far[slots - 1], here = lax.optimization_barrier((far[slots - 1], bring(got)))
     weights = [weight] + [far[slot] for slot in range(1, slots)]
     weights = weights + [swap(w, "scen", 1) for w in weights]
 
-    away, partner, handled, plain = tail_sums(where, weights, [mine, got], slots, lines)
+    away, partner, handled, plain = tail_sums(where, weights, [mine, here], slots, lines)
     half = books // lines // CORES
     groups = []
     for side in range(CORES):
@@ -583,8 +585,7 @@
             block = sent[(k - 1) * half : k * half]
             words.append(swap(block, "scen", (CORES * (2 * k + 1)) ^ side))
         first = plain[0] if side == 0 else swap(plain[1], "scen", 1)
-        first = merge(first, swap(partner[side], "scen", CORES ^ side))
-        groups.append([first, *words])
+        groups.append([first, swap(partner[side], "scen", CORES ^ side), *words])
     return finish(where, groups), row[0, :share]
 
 

time: 85.4 us -> 84 us (0.984)
  Pallas kernels: 26.4 us -> 25.1 us
    pallas_call x2, Pallas kernels: 5.67 us -> 3.35 us  [tail_call(): pl.pallas_call(kernel, out_shape=[jax.ShapeDtypeStruct(shape, kind) for s...]
    pallas_call x2 -> x1, Pallas kernels: 0.44 us -> 1.6 us  [bring(): pl.pallas_call(bring_kernel, out_shape=jax.ShapeDtypeStruct(far.shape, fa...]
  transfers between devices with their start and end apart: 29 -> 29, of which waited for: 14 -> 16; matrix products, arithmetic and copies ran while one was open for 1% -> 1% of each run, Pallas kernels for 19% -> 20%
where the time goes in v5:
time: 84 us; the launch traced here: 83.7 us
  waiting for transfers between devices  28.2 us (34%)
  starting transfers between devices  26.5 us (32%)
  Pallas kernels  25.1 us (30%)
  local copies, waits for them, and re-layouts  2.83 us (3%)
  between operations  1 us (1%)
    ppermute x29, waiting for transfers between devices, swap(): return lax.ppermute(value, axis, [(k, k ^ flip) for k in range(n)])  28.2 us
    ppermute x29, starting transfers between devices, swap(): return lax.ppermute(value, axis, [(k, k ^ flip) for k in range(n)])  26.5 us
    pallas_call x1, Pallas kernels, stage(): pl.pallas_call(functools.partial(stage_kernel, slots, near, far), out_sha...  7 us
    pallas_call x1, Pallas kernels, add_moves(): pl.pallas_call(add_moves_kernel, out_shape=jax.ShapeDtypeStruct((rows, co...  5.11 us
    pallas_call x1, Pallas kernels, profits(): pl.pallas_call(functools.partial(profit_kernel, len(tops)), out_shape=out...  4.83 us
    pallas_call x2, Pallas kernels, tail_call(): pl.pallas_call(kernel, out_shape=[jax.ShapeDtypeStruct(shape, kind) for s...  3.35 us
    unnamed x16, local copies, waits for them, and re-layouts  1.79 us
  transfers between devices with their start and end apart: 29, of which 16 were waited for; matrix products, arithmetic and copies ran while one was open for 1% of the time, Pallas kernels for 20%

profile of v5, /device:TPU:0, one launch (start us, length us, event | category | flops | bytes accessed | tf_op | source)
XLA Modules:
  0.0 83.7 jit_solution(15606777051511265523)
XLA Ops:
  0.6 3.0 %collective-permute-start = (bf16[512,512]{1,0:T(8,128)(2,1)}, bf16[512,512]{1,0:T(8,128)(2,1)S(1)}, u32[]{:S(2)}, u32[]{:S(2)}) collective-permute-start(bf16[512,512]{1,0:T(8,128)(2,1)} %shocks_ref.1), channel_id=1, source_target_pairs={{0,1},{1,0},{2,3},{3,2},{4,5},{5,4},{6,7},{7,6},{8,9},{9,8},{10,11... | collective-permute-start | bytes 1572872 | tf_op jit(solution)/shard_map/ppermute | solution.py:37
  3.6 1.5 %collective-permute-start.2 = (bf16[512,512]{1,0:T(8,128)(2,1)}, bf16[512,512]{1,0:T(8,128)(2,1)S(1)}, u32[]{:S(2)}, u32[]{:S(2)}) collective-permute-start(bf16[512,512]{1,0:T(8,128)(2,1)} %shocks_ref.1), channel_id=1, source_target_pairs={{0,2},{1,3},{2,0},{3,1},{4,6},{5,7},{6,4},{7,5},{8,10},{9,11},{10,... | collective-permute-start | bytes 1572872 | tf_op jit(solution)/shard_map/ppermute | solution.py:37
  5.2 1.0 %copy-done = bf16[512,512]{1,0:T(8,128)(2,1)S(1)} copy-done((bf16[512,512]{1,0:T(8,128)(2,1)S(1)}, bf16[512,512]{1,0:T(8,128)(2,1)}, u32[]{:S(2)}) %copy-start) | copy-done | bytes 524312
  7.0 7.0 %stage.1 = (f32[512,4096]{1,0:T(8,128)S(1)}, bf16[1024,4096]{1,0:T(8,128)(2,1)S(1)}, bf16[512,4096]{1,0:T(8,128)(2,1)S(1)}, bf16[4096,256]{1,0:T(8,128)(2,1)S(1)}) custom-call(s32[3]{0:T(128)S(1)} %pad_add_fusion.where_ref, bf16[512,512]{1,0:T(8,128)(2,1)S(1)} %copy-done, s32[1,4096]{1,0:T(1,128)S(1)} %bitcast.9, bf16[2048,4096]{1,0:T(8,128)(2,1)} %loadings_ref.1), custom_call_target="tpu_custom_call" | custom-call | flops 2147483648 | bytes 16777216 | tf_op jit(solution)/shard_map/stage/pallas_call | solution.py:83
  14.0 1.8 %collective-permute-done.refs_0_ = bf16[512,512]{1,0:T(8,128)(2,1)S(1)} collective-permute-done((bf16[512,512]{1,0:T(8,128)(2,1)}, bf16[512,512]{1,0:T(8,128)(2,1)S(1)}, u32[]{:S(2)}, u32[]{:S(2)}) %collective-permute-start) | collective-permute-done | bytes 524320 | tf_op jit(solution)/shard_map/ppermute | solution.py:37
  15.8 1.8 %collective-permute-start.1 = (bf16[256,512]{1,0:T(8,128)(2,1)S(1)}, bf16[256,512]{1,0:T(8,128)(2,1)S(1)}, u32[]{:S(2)}, u32[]{:S(2)}) collective-permute-start(bf16[256,512]{1,0:T(8,128)(2,1)S(1)} %slice.12), channel_id=1, source_target_pairs={{0,2},{1,3},{2,0},{3,1},{4,6},{5,7},{6,4},{7,5},{8,10},{9,11},{10,... | collective-permute-start | bytes 786440 | tf_op jit(solution)/shard_map/ppermute | solution.py:37
  17.6 1.6 %collective-permute-start.3 = (bf16[256,512]{1,0:T(8,128)(2,1)S(1)}, bf16[256,512]{1,0:T(8,128)(2,1)S(1)}, u32[]{:S(2)}, u32[]{:S(2)}) collective-permute-start(bf16[256,512]{1,0:T(8,128)(2,1)S(1)} %slice.13), channel_id=1, source_target_pairs={{0,1},{1,0},{2,3},{3,2},{4,5},{5,4},{6,7},{7,6},{8,9},{9,8},{10,11... | collective-permute-start | bytes 786440 | tf_op jit(solution)/shard_map/ppermute | solution.py:37
  19.2 5.1 %add_moves.1.refs_3_ = f32[512,4096]{1,0:T(8,128)S(1)} custom-call(bf16[512,512]{1,0:T(8,128)(2,1)S(1)} %collective-permute-done.refs_0_, bf16[512,512]{1,0:T(8,128)(2,1)S(1)} %collective-permute-done.2.refs_1_, bf16[1024,4096]{1,0:T(8,128)(2,1)S(1)} %get-tuple-element.28.refs_2_, ...), custom_call_target="tpu_custom_call", output_to_operand_aliasing={{}: (3, {})} | custom-call | flops 4294967296 | bytes 16777216 | tf_op jit(solution)/shard_map/add_moves/pallas_call | solution.py:117
  24.7 4.8 %profits.1 = (bf16[512,2048]{1,0:T(8,128)(2,1)S(1)}, bf16[512,2048]{1,0:T(8,128)(2,1)}, f32[64,512]{1,0:T(8,128)S(1)}, f32[64,512]{1,0:T(8,128)S(1)}, f32[64,512]{1,0:T(8,128)S(1)}, /*index=5*/f32[64,512]{1,0:T(8,128)S(1)}) custom-call(s32[3]{0:T(128)S(1)} %pad_add_fusion.where_ref, bf16[256,512]{1,0:T(8,128)(2,1)S(1)} %collective-permute-done.1.refs_0_, ...), custom_call_target="tpu_custom_call" | custom-call | flops 3221225472 | bytes 12582912 | tf_op jit(solution)/shard_map/profits/pallas_call | solution.py:173
  29.6 1.5 %collective-permute-start.4 = (f32[64,512]{1,0:T(8,128)S(1)}, f32[64,512]{1,0:T(8,128)S(1)}, u32[]{:S(2)}, u32[]{:S(2)}) collective-permute-start(f32[64,512]{1,0:T(8,128)S(1)} %get-tuple-element.32), channel_id=1, source_target_pairs={{0,3},{1,2},{2,1},{3,0},{4,7},{5,6},{6,5},{7,4},{8,11},{9,10},{10,... | collective-permute-start | bytes 393224 | tf_op jit(solution)/shard_map/ppermute | solution.py:37
  31.1 1.5 %collective-permute-start.5 = (f32[64,512]{1,0:T(8,128)S(1)}, f32[64,512]{1,0:T(8,128)S(1)}, u32[]{:S(2)}, u32[]{:S(2)}) collective-permute-start(f32[64,512]{1,0:T(8,128)S(1)} %get-tuple-element.33), channel_id=1, source_target_pairs={{0,2},{1,3},{2,0},{3,1},{4,6},{5,7},{6,4},{7,5},{8,10},{9,11},{10,... | collective-permute-start | bytes 393224 | tf_op jit(solution)/shard_map/ppermute | solution.py:37
  33.1 3.7 %collective-permute-done.4.refs_1_ = f32[64,512]{1,0:T(8,128)S(1)} collective-permute-done((f32[64,512]{1,0:T(8,128)S(1)}, f32[64,512]{1,0:T(8,128)S(1)}, u32[]{:S(2)}, u32[]{:S(2)}) %collective-permute-start.4) | collective-permute-done | bytes 131104 | tf_op jit(solution)/shard_map/ppermute | solution.py:37
  36.9 2.3 %collective-permute-done.5.refs_2_ = f32[64,512]{1,0:T(8,128)S(1)} collective-permute-done((f32[64,512]{1,0:T(8,128)S(1)}, f32[64,512]{1,0:T(8,128)S(1)}, u32[]{:S(2)}, u32[]{:S(2)}) %collective-permute-start.5) | collective-permute-done | bytes 131104 | tf_op jit(solution)/shard_map/ppermute | solution.py:37
  39.7 1.6 %collective-permute-start.7 = (f32[32,128]{1,0:T(8,128)S(1)}, f32[32,128]{1,0:T(8,128)S(1)}, u32[]{:S(2)}, u32[]{:S(2)}) collective-permute-start(f32[32,128]{1,0:T(8,128)S(1)} %get-tuple-element.36.refs_0_), channel_id=1, source_target_pairs={{0,8},{4,12},{8,0},{12,4},{16,24},{20,28},{24,16},{28,20},{1,9},{5... | collective-permute-start | bytes 49160 | tf_op jit(solution)/shard_map/ppermute | solution.py:37
  41.4 2.5 %collective-permute-start.8 = (f32[32,128]{1,0:T(8,128)S(1)}, f32[32,128]{1,0:T(8,128)S(1)}, u32[]{:S(2)}, u32[]{:S(2)}) collective-permute-start(f32[32,128]{1,0:T(8,128)S(1)} %get-tuple-element.36.refs_0_), channel_id=1, source_target_pairs={{0,24},{4,28},{8,16},{12,20},{16,8},{20,12},{24,0},{28,4},{1,25},{... | collective-permute-start | bytes 49160 | tf_op jit(solution)/shard_map/ppermute | solution.py:37
  44.5 2.4 %collective-permute-done.8.refs_2_ = f32[32,128]{1,0:T(8,128)S(1)} collective-permute-done((f32[32,128]{1,0:T(8,128)S(1)}, f32[32,128]{1,0:T(8,128)S(1)}, u32[]{:S(2)}, u32[]{:S(2)}) %collective-permute-start.8) | collective-permute-done | bytes 16416 | tf_op jit(solution)/shard_map/ppermute | solution.py:37
  46.9 1.6 %collective-permute-done.9.refs_3_ = f32[32,128]{1,0:T(8,128)S(1)} collective-permute-done((f32[32,128]{1,0:T(8,128)S(1)}, f32[32,128]{1,0:T(8,128)S(1)}, u32[]{:S(2)}, u32[]{:S(2)}) %collective-permute-start.9) | collective-permute-done | bytes 16416 | tf_op jit(solution)/shard_map/ppermute | solution.py:37
  50.3 1.4 %collective-permute-start.14 = (bf16[64,512]{1,0:T(8,128)(2,1)S(1)}, bf16[64,512]{1,0:T(8,128)(2,1)S(1)}, u32[]{:S(2)}, u32[]{:S(2)}) collective-permute-start(bf16[64,512]{1,0:T(8,128)(2,1)S(1)} %get-tuple-element.37.refs_0_), channel_id=1, source_target_pairs={{0,1},{1,0},{2,3},{3,2},{4,5},{5,4},{6,7},{7,6},{8,9},{9,8},{10,11... | collective-permute-start | bytes 196616 | tf_op jit(solution)/shard_map/ppermute | solution.py:37
  52.4 1.4 %collective-permute-start.16 = (bf16[64,512]{1,0:T(8,128)(2,1)S(1)}, bf16[64,512]{1,0:T(8,128)(2,1)S(1)}, u32[]{:S(2)}, u32[]{:S(2)}) collective-permute-start(bf16[64,512]{1,0:T(8,128)(2,1)S(1)} %get-tuple-element.37.refs_0_), channel_id=1, source_target_pairs={{0,3},{1,2},{2,1},{3,0},{4,7},{5,6},{6,5},{7,4},{8,11},{9,10},{10,... | collective-permute-start | bytes 196616 | tf_op jit(solution)/shard_map/ppermute | solution.py:37
  54.6 2.1 %collective-permute-done.15.refs_2_ = bf16[64,512]{1,0:T(8,128)(2,1)S(1)} collective-permute-done((bf16[64,512]{1,0:T(8,128)(2,1)S(1)}, bf16[64,512]{1,0:T(8,128)(2,1)S(1)}, u32[]{:S(2)}, u32[]{:S(2)}) %collective-permute-start.15) | collective-permute-done | bytes 65568 | tf_op jit(solution)/shard_map/ppermute | solution.py:37
  56.7 1.6 %bring.1.refs_9_.refs_1_ = bf16[512,2048]{1,0:T(8,128)(2,1)S(1)} custom-call(bf16[512,2048]{1,0:T(8,128)(2,1)} %collective-permute-done.17.far_ref), custom_call_target="tpu_custom_call" | custom-call | bytes 8388608 | tf_op jit(solution)/shard_map/bring/pallas_call | solution.py:445
  59.8 1.6 %away_sums.1 = (s16[32,2176]{1,0:T(8,128)(2,1)S(1)}, s16[32,2176]{1,0:T(8,128)(2,1)S(1)}, bf16[256,1024]{1,0:T(8,128)(2,1)S(1)}) custom-call(s32[3]{0:T(128)S(1)} %pad_add_fusion.where_ref, bf16[64,512]{1,0:T(8,128)(2,1)S(1)} %get-tuple-element.37.refs_0_, bf16[64,512]{1,0:T(8,128)(2,1)S(1)} %collective-permute-done.14.refs_1_, ...), custom_call_target="tpu_custom_call" | custom-call | tf_op jit(solution)/shard_map/away_sums/pallas_call | solution.py:459
  62.2 1.3 %collective-permute-start.23 = (s16[32,2176]{1,0:T(8,128)(2,1)S(1)}, s16[32,2176]{1,0:T(8,128)(2,1)S(1)}, u32[]{:S(2)}, u32[]{:S(2)}) collective-permute-start(s16[32,2176]{1,0:T(8,128)(2,1)S(1)} %get-tuple-element.45), channel_id=1, source_target_pairs={{0,8},{4,12},{8,0},{12,4},{16,24},{20,28},{24,16},{28,20},{1,9},{5... | collective-permute-start | bytes 417800 | tf_op jit(solution)/shard_map/ppermute | solution.py:37
  63.4 1.8 %home_sums.1 = (s16[32,2176]{1,0:T(8,128)(2,1)S(1)}, s16[32,2176]{1,0:T(8,128)(2,1)S(1)}, f32[32,2176]{1,0:T(8,128)S(1)}, f32[32,2176]{1,0:T(8,128)S(1)}, f32[32...) custom-call(s32[3]{0:T(128)S(1)} %pad_add_fusion.where_ref, bf16[256,1024]{1,0:T(8,128)(2,1)S(1)} %get-tuple-element.42.held, ...), custom_call_target="tpu_custom_call" | custom-call | tf_op jit(solution)/shard_map/home_sums/pallas_call | solution.py:459
  66.1 1.1 %collective-permute-start.26 = (s16[32,2176]{1,0:T(8,128)(2,1)S(1)}, s16[32,2176]{1,0:T(8,128)(2,1)S(1)}, u32[]{:S(2)}, u32[]{:S(2)}) collective-permute-start(s16[32,2176]{1,0:T(8,128)(2,1)S(1)} %get-tuple-element.48), channel_id=1, source_target_pairs={{0,12},{4,8},{8,4},{12,0},{16,28},{20,24},{24,20},{28,16},{1,13},{... | collective-permute-start | bytes 417800 | tf_op jit(solution)/shard_map/ppermute | solution.py:37
  68.7 2.1 %collective-permute-done.23.words_ref = s16[32,2176]{1,0:T(8,128)(2,1)S(1)} collective-permute-done((s16[32,2176]{1,0:T(8,128)(2,1)S(1)}, s16[32,2176]{1,0:T(8,128)(2,1)S(1)}, u32[]{:S(2)}, u32[]{:S(2)}) %collective-permute-start.23) | collective-permute-done | bytes 139296 | tf_op jit(solution)/shard_map/ppermute | solution.py:37
  71.1 1.4 %collective-permute-start.24 = (s16[32,2176]{1,0:T(8,128)(2,1)S(1)}, s16[32,2176]{1,0:T(8,128)(2,1)S(1)}, u32[]{:S(2)}, u32[]{:S(2)}) collective-permute-start(s16[32,2176]{1,0:T(8,128)(2,1)S(1)} %relay.2), channel_id=1, source_target_pairs={{0,24},{4,28},{8,16},{12,20},{16,8},{20,12},{24,0},{28,4},{1,25},{... | collective-permute-start | bytes 417800 | tf_op jit(solution)/shard_map/ppermute | solution.py:37
  73.0 0.8 %collective-permute-done.22.refs_1_ = s16[32,2176]{1,0:T(8,128)(2,1)S(1)} collective-permute-done((s16[32,2176]{1,0:T(8,128)(2,1)S(1)}, s16[32,2176]{1,0:T(8,128)(2,1)S(1)}, u32[]{:S(2)}, u32[]{:S(2)}) %collective-permute-start.22) | collective-permute-done | bytes 139296 | tf_op jit(solution)/shard_map/ppermute | solution.py:37
  73.9 2.2 %collective-permute-done.26.refs_4_ = s16[32,2176]{1,0:T(8,128)(2,1)S(1)} collective-permute-done((s16[32,2176]{1,0:T(8,128)(2,1)S(1)}, s16[32,2176]{1,0:T(8,128)(2,1)S(1)}, u32[]{:S(2)}, u32[]{:S(2)}) %collective-permute-start.26) | collective-permute-done | bytes 139296 | tf_op jit(solution)/shard_map/ppermute | solution.py:37
  76.1 2.4 %collective-permute-done.28.refs_5_ = s16[32,2176]{1,0:T(8,128)(2,1)S(1)} collective-permute-done((s16[32,2176]{1,0:T(8,128)(2,1)S(1)}, s16[32,2176]{1,0:T(8,128)(2,1)S(1)}, u32[]{:S(2)}, u32[]{:S(2)}) %collective-permute-start.28) | collective-permute-done | bytes 139296 | tf_op jit(solution)/shard_map/ppermute | solution.py:37
  78.5 3.6 %collective-permute-done.24.refs_2_ = s16[32,2176]{1,0:T(8,128)(2,1)S(1)} collective-permute-done((s16[32,2176]{1,0:T(8,128)(2,1)S(1)}, s16[32,2176]{1,0:T(8,128)(2,1)S(1)}, u32[]{:S(2)}, u32[]{:S(2)}) %collective-permute-start.24) | collective-permute-done | bytes 139296 | tf_op jit(solution)/shard_map/ppermute | solution.py:37
  82.0 1.7 %finish.1 = f32[32,4096]{1,0:T(8,128)} custom-call(s32[3]{0:T(128)S(1)} %pad_add_fusion.where_ref, f32[32,2176]{1,0:T(8,128)S(1)} %get-tuple-element.43.refs_0_, s16[32,2176]{1,0:T(8,128)(2,1)S(1)} %collective-permute-done.22.refs_1_, s16[32,2176]{1,0:T(8,128)(2,1)S(1)} %collective-permute-done.24.refs_2_, f32[32,2176]{1,0:T(8,128)S(1)} %collective-permute-done.25.refs_3_, ...), custom_call_target="tpu_custom_call" | custom-call | tf_op jit(solution)/shard_map/finish/pallas_call | solution.py:530
  (66 shorter events, 11.4 us)
Async XLA Ops:
  0.6 15.1 %collective-permute-start = (bf16[512,512]{1,0:T(8,128)(2,1)}, bf16[512,512]{1,0:T(8,128)(2,1)S(1)}, u32[]{:S(2)}, u32[]{:S(2)}) collective-permute-start(bf16[512,512]{1,0:T(8,128)(2,1)} %shocks_ref.1), channel_id=1, source_target_pairs={{0,1},{1,0},{2,3},{3,2},{4,5},{5,4},{6,7},{7,6},{8,9},{9,8},{10,11... | collective-permute-start | bytes 1572872 | tf_op jit(solution)/shard_map/ppermute | solution.py:37
  3.6 14.0 %collective-permute-start.2 = (bf16[512,512]{1,0:T(8,128)(2,1)}, bf16[512,512]{1,0:T(8,128)(2,1)S(1)}, u32[]{:S(2)}, u32[]{:S(2)}) collective-permute-start(bf16[512,512]{1,0:T(8,128)(2,1)} %shocks_ref.1), channel_id=1, source_target_pairs={{0,2},{1,3},{2,0},{3,1},{4,6},{5,7},{6,4},{7,5},{8,10},{9,11},{10,... | collective-permute-start | bytes 1572872 | tf_op jit(solution)/shard_map/ppermute | solution.py:37
  15.8 8.5 %collective-permute-start.1 = (bf16[256,512]{1,0:T(8,128)(2,1)S(1)}, bf16[256,512]{1,0:T(8,128)(2,1)S(1)}, u32[]{:S(2)}, u32[]{:S(2)}) collective-permute-start(bf16[256,512]{1,0:T(8,128)(2,1)S(1)} %slice.12), channel_id=1, source_target_pairs={{0,2},{1,3},{2,0},{3,1},{4,6},{5,7},{6,4},{7,5},{8,10},{9,11},{10,... | collective-permute-start | bytes 786440 | tf_op jit(solution)/shard_map/ppermute | solution.py:37
  17.6 7.0 %collective-permute-start.3 = (bf16[256,512]{1,0:T(8,128)(2,1)S(1)}, bf16[256,512]{1,0:T(8,128)(2,1)S(1)}, u32[]{:S(2)}, u32[]{:S(2)}) collective-permute-start(bf16[256,512]{1,0:T(8,128)(2,1)S(1)} %slice.13), channel_id=1, source_target_pairs={{0,1},{1,0},{2,3},{3,2},{4,5},{5,4},{6,7},{7,6},{8,9},{9,8},{10,11... | collective-permute-start | bytes 786440 | tf_op jit(solution)/shard_map/ppermute | solution.py:37
  24.6 23.9 %copy-start.5 = (s32[256]{0:T(256)S(1)}, s32[256]{0:T(256)}, u32[]{:S(2)}) copy-start(s32[256]{0:T(256)} %param.16) | copy-start | bytes 3076
  24.6 24.0 %copy-start.6 = (s32[256]{0:T(256)S(1)}, s32[256]{0:T(256)}, u32[]{:S(2)}) copy-start(s32[256]{0:T(256)} %param.17) | copy-start | bytes 3076
  24.6 24.2 %copy-start.7 = (s32[256]{0:T(256)S(1)}, s32[256]{0:T(256)}, u32[]{:S(2)}) copy-start(s32[256]{0:T(256)} %param.15) | copy-start | bytes 3076
  29.5 27.2 %collective-permute-start.17 = (bf16[512,2048]{1,0:T(8,128)(2,1)}, bf16[512,2048]{1,0:T(8,128)(2,1)}, u32[]{:S(2)}, u32[]{:S(2)}) collective-permute-start(bf16[512,2048]{1,0:T(8,128)(2,1)} %get-tuple-element.38), channel_id=1, source_target_pairs={{0,4},{4,0},{8,12},{12,8},{16,20},{20,16},{24,28},{28,24},{1,5},{5... | collective-permute-start | bytes 6291464 | tf_op jit(solution)/shard_map/ppermute | solution.py:37
  29.6 7.3 %collective-permute-start.4 = (f32[64,512]{1,0:T(8,128)S(1)}, f32[64,512]{1,0:T(8,128)S(1)}, u32[]{:S(2)}, u32[]{:S(2)}) collective-permute-start(f32[64,512]{1,0:T(8,128)S(1)} %get-tuple-element.32), channel_id=1, source_target_pairs={{0,3},{1,2},{2,1},{3,0},{4,7},{5,6},{6,5},{7,4},{8,11},{9,10},{10,... | collective-permute-start | bytes 393224 | tf_op jit(solution)/shard_map/ppermute | solution.py:37
  31.1 8.1 %collective-permute-start.5 = (f32[64,512]{1,0:T(8,128)S(1)}, f32[64,512]{1,0:T(8,128)S(1)}, u32[]{:S(2)}, u32[]{:S(2)}) collective-permute-start(f32[64,512]{1,0:T(8,128)S(1)} %get-tuple-element.33), channel_id=1, source_target_pairs={{0,2},{1,3},{2,0},{3,1},{4,6},{5,7},{6,4},{7,5},{8,10},{9,11},{10,... | collective-permute-start | bytes 393224 | tf_op jit(solution)/shard_map/ppermute | solution.py:37
  32.6 6.6 %collective-permute-start.6 = (f32[64,512]{1,0:T(8,128)S(1)}, f32[64,512]{1,0:T(8,128)S(1)}, u32[]{:S(2)}, u32[]{:S(2)}) collective-permute-start(f32[64,512]{1,0:T(8,128)S(1)} %get-tuple-element.34), channel_id=1, source_target_pairs={{0,1},{1,0},{2,3},{3,2},{4,5},{5,4},{6,7},{7,6},{8,9},{9,8},{10,11... | collective-permute-start | bytes 393224 | tf_op jit(solution)/shard_map/ppermute | solution.py:37
  39.7 4.2 %collective-permute-start.7 = (f32[32,128]{1,0:T(8,128)S(1)}, f32[32,128]{1,0:T(8,128)S(1)}, u32[]{:S(2)}, u32[]{:S(2)}) collective-permute-start(f32[32,128]{1,0:T(8,128)S(1)} %get-tuple-element.36.refs_0_), channel_id=1, source_target_pairs={{0,8},{4,12},{8,0},{12,4},{16,24},{20,28},{24,16},{28,20},{1,9},{5... | collective-permute-start | bytes 49160 | tf_op jit(solution)/shard_map/ppermute | solution.py:37
  41.4 5.5 %collective-permute-start.8 = (f32[32,128]{1,0:T(8,128)S(1)}, f32[32,128]{1,0:T(8,128)S(1)}, u32[]{:S(2)}, u32[]{:S(2)}) collective-permute-start(f32[32,128]{1,0:T(8,128)S(1)} %get-tuple-element.36.refs_0_), channel_id=1, source_target_pairs={{0,24},{4,28},{8,16},{12,20},{16,8},{20,12},{24,0},{28,4},{1,25},{... | collective-permute-start | bytes 49160 | tf_op jit(solution)/shard_map/ppermute | solution.py:37
  43.8 4.6 %collective-permute-start.9 = (f32[32,128]{1,0:T(8,128)S(1)}, f32[32,128]{1,0:T(8,128)S(1)}, u32[]{:S(2)}, u32[]{:S(2)}) collective-permute-start(f32[32,128]{1,0:T(8,128)S(1)} %get-tuple-element.36.refs_0_), channel_id=1, source_target_pairs={{0,16},{4,20},{8,24},{12,28},{16,0},{20,4},{24,8},{28,12},{1,17},{... | collective-permute-start | bytes 49160 | tf_op jit(solution)/shard_map/ppermute | solution.py:37
  44.0 5.0 %collective-permute-start.10 = (f32[32,128]{1,0:T(8,128)S(1)}, f32[32,128]{1,0:T(8,128)S(1)}, u32[]{:S(2)}, u32[]{:S(2)}) collective-permute-start(f32[32,128]{1,0:T(8,128)S(1)} %get-tuple-element.36.refs_0_), channel_id=1, source_target_pairs={{0,4},{4,0},{8,12},{12,8},{16,20},{20,16},{24,28},{28,24},{1,5},{5... | collective-permute-start | bytes 49160 | tf_op jit(solution)/shard_map/ppermute | solution.py:37
  44.0 5.0 %collective-permute-start.11 = (f32[32,128]{1,0:T(8,128)S(1)}, f32[32,128]{1,0:T(8,128)S(1)}, u32[]{:S(2)}, u32[]{:S(2)}) collective-permute-start(f32[32,128]{1,0:T(8,128)S(1)} %collective-permute-done.7.refs_1_), channel_id=1, source_target_pairs={{0,4},{4,0},{8,12},{12,8},{16,20},{20,16},{24,28},{28,24},{1,5},{5... | collective-permute-start | bytes 49160 | tf_op jit(solution)/shard_map/ppermute | solution.py:37
  46.9 2.1 %collective-permute-start.12 = (f32[32,128]{1,0:T(8,128)S(1)}, f32[32,128]{1,0:T(8,128)S(1)}, u32[]{:S(2)}, u32[]{:S(2)}) collective-permute-start(f32[32,128]{1,0:T(8,128)S(1)} %collective-permute-done.8.refs_2_), channel_id=1, source_target_pairs={{0,4},{4,0},{8,12},{12,8},{16,20},{20,16},{24,28},{28,24},{1,5},{5... | collective-permute-start | bytes 49160 | tf_op jit(solution)/shard_map/ppermute | solution.py:37
  48.5 1.2 %collective-permute-start.13 = (f32[32,128]{1,0:T(8,128)S(1)}, f32[32,128]{1,0:T(8,128)S(1)}, u32[]{:S(2)}, u32[]{:S(2)}) collective-permute-start(f32[32,128]{1,0:T(8,128)S(1)} %collective-permute-done.9.refs_3_), channel_id=1, source_target_pairs={{0,4},{4,0},{8,12},{12,8},{16,20},{20,16},{24,28},{28,24},{1,5},{5... | collective-permute-start | bytes 49160 | tf_op jit(solution)/shard_map/ppermute | solution.py:37
  50.3 4.3 %collective-permute-start.14 = (bf16[64,512]{1,0:T(8,128)(2,1)S(1)}, bf16[64,512]{1,0:T(8,128)(2,1)S(1)}, u32[]{:S(2)}, u32[]{:S(2)}) collective-permute-start(bf16[64,512]{1,0:T(8,128)(2,1)S(1)} %get-tuple-element.37.refs_0_), channel_id=1, source_target_pairs={{0,1},{1,0},{2,3},{3,2},{4,5},{5,4},{6,7},{7,6},{8,9},{9,8},{10,11... | collective-permute-start | bytes 196616 | tf_op jit(solution)/shard_map/ppermute | solution.py:37
  51.7 5.0 %collective-permute-start.15 = (bf16[64,512]{1,0:T(8,128)(2,1)S(1)}, bf16[64,512]{1,0:T(8,128)(2,1)S(1)}, u32[]{:S(2)}, u32[]{:S(2)}) collective-permute-start(bf16[64,512]{1,0:T(8,128)(2,1)S(1)} %get-tuple-element.37.refs_0_), channel_id=1, source_target_pairs={{0,2},{1,3},{2,0},{3,1},{4,6},{5,7},{6,4},{7,5},{8,10},{9,11},{10,... | collective-permute-start | bytes 196616 | tf_op jit(solution)/shard_map/ppermute | solution.py:37
  52.4 5.9 %collective-permute-start.16 = (bf16[64,512]{1,0:T(8,128)(2,1)S(1)}, bf16[64,512]{1,0:T(8,128)(2,1)S(1)}, u32[]{:S(2)}, u32[]{:S(2)}) collective-permute-start(bf16[64,512]{1,0:T(8,128)(2,1)S(1)} %get-tuple-element.37.refs_0_), channel_id=1, source_target_pairs={{0,3},{1,2},{2,1},{3,0},{4,7},{5,6},{6,5},{7,4},{8,11},{9,10},{10,... | collective-permute-start | bytes 196616 | tf_op jit(solution)/shard_map/ppermute | solution.py:37
  53.8 5.0 %collective-permute-start.18 = (bf16[64,512]{1,0:T(8,128)(2,1)S(1)}, bf16[64,512]{1,0:T(8,128)(2,1)S(1)}, u32[]{:S(2)}, u32[]{:S(2)}) collective-permute-start(bf16[64,512]{1,0:T(8,128)(2,1)S(1)} %get-tuple-element.37.refs_0_), channel_id=1, source_target_pairs={{0,4},{4,0},{8,12},{12,8},{16,20},{20,16},{24,28},{28,24},{1,5},{5... | collective-permute-start | bytes 196616 | tf_op jit(solution)/shard_map/ppermute | solution.py:37
  54.6 4.3 %collective-permute-start.19 = (bf16[64,512]{1,0:T(8,128)(2,1)S(1)}, bf16[64,512]{1,0:T(8,128)(2,1)S(1)}, u32[]{:S(2)}, u32[]{:S(2)}) collective-permute-start(bf16[64,512]{1,0:T(8,128)(2,1)S(1)} %collective-permute-done.14.refs_1_), channel_id=1, source_target_pairs={{0,4},{4,0},{8,12},{12,8},{16,20},{20,16},{24,28},{28,24},{1,5},{5... | collective-permute-start | bytes 196616 | tf_op jit(solution)/shard_map/ppermute | solution.py:37
  56.7 2.2 %collective-permute-start.20 = (bf16[64,512]{1,0:T(8,128)(2,1)S(1)}, bf16[64,512]{1,0:T(8,128)(2,1)S(1)}, u32[]{:S(2)}, u32[]{:S(2)}) collective-permute-start(bf16[64,512]{1,0:T(8,128)(2,1)S(1)} %collective-permute-done.15.refs_2_), channel_id=1, source_target_pairs={{0,4},{4,0},{8,12},{12,8},{16,20},{20,16},{24,28},{28,24},{1,5},{5... | collective-permute-start | bytes 196616 | tf_op jit(solution)/shard_map/ppermute | solution.py:37
  58.3 1.5 %collective-permute-start.21 = (bf16[64,512]{1,0:T(8,128)(2,1)S(1)}, bf16[64,512]{1,0:T(8,128)(2,1)S(1)}, u32[]{:S(2)}, u32[]{:S(2)}) collective-permute-start(bf16[64,512]{1,0:T(8,128)(2,1)S(1)} %collective-permute-done.16.refs_3_), channel_id=1, source_target_pairs={{0,4},{4,0},{8,12},{12,8},{16,20},{20,16},{24,28},{28,24},{1,5},{5... | collective-permute-start | bytes 196616 | tf_op jit(solution)/shard_map/ppermute | solution.py:37
  61.4 6.6 %collective-permute-start.27 = (s16[32,2176]{1,0:T(8,128)(2,1)S(1)}, s16[32,2176]{1,0:T(8,128)(2,1)S(1)}, u32[]{:S(2)}, u32[]{:S(2)}) collective-permute-start(s16[32,2176]{1,0:T(8,128)(2,1)S(1)} %get-tuple-element.49), channel_id=1, source_target_pairs={{0,8},{4,12},{8,0},{12,4},{16,24},{20,28},{24,16},{28,20},{1,9},{5... | collective-permute-start | bytes 417800 | tf_op jit(solution)/shard_map/ppermute | solution.py:37
  62.2 8.7 %collective-permute-start.23 = (s16[32,2176]{1,0:T(8,128)(2,1)S(1)}, s16[32,2176]{1,0:T(8,128)(2,1)S(1)}, u32[]{:S(2)}, u32[]{:S(2)}) collective-permute-start(s16[32,2176]{1,0:T(8,128)(2,1)S(1)} %get-tuple-element.45), channel_id=1, source_target_pairs={{0,8},{4,12},{8,0},{12,4},{16,24},{20,28},{24,16},{28,20},{1,9},{5... | collective-permute-start | bytes 417800 | tf_op jit(solution)/shard_map/ppermute | solution.py:37
  65.2 16.8 %collective-permute-start.25 = (f32[32,2176]{1,0:T(8,128)S(1)}, f32[32,2176]{1,0:T(8,128)S(1)}, u32[]{:S(2)}, u32[]{:S(2)}) collective-permute-start(f32[32,2176]{1,0:T(8,128)S(1)} %get-tuple-element.47), channel_id=1, source_target_pairs={{0,4},{4,0},{8,12},{12,8},{16,20},{20,16},{24,28},{28,24},{1,5},{5... | collective-permute-start | bytes 835592 | tf_op jit(solution)/shard_map/ppermute | solution.py:37
  65.3 8.6 %collective-permute-start.22 = (s16[32,2176]{1,0:T(8,128)(2,1)S(1)}, s16[32,2176]{1,0:T(8,128)(2,1)S(1)}, u32[]{:S(2)}, u32[]{:S(2)}) collective-permute-start(s16[32,2176]{1,0:T(8,128)(2,1)S(1)} %get-tuple-element.44), channel_id=1, source_target_pairs={{0,8},{4,12},{8,0},{12,4},{16,24},{20,28},{24,16},{28,20},{1,9},{5... | collective-permute-start | bytes 417800 | tf_op jit(solution)/shard_map/ppermute | solution.py:37
  66.1 10.0 %collective-permute-start.26 = (s16[32,2176]{1,0:T(8,128)(2,1)S(1)}, s16[32,2176]{1,0:T(8,128)(2,1)S(1)}, u32[]{:S(2)}, u32[]{:S(2)}) collective-permute-start(s16[32,2176]{1,0:T(8,128)(2,1)S(1)} %get-tuple-element.48), channel_id=1, source_target_pairs={{0,12},{4,8},{8,4},{12,0},{16,28},{20,24},{24,20},{28,16},{1,13},{... | collective-permute-start | bytes 417800 | tf_op jit(solution)/shard_map/ppermute | solution.py:37
  68.1 10.3 %collective-permute-start.28 = (s16[32,2176]{1,0:T(8,128)(2,1)S(1)}, s16[32,2176]{1,0:T(8,128)(2,1)S(1)}, u32[]{:S(2)}, u32[]{:S(2)}) collective-permute-start(s16[32,2176]{1,0:T(8,128)(2,1)S(1)} %relay.3), channel_id=1, source_target_pairs={{0,28},{4,24},{8,20},{12,16},{16,12},{20,8},{24,4},{28,0},{1,29},{... | collective-permute-start | bytes 417800 | tf_op jit(solution)/shard_map/ppermute | solution.py:37
  71.1 10.9 %collective-permute-start.24 = (s16[32,2176]{1,0:T(8,128)(2,1)S(1)}, s16[32,2176]{1,0:T(8,128)(2,1)S(1)}, u32[]{:S(2)}, u32[]{:S(2)}) collective-permute-start(s16[32,2176]{1,0:T(8,128)(2,1)S(1)} %relay.2), channel_id=1, source_target_pairs={{0,24},{4,28},{8,16},{12,20},{16,8},{20,12},{24,0},{28,4},{1,25},{... | collective-permute-start | bytes 417800 | tf_op jit(solution)/shard_map/ppermute | solution.py:37
  (5 other events, 18.0 us)

commit v6 on v5

--- a/solution.py
+++ b/solution.py
@@ -11,6 +11,8 @@
 ROUNDS = 3
 CORES = 2
 LANES = 128
+UPPER = 9
+ROW_RUN = 256
 RANK_PART = 64
 
 tail_width = 0.5
@@ -132,20 +134,23 @@
     top_refs, low_refs = refs[:count], refs[count : 2 * count]
     rest_ref, first_ref, delta_ref, gamma_ref, kappa_ref, onehot_ref = refs[2 * count : 2 * count + 6]
     mine_ref, theirs_ref = refs[2 * count + 6 : 2 * count + 8]
-    sum_refs, (total, held, sems) = refs[2 * count + 8 : -3], refs[-3:]
-    half, depth = top_refs[0].shape
+    sum_refs, (total, held, joined, sems) = refs[2 * count + 8 : -4], refs[-4:]
+    upper, depth = top_refs[0].shape
     part_cols = mine_ref.shape[1]
     tile = part_cols // 4
     share = sum_refs[0].shape[0]
+    for k in range(count):
+        joined[k, :upper, :] = top_refs[k][...]
+        joined[k, upper:, :] = low_refs[k][...]
     fresh, copies = True, []
     for side, out_ref in ((1 - where_ref[1], held), (where_ref[1], mine_ref)):
         for spot in tiles(part_cols, tile):
             part = pl.ds(pl.multiple_of(side * part_cols + spot.start, tile), tile)
             pieces = []
-            for at, shock_refs in ((0, top_refs), (half, low_refs)):
-                moves = first_ref[at : at + half, part]
-                for k, shock_ref in enumerate(shock_refs):
-                    moves = moves + dot(shock_ref[...], rest_ref[k * depth : (k + 1) * depth, part])
+            for run in tiles(joined.shape[1], ROW_RUN):
+                moves = first_ref[run, part]
+                for k in range(count):
+                    moves = moves + dot(joined[k, run, :], rest_ref[k * depth : (k + 1) * depth, part])
                 value = moves * (delta_ref[:, part] + moves * (gamma_ref[:, part] + moves * kappa_ref[:, part]))
                 pieces.append(value.astype(BF16))
             profit = jnp.concatenate(pieces, axis=0)
@@ -178,6 +183,7 @@
         scratch_shapes=[
             pltpu.VMEM((rows, books), F32),
             pltpu.VMEM((rows, cols // CORES), BF16),
+            pltpu.VMEM((len(tops), rows, depth), BF16),
             pltpu.SemaphoreType.DMA((4,)),
         ],
         compiler_params=params(16),
@@ -196,7 +202,7 @@
     while inner * inner * 4 <= slots:
         inner *= 2
     outer = slots // inner
-    half = shocks.shape[0] // 2
+    upper = shocks.shape[0] // 16 * UPPER
     along = [f for f in range(1, inner)]
     across = [f * inner for f in range(1, outer)]
     corners = [(a, b) for a in along for b in across]
@@ -204,8 +210,8 @@
     first, near_loads, far_loads, onehot = stage(
         where, shocks, book_of, loadings, slots, along + across, [a ^ b for a, b in corners], books
     )
-    tops = [swap(near[a][:half], "inst", b) for a, b in corners]
-    lows = [swap(near[b][half:], "inst", a) for a, b in corners]
+    tops = [swap(near[a][:upper], "inst", b) for a, b in corners]
+    lows = [swap(near[b][upper:], "inst", a) for a, b in corners]
     first = add_moves([near[f] for f in along + across], near_loads, first)
     return profits(where, tops, lows, far_loads, first, delta, gamma, kappa, onehot, slots)
 
@@ -370,14 +376,19 @@
     return ref[:, :cols], ref[:, cols : cols + 1]
 
 
-def tail_part(held, profit_refs, total, spot, rows):
+def sum_rows(weights, profit_refs, total, spot):
     cols = total.shape[1] - LANES
-    weight = held[spot, :]
-    mass = jnp.sum(weight.astype(F32), axis=1, keepdims=True)
-    total[spot, cols:] = jnp.broadcast_to(mass, (weight.shape[0], LANES))
     for part in tiles(cols, cols // 4):
-        result = dot(weight[:, :rows], profit_refs[0][:, part])
-        total[spot, part] = result + dot(weight[:, rows:], profit_refs[1][:, part])
+        result = dot(weights[0], profit_refs[0][:, part])
+        for weight, profit_ref in zip(weights[1:], profit_refs[1:]):
+            result = result + dot(weight, profit_ref[:, part])
+        total[spot, part] = result
+    put_mass(weights, total, spot)
+
+
+def put_mass(weights, total, spot):
+    mass = sum(jnp.sum(weight.astype(F32), axis=1, keepdims=True) for weight in weights)
+    total[spot, total.shape[1] - LANES :] = jnp.broadcast_to(mass, (mass.shape[0], LANES))
 
 
 def halves(where_ref, total, line, block):
@@ -388,44 +399,55 @@
         yield side, value
 
 
-def away_kernel(slots, lines, where_ref, *refs):
-    count = CORES * slots
-    weight_refs, profit_refs = refs[:count], refs[count : count + CORES]
-    away_refs, (held, total) = refs[count + CORES : -2], refs[-2:]
-    share, rows = weight_refs[0].shape
+def arrange(slots, lines, where_ref, weight_refs, held):
+    share = weight_refs[0].shape[0]
     block = share * slots // lines
     piece = min(share, block)
-    cols = total.shape[1] - LANES
-    half = block // CORES
     away = [line for line in range(2, lines, 2)]
     order = away + [1] + [line for line in range(3, lines, 2)] + [0]
-    for slot in range(slots):
-        for core in range(CORES):
-            ref = weight_refs[core * slots + slot]
-            for at in range(0, share, piece):
-                start = (where_ref[0] ^ slot) * share + at
-                line = start // block
-                flip = where_ref[2] ^ line
-                place = 0
-                for k, known in enumerate(order):
-                    place = place + jnp.where(flip == known, k, 0)
-                to = pl.multiple_of(place * block + (start - line * block), piece)
-                held[pl.ds(to, piece), core * rows : (core + 1) * rows] = ref[at : at + piece, :]
-    tail_part(held, profit_refs, total, slice(0, len(away) * block), rows)
-    for k in range(len(away)):
+    for slot, ref in enumerate(weight_refs):
+        for at in range(0, share, piece):
+            start = (where_ref[0] ^ slot) * share + at
+            line = start // block
+            flip = where_ref[2] ^ line
+            place = 0
+            for k, known in enumerate(order):
+                place = place + jnp.where(flip == known, k, 0)
+            to = pl.multiple_of(place * block + (start - line * block), piece)
+            held[pl.ds(to, piece), :] = ref[at : at + piece, :]
+    return len(away) * block
+
+
+def own_kernel(slots, lines, where_ref, *refs):
+    weight_refs, (profit_ref, held, part_ref) = refs[:slots], refs[slots:]
+    depth = arrange(slots, lines, where_ref, weight_refs, held)
+    sum_rows([held[:depth, :]], [profit_ref], part_ref, slice(0, depth))
+
+
+def away_kernel(slots, lines, where_ref, *refs):
+    weight_refs, (part_ref, profit_ref) = refs[:slots], refs[slots : slots + 2]
+    away_refs, (held, total) = refs[slots + 2 : -2], refs[-2:]
+    depth = arrange(slots, lines, where_ref, weight_refs, held)
+    sum_rows([held[:depth, :]], [profit_ref], total, slice(0, depth))
+    total[...] += part_ref[...]
+    cols = total.shape[1] - LANES
+    block = held.shape[0] // lines
+    half = block // CORES
+    for k in range(depth // block):
         for side, value in halves(where_ref, total, k, block):
             put_words(away_refs[side].at[k * half : (k + 1) * half, :], value[:, :cols], value[:, cols : cols + 1])
 
 
-def home_kernel(lines, where_ref, held, *refs):
-    profit_refs, (partner_refs, handled_refs, own_refs) = refs[:CORES], (refs[k : k + 2] for k in (2, 4, 6))
+def home_kernel(lines, where_ref, *refs):
+    helds, profit_refs = refs[:CORES], refs[CORES : 2 * CORES]
+    partner_refs, handled_refs, own_refs = (refs[k : k + 2] for k in range(2 * CORES, 2 * CORES + 6, 2))
     total = refs[-1]
-    rows = held.shape[1] // CORES
-    block = held.shape[0] // lines
+    block = helds[0].shape[0] // lines
     half = block // CORES
     cols = total.shape[1] - LANES
     skip = lines // 2 - 1
-    tail_part(held, profit_refs, total, slice(skip * block, lines * block), rows)
+    spot = slice(skip * block, lines * block)
+    sum_rows([held[spot, :] for held in helds], profit_refs, total, spot)
     for side, value in halves(where_ref, total, skip, block):
         put_words(partner_refs[side], value[:, :cols], value[:, cols : cols + 1])
     for k in range(skip):
@@ -463,35 +485,46 @@
         out_specs=[vmem] * len(out_shape),
         scratch_shapes=scratch,
         compiler_params=params(24),
+        cost_estimate=pl.CostEstimate(
+            flops=0, bytes_accessed=4 * sum(v.size * v.dtype.itemsize for v in inputs), transcendentals=0
+        ),
         name=name,
     )(where, *inputs)
 
 
-def tail_sums(where, weights, profit_pair, slots, lines):
+def tail_sums(where, weights, others, profit_pair, slots, lines):
     share, rows = weights[0].shape
     cols = profit_pair[0].shape[1]
     books = share * slots
     half = books // lines // CORES
-    others = (lines // 2 - 1) * half
+    away_rows = (lines // 2 - 1) * half
     wide = cols + LANES
-    total = pltpu.VMEM((books, wide), F32)
-    kept = [((books, CORES * rows), BF16)]
-    *away, held = tail_call(
+    held = ((books, rows), BF16)
+    part_shape = (away_rows * CORES, wide)
+    first, part = tail_call(
+        functools.partial(own_kernel, slots, lines),
+        "own_sums",
+        [held, (part_shape, F32)],
+        [],
+        where,
+        [*weights, profit_pair[0]],
+    )
+    *away, second = tail_call(
         functools.partial(away_kernel, slots, lines),
         "away_sums",
-        [((others, wide), jnp.int16)] * CORES + kept,
-        [total],
+        [((away_rows, wide), jnp.int16)] * CORES + [held],
+        [pltpu.VMEM(part_shape, F32)],
         where,
-        [*weights, *profit_pair],
+        [*others, part, profit_pair[1]],
     )
-    kinds = [(half, jnp.int16), (others, F32), (half, F32)]
+    kinds = [(half, jnp.int16), (away_rows, F32), (half, F32)]
     outs = tail_call(
         functools.partial(home_kernel, lines),
         "home_sums",
         [((n, wide), kind) for n, kind in kinds for _ in range(CORES)],
-        [total],
+        [pltpu.VMEM((books, wide), F32)],
         where,
-        [held, *profit_pair],
+        [first, second, *profit_pair],
     )
     return away, outs[0:2], outs[2:4], outs[4:6]
 
@@ -572,9 +605,9 @@
     far = {slot: swap(weight, "inst", slot) for slot in range(slots - 1, 0, -1)}
     far[slots - 1], here = lax.optimization_barrier((far[slots - 1], bring(got)))
     weights = [weight] + [far[slot] for slot in range(1, slots)]
-    weights = weights + [swap(w, "scen", 1) for w in weights]
-
-    away, partner, handled, plain = tail_sums(where, weights, [mine, here], slots, lines)
+    others = [swap(w, "scen", 1) for w in weights]
+
+    away, partner, handled, plain = tail_sums(where, weights, others, [mine, here], slots, lines)
     half = books // lines // CORES
     groups = []
     for side in range(CORES):

time: 84 us -> 82.8 us (0.986)
  waiting for transfers between devices: 28.2 us -> 26.8 us
    ppermute x29, waiting for transfers between devices: 28.2 us -> 26.8 us  [swap(): return lax.ppermute(value, axis, [(k, k ^ flip) for k in range(n)])]
    pallas_call x2 -> x3, Pallas kernels: 3.35 us -> 4.14 us  [tail_call(): pl.pallas_call(kernel, out_shape=[jax.ShapeDtypeStruct(shape, kind) for s...]
  transfers between devices with their start and end apart: 29 -> 29, of which waited for: 16 -> 15; matrix products, arithmetic and copies ran while one was open for 1% -> 1% of each run, Pallas kernels for 20% -> 22%
where the time goes in v6:
time: 82.8 us; the launch traced here: 82.5 us
  waiting for transfers between devices  26.8 us (32%)
  starting transfers between devices  26 us (31%)
  Pallas kernels  25.9 us (31%)
  local copies, waits for them, and re-layouts  2.83 us (3%)
  between operations  0.88 us (1%)
    ppermute x29, waiting for transfers between devices, swap(): return lax.ppermute(value, axis, [(k, k ^ flip) for k in range(n)])  26.8 us
    ppermute x29, starting transfers between devices, swap(): return lax.ppermute(value, axis, [(k, k ^ flip) for k in range(n)])  26 us
    pallas_call x1, Pallas kernels, stage(): pl.pallas_call(functools.partial(stage_kernel, slots, near, far), out_sha...  7 us
    pallas_call x1, Pallas kernels, add_moves(): pl.pallas_call(add_moves_kernel, out_shape=jax.ShapeDtypeStruct((rows, co...  5.11 us
    pallas_call x1, Pallas kernels, profits(): pl.pallas_call(functools.partial(profit_kernel, len(tops)), out_shape=out...  4.79 us
    pallas_call x3, Pallas kernels, tail_call(): pl.pallas_call(kernel, out_shape=[jax.ShapeDtypeStruct(shape, kind) for s...  4.14 us
    unnamed x16, local copies, waits for them, and re-layouts  1.79 us
    pallas_call x1, Pallas kernels, finish(): pl.pallas_call(finish_kernel, out_shape=jax.ShapeDtypeStruct((half, (wide...  1.67 us
  transfers between devices with their start and end apart: 29, of which 15 were waited for; matrix products, arithmetic and copies ran while one was open for 1% of the time, Pallas kernels for 22%

profile of v6, /device:TPU:0, one launch (start us, length us, event | category | flops | bytes accessed | tf_op | source)
XLA Modules:
  0.0 82.5 jit_solution(4876194921499449142)
XLA Ops:
  0.6 3.0 %collective-permute-start = (bf16[512,512]{1,0:T(8,128)(2,1)}, bf16[512,512]{1,0:T(8,128)(2,1)S(1)}, u32[]{:S(2)}, u32[]{:S(2)}) collective-permute-start(bf16[512,512]{1,0:T(8,128)(2,1)} %shocks_ref.1), channel_id=1, source_target_pairs={{0,1},{1,0},{2,3},{3,2},{4,5},{5,4},{6,7},{7,6},{8,9},{9,8},{10,11... | collective-permute-start | bytes 1572872 | tf_op jit(solution)/shard_map/ppermute | solution.py:39
  3.6 1.5 %collective-permute-start.2 = (bf16[512,512]{1,0:T(8,128)(2,1)}, bf16[512,512]{1,0:T(8,128)(2,1)S(1)}, u32[]{:S(2)}, u32[]{:S(2)}) collective-permute-start(bf16[512,512]{1,0:T(8,128)(2,1)} %shocks_ref.1), channel_id=1, source_target_pairs={{0,2},{1,3},{2,0},{3,1},{4,6},{5,7},{6,4},{7,5},{8,10},{9,11},{10,... | collective-permute-start | bytes 1572872 | tf_op jit(solution)/shard_map/ppermute | solution.py:39
  5.2 1.0 %copy-done = bf16[512,512]{1,0:T(8,128)(2,1)S(1)} copy-done((bf16[512,512]{1,0:T(8,128)(2,1)S(1)}, bf16[512,512]{1,0:T(8,128)(2,1)}, u32[]{:S(2)}) %copy-start) | copy-done | bytes 524312
  7.0 7.0 %stage.1 = (f32[512,4096]{1,0:T(8,128)S(1)}, bf16[1024,4096]{1,0:T(8,128)(2,1)S(1)}, bf16[512,4096]{1,0:T(8,128)(2,1)S(1)}, bf16[4096,256]{1,0:T(8,128)(2,1)S(1)}) custom-call(s32[3]{0:T(128)S(1)} %pad_add_fusion.where_ref, bf16[512,512]{1,0:T(8,128)(2,1)S(1)} %copy-done, s32[1,4096]{1,0:T(1,128)S(1)} %bitcast.9, bf16[2048,4096]{1,0:T(8,128)(2,1)} %loadings_ref.1), custom_call_target="tpu_custom_call" | custom-call | flops 2147483648 | bytes 16777216 | tf_op jit(solution)/shard_map/stage/pallas_call | solution.py:85
  14.0 1.8 %collective-permute-done.refs_0_ = bf16[512,512]{1,0:T(8,128)(2,1)S(1)} collective-permute-done((bf16[512,512]{1,0:T(8,128)(2,1)}, bf16[512,512]{1,0:T(8,128)(2,1)S(1)}, u32[]{:S(2)}, u32[]{:S(2)}) %collective-permute-start) | collective-permute-done | bytes 524320 | tf_op jit(solution)/shard_map/ppermute | solution.py:39
  15.8 1.8 %collective-permute-start.1 = (bf16[288,512]{1,0:T(8,128)(2,1)S(1)}, bf16[288,512]{1,0:T(8,128)(2,1)S(1)}, u32[]{:S(2)}, u32[]{:S(2)}) collective-permute-start(bf16[288,512]{1,0:T(8,128)(2,1)S(1)} %slice.12), channel_id=1, source_target_pairs={{0,2},{1,3},{2,0},{3,1},{4,6},{5,7},{6,4},{7,5},{8,10},{9,11},{10,... | collective-permute-start | bytes 884744 | tf_op jit(solution)/shard_map/ppermute | solution.py:39
  17.6 1.6 %collective-permute-start.3 = (bf16[224,512]{1,0:T(8,128)(2,1)S(1)}, bf16[224,512]{1,0:T(8,128)(2,1)S(1)}, u32[]{:S(2)}, u32[]{:S(2)}) collective-permute-start(bf16[224,512]{1,0:T(8,128)(2,1)S(1)} %slice.13), channel_id=1, source_target_pairs={{0,1},{1,0},{2,3},{3,2},{4,5},{5,4},{6,7},{7,6},{8,9},{9,8},{10,11... | collective-permute-start | bytes 688136 | tf_op jit(solution)/shard_map/ppermute | solution.py:39
  19.2 5.1 %add_moves.1.refs_3_ = f32[512,4096]{1,0:T(8,128)S(1)} custom-call(bf16[512,512]{1,0:T(8,128)(2,1)S(1)} %collective-permute-done.refs_0_, bf16[512,512]{1,0:T(8,128)(2,1)S(1)} %collective-permute-done.2.refs_1_, bf16[1024,4096]{1,0:T(8,128)(2,1)S(1)} %get-tuple-element.30.refs_2_, ...), custom_call_target="tpu_custom_call", output_to_operand_aliasing={{}: (3, {})} | custom-call | flops 4294967296 | bytes 16777216 | tf_op jit(solution)/shard_map/add_moves/pallas_call | solution.py:119
  24.4 4.8 %profits.1 = (bf16[512,2048]{1,0:T(8,128)(2,1)S(1)}, bf16[512,2048]{1,0:T(8,128)(2,1)}, f32[64,512]{1,0:T(8,128)S(1)}, f32[64,512]{1,0:T(8,128)S(1)}, f32[64,512]{1,0:T(8,128)S(1)}, /*index=5*/f32[64,512]{1,0:T(8,128)S(1)}) custom-call(s32[3]{0:T(128)S(1)} %pad_add_fusion.where_ref, bf16[288,512]{1,0:T(8,128)(2,1)S(1)} %collective-permute-done.1.refs_0_, ...), custom_call_target="tpu_custom_call" | custom-call | flops 3221225472 | bytes 12582912 | tf_op jit(solution)/shard_map/profits/pallas_call | solution.py:178
  29.3 2.1 %collective-permute-start.4 = (f32[64,512]{1,0:T(8,128)S(1)}, f32[64,512]{1,0:T(8,128)S(1)}, u32[]{:S(2)}, u32[]{:S(2)}) collective-permute-start(f32[64,512]{1,0:T(8,128)S(1)} %get-tuple-element.34), channel_id=1, source_target_pairs={{0,3},{1,2},{2,1},{3,0},{4,7},{5,6},{6,5},{7,4},{8,11},{9,10},{10,... | collective-permute-start | bytes 393224 | tf_op jit(solution)/shard_map/ppermute | solution.py:39
  32.9 3.7 %collective-permute-done.4.refs_1_ = f32[64,512]{1,0:T(8,128)S(1)} collective-permute-done((f32[64,512]{1,0:T(8,128)S(1)}, f32[64,512]{1,0:T(8,128)S(1)}, u32[]{:S(2)}, u32[]{:S(2)}) %collective-permute-start.4) | collective-permute-done | bytes 131104 | tf_op jit(solution)/shard_map/ppermute | solution.py:39
  36.6 2.4 %collective-permute-done.5.refs_2_ = f32[64,512]{1,0:T(8,128)S(1)} collective-permute-done((f32[64,512]{1,0:T(8,128)S(1)}, f32[64,512]{1,0:T(8,128)S(1)}, u32[]{:S(2)}, u32[]{:S(2)}) %collective-permute-start.5) | collective-permute-done | bytes 131104 | tf_op jit(solution)/shard_map/ppermute | solution.py:39
  39.4 1.6 %collective-permute-start.7 = (f32[32,128]{1,0:T(8,128)S(1)}, f32[32,128]{1,0:T(8,128)S(1)}, u32[]{:S(2)}, u32[]{:S(2)}) collective-permute-start(f32[32,128]{1,0:T(8,128)S(1)} %get-tuple-element.38.refs_0_), channel_id=1, source_target_pairs={{0,8},{4,12},{8,0},{12,4},{16,24},{20,28},{24,16},{28,20},{1,9},{5... | collective-permute-start | bytes 49160 | tf_op jit(solution)/shard_map/ppermute | solution.py:39
  41.1 2.5 %collective-permute-start.8 = (f32[32,128]{1,0:T(8,128)S(1)}, f32[32,128]{1,0:T(8,128)S(1)}, u32[]{:S(2)}, u32[]{:S(2)}) collective-permute-start(f32[32,128]{1,0:T(8,128)S(1)} %get-tuple-element.38.refs_0_), channel_id=1, source_target_pairs={{0,24},{4,28},{8,16},{12,20},{16,8},{20,12},{24,0},{28,4},{1,25},{... | collective-permute-start | bytes 49160 | tf_op jit(solution)/shard_map/ppermute | solution.py:39
  44.2 2.4 %collective-permute-done.8.refs_2_ = f32[32,128]{1,0:T(8,128)S(1)} collective-permute-done((f32[32,128]{1,0:T(8,128)S(1)}, f32[32,128]{1,0:T(8,128)S(1)}, u32[]{:S(2)}, u32[]{:S(2)}) %collective-permute-start.8) | collective-permute-done | bytes 16416 | tf_op jit(solution)/shard_map/ppermute | solution.py:39
  46.6 1.6 %collective-permute-done.9.refs_3_ = f32[32,128]{1,0:T(8,128)S(1)} collective-permute-done((f32[32,128]{1,0:T(8,128)S(1)}, f32[32,128]{1,0:T(8,128)S(1)}, u32[]{:S(2)}, u32[]{:S(2)}) %collective-permute-start.9) | collective-permute-done | bytes 16416 | tf_op jit(solution)/shard_map/ppermute | solution.py:39
  50.0 1.3 %collective-permute-start.14 = (bf16[64,512]{1,0:T(8,128)(2,1)S(1)}, bf16[64,512]{1,0:T(8,128)(2,1)S(1)}, u32[]{:S(2)}, u32[]{:S(2)}) collective-permute-start(bf16[64,512]{1,0:T(8,128)(2,1)S(1)} %get-tuple-element.39.refs_0_), channel_id=1, source_target_pairs={{0,1},{1,0},{2,3},{3,2},{4,5},{5,4},{6,7},{7,6},{8,9},{9,8},{10,11... | collective-permute-start | bytes 196616 | tf_op jit(solution)/shard_map/ppermute | solution.py:39
  51.3 1.1 %collective-permute-start.15 = (bf16[64,512]{1,0:T(8,128)(2,1)S(1)}, bf16[64,512]{1,0:T(8,128)(2,1)S(1)}, u32[]{:S(2)}, u32[]{:S(2)}) collective-permute-start(bf16[64,512]{1,0:T(8,128)(2,1)S(1)} %get-tuple-element.39.refs_0_), channel_id=1, source_target_pairs={{0,2},{1,3},{2,0},{3,1},{4,6},{5,7},{6,4},{7,5},{8,10},{9,11},{10,... | collective-permute-start | bytes 196616 | tf_op jit(solution)/shard_map/ppermute | solution.py:39
  52.4 1.2 %collective-permute-start.16 = (bf16[64,512]{1,0:T(8,128)(2,1)S(1)}, bf16[64,512]{1,0:T(8,128)(2,1)S(1)}, u32[]{:S(2)}, u32[]{:S(2)}) collective-permute-start(bf16[64,512]{1,0:T(8,128)(2,1)S(1)} %get-tuple-element.39.refs_0_), channel_id=1, source_target_pairs={{0,3},{1,2},{2,1},{3,0},{4,7},{5,6},{6,5},{7,4},{8,11},{9,10},{10,... | collective-permute-start | bytes 196616 | tf_op jit(solution)/shard_map/ppermute | solution.py:39
  54.3 1.2 %collective-permute-done.15.refs_2_ = bf16[64,512]{1,0:T(8,128)(2,1)S(1)} collective-permute-done((bf16[64,512]{1,0:T(8,128)(2,1)S(1)}, bf16[64,512]{1,0:T(8,128)(2,1)S(1)}, u32[]{:S(2)}, u32[]{:S(2)}) %collective-permute-start.15) | collective-permute-done | bytes 65568 | tf_op jit(solution)/shard_map/ppermute | solution.py:39
  55.5 1.6 %bring.1.refs_5_.refs_3_ = bf16[512,2048]{1,0:T(8,128)(2,1)S(1)} custom-call(bf16[512,2048]{1,0:T(8,128)(2,1)} %collective-permute-done.17.far_ref), custom_call_target="tpu_custom_call" | custom-call | bytes 8388608 | tf_op jit(solution)/shard_map/bring/pallas_call | solution.py:467
  57.7 1.2 %own_sums.1 = (bf16[256,512]{1,0:T(8,128)(2,1)S(1)}, f32[64,2176]{1,0:T(8,128)S(1)}) custom-call(s32[3]{0:T(128)S(1)} %pad_add_fusion.where_ref, bf16[64,512]{1,0:T(8,128)(2,1)S(1)} %get-tuple-element.39.refs_0_, bf16[64,512]{1,0:T(8,128)(2,1)S(1)} %collective-permute-done.14.refs_1_, bf16[64,512]{1,0:T(8,128)(2,1)S(1)} %collective-permute-done.15.refs_2_, ...), custom_call_target="tpu_custom_call" | custom-call | bytes 9437184 | tf_op jit(solution)/shard_map/own_sums/pallas_call | solution.py:481
  59.0 1.2 %away_sums.1 = (s16[32,2176]{1,0:T(8,128)(2,1)S(1)}, s16[32,2176]{1,0:T(8,128)(2,1)S(1)}, bf16[256,512]{1,0:T(8,128)(2,1)S(1)}) custom-call(s32[3]{0:T(128)S(1)} %pad_add_fusion.where_ref, bf16[64,512]{1,0:T(8,128)(2,1)S(1)} %collective-permute-done.18.refs_0_, bf16[64,512]{1,0:T(8,128)(2,1)S(1)} %collective-permute-done.19.refs_1_, ...), custom_call_target="tpu_custom_call" | custom-call | bytes 11665408 | tf_op jit(solution)/shard_map/away_sums/pallas_call | solution.py:481
  61.0 1.3 %collective-permute-start.23 = (s16[32,2176]{1,0:T(8,128)(2,1)S(1)}, s16[32,2176]{1,0:T(8,128)(2,1)S(1)}, u32[]{:S(2)}, u32[]{:S(2)}) collective-permute-start(s16[32,2176]{1,0:T(8,128)(2,1)S(1)} %get-tuple-element.49), channel_id=1, source_target_pairs={{0,8},{4,12},{8,0},{12,4},{16,24},{20,28},{24,16},{28,20},{1,9},{5... | collective-permute-start | bytes 417800 | tf_op jit(solution)/shard_map/ppermute | solution.py:39
  62.3 1.7 %home_sums.1 = (s16[32,2176]{1,0:T(8,128)(2,1)S(1)}, s16[32,2176]{1,0:T(8,128)(2,1)S(1)}, f32[32,2176]{1,0:T(8,128)S(1)}, f32[32,2176]{1,0:T(8,128)S(1)}, f32[32...) custom-call(s32[3]{0:T(128)S(1)} %pad_add_fusion.where_ref, bf16[256,512]{1,0:T(8,128)(2,1)S(1)} %get-tuple-element.43.refs_0_, ...), custom_call_target="tpu_custom_call" | custom-call | bytes 18874368 | tf_op jit(solution)/shard_map/home_sums/pallas_call | solution.py:481
  64.9 1.1 %collective-permute-start.26 = (s16[32,2176]{1,0:T(8,128)(2,1)S(1)}, s16[32,2176]{1,0:T(8,128)(2,1)S(1)}, u32[]{:S(2)}, u32[]{:S(2)}) collective-permute-start(s16[32,2176]{1,0:T(8,128)(2,1)S(1)} %get-tuple-element.52), channel_id=1, source_target_pairs={{0,12},{4,8},{8,4},{12,0},{16,28},{20,24},{24,20},{28,16},{1,13},{... | collective-permute-start | bytes 417800 | tf_op jit(solution)/shard_map/ppermute | solution.py:39
  67.6 2.2 %collective-permute-done.23.words_ref = s16[32,2176]{1,0:T(8,128)(2,1)S(1)} collective-permute-done((s16[32,2176]{1,0:T(8,128)(2,1)S(1)}, s16[32,2176]{1,0:T(8,128)(2,1)S(1)}, u32[]{:S(2)}, u32[]{:S(2)}) %collective-permute-start.23) | collective-permute-done | bytes 139296 | tf_op jit(solution)/shard_map/ppermute | solution.py:39
  70.0 1.4 %collective-permute-start.24 = (s16[32,2176]{1,0:T(8,128)(2,1)S(1)}, s16[32,2176]{1,0:T(8,128)(2,1)S(1)}, u32[]{:S(2)}, u32[]{:S(2)}) collective-permute-start(s16[32,2176]{1,0:T(8,128)(2,1)S(1)} %relay.2), channel_id=1, source_target_pairs={{0,24},{4,28},{8,16},{12,20},{16,8},{20,12},{24,0},{28,4},{1,25},{... | collective-permute-start | bytes 417800 | tf_op jit(solution)/shard_map/ppermute | solution.py:39
  72.7 2.2 %collective-permute-done.26.refs_4_ = s16[32,2176]{1,0:T(8,128)(2,1)S(1)} collective-permute-done((s16[32,2176]{1,0:T(8,128)(2,1)S(1)}, s16[32,2176]{1,0:T(8,128)(2,1)S(1)}, u32[]{:S(2)}, u32[]{:S(2)}) %collective-permute-start.26) | collective-permute-done | bytes 139296 | tf_op jit(solution)/shard_map/ppermute | solution.py:39
  74.9 2.3 %collective-permute-done.28.refs_5_ = s16[32,2176]{1,0:T(8,128)(2,1)S(1)} collective-permute-done((s16[32,2176]{1,0:T(8,128)(2,1)S(1)}, s16[32,2176]{1,0:T(8,128)(2,1)S(1)}, u32[]{:S(2)}, u32[]{:S(2)}) %collective-permute-start.28) | collective-permute-done | bytes 139296 | tf_op jit(solution)/shard_map/ppermute | solution.py:39
  77.3 3.6 %collective-permute-done.24.refs_2_ = s16[32,2176]{1,0:T(8,128)(2,1)S(1)} collective-permute-done((s16[32,2176]{1,0:T(8,128)(2,1)S(1)}, s16[32,2176]{1,0:T(8,128)(2,1)S(1)}, u32[]{:S(2)}, u32[]{:S(2)}) %collective-permute-start.24) | collective-permute-done | bytes 139296 | tf_op jit(solution)/shard_map/ppermute | solution.py:39
  80.9 1.7 %finish.1 = f32[32,4096]{1,0:T(8,128)} custom-call(s32[3]{0:T(128)S(1)} %pad_add_fusion.where_ref, f32[32,2176]{1,0:T(8,128)S(1)} %get-tuple-element.47.refs_0_, s16[32,2176]{1,0:T(8,128)(2,1)S(1)} %collective-permute-done.22.refs_1_, s16[32,2176]{1,0:T(8,128)(2,1)S(1)} %collective-permute-done.24.refs_2_, f32[32,2176]{1,0:T(8,128)S(1)} %collective-permute-done.25.refs_3_, ...), custom_call_target="tpu_custom_call" | custom-call | tf_op jit(solution)/shard_map/finish/pallas_call | solution.py:563
  (67 shorter events, 11.5 us)
Async XLA Ops:
  0.6 15.1 %collective-permute-start = (bf16[512,512]{1,0:T(8,128)(2,1)}, bf16[512,512]{1,0:T(8,128)(2,1)S(1)}, u32[]{:S(2)}, u32[]{:S(2)}) collective-permute-start(bf16[512,512]{1,0:T(8,128)(2,1)} %shocks_ref.1), channel_id=1, source_target_pairs={{0,1},{1,0},{2,3},{3,2},{4,5},{5,4},{6,7},{7,6},{8,9},{9,8},{10,11... | collective-permute-start | bytes 1572872 | tf_op jit(solution)/shard_map/ppermute | solution.py:39
  3.6 14.0 %collective-permute-start.2 = (bf16[512,512]{1,0:T(8,128)(2,1)}, bf16[512,512]{1,0:T(8,128)(2,1)S(1)}, u32[]{:S(2)}, u32[]{:S(2)}) collective-permute-start(bf16[512,512]{1,0:T(8,128)(2,1)} %shocks_ref.1), channel_id=1, source_target_pairs={{0,2},{1,3},{2,0},{3,1},{4,6},{5,7},{6,4},{7,5},{8,10},{9,11},{10,... | collective-permute-start | bytes 1572872 | tf_op jit(solution)/shard_map/ppermute | solution.py:39
  15.8 8.6 %collective-permute-start.1 = (bf16[288,512]{1,0:T(8,128)(2,1)S(1)}, bf16[288,512]{1,0:T(8,128)(2,1)S(1)}, u32[]{:S(2)}, u32[]{:S(2)}) collective-permute-start(bf16[288,512]{1,0:T(8,128)(2,1)S(1)} %slice.12), channel_id=1, source_target_pairs={{0,2},{1,3},{2,0},{3,1},{4,6},{5,7},{6,4},{7,5},{8,10},{9,11},{10,... | collective-permute-start | bytes 884744 | tf_op jit(solution)/shard_map/ppermute | solution.py:39
  17.6 6.7 %collective-permute-start.3 = (bf16[224,512]{1,0:T(8,128)(2,1)S(1)}, bf16[224,512]{1,0:T(8,128)(2,1)S(1)}, u32[]{:S(2)}, u32[]{:S(2)}) collective-permute-start(bf16[224,512]{1,0:T(8,128)(2,1)S(1)} %slice.13), channel_id=1, source_target_pairs={{0,1},{1,0},{2,3},{3,2},{4,5},{5,4},{6,7},{7,6},{8,9},{9,8},{10,11... | collective-permute-start | bytes 688136 | tf_op jit(solution)/shard_map/ppermute | solution.py:39
  24.4 23.8 %copy-start.5 = (s32[256]{0:T(256)S(1)}, s32[256]{0:T(256)}, u32[]{:S(2)}) copy-start(s32[256]{0:T(256)} %param.16) | copy-start | bytes 3076
  24.4 24.0 %copy-start.6 = (s32[256]{0:T(256)S(1)}, s32[256]{0:T(256)}, u32[]{:S(2)}) copy-start(s32[256]{0:T(256)} %param.17) | copy-start | bytes 3076
  24.4 24.1 %copy-start.7 = (s32[256]{0:T(256)S(1)}, s32[256]{0:T(256)}, u32[]{:S(2)}) copy-start(s32[256]{0:T(256)} %param.15) | copy-start | bytes 3076
  29.2 26.3 %collective-permute-start.17 = (bf16[512,2048]{1,0:T(8,128)(2,1)}, bf16[512,2048]{1,0:T(8,128)(2,1)}, u32[]{:S(2)}, u32[]{:S(2)}) collective-permute-start(bf16[512,2048]{1,0:T(8,128)(2,1)} %get-tuple-element.40), channel_id=1, source_target_pairs={{0,4},{4,0},{8,12},{12,8},{16,20},{20,16},{24,28},{28,24},{1,5},{5... | collective-permute-start | bytes 6291464 | tf_op jit(solution)/shard_map/ppermute | solution.py:39
  29.3 7.3 %collective-permute-start.4 = (f32[64,512]{1,0:T(8,128)S(1)}, f32[64,512]{1,0:T(8,128)S(1)}, u32[]{:S(2)}, u32[]{:S(2)}) collective-permute-start(f32[64,512]{1,0:T(8,128)S(1)} %get-tuple-element.34), channel_id=1, source_target_pairs={{0,3},{1,2},{2,1},{3,0},{4,7},{5,6},{6,5},{7,4},{8,11},{9,10},{10,... | collective-permute-start | bytes 393224 | tf_op jit(solution)/shard_map/ppermute | solution.py:39
  31.4 7.5 %collective-permute-start.5 = (f32[64,512]{1,0:T(8,128)S(1)}, f32[64,512]{1,0:T(8,128)S(1)}, u32[]{:S(2)}, u32[]{:S(2)}) collective-permute-start(f32[64,512]{1,0:T(8,128)S(1)} %get-tuple-element.35), channel_id=1, source_target_pairs={{0,2},{1,3},{2,0},{3,1},{4,6},{5,7},{6,4},{7,5},{8,10},{9,11},{10,... | collective-permute-start | bytes 393224 | tf_op jit(solution)/shard_map/ppermute | solution.py:39
  31.9 7.0 %collective-permute-start.6 = (f32[64,512]{1,0:T(8,128)S(1)}, f32[64,512]{1,0:T(8,128)S(1)}, u32[]{:S(2)}, u32[]{:S(2)}) collective-permute-start(f32[64,512]{1,0:T(8,128)S(1)} %get-tuple-element.36), channel_id=1, source_target_pairs={{0,1},{1,0},{2,3},{3,2},{4,5},{5,4},{6,7},{7,6},{8,9},{9,8},{10,11... | collective-permute-start | bytes 393224 | tf_op jit(solution)/shard_map/ppermute | solution.py:39
  39.4 4.2 %collective-permute-start.7 = (f32[32,128]{1,0:T(8,128)S(1)}, f32[32,128]{1,0:T(8,128)S(1)}, u32[]{:S(2)}, u32[]{:S(2)}) collective-permute-start(f32[32,128]{1,0:T(8,128)S(1)} %get-tuple-element.38.refs_0_), channel_id=1, source_target_pairs={{0,8},{4,12},{8,0},{12,4},{16,24},{20,28},{24,16},{28,20},{1,9},{5... | collective-permute-start | bytes 49160 | tf_op jit(solution)/shard_map/ppermute | solution.py:39
  41.1 5.5 %collective-permute-start.8 = (f32[32,128]{1,0:T(8,128)S(1)}, f32[32,128]{1,0:T(8,128)S(1)}, u32[]{:S(2)}, u32[]{:S(2)}) collective-permute-start(f32[32,128]{1,0:T(8,128)S(1)} %get-tuple-element.38.refs_0_), channel_id=1, source_target_pairs={{0,24},{4,28},{8,16},{12,20},{16,8},{20,12},{24,0},{28,4},{1,25},{... | collective-permute-start | bytes 49160 | tf_op jit(solution)/shard_map/ppermute | solution.py:39
  43.6 4.6 %collective-permute-start.9 = (f32[32,128]{1,0:T(8,128)S(1)}, f32[32,128]{1,0:T(8,128)S(1)}, u32[]{:S(2)}, u32[]{:S(2)}) collective-permute-start(f32[32,128]{1,0:T(8,128)S(1)} %get-tuple-element.38.refs_0_), channel_id=1, source_target_pairs={{0,16},{4,20},{8,24},{12,28},{16,0},{20,4},{24,8},{28,12},{1,17},{... | collective-permute-start | bytes 49160 | tf_op jit(solution)/shard_map/ppermute | solution.py:39
  43.7 5.1 %collective-permute-start.10 = (f32[32,128]{1,0:T(8,128)S(1)}, f32[32,128]{1,0:T(8,128)S(1)}, u32[]{:S(2)}, u32[]{:S(2)}) collective-permute-start(f32[32,128]{1,0:T(8,128)S(1)} %get-tuple-element.38.refs_0_), channel_id=1, source_target_pairs={{0,4},{4,0},{8,12},{12,8},{16,20},{20,16},{24,28},{28,24},{1,5},{5... | collective-permute-start | bytes 49160 | tf_op jit(solution)/shard_map/ppermute | solution.py:39
  43.7 5.1 %collective-permute-start.11 = (f32[32,128]{1,0:T(8,128)S(1)}, f32[32,128]{1,0:T(8,128)S(1)}, u32[]{:S(2)}, u32[]{:S(2)}) collective-permute-start(f32[32,128]{1,0:T(8,128)S(1)} %collective-permute-done.7.refs_1_), channel_id=1, source_target_pairs={{0,4},{4,0},{8,12},{12,8},{16,20},{20,16},{24,28},{28,24},{1,5},{5... | collective-permute-start | bytes 49160 | tf_op jit(solution)/shard_map/ppermute | solution.py:39
  46.6 2.1 %collective-permute-start.12 = (f32[32,128]{1,0:T(8,128)S(1)}, f32[32,128]{1,0:T(8,128)S(1)}, u32[]{:S(2)}, u32[]{:S(2)}) collective-permute-start(f32[32,128]{1,0:T(8,128)S(1)} %collective-permute-done.8.refs_2_), channel_id=1, source_target_pairs={{0,4},{4,0},{8,12},{12,8},{16,20},{20,16},{24,28},{28,24},{1,5},{5... | collective-permute-start | bytes 49160 | tf_op jit(solution)/shard_map/ppermute | solution.py:39
  48.2 1.2 %collective-permute-start.13 = (f32[32,128]{1,0:T(8,128)S(1)}, f32[32,128]{1,0:T(8,128)S(1)}, u32[]{:S(2)}, u32[]{:S(2)}) collective-permute-start(f32[32,128]{1,0:T(8,128)S(1)} %collective-permute-done.9.refs_3_), channel_id=1, source_target_pairs={{0,4},{4,0},{8,12},{12,8},{16,20},{20,16},{24,28},{28,24},{1,5},{5... | collective-permute-start | bytes 49160 | tf_op jit(solution)/shard_map/ppermute | solution.py:39
  50.0 4.3 %collective-permute-start.14 = (bf16[64,512]{1,0:T(8,128)(2,1)S(1)}, bf16[64,512]{1,0:T(8,128)(2,1)S(1)}, u32[]{:S(2)}, u32[]{:S(2)}) collective-permute-start(bf16[64,512]{1,0:T(8,128)(2,1)S(1)} %get-tuple-element.39.refs_0_), channel_id=1, source_target_pairs={{0,1},{1,0},{2,3},{3,2},{4,5},{5,4},{6,7},{7,6},{8,9},{9,8},{10,11... | collective-permute-start | bytes 196616 | tf_op jit(solution)/shard_map/ppermute | solution.py:39
  51.3 4.3 %collective-permute-start.15 = (bf16[64,512]{1,0:T(8,128)(2,1)S(1)}, bf16[64,512]{1,0:T(8,128)(2,1)S(1)}, u32[]{:S(2)}, u32[]{:S(2)}) collective-permute-start(bf16[64,512]{1,0:T(8,128)(2,1)S(1)} %get-tuple-element.39.refs_0_), channel_id=1, source_target_pairs={{0,2},{1,3},{2,0},{3,1},{4,6},{5,7},{6,4},{7,5},{8,10},{9,11},{10,... | collective-permute-start | bytes 196616 | tf_op jit(solution)/shard_map/ppermute | solution.py:39
  52.4 5.2 %collective-permute-start.16 = (bf16[64,512]{1,0:T(8,128)(2,1)S(1)}, bf16[64,512]{1,0:T(8,128)(2,1)S(1)}, u32[]{:S(2)}, u32[]{:S(2)}) collective-permute-start(bf16[64,512]{1,0:T(8,128)(2,1)S(1)} %get-tuple-element.39.refs_0_), channel_id=1, source_target_pairs={{0,3},{1,2},{2,1},{3,0},{4,7},{5,6},{6,5},{7,4},{8,11},{9,10},{10,... | collective-permute-start | bytes 196616 | tf_op jit(solution)/shard_map/ppermute | solution.py:39
  53.6 5.4 %collective-permute-start.18 = (bf16[64,512]{1,0:T(8,128)(2,1)S(1)}, bf16[64,512]{1,0:T(8,128)(2,1)S(1)}, u32[]{:S(2)}, u32[]{:S(2)}) collective-permute-start(bf16[64,512]{1,0:T(8,128)(2,1)S(1)} %get-tuple-element.39.refs_0_), channel_id=1, source_target_pairs={{0,4},{4,0},{8,12},{12,8},{16,20},{20,16},{24,28},{28,24},{1,5},{5... | collective-permute-start | bytes 196616 | tf_op jit(solution)/shard_map/ppermute | solution.py:39
  54.3 4.6 %collective-permute-start.19 = (bf16[64,512]{1,0:T(8,128)(2,1)S(1)}, bf16[64,512]{1,0:T(8,128)(2,1)S(1)}, u32[]{:S(2)}, u32[]{:S(2)}) collective-permute-start(bf16[64,512]{1,0:T(8,128)(2,1)S(1)} %collective-permute-done.14.refs_1_), channel_id=1, source_target_pairs={{0,4},{4,0},{8,12},{12,8},{16,20},{20,16},{24,28},{28,24},{1,5},{5... | collective-permute-start | bytes 196616 | tf_op jit(solution)/shard_map/ppermute | solution.py:39
  55.5 3.4 %collective-permute-start.20 = (bf16[64,512]{1,0:T(8,128)(2,1)S(1)}, bf16[64,512]{1,0:T(8,128)(2,1)S(1)}, u32[]{:S(2)}, u32[]{:S(2)}) collective-permute-start(bf16[64,512]{1,0:T(8,128)(2,1)S(1)} %collective-permute-done.15.refs_2_), channel_id=1, source_target_pairs={{0,4},{4,0},{8,12},{12,8},{16,20},{20,16},{24,28},{28,24},{1,5},{5... | collective-permute-start | bytes 196616 | tf_op jit(solution)/shard_map/ppermute | solution.py:39
  57.5 1.4 %collective-permute-start.21 = (bf16[64,512]{1,0:T(8,128)(2,1)S(1)}, bf16[64,512]{1,0:T(8,128)(2,1)S(1)}, u32[]{:S(2)}, u32[]{:S(2)}) collective-permute-start(bf16[64,512]{1,0:T(8,128)(2,1)S(1)} %collective-permute-done.16.refs_3_), channel_id=1, source_target_pairs={{0,4},{4,0},{8,12},{12,8},{16,20},{20,16},{24,28},{28,24},{1,5},{5... | collective-permute-start | bytes 196616 | tf_op jit(solution)/shard_map/ppermute | solution.py:39
  60.2 6.6 %collective-permute-start.27 = (s16[32,2176]{1,0:T(8,128)(2,1)S(1)}, s16[32,2176]{1,0:T(8,128)(2,1)S(1)}, u32[]{:S(2)}, u32[]{:S(2)}) collective-permute-start(s16[32,2176]{1,0:T(8,128)(2,1)S(1)} %get-tuple-element.53), channel_id=1, source_target_pairs={{0,8},{4,12},{8,0},{12,4},{16,24},{20,28},{24,16},{28,20},{1,9},{5... | collective-permute-start | bytes 417800 | tf_op jit(solution)/shard_map/ppermute | solution.py:39
  61.0 8.7 %collective-permute-start.23 = (s16[32,2176]{1,0:T(8,128)(2,1)S(1)}, s16[32,2176]{1,0:T(8,128)(2,1)S(1)}, u32[]{:S(2)}, u32[]{:S(2)}) collective-permute-start(s16[32,2176]{1,0:T(8,128)(2,1)S(1)} %get-tuple-element.49), channel_id=1, source_target_pairs={{0,8},{4,12},{8,0},{12,4},{16,24},{20,28},{24,16},{28,20},{1,9},{5... | collective-permute-start | bytes 417800 | tf_op jit(solution)/shard_map/ppermute | solution.py:39
  64.0 16.8 %collective-permute-start.25 = (f32[32,2176]{1,0:T(8,128)S(1)}, f32[32,2176]{1,0:T(8,128)S(1)}, u32[]{:S(2)}, u32[]{:S(2)}) collective-permute-start(f32[32,2176]{1,0:T(8,128)S(1)} %get-tuple-element.51), channel_id=1, source_target_pairs={{0,4},{4,0},{8,12},{12,8},{16,20},{20,16},{24,28},{28,24},{1,5},{5... | collective-permute-start | bytes 835592 | tf_op jit(solution)/shard_map/ppermute | solution.py:39
  64.1 8.6 %collective-permute-start.22 = (s16[32,2176]{1,0:T(8,128)(2,1)S(1)}, s16[32,2176]{1,0:T(8,128)(2,1)S(1)}, u32[]{:S(2)}, u32[]{:S(2)}) collective-permute-start(s16[32,2176]{1,0:T(8,128)(2,1)S(1)} %get-tuple-element.48), channel_id=1, source_target_pairs={{0,8},{4,12},{8,0},{12,4},{16,24},{20,28},{24,16},{28,20},{1,9},{5... | collective-permute-start | bytes 417800 | tf_op jit(solution)/shard_map/ppermute | solution.py:39
  64.9 10.0 %collective-permute-start.26 = (s16[32,2176]{1,0:T(8,128)(2,1)S(1)}, s16[32,2176]{1,0:T(8,128)(2,1)S(1)}, u32[]{:S(2)}, u32[]{:S(2)}) collective-permute-start(s16[32,2176]{1,0:T(8,128)(2,1)S(1)} %get-tuple-element.52), channel_id=1, source_target_pairs={{0,12},{4,8},{8,4},{12,0},{16,28},{20,24},{24,20},{28,16},{1,13},{... | collective-permute-start | bytes 417800 | tf_op jit(solution)/shard_map/ppermute | solution.py:39
  67.0 10.2 %collective-permute-start.28 = (s16[32,2176]{1,0:T(8,128)(2,1)S(1)}, s16[32,2176]{1,0:T(8,128)(2,1)S(1)}, u32[]{:S(2)}, u32[]{:S(2)}) collective-permute-start(s16[32,2176]{1,0:T(8,128)(2,1)S(1)} %relay.3), channel_id=1, source_target_pairs={{0,28},{4,24},{8,20},{12,16},{16,12},{20,8},{24,4},{28,0},{1,29},{... | collective-permute-start | bytes 417800 | tf_op jit(solution)/shard_map/ppermute | solution.py:39
  70.0 10.9 %collective-permute-start.24 = (s16[32,2176]{1,0:T(8,128)(2,1)S(1)}, s16[32,2176]{1,0:T(8,128)(2,1)S(1)}, u32[]{:S(2)}, u32[]{:S(2)}) collective-permute-start(s16[32,2176]{1,0:T(8,128)(2,1)S(1)} %relay.2), channel_id=1, source_target_pairs={{0,24},{4,28},{8,16},{12,20},{16,8},{20,12},{24,0},{28,4},{1,25},{... | collective-permute-start | bytes 417800 | tf_op jit(solution)/shard_map/ppermute | solution.py:39
  (5 other events, 17.2 us)

commit v7 on v6

--- a/solution.py
+++ b/solution.py
@@ -592,13 +592,14 @@
         book_of[None, :],
         books,
     )
-    got = swap(theirs, "scen", 1)
 
     most = shocks.shape[0] * lax.axis_size("scen") // RANK_PART
     own = lambda v: jnp.tile(lax.dynamic_slice_in_dim(v, inst * share, share, 0), LANES // share)[None, :]
     low, high, own_rank = own(bracket_low), own(bracket_high), own(rank)
     parts = [sums[0]] + [swap(sums[slot], "inst", slot) for slot in range(slots - 1, 0, -1)]
     value, lows = book_values(scale, most, parts)
+    lows, theirs = lax.optimization_barrier((lows, theirs))
+    got = swap(theirs, "scen", 1)
     lists = [lows] + [swap(lows, "scen", CORES * k) for k in [*range(1, lines, 2), *range(2, lines, 2)]]
     lists = lists + [swap(v, "scen", 1) for v in lists]
     weight, row = quantiles(most, low, high, own_rank, value, lists)

time: 82.8 us -> 80.8 us (0.976)
  waiting for transfers between devices: 26.8 us -> 25 us
    ppermute x29, waiting for transfers between devices: 26.8 us -> 25 us  [swap(): return lax.ppermute(value, axis, [(k, k ^ flip) for k in range(n)])]
where the time goes in v7:
time: 80.8 us; the launch traced here: 80.5 us
  starting transfers between devices  25.9 us (32%)
  Pallas kernels  25.9 us (32%)
  waiting for transfers between devices  25 us (31%)
  local copies, waits for them, and re-layouts  2.83 us (4%)
  between operations  0.87 us (1%)
    ppermute x29, starting transfers between devices, swap(): return lax.ppermute(value, axis, [(k, k ^ flip) for k in range(n)])  25.9 us
    ppermute x29, waiting for transfers between devices, swap(): return lax.ppermute(value, axis, [(k, k ^ flip) for k in range(n)])  25 us
    pallas_call x1, Pallas kernels, stage(): pl.pallas_call(functools.partial(stage_kernel, slots, near, far), out_sha...  7 us
    pallas_call x1, Pallas kernels, add_moves(): pl.pallas_call(add_moves_kernel, out_shape=jax.ShapeDtypeStruct((rows, co...  5.11 us
    pallas_call x1, Pallas kernels, profits(): pl.pallas_call(functools.partial(profit_kernel, len(tops)), out_shape=out...  4.79 us
    pallas_call x3, Pallas kernels, tail_call(): pl.pallas_call(kernel, out_shape=[jax.ShapeDtypeStruct(shape, kind) for s...  4.15 us
    unnamed x16, local copies, waits for them, and re-layouts  1.79 us
    pallas_call x1, Pallas kernels, finish(): pl.pallas_call(finish_kernel, out_shape=jax.ShapeDtypeStruct((half, (wide...  1.67 us
  transfers between devices with their start and end apart: 29, of which 15 were waited for; matrix products, arithmetic and copies ran while one was open for 1% of the time, Pallas kernels for 22%

profile of v7, /device:TPU:0, one launch (start us, length us, event | category | flops | bytes accessed | tf_op | source)
XLA Modules:
  0.0 80.5 jit_solution(14382917348825206888)
XLA Ops:
  0.6 3.0 %collective-permute-start = (bf16[512,512]{1,0:T(8,128)(2,1)}, bf16[512,512]{1,0:T(8,128)(2,1)S(1)}, u32[]{:S(2)}, u32[]{:S(2)}) collective-permute-start(bf16[512,512]{1,0:T(8,128)(2,1)} %shocks_ref.1), channel_id=1, source_target_pairs={{0,1},{1,0},{2,3},{3,2},{4,5},{5,4},{6,7},{7,6},{8,9},{9,8},{10,11... | collective-permute-start | bytes 1572872 | tf_op jit(solution)/shard_map/ppermute | solution.py:39
  3.6 1.5 %collective-permute-start.2 = (bf16[512,512]{1,0:T(8,128)(2,1)}, bf16[512,512]{1,0:T(8,128)(2,1)S(1)}, u32[]{:S(2)}, u32[]{:S(2)}) collective-permute-start(bf16[512,512]{1,0:T(8,128)(2,1)} %shocks_ref.1), channel_id=1, source_target_pairs={{0,2},{1,3},{2,0},{3,1},{4,6},{5,7},{6,4},{7,5},{8,10},{9,11},{10,... | collective-permute-start | bytes 1572872 | tf_op jit(solution)/shard_map/ppermute | solution.py:39
  5.2 1.0 %copy-done = bf16[512,512]{1,0:T(8,128)(2,1)S(1)} copy-done((bf16[512,512]{1,0:T(8,128)(2,1)S(1)}, bf16[512,512]{1,0:T(8,128)(2,1)}, u32[]{:S(2)}) %copy-start) | copy-done | bytes 524312
  7.0 7.0 %stage.1 = (f32[512,4096]{1,0:T(8,128)S(1)}, bf16[1024,4096]{1,0:T(8,128)(2,1)S(1)}, bf16[512,4096]{1,0:T(8,128)(2,1)S(1)}, bf16[4096,256]{1,0:T(8,128)(2,1)S(1)}) custom-call(s32[3]{0:T(128)S(1)} %pad_add_fusion.where_ref, bf16[512,512]{1,0:T(8,128)(2,1)S(1)} %copy-done, s32[1,4096]{1,0:T(1,128)S(1)} %bitcast.9, bf16[2048,4096]{1,0:T(8,128)(2,1)} %loadings_ref.1), custom_call_target="tpu_custom_call" | custom-call | flops 2147483648 | bytes 16777216 | tf_op jit(solution)/shard_map/stage/pallas_call | solution.py:85
  14.0 1.8 %collective-permute-done.refs_0_ = bf16[512,512]{1,0:T(8,128)(2,1)S(1)} collective-permute-done((bf16[512,512]{1,0:T(8,128)(2,1)}, bf16[512,512]{1,0:T(8,128)(2,1)S(1)}, u32[]{:S(2)}, u32[]{:S(2)}) %collective-permute-start) | collective-permute-done | bytes 524320 | tf_op jit(solution)/shard_map/ppermute | solution.py:39
  15.8 1.8 %collective-permute-start.1 = (bf16[288,512]{1,0:T(8,128)(2,1)S(1)}, bf16[288,512]{1,0:T(8,128)(2,1)S(1)}, u32[]{:S(2)}, u32[]{:S(2)}) collective-permute-start(bf16[288,512]{1,0:T(8,128)(2,1)S(1)} %slice.12), channel_id=1, source_target_pairs={{0,2},{1,3},{2,0},{3,1},{4,6},{5,7},{6,4},{7,5},{8,10},{9,11},{10,... | collective-permute-start | bytes 884744 | tf_op jit(solution)/shard_map/ppermute | solution.py:39
  17.6 1.6 %collective-permute-start.3 = (bf16[224,512]{1,0:T(8,128)(2,1)S(1)}, bf16[224,512]{1,0:T(8,128)(2,1)S(1)}, u32[]{:S(2)}, u32[]{:S(2)}) collective-permute-start(bf16[224,512]{1,0:T(8,128)(2,1)S(1)} %slice.13), channel_id=1, source_target_pairs={{0,1},{1,0},{2,3},{3,2},{4,5},{5,4},{6,7},{7,6},{8,9},{9,8},{10,11... | collective-permute-start | bytes 688136 | tf_op jit(solution)/shard_map/ppermute | solution.py:39
  19.2 5.1 %add_moves.1.refs_3_ = f32[512,4096]{1,0:T(8,128)S(1)} custom-call(bf16[512,512]{1,0:T(8,128)(2,1)S(1)} %collective-permute-done.refs_0_, bf16[512,512]{1,0:T(8,128)(2,1)S(1)} %collective-permute-done.2.refs_1_, bf16[1024,4096]{1,0:T(8,128)(2,1)S(1)} %get-tuple-element.32.refs_2_, ...), custom_call_target="tpu_custom_call", output_to_operand_aliasing={{}: (3, {})} | custom-call | flops 4294967296 | bytes 16777216 | tf_op jit(solution)/shard_map/add_moves/pallas_call | solution.py:119
  24.4 4.8 %profits.1 = (bf16[512,2048]{1,0:T(8,128)(2,1)S(1)}, bf16[512,2048]{1,0:T(8,128)(2,1)}, f32[64,512]{1,0:T(8,128)S(1)}, f32[64,512]{1,0:T(8,128)S(1)}, f32[64,512]{1,0:T(8,128)S(1)}, /*index=5*/f32[64,512]{1,0:T(8,128)S(1)}) custom-call(s32[3]{0:T(128)S(1)} %pad_add_fusion.where_ref, bf16[288,512]{1,0:T(8,128)(2,1)S(1)} %collective-permute-done.1.refs_0_, ...), custom_call_target="tpu_custom_call" | custom-call | flops 3221225472 | bytes 12582912 | tf_op jit(solution)/shard_map/profits/pallas_call | solution.py:178
  29.2 2.1 %collective-permute-start.4 = (f32[64,512]{1,0:T(8,128)S(1)}, f32[64,512]{1,0:T(8,128)S(1)}, u32[]{:S(2)}, u32[]{:S(2)}) collective-permute-start(f32[64,512]{1,0:T(8,128)S(1)} %get-tuple-element.36), channel_id=1, source_target_pairs={{0,3},{1,2},{2,1},{3,0},{4,7},{5,6},{6,5},{7,4},{8,11},{9,10},{10,... | collective-permute-start | bytes 393224 | tf_op jit(solution)/shard_map/ppermute | solution.py:39
  31.8 0.9 %collective-permute-start.6 = (f32[64,512]{1,0:T(8,128)S(1)}, f32[64,512]{1,0:T(8,128)S(1)}, u32[]{:S(2)}, u32[]{:S(2)}) collective-permute-start(f32[64,512]{1,0:T(8,128)S(1)} %get-tuple-element.38), channel_id=1, source_target_pairs={{0,1},{1,0},{2,3},{3,2},{4,5},{5,4},{6,7},{7,6},{8,9},{9,8},{10,11... | collective-permute-start | bytes 393224 | tf_op jit(solution)/shard_map/ppermute | solution.py:39
  32.8 3.0 %collective-permute-done.4.refs_1_ = f32[64,512]{1,0:T(8,128)S(1)} collective-permute-done((f32[64,512]{1,0:T(8,128)S(1)}, f32[64,512]{1,0:T(8,128)S(1)}, u32[]{:S(2)}, u32[]{:S(2)}) %collective-permute-start.4) | collective-permute-done | bytes 131104 | tf_op jit(solution)/shard_map/ppermute | solution.py:39
  35.8 1.3 %collective-permute-done.5.refs_2_ = f32[64,512]{1,0:T(8,128)S(1)} collective-permute-done((f32[64,512]{1,0:T(8,128)S(1)}, f32[64,512]{1,0:T(8,128)S(1)}, u32[]{:S(2)}, u32[]{:S(2)}) %collective-permute-start.5) | collective-permute-done | bytes 131104 | tf_op jit(solution)/shard_map/ppermute | solution.py:39
  37.7 1.6 %collective-permute-start.7 = (f32[32,128]{1,0:T(8,128)S(1)}, f32[32,128]{1,0:T(8,128)S(1)}, u32[]{:S(2)}, u32[]{:S(2)}) collective-permute-start(f32[32,128]{1,0:T(8,128)S(1)} %get-tuple-element.42.refs_0_), channel_id=1, source_target_pairs={{0,8},{4,12},{8,0},{12,4},{16,24},{20,28},{24,16},{28,20},{1,9},{5... | collective-permute-start | bytes 49160 | tf_op jit(solution)/shard_map/ppermute | solution.py:39
  39.3 2.5 %collective-permute-start.8 = (f32[32,128]{1,0:T(8,128)S(1)}, f32[32,128]{1,0:T(8,128)S(1)}, u32[]{:S(2)}, u32[]{:S(2)}) collective-permute-start(f32[32,128]{1,0:T(8,128)S(1)} %get-tuple-element.42.refs_0_), channel_id=1, source_target_pairs={{0,24},{4,28},{8,16},{12,20},{16,8},{20,12},{24,0},{28,4},{1,25},{... | collective-permute-start | bytes 49160 | tf_op jit(solution)/shard_map/ppermute | solution.py:39
  42.4 2.4 %collective-permute-done.8.refs_2_ = f32[32,128]{1,0:T(8,128)S(1)} collective-permute-done((f32[32,128]{1,0:T(8,128)S(1)}, f32[32,128]{1,0:T(8,128)S(1)}, u32[]{:S(2)}, u32[]{:S(2)}) %collective-permute-start.8) | collective-permute-done | bytes 16416 | tf_op jit(solution)/shard_map/ppermute | solution.py:39
  44.9 1.6 %collective-permute-done.9.refs_3_ = f32[32,128]{1,0:T(8,128)S(1)} collective-permute-done((f32[32,128]{1,0:T(8,128)S(1)}, f32[32,128]{1,0:T(8,128)S(1)}, u32[]{:S(2)}, u32[]{:S(2)}) %collective-permute-start.9) | collective-permute-done | bytes 16416 | tf_op jit(solution)/shard_map/ppermute | solution.py:39
  49.0 1.4 %collective-permute-start.15 = (bf16[64,512]{1,0:T(8,128)(2,1)S(1)}, bf16[64,512]{1,0:T(8,128)(2,1)S(1)}, u32[]{:S(2)}, u32[]{:S(2)}) collective-permute-start(bf16[64,512]{1,0:T(8,128)(2,1)S(1)} %get-tuple-element.43.refs_0_), channel_id=1, source_target_pairs={{0,2},{1,3},{2,0},{3,1},{4,6},{5,7},{6,4},{7,5},{8,10},{9,11},{10,... | collective-permute-start | bytes 196616 | tf_op jit(solution)/shard_map/ppermute | solution.py:39
  50.4 1.4 %collective-permute-start.16 = (bf16[64,512]{1,0:T(8,128)(2,1)S(1)}, bf16[64,512]{1,0:T(8,128)(2,1)S(1)}, u32[]{:S(2)}, u32[]{:S(2)}) collective-permute-start(bf16[64,512]{1,0:T(8,128)(2,1)S(1)} %get-tuple-element.43.refs_0_), channel_id=1, source_target_pairs={{0,3},{1,2},{2,1},{3,0},{4,7},{5,6},{6,5},{7,4},{8,11},{9,10},{10,... | collective-permute-start | bytes 196616 | tf_op jit(solution)/shard_map/ppermute | solution.py:39
  53.2 1.6 %bring.1.refs_5_.refs_3_ = bf16[512,2048]{1,0:T(8,128)(2,1)S(1)} custom-call(bf16[512,2048]{1,0:T(8,128)(2,1)} %collective-permute-done.17.far_ref), custom_call_target="tpu_custom_call" | custom-call | bytes 8388608 | tf_op jit(solution)/shard_map/bring/pallas_call | solution.py:467
  55.5 1.2 %own_sums.1 = (bf16[256,512]{1,0:T(8,128)(2,1)S(1)}, f32[64,2176]{1,0:T(8,128)S(1)}) custom-call(s32[3]{0:T(128)S(1)} %pad_add_fusion.where_ref, bf16[64,512]{1,0:T(8,128)(2,1)S(1)} %get-tuple-element.43.refs_0_, bf16[64,512]{1,0:T(8,128)(2,1)S(1)} %collective-permute-done.14.refs_1_, bf16[64,512]{1,0:T(8,128)(2,1)S(1)} %collective-permute-done.15.refs_2_, ...), custom_call_target="tpu_custom_call" | custom-call | bytes 9437184 | tf_op jit(solution)/shard_map/own_sums/pallas_call | solution.py:481
  56.8 1.2 %away_sums.1 = (s16[32,2176]{1,0:T(8,128)(2,1)S(1)}, s16[32,2176]{1,0:T(8,128)(2,1)S(1)}, bf16[256,512]{1,0:T(8,128)(2,1)S(1)}) custom-call(s32[3]{0:T(128)S(1)} %pad_add_fusion.where_ref, bf16[64,512]{1,0:T(8,128)(2,1)S(1)} %collective-permute-done.18.refs_0_, bf16[64,512]{1,0:T(8,128)(2,1)S(1)} %collective-permute-done.19.refs_1_, ...), custom_call_target="tpu_custom_call" | custom-call | bytes 11665408 | tf_op jit(solution)/shard_map/away_sums/pallas_call | solution.py:481
  58.8 1.3 %collective-permute-start.23 = (s16[32,2176]{1,0:T(8,128)(2,1)S(1)}, s16[32,2176]{1,0:T(8,128)(2,1)S(1)}, u32[]{:S(2)}, u32[]{:S(2)}) collective-permute-start(s16[32,2176]{1,0:T(8,128)(2,1)S(1)} %get-tuple-element.53), channel_id=1, source_target_pairs={{0,8},{4,12},{8,0},{12,4},{16,24},{20,28},{24,16},{28,20},{1,9},{5... | collective-permute-start | bytes 417800 | tf_op jit(solution)/shard_map/ppermute | solution.py:39
  60.1 1.7 %home_sums.1 = (s16[32,2176]{1,0:T(8,128)(2,1)S(1)}, s16[32,2176]{1,0:T(8,128)(2,1)S(1)}, f32[32,2176]{1,0:T(8,128)S(1)}, f32[32,2176]{1,0:T(8,128)S(1)}, f32[32...) custom-call(s32[3]{0:T(128)S(1)} %pad_add_fusion.where_ref, bf16[256,512]{1,0:T(8,128)(2,1)S(1)} %get-tuple-element.47.refs_0_, ...), custom_call_target="tpu_custom_call" | custom-call | bytes 18874368 | tf_op jit(solution)/shard_map/home_sums/pallas_call | solution.py:481
  62.7 1.1 %collective-permute-start.26 = (s16[32,2176]{1,0:T(8,128)(2,1)S(1)}, s16[32,2176]{1,0:T(8,128)(2,1)S(1)}, u32[]{:S(2)}, u32[]{:S(2)}) collective-permute-start(s16[32,2176]{1,0:T(8,128)(2,1)S(1)} %get-tuple-element.56), channel_id=1, source_target_pairs={{0,12},{4,8},{8,4},{12,0},{16,28},{20,24},{24,20},{28,16},{1,13},{... | collective-permute-start | bytes 417800 | tf_op jit(solution)/shard_map/ppermute | solution.py:39
  65.4 2.2 %collective-permute-done.23.words_ref = s16[32,2176]{1,0:T(8,128)(2,1)S(1)} collective-permute-done((s16[32,2176]{1,0:T(8,128)(2,1)S(1)}, s16[32,2176]{1,0:T(8,128)(2,1)S(1)}, u32[]{:S(2)}, u32[]{:S(2)}) %collective-permute-start.23) | collective-permute-done | bytes 139296 | tf_op jit(solution)/shard_map/ppermute | solution.py:39
  67.8 1.4 %collective-permute-start.24 = (s16[32,2176]{1,0:T(8,128)(2,1)S(1)}, s16[32,2176]{1,0:T(8,128)(2,1)S(1)}, u32[]{:S(2)}, u32[]{:S(2)}) collective-permute-start(s16[32,2176]{1,0:T(8,128)(2,1)S(1)} %relay.2), channel_id=1, source_target_pairs={{0,24},{4,28},{8,16},{12,20},{16,8},{20,12},{24,0},{28,4},{1,25},{... | collective-permute-start | bytes 417800 | tf_op jit(solution)/shard_map/ppermute | solution.py:39
  69.7 0.8 %collective-permute-done.22.refs_1_ = s16[32,2176]{1,0:T(8,128)(2,1)S(1)} collective-permute-done((s16[32,2176]{1,0:T(8,128)(2,1)S(1)}, s16[32,2176]{1,0:T(8,128)(2,1)S(1)}, u32[]{:S(2)}, u32[]{:S(2)}) %collective-permute-start.22) | collective-permute-done | bytes 139296 | tf_op jit(solution)/shard_map/ppermute | solution.py:39
  70.5 2.6 %collective-permute-done.26.refs_4_ = s16[32,2176]{1,0:T(8,128)(2,1)S(1)} collective-permute-done((s16[32,2176]{1,0:T(8,128)(2,1)S(1)}, s16[32,2176]{1,0:T(8,128)(2,1)S(1)}, u32[]{:S(2)}, u32[]{:S(2)}) %collective-permute-start.26) | collective-permute-done | bytes 139296 | tf_op jit(solution)/shard_map/ppermute | solution.py:39
  73.1 2.4 %collective-permute-done.28.refs_5_ = s16[32,2176]{1,0:T(8,128)(2,1)S(1)} collective-permute-done((s16[32,2176]{1,0:T(8,128)(2,1)S(1)}, s16[32,2176]{1,0:T(8,128)(2,1)S(1)}, u32[]{:S(2)}, u32[]{:S(2)}) %collective-permute-start.28) | collective-permute-done | bytes 139296 | tf_op jit(solution)/shard_map/ppermute | solution.py:39
  75.5 3.4 %collective-permute-done.24.refs_2_ = s16[32,2176]{1,0:T(8,128)(2,1)S(1)} collective-permute-done((s16[32,2176]{1,0:T(8,128)(2,1)S(1)}, s16[32,2176]{1,0:T(8,128)(2,1)S(1)}, u32[]{:S(2)}, u32[]{:S(2)}) %collective-permute-start.24) | collective-permute-done | bytes 139296 | tf_op jit(solution)/shard_map/ppermute | solution.py:39
  78.9 1.7 %finish.1 = f32[32,4096]{1,0:T(8,128)} custom-call(s32[3]{0:T(128)S(1)} %pad_add_fusion.where_ref, f32[32,2176]{1,0:T(8,128)S(1)} %get-tuple-element.51.refs_0_, s16[32,2176]{1,0:T(8,128)(2,1)S(1)} %collective-permute-done.22.refs_1_, s16[32,2176]{1,0:T(8,128)(2,1)S(1)} %collective-permute-done.24.refs_2_, f32[32,2176]{1,0:T(8,128)S(1)} %collective-permute-done.25.refs_3_, ...), custom_call_target="tpu_custom_call" | custom-call | tf_op jit(solution)/shard_map/finish/pallas_call | solution.py:563
  (67 shorter events, 11.2 us)
Async XLA Ops:
  0.6 15.1 %collective-permute-start = (bf16[512,512]{1,0:T(8,128)(2,1)}, bf16[512,512]{1,0:T(8,128)(2,1)S(1)}, u32[]{:S(2)}, u32[]{:S(2)}) collective-permute-start(bf16[512,512]{1,0:T(8,128)(2,1)} %shocks_ref.1), channel_id=1, source_target_pairs={{0,1},{1,0},{2,3},{3,2},{4,5},{5,4},{6,7},{7,6},{8,9},{9,8},{10,11... | collective-permute-start | bytes 1572872 | tf_op jit(solution)/shard_map/ppermute | solution.py:39
  3.6 14.0 %collective-permute-start.2 = (bf16[512,512]{1,0:T(8,128)(2,1)}, bf16[512,512]{1,0:T(8,128)(2,1)S(1)}, u32[]{:S(2)}, u32[]{:S(2)}) collective-permute-start(bf16[512,512]{1,0:T(8,128)(2,1)} %shocks_ref.1), channel_id=1, source_target_pairs={{0,2},{1,3},{2,0},{3,1},{4,6},{5,7},{6,4},{7,5},{8,10},{9,11},{10,... | collective-permute-start | bytes 1572872 | tf_op jit(solution)/shard_map/ppermute | solution.py:39
  15.8 8.6 %collective-permute-start.1 = (bf16[288,512]{1,0:T(8,128)(2,1)S(1)}, bf16[288,512]{1,0:T(8,128)(2,1)S(1)}, u32[]{:S(2)}, u32[]{:S(2)}) collective-permute-start(bf16[288,512]{1,0:T(8,128)(2,1)S(1)} %slice.12), channel_id=1, source_target_pairs={{0,2},{1,3},{2,0},{3,1},{4,6},{5,7},{6,4},{7,5},{8,10},{9,11},{10,... | collective-permute-start | bytes 884744 | tf_op jit(solution)/shard_map/ppermute | solution.py:39
  17.6 6.7 %collective-permute-start.3 = (bf16[224,512]{1,0:T(8,128)(2,1)S(1)}, bf16[224,512]{1,0:T(8,128)(2,1)S(1)}, u32[]{:S(2)}, u32[]{:S(2)}) collective-permute-start(bf16[224,512]{1,0:T(8,128)(2,1)S(1)} %slice.13), channel_id=1, source_target_pairs={{0,1},{1,0},{2,3},{3,2},{4,5},{5,4},{6,7},{7,6},{8,9},{9,8},{10,11... | collective-permute-start | bytes 688136 | tf_op jit(solution)/shard_map/ppermute | solution.py:39
  24.4 22.1 %copy-start.5 = (s32[256]{0:T(256)S(1)}, s32[256]{0:T(256)}, u32[]{:S(2)}) copy-start(s32[256]{0:T(256)} %param.16) | copy-start | bytes 3076
  24.4 22.2 %copy-start.6 = (s32[256]{0:T(256)S(1)}, s32[256]{0:T(256)}, u32[]{:S(2)}) copy-start(s32[256]{0:T(256)} %param.17) | copy-start | bytes 3076
  24.4 22.4 %copy-start.7 = (s32[256]{0:T(256)S(1)}, s32[256]{0:T(256)}, u32[]{:S(2)}) copy-start(s32[256]{0:T(256)} %param.15) | copy-start | bytes 3076
  29.2 6.5 %collective-permute-start.4 = (f32[64,512]{1,0:T(8,128)S(1)}, f32[64,512]{1,0:T(8,128)S(1)}, u32[]{:S(2)}, u32[]{:S(2)}) collective-permute-start(f32[64,512]{1,0:T(8,128)S(1)} %get-tuple-element.36), channel_id=1, source_target_pairs={{0,3},{1,2},{2,1},{3,0},{4,7},{5,6},{6,5},{7,4},{8,11},{9,10},{10,... | collective-permute-start | bytes 393224 | tf_op jit(solution)/shard_map/ppermute | solution.py:39
  31.3 5.8 %collective-permute-start.5 = (f32[64,512]{1,0:T(8,128)S(1)}, f32[64,512]{1,0:T(8,128)S(1)}, u32[]{:S(2)}, u32[]{:S(2)}) collective-permute-start(f32[64,512]{1,0:T(8,128)S(1)} %get-tuple-element.37), channel_id=1, source_target_pairs={{0,2},{1,3},{2,0},{3,1},{4,6},{5,7},{6,4},{7,5},{8,10},{9,11},{10,... | collective-permute-start | bytes 393224 | tf_op jit(solution)/shard_map/ppermute | solution.py:39
  31.8 5.3 %collective-permute-start.6 = (f32[64,512]{1,0:T(8,128)S(1)}, f32[64,512]{1,0:T(8,128)S(1)}, u32[]{:S(2)}, u32[]{:S(2)}) collective-permute-start(f32[64,512]{1,0:T(8,128)S(1)} %get-tuple-element.38), channel_id=1, source_target_pairs={{0,1},{1,0},{2,3},{3,2},{4,5},{5,4},{6,7},{7,6},{8,9},{9,8},{10,11... | collective-permute-start | bytes 393224 | tf_op jit(solution)/shard_map/ppermute | solution.py:39
  37.6 15.6 %collective-permute-start.17 = (bf16[512,2048]{1,0:T(8,128)(2,1)}, bf16[512,2048]{1,0:T(8,128)(2,1)}, u32[]{:S(2)}, u32[]{:S(2)}) collective-permute-start(bf16[512,2048]{1,0:T(8,128)(2,1)} %get-tuple-element.44), channel_id=1, source_target_pairs={{0,4},{4,0},{8,12},{12,8},{16,20},{20,16},{24,28},{28,24},{1,5},{5... | collective-permute-start | bytes 6291464 | tf_op jit(solution)/shard_map/ppermute | solution.py:39
  37.7 4.2 %collective-permute-start.7 = (f32[32,128]{1,0:T(8,128)S(1)}, f32[32,128]{1,0:T(8,128)S(1)}, u32[]{:S(2)}, u32[]{:S(2)}) collective-permute-start(f32[32,128]{1,0:T(8,128)S(1)} %get-tuple-element.42.refs_0_), channel_id=1, source_target_pairs={{0,8},{4,12},{8,0},{12,4},{16,24},{20,28},{24,16},{28,20},{1,9},{5... | collective-permute-start | bytes 49160 | tf_op jit(solution)/shard_map/ppermute | solution.py:39
  39.3 5.5 %collective-permute-start.8 = (f32[32,128]{1,0:T(8,128)S(1)}, f32[32,128]{1,0:T(8,128)S(1)}, u32[]{:S(2)}, u32[]{:S(2)}) collective-permute-start(f32[32,128]{1,0:T(8,128)S(1)} %get-tuple-element.42.refs_0_), channel_id=1, source_target_pairs={{0,24},{4,28},{8,16},{12,20},{16,8},{20,12},{24,0},{28,4},{1,25},{... | collective-permute-start | bytes 49160 | tf_op jit(solution)/shard_map/ppermute | solution.py:39
  41.8 4.6 %collective-permute-start.9 = (f32[32,128]{1,0:T(8,128)S(1)}, f32[32,128]{1,0:T(8,128)S(1)}, u32[]{:S(2)}, u32[]{:S(2)}) collective-permute-start(f32[32,128]{1,0:T(8,128)S(1)} %get-tuple-element.42.refs_0_), channel_id=1, source_target_pairs={{0,16},{4,20},{8,24},{12,28},{16,0},{20,4},{24,8},{28,12},{1,17},{... | collective-permute-start | bytes 49160 | tf_op jit(solution)/shard_map/ppermute | solution.py:39
  41.9 5.0 %collective-permute-start.10 = (f32[32,128]{1,0:T(8,128)S(1)}, f32[32,128]{1,0:T(8,128)S(1)}, u32[]{:S(2)}, u32[]{:S(2)}) collective-permute-start(f32[32,128]{1,0:T(8,128)S(1)} %get-tuple-element.42.refs_0_), channel_id=1, source_target_pairs={{0,4},{4,0},{8,12},{12,8},{16,20},{20,16},{24,28},{28,24},{1,5},{5... | collective-permute-start | bytes 49160 | tf_op jit(solution)/shard_map/ppermute | solution.py:39
  41.9 5.0 %collective-permute-start.11 = (f32[32,128]{1,0:T(8,128)S(1)}, f32[32,128]{1,0:T(8,128)S(1)}, u32[]{:S(2)}, u32[]{:S(2)}) collective-permute-start(f32[32,128]{1,0:T(8,128)S(1)} %collective-permute-done.7.refs_1_), channel_id=1, source_target_pairs={{0,4},{4,0},{8,12},{12,8},{16,20},{20,16},{24,28},{28,24},{1,5},{5... | collective-permute-start | bytes 49160 | tf_op jit(solution)/shard_map/ppermute | solution.py:39
  44.9 2.1 %collective-permute-start.12 = (f32[32,128]{1,0:T(8,128)S(1)}, f32[32,128]{1,0:T(8,128)S(1)}, u32[]{:S(2)}, u32[]{:S(2)}) collective-permute-start(f32[32,128]{1,0:T(8,128)S(1)} %collective-permute-done.8.refs_2_), channel_id=1, source_target_pairs={{0,4},{4,0},{8,12},{12,8},{16,20},{20,16},{24,28},{28,24},{1,5},{5... | collective-permute-start | bytes 49160 | tf_op jit(solution)/shard_map/ppermute | solution.py:39
  46.5 1.2 %collective-permute-start.13 = (f32[32,128]{1,0:T(8,128)S(1)}, f32[32,128]{1,0:T(8,128)S(1)}, u32[]{:S(2)}, u32[]{:S(2)}) collective-permute-start(f32[32,128]{1,0:T(8,128)S(1)} %collective-permute-done.9.refs_3_), channel_id=1, source_target_pairs={{0,4},{4,0},{8,12},{12,8},{16,20},{20,16},{24,28},{28,24},{1,5},{5... | collective-permute-start | bytes 49160 | tf_op jit(solution)/shard_map/ppermute | solution.py:39
  48.2 4.3 %collective-permute-start.14 = (bf16[64,512]{1,0:T(8,128)(2,1)S(1)}, bf16[64,512]{1,0:T(8,128)(2,1)S(1)}, u32[]{:S(2)}, u32[]{:S(2)}) collective-permute-start(bf16[64,512]{1,0:T(8,128)(2,1)S(1)} %get-tuple-element.43.refs_0_), channel_id=1, source_target_pairs={{0,1},{1,0},{2,3},{3,2},{4,5},{5,4},{6,7},{7,6},{8,9},{9,8},{10,11... | collective-permute-start | bytes 196616 | tf_op jit(solution)/shard_map/ppermute | solution.py:39
  49.0 4.3 %collective-permute-start.15 = (bf16[64,512]{1,0:T(8,128)(2,1)S(1)}, bf16[64,512]{1,0:T(8,128)(2,1)S(1)}, u32[]{:S(2)}, u32[]{:S(2)}) collective-permute-start(bf16[64,512]{1,0:T(8,128)(2,1)S(1)} %get-tuple-element.43.refs_0_), channel_id=1, source_target_pairs={{0,2},{1,3},{2,0},{3,1},{4,6},{5,7},{6,4},{7,5},{8,10},{9,11},{10,... | collective-permute-start | bytes 196616 | tf_op jit(solution)/shard_map/ppermute | solution.py:39
  50.4 5.2 %collective-permute-start.16 = (bf16[64,512]{1,0:T(8,128)(2,1)S(1)}, bf16[64,512]{1,0:T(8,128)(2,1)S(1)}, u32[]{:S(2)}, u32[]{:S(2)}) collective-permute-start(bf16[64,512]{1,0:T(8,128)(2,1)S(1)} %get-tuple-element.43.refs_0_), channel_id=1, source_target_pairs={{0,3},{1,2},{2,1},{3,0},{4,7},{5,6},{6,5},{7,4},{8,11},{9,10},{10,... | collective-permute-start | bytes 196616 | tf_op jit(solution)/shard_map/ppermute | solution.py:39
  51.8 5.0 %collective-permute-start.18 = (bf16[64,512]{1,0:T(8,128)(2,1)S(1)}, bf16[64,512]{1,0:T(8,128)(2,1)S(1)}, u32[]{:S(2)}, u32[]{:S(2)}) collective-permute-start(bf16[64,512]{1,0:T(8,128)(2,1)S(1)} %get-tuple-element.43.refs_0_), channel_id=1, source_target_pairs={{0,4},{4,0},{8,12},{12,8},{16,20},{20,16},{24,28},{28,24},{1,5},{5... | collective-permute-start | bytes 196616 | tf_op jit(solution)/shard_map/ppermute | solution.py:39
  52.6 4.2 %collective-permute-start.19 = (bf16[64,512]{1,0:T(8,128)(2,1)S(1)}, bf16[64,512]{1,0:T(8,128)(2,1)S(1)}, u32[]{:S(2)}, u32[]{:S(2)}) collective-permute-start(bf16[64,512]{1,0:T(8,128)(2,1)S(1)} %collective-permute-done.14.refs_1_), channel_id=1, source_target_pairs={{0,4},{4,0},{8,12},{12,8},{16,20},{20,16},{24,28},{28,24},{1,5},{5... | collective-permute-start | bytes 196616 | tf_op jit(solution)/shard_map/ppermute | solution.py:39
  53.2 3.5 %collective-permute-start.20 = (bf16[64,512]{1,0:T(8,128)(2,1)S(1)}, bf16[64,512]{1,0:T(8,128)(2,1)S(1)}, u32[]{:S(2)}, u32[]{:S(2)}) collective-permute-start(bf16[64,512]{1,0:T(8,128)(2,1)S(1)} %collective-permute-done.15.refs_2_), channel_id=1, source_target_pairs={{0,4},{4,0},{8,12},{12,8},{16,20},{20,16},{24,28},{28,24},{1,5},{5... | collective-permute-start | bytes 196616 | tf_op jit(solution)/shard_map/ppermute | solution.py:39
  55.5 1.3 %collective-permute-start.21 = (bf16[64,512]{1,0:T(8,128)(2,1)S(1)}, bf16[64,512]{1,0:T(8,128)(2,1)S(1)}, u32[]{:S(2)}, u32[]{:S(2)}) collective-permute-start(bf16[64,512]{1,0:T(8,128)(2,1)S(1)} %collective-permute-done.16.refs_3_), channel_id=1, source_target_pairs={{0,4},{4,0},{8,12},{12,8},{16,20},{20,16},{24,28},{28,24},{1,5},{5... | collective-permute-start | bytes 196616 | tf_op jit(solution)/shard_map/ppermute | solution.py:39
  58.0 6.5 %collective-permute-start.27 = (s16[32,2176]{1,0:T(8,128)(2,1)S(1)}, s16[32,2176]{1,0:T(8,128)(2,1)S(1)}, u32[]{:S(2)}, u32[]{:S(2)}) collective-permute-start(s16[32,2176]{1,0:T(8,128)(2,1)S(1)} %get-tuple-element.57), channel_id=1, source_target_pairs={{0,8},{4,12},{8,0},{12,4},{16,24},{20,28},{24,16},{28,20},{1,9},{5... | collective-permute-start | bytes 417800 | tf_op jit(solution)/shard_map/ppermute | solution.py:39
  58.8 8.7 %collective-permute-start.23 = (s16[32,2176]{1,0:T(8,128)(2,1)S(1)}, s16[32,2176]{1,0:T(8,128)(2,1)S(1)}, u32[]{:S(2)}, u32[]{:S(2)}) collective-permute-start(s16[32,2176]{1,0:T(8,128)(2,1)S(1)} %get-tuple-element.53), channel_id=1, source_target_pairs={{0,8},{4,12},{8,0},{12,4},{16,24},{20,28},{24,16},{28,20},{1,9},{5... | collective-permute-start | bytes 417800 | tf_op jit(solution)/shard_map/ppermute | solution.py:39
  61.8 17.0 %collective-permute-start.25 = (f32[32,2176]{1,0:T(8,128)S(1)}, f32[32,2176]{1,0:T(8,128)S(1)}, u32[]{:S(2)}, u32[]{:S(2)}) collective-permute-start(f32[32,2176]{1,0:T(8,128)S(1)} %get-tuple-element.55), channel_id=1, source_target_pairs={{0,4},{4,0},{8,12},{12,8},{16,20},{20,16},{24,28},{28,24},{1,5},{5... | collective-permute-start | bytes 835592 | tf_op jit(solution)/shard_map/ppermute | solution.py:39
  61.9 8.6 %collective-permute-start.22 = (s16[32,2176]{1,0:T(8,128)(2,1)S(1)}, s16[32,2176]{1,0:T(8,128)(2,1)S(1)}, u32[]{:S(2)}, u32[]{:S(2)}) collective-permute-start(s16[32,2176]{1,0:T(8,128)(2,1)S(1)} %get-tuple-element.52), channel_id=1, source_target_pairs={{0,8},{4,12},{8,0},{12,4},{16,24},{20,28},{24,16},{28,20},{1,9},{5... | collective-permute-start | bytes 417800 | tf_op jit(solution)/shard_map/ppermute | solution.py:39
  62.7 10.4 %collective-permute-start.26 = (s16[32,2176]{1,0:T(8,128)(2,1)S(1)}, s16[32,2176]{1,0:T(8,128)(2,1)S(1)}, u32[]{:S(2)}, u32[]{:S(2)}) collective-permute-start(s16[32,2176]{1,0:T(8,128)(2,1)S(1)} %get-tuple-element.56), channel_id=1, source_target_pairs={{0,12},{4,8},{8,4},{12,0},{16,28},{20,24},{24,20},{28,16},{1,13},{... | collective-permute-start | bytes 417800 | tf_op jit(solution)/shard_map/ppermute | solution.py:39
  64.8 10.7 %collective-permute-start.28 = (s16[32,2176]{1,0:T(8,128)(2,1)S(1)}, s16[32,2176]{1,0:T(8,128)(2,1)S(1)}, u32[]{:S(2)}, u32[]{:S(2)}) collective-permute-start(s16[32,2176]{1,0:T(8,128)(2,1)S(1)} %relay.3), channel_id=1, source_target_pairs={{0,28},{4,24},{8,20},{12,16},{16,12},{20,8},{24,4},{28,0},{1,29},{... | collective-permute-start | bytes 417800 | tf_op jit(solution)/shard_map/ppermute | solution.py:39
  67.8 11.1 %collective-permute-start.24 = (s16[32,2176]{1,0:T(8,128)(2,1)S(1)}, s16[32,2176]{1,0:T(8,128)(2,1)S(1)}, u32[]{:S(2)}, u32[]{:S(2)}) collective-permute-start(s16[32,2176]{1,0:T(8,128)(2,1)S(1)} %relay.2), channel_id=1, source_target_pairs={{0,24},{4,28},{8,16},{12,20},{16,8},{20,12},{24,0},{28,4},{1,25},{... | collective-permute-start | bytes 417800 | tf_op jit(solution)/shard_map/ppermute | solution.py:39
  (5 other events, 17.2 us)

commit v8 on v7

--- a/solution.py
+++ b/solution.py
@@ -457,10 +457,16 @@
         own_refs[side][...] = value
 
 
-def bring_kernel(far_ref, near_ref, sem):
-    copy = pltpu.make_async_copy(far_ref, near_ref, sem)
-    copy.start()
-    copy.wait()
+def bring_kernel(far_ref, near_ref, sems):
+    rows = far_ref.shape[0]
+    copies = [
+        pltpu.make_async_copy(far_ref.at[run, :], near_ref.at[run, :], sems.at[k])
+        for k, run in enumerate(tiles(rows, rows // 8))
+    ]
+    for copy in copies:
+        copy.start()
+    for copy in copies:
+        copy.wait()
 
 
 def bring(far):
@@ -469,7 +475,7 @@
         out_shape=jax.ShapeDtypeStruct(far.shape, far.dtype),
         in_specs=[pl.BlockSpec(memory_space=pltpu.HBM)],
         out_specs=pl.BlockSpec(memory_space=pltpu.VMEM),
-        scratch_shapes=[pltpu.SemaphoreType.DMA],
+        scratch_shapes=[pltpu.SemaphoreType.DMA((8,))],
         compiler_params=params(16),
         cost_estimate=pl.CostEstimate(flops=0, bytes_accessed=8 * far.size, transcendentals=0),
         name="bring",

time: 80.8 us -> 80.6 us (level)
  transfers between devices with their start and end apart: 29 -> 29, of which waited for: 15 -> 16; matrix products, arithmetic and copies ran while one was open for 1% -> 1% of each run, Pallas kernels for 22% -> 22%
where the time goes in v8:
time: 80.6 us; the launch traced here: 80.3 us
  starting transfers between devices  25.9 us (32%)
  Pallas kernels  25.7 us (32%)
  waiting for transfers between devices  25 us (31%)
  local copies, waits for them, and re-layouts  2.83 us (4%)
  between operations  0.87 us (1%)
    ppermute x29, starting transfers between devices, swap(): return lax.ppermute(value, axis, [(k, k ^ flip) for k in range(n)])  25.9 us
    ppermute x29, waiting for transfers between devices, swap(): return lax.ppermute(value, axis, [(k, k ^ flip) for k in range(n)])  25 us
    pallas_call x1, Pallas kernels, stage(): pl.pallas_call(functools.partial(stage_kernel, slots, near, far), out_sha...  7 us
    pallas_call x1, Pallas kernels, add_moves(): pl.pallas_call(add_moves_kernel, out_shape=jax.ShapeDtypeStruct((rows, co...  5.11 us
    pallas_call x1, Pallas kernels, profits(): pl.pallas_call(functools.partial(profit_kernel, len(tops)), out_shape=out...  4.79 us
    pallas_call x3, Pallas kernels, tail_call(): pl.pallas_call(kernel, out_shape=[jax.ShapeDtypeStruct(shape, kind) for s...  3.96 us
    unnamed x16, local copies, waits for them, and re-layouts  1.79 us
    pallas_call x1, Pallas kernels, finish(): pl.pallas_call(finish_kernel, out_shape=jax.ShapeDtypeStruct((half, (wide...  1.67 us
  transfers between devices with their start and end apart: 29, of which 16 were waited for; matrix products, arithmetic and copies ran while one was open for 1% of the time, Pallas kernels for 22%

profile of v8, /device:TPU:0, one launch (start us, length us, event | category | flops | bytes accessed | tf_op | source)
XLA Modules:
  0.0 80.3 jit_solution(5127152747398943934)
XLA Ops:
  0.6 3.0 %collective-permute-start = (bf16[512,512]{1,0:T(8,128)(2,1)}, bf16[512,512]{1,0:T(8,128)(2,1)S(1)}, u32[]{:S(2)}, u32[]{:S(2)}) collective-permute-start(bf16[512,512]{1,0:T(8,128)(2,1)} %shocks_ref.1), channel_id=1, source_target_pairs={{0,1},{1,0},{2,3},{3,2},{4,5},{5,4},{6,7},{7,6},{8,9},{9,8},{10,11... | collective-permute-start | bytes 1572872 | tf_op jit(solution)/shard_map/ppermute | solution.py:39
  3.6 1.5 %collective-permute-start.2 = (bf16[512,512]{1,0:T(8,128)(2,1)}, bf16[512,512]{1,0:T(8,128)(2,1)S(1)}, u32[]{:S(2)}, u32[]{:S(2)}) collective-permute-start(bf16[512,512]{1,0:T(8,128)(2,1)} %shocks_ref.1), channel_id=1, source_target_pairs={{0,2},{1,3},{2,0},{3,1},{4,6},{5,7},{6,4},{7,5},{8,10},{9,11},{10,... | collective-permute-start | bytes 1572872 | tf_op jit(solution)/shard_map/ppermute | solution.py:39
  5.2 1.0 %copy-done = bf16[512,512]{1,0:T(8,128)(2,1)S(1)} copy-done((bf16[512,512]{1,0:T(8,128)(2,1)S(1)}, bf16[512,512]{1,0:T(8,128)(2,1)}, u32[]{:S(2)}) %copy-start) | copy-done | bytes 524312
  7.0 7.0 %stage.1 = (f32[512,4096]{1,0:T(8,128)S(1)}, bf16[1024,4096]{1,0:T(8,128)(2,1)S(1)}, bf16[512,4096]{1,0:T(8,128)(2,1)S(1)}, bf16[4096,256]{1,0:T(8,128)(2,1)S(1)}) custom-call(s32[3]{0:T(128)S(1)} %pad_add_fusion.where_ref, bf16[512,512]{1,0:T(8,128)(2,1)S(1)} %copy-done, s32[1,4096]{1,0:T(1,128)S(1)} %bitcast.9, bf16[2048,4096]{1,0:T(8,128)(2,1)} %loadings_ref.1), custom_call_target="tpu_custom_call" | custom-call | flops 2147483648 | bytes 16777216 | tf_op jit(solution)/shard_map/stage/pallas_call | solution.py:85
  14.0 1.8 %collective-permute-done.refs_0_ = bf16[512,512]{1,0:T(8,128)(2,1)S(1)} collective-permute-done((bf16[512,512]{1,0:T(8,128)(2,1)}, bf16[512,512]{1,0:T(8,128)(2,1)S(1)}, u32[]{:S(2)}, u32[]{:S(2)}) %collective-permute-start) | collective-permute-done | bytes 524320 | tf_op jit(solution)/shard_map/ppermute | solution.py:39
  15.8 1.8 %collective-permute-start.1 = (bf16[288,512]{1,0:T(8,128)(2,1)S(1)}, bf16[288,512]{1,0:T(8,128)(2,1)S(1)}, u32[]{:S(2)}, u32[]{:S(2)}) collective-permute-start(bf16[288,512]{1,0:T(8,128)(2,1)S(1)} %slice.12), channel_id=1, source_target_pairs={{0,2},{1,3},{2,0},{3,1},{4,6},{5,7},{6,4},{7,5},{8,10},{9,11},{10,... | collective-permute-start | bytes 884744 | tf_op jit(solution)/shard_map/ppermute | solution.py:39
  17.6 1.6 %collective-permute-start.3 = (bf16[224,512]{1,0:T(8,128)(2,1)S(1)}, bf16[224,512]{1,0:T(8,128)(2,1)S(1)}, u32[]{:S(2)}, u32[]{:S(2)}) collective-permute-start(bf16[224,512]{1,0:T(8,128)(2,1)S(1)} %slice.13), channel_id=1, source_target_pairs={{0,1},{1,0},{2,3},{3,2},{4,5},{5,4},{6,7},{7,6},{8,9},{9,8},{10,11... | collective-permute-start | bytes 688136 | tf_op jit(solution)/shard_map/ppermute | solution.py:39
  19.2 5.1 %add_moves.1.refs_3_ = f32[512,4096]{1,0:T(8,128)S(1)} custom-call(bf16[512,512]{1,0:T(8,128)(2,1)S(1)} %collective-permute-done.refs_0_, bf16[512,512]{1,0:T(8,128)(2,1)S(1)} %collective-permute-done.2.refs_1_, bf16[1024,4096]{1,0:T(8,128)(2,1)S(1)} %get-tuple-element.32.refs_2_, ...), custom_call_target="tpu_custom_call", output_to_operand_aliasing={{}: (3, {})} | custom-call | flops 4294967296 | bytes 16777216 | tf_op jit(solution)/shard_map/add_moves/pallas_call | solution.py:119
  24.4 4.8 %profits.1 = (bf16[512,2048]{1,0:T(8,128)(2,1)S(1)}, bf16[512,2048]{1,0:T(8,128)(2,1)}, f32[64,512]{1,0:T(8,128)S(1)}, f32[64,512]{1,0:T(8,128)S(1)}, f32[64,512]{1,0:T(8,128)S(1)}, /*index=5*/f32[64,512]{1,0:T(8,128)S(1)}) custom-call(s32[3]{0:T(128)S(1)} %pad_add_fusion.where_ref, bf16[288,512]{1,0:T(8,128)(2,1)S(1)} %collective-permute-done.1.refs_0_, ...), custom_call_target="tpu_custom_call" | custom-call | flops 3221225472 | bytes 12582912 | tf_op jit(solution)/shard_map/profits/pallas_call | solution.py:178
  29.2 2.1 %collective-permute-start.4 = (f32[64,512]{1,0:T(8,128)S(1)}, f32[64,512]{1,0:T(8,128)S(1)}, u32[]{:S(2)}, u32[]{:S(2)}) collective-permute-start(f32[64,512]{1,0:T(8,128)S(1)} %get-tuple-element.36), channel_id=1, source_target_pairs={{0,3},{1,2},{2,1},{3,0},{4,7},{5,6},{6,5},{7,4},{8,11},{9,10},{10,... | collective-permute-start | bytes 393224 | tf_op jit(solution)/shard_map/ppermute | solution.py:39
  31.8 0.9 %collective-permute-start.6 = (f32[64,512]{1,0:T(8,128)S(1)}, f32[64,512]{1,0:T(8,128)S(1)}, u32[]{:S(2)}, u32[]{:S(2)}) collective-permute-start(f32[64,512]{1,0:T(8,128)S(1)} %get-tuple-element.38), channel_id=1, source_target_pairs={{0,1},{1,0},{2,3},{3,2},{4,5},{5,4},{6,7},{7,6},{8,9},{9,8},{10,11... | collective-permute-start | bytes 393224 | tf_op jit(solution)/shard_map/ppermute | solution.py:39
  32.8 3.0 %collective-permute-done.4.refs_1_ = f32[64,512]{1,0:T(8,128)S(1)} collective-permute-done((f32[64,512]{1,0:T(8,128)S(1)}, f32[64,512]{1,0:T(8,128)S(1)}, u32[]{:S(2)}, u32[]{:S(2)}) %collective-permute-start.4) | collective-permute-done | bytes 131104 | tf_op jit(solution)/shard_map/ppermute | solution.py:39
  35.8 1.3 %collective-permute-done.5.refs_2_ = f32[64,512]{1,0:T(8,128)S(1)} collective-permute-done((f32[64,512]{1,0:T(8,128)S(1)}, f32[64,512]{1,0:T(8,128)S(1)}, u32[]{:S(2)}, u32[]{:S(2)}) %collective-permute-start.5) | collective-permute-done | bytes 131104 | tf_op jit(solution)/shard_map/ppermute | solution.py:39
  37.7 1.6 %collective-permute-start.7 = (f32[32,128]{1,0:T(8,128)S(1)}, f32[32,128]{1,0:T(8,128)S(1)}, u32[]{:S(2)}, u32[]{:S(2)}) collective-permute-start(f32[32,128]{1,0:T(8,128)S(1)} %get-tuple-element.42.refs_0_), channel_id=1, source_target_pairs={{0,8},{4,12},{8,0},{12,4},{16,24},{20,28},{24,16},{28,20},{1,9},{5... | collective-permute-start | bytes 49160 | tf_op jit(solution)/shard_map/ppermute | solution.py:39
  39.3 2.5 %collective-permute-start.8 = (f32[32,128]{1,0:T(8,128)S(1)}, f32[32,128]{1,0:T(8,128)S(1)}, u32[]{:S(2)}, u32[]{:S(2)}) collective-permute-start(f32[32,128]{1,0:T(8,128)S(1)} %get-tuple-element.42.refs_0_), channel_id=1, source_target_pairs={{0,24},{4,28},{8,16},{12,20},{16,8},{20,12},{24,0},{28,4},{1,25},{... | collective-permute-start | bytes 49160 | tf_op jit(solution)/shard_map/ppermute | solution.py:39
  42.4 2.4 %collective-permute-done.8.refs_2_ = f32[32,128]{1,0:T(8,128)S(1)} collective-permute-done((f32[32,128]{1,0:T(8,128)S(1)}, f32[32,128]{1,0:T(8,128)S(1)}, u32[]{:S(2)}, u32[]{:S(2)}) %collective-permute-start.8) | collective-permute-done | bytes 16416 | tf_op jit(solution)/shard_map/ppermute | solution.py:39
  44.9 1.6 %collective-permute-done.9.refs_3_ = f32[32,128]{1,0:T(8,128)S(1)} collective-permute-done((f32[32,128]{1,0:T(8,128)S(1)}, f32[32,128]{1,0:T(8,128)S(1)}, u32[]{:S(2)}, u32[]{:S(2)}) %collective-permute-start.9) | collective-permute-done | bytes 16416 | tf_op jit(solution)/shard_map/ppermute | solution.py:39
  49.0 1.4 %collective-permute-start.15 = (bf16[64,512]{1,0:T(8,128)(2,1)S(1)}, bf16[64,512]{1,0:T(8,128)(2,1)S(1)}, u32[]{:S(2)}, u32[]{:S(2)}) collective-permute-start(bf16[64,512]{1,0:T(8,128)(2,1)S(1)} %get-tuple-element.43.refs_0_), channel_id=1, source_target_pairs={{0,2},{1,3},{2,0},{3,1},{4,6},{5,7},{6,4},{7,5},{8,10},{9,11},{10,... | collective-permute-start | bytes 196616 | tf_op jit(solution)/shard_map/ppermute | solution.py:39
  50.4 1.4 %collective-permute-start.16 = (bf16[64,512]{1,0:T(8,128)(2,1)S(1)}, bf16[64,512]{1,0:T(8,128)(2,1)S(1)}, u32[]{:S(2)}, u32[]{:S(2)}) collective-permute-start(bf16[64,512]{1,0:T(8,128)(2,1)S(1)} %get-tuple-element.43.refs_0_), channel_id=1, source_target_pairs={{0,3},{1,2},{2,1},{3,0},{4,7},{5,6},{6,5},{7,4},{8,11},{9,10},{10,... | collective-permute-start | bytes 196616 | tf_op jit(solution)/shard_map/ppermute | solution.py:39
  53.2 1.6 %bring.1.refs_5_.refs_3_ = bf16[512,2048]{1,0:T(8,128)(2,1)S(1)} custom-call(bf16[512,2048]{1,0:T(8,128)(2,1)} %collective-permute-done.17.far_ref), custom_call_target="tpu_custom_call" | custom-call | bytes 8388608 | tf_op jit(solution)/shard_map/bring/pallas_call | solution.py:473
  55.6 1.0 %own_sums.1 = (bf16[256,512]{1,0:T(8,128)(2,1)S(1)}, f32[64,2176]{1,0:T(8,128)S(1)}) custom-call(s32[3]{0:T(128)S(1)} %pad_add_fusion.where_ref, bf16[64,512]{1,0:T(8,128)(2,1)S(1)} %get-tuple-element.43.refs_0_, bf16[64,512]{1,0:T(8,128)(2,1)S(1)} %collective-permute-done.14.refs_1_, bf16[64,512]{1,0:T(8,128)(2,1)S(1)} %collective-permute-done.15.refs_2_, ...), custom_call_target="tpu_custom_call" | custom-call | bytes 9437184 | tf_op jit(solution)/shard_map/own_sums/pallas_call | solution.py:487
  56.8 1.2 %away_sums.1 = (s16[32,2176]{1,0:T(8,128)(2,1)S(1)}, s16[32,2176]{1,0:T(8,128)(2,1)S(1)}, bf16[256,512]{1,0:T(8,128)(2,1)S(1)}) custom-call(s32[3]{0:T(128)S(1)} %pad_add_fusion.where_ref, bf16[64,512]{1,0:T(8,128)(2,1)S(1)} %collective-permute-done.18.refs_0_, bf16[64,512]{1,0:T(8,128)(2,1)S(1)} %collective-permute-done.19.refs_1_, ...), custom_call_target="tpu_custom_call" | custom-call | bytes 11665408 | tf_op jit(solution)/shard_map/away_sums/pallas_call | solution.py:487
  58.8 1.3 %collective-permute-start.23 = (s16[32,2176]{1,0:T(8,128)(2,1)S(1)}, s16[32,2176]{1,0:T(8,128)(2,1)S(1)}, u32[]{:S(2)}, u32[]{:S(2)}) collective-permute-start(s16[32,2176]{1,0:T(8,128)(2,1)S(1)} %get-tuple-element.53), channel_id=1, source_target_pairs={{0,8},{4,12},{8,0},{12,4},{16,24},{20,28},{24,16},{28,20},{1,9},{5... | collective-permute-start | bytes 417800 | tf_op jit(solution)/shard_map/ppermute | solution.py:39
  60.1 1.7 %home_sums.1 = (s16[32,2176]{1,0:T(8,128)(2,1)S(1)}, s16[32,2176]{1,0:T(8,128)(2,1)S(1)}, f32[32,2176]{1,0:T(8,128)S(1)}, f32[32,2176]{1,0:T(8,128)S(1)}, f32[32...) custom-call(s32[3]{0:T(128)S(1)} %pad_add_fusion.where_ref, bf16[256,512]{1,0:T(8,128)(2,1)S(1)} %get-tuple-element.47.refs_0_, ...), custom_call_target="tpu_custom_call" | custom-call | bytes 18874368 | tf_op jit(solution)/shard_map/home_sums/pallas_call | solution.py:487
  62.7 1.1 %collective-permute-start.26 = (s16[32,2176]{1,0:T(8,128)(2,1)S(1)}, s16[32,2176]{1,0:T(8,128)(2,1)S(1)}, u32[]{:S(2)}, u32[]{:S(2)}) collective-permute-start(s16[32,2176]{1,0:T(8,128)(2,1)S(1)} %get-tuple-element.56), channel_id=1, source_target_pairs={{0,12},{4,8},{8,4},{12,0},{16,28},{20,24},{24,20},{28,16},{1,13},{... | collective-permute-start | bytes 417800 | tf_op jit(solution)/shard_map/ppermute | solution.py:39
  65.4 2.2 %collective-permute-done.23.words_ref = s16[32,2176]{1,0:T(8,128)(2,1)S(1)} collective-permute-done((s16[32,2176]{1,0:T(8,128)(2,1)S(1)}, s16[32,2176]{1,0:T(8,128)(2,1)S(1)}, u32[]{:S(2)}, u32[]{:S(2)}) %collective-permute-start.23) | collective-permute-done | bytes 139296 | tf_op jit(solution)/shard_map/ppermute | solution.py:39
  67.8 1.4 %collective-permute-start.24 = (s16[32,2176]{1,0:T(8,128)(2,1)S(1)}, s16[32,2176]{1,0:T(8,128)(2,1)S(1)}, u32[]{:S(2)}, u32[]{:S(2)}) collective-permute-start(s16[32,2176]{1,0:T(8,128)(2,1)S(1)} %relay.2), channel_id=1, source_target_pairs={{0,24},{4,28},{8,16},{12,20},{16,8},{20,12},{24,0},{28,4},{1,25},{... | collective-permute-start | bytes 417800 | tf_op jit(solution)/shard_map/ppermute | solution.py:39
  69.7 0.8 %collective-permute-done.22.refs_1_ = s16[32,2176]{1,0:T(8,128)(2,1)S(1)} collective-permute-done((s16[32,2176]{1,0:T(8,128)(2,1)S(1)}, s16[32,2176]{1,0:T(8,128)(2,1)S(1)}, u32[]{:S(2)}, u32[]{:S(2)}) %collective-permute-start.22) | collective-permute-done | bytes 139296 | tf_op jit(solution)/shard_map/ppermute | solution.py:39
  70.5 2.2 %collective-permute-done.26.refs_4_ = s16[32,2176]{1,0:T(8,128)(2,1)S(1)} collective-permute-done((s16[32,2176]{1,0:T(8,128)(2,1)S(1)}, s16[32,2176]{1,0:T(8,128)(2,1)S(1)}, u32[]{:S(2)}, u32[]{:S(2)}) %collective-permute-start.26) | collective-permute-done | bytes 139296 | tf_op jit(solution)/shard_map/ppermute | solution.py:39
  72.7 2.3 %collective-permute-done.28.refs_5_ = s16[32,2176]{1,0:T(8,128)(2,1)S(1)} collective-permute-done((s16[32,2176]{1,0:T(8,128)(2,1)S(1)}, s16[32,2176]{1,0:T(8,128)(2,1)S(1)}, u32[]{:S(2)}, u32[]{:S(2)}) %collective-permute-start.28) | collective-permute-done | bytes 139296 | tf_op jit(solution)/shard_map/ppermute | solution.py:39
  75.1 3.6 %collective-permute-done.24.refs_2_ = s16[32,2176]{1,0:T(8,128)(2,1)S(1)} collective-permute-done((s16[32,2176]{1,0:T(8,128)(2,1)S(1)}, s16[32,2176]{1,0:T(8,128)(2,1)S(1)}, u32[]{:S(2)}, u32[]{:S(2)}) %collective-permute-start.24) | collective-permute-done | bytes 139296 | tf_op jit(solution)/shard_map/ppermute | solution.py:39
  78.7 1.7 %finish.1 = f32[32,4096]{1,0:T(8,128)} custom-call(s32[3]{0:T(128)S(1)} %pad_add_fusion.where_ref, f32[32,2176]{1,0:T(8,128)S(1)} %get-tuple-element.51.refs_0_, s16[32,2176]{1,0:T(8,128)(2,1)S(1)} %collective-permute-done.22.refs_1_, s16[32,2176]{1,0:T(8,128)(2,1)S(1)} %collective-permute-done.24.refs_2_, f32[32,2176]{1,0:T(8,128)S(1)} %collective-permute-done.25.refs_3_, ...), custom_call_target="tpu_custom_call" | custom-call | tf_op jit(solution)/shard_map/finish/pallas_call | solution.py:569
  (67 shorter events, 11.4 us)
Async XLA Ops:
  0.6 15.1 %collective-permute-start = (bf16[512,512]{1,0:T(8,128)(2,1)}, bf16[512,512]{1,0:T(8,128)(2,1)S(1)}, u32[]{:S(2)}, u32[]{:S(2)}) collective-permute-start(bf16[512,512]{1,0:T(8,128)(2,1)} %shocks_ref.1), channel_id=1, source_target_pairs={{0,1},{1,0},{2,3},{3,2},{4,5},{5,4},{6,7},{7,6},{8,9},{9,8},{10,11... | collective-permute-start | bytes 1572872 | tf_op jit(solution)/shard_map/ppermute | solution.py:39
  3.6 14.0 %collective-permute-start.2 = (bf16[512,512]{1,0:T(8,128)(2,1)}, bf16[512,512]{1,0:T(8,128)(2,1)S(1)}, u32[]{:S(2)}, u32[]{:S(2)}) collective-permute-start(bf16[512,512]{1,0:T(8,128)(2,1)} %shocks_ref.1), channel_id=1, source_target_pairs={{0,2},{1,3},{2,0},{3,1},{4,6},{5,7},{6,4},{7,5},{8,10},{9,11},{10,... | collective-permute-start | bytes 1572872 | tf_op jit(solution)/shard_map/ppermute | solution.py:39
  15.8 8.6 %collective-permute-start.1 = (bf16[288,512]{1,0:T(8,128)(2,1)S(1)}, bf16[288,512]{1,0:T(8,128)(2,1)S(1)}, u32[]{:S(2)}, u32[]{:S(2)}) collective-permute-start(bf16[288,512]{1,0:T(8,128)(2,1)S(1)} %slice.12), channel_id=1, source_target_pairs={{0,2},{1,3},{2,0},{3,1},{4,6},{5,7},{6,4},{7,5},{8,10},{9,11},{10,... | collective-permute-start | bytes 884744 | tf_op jit(solution)/shard_map/ppermute | solution.py:39
  17.6 6.7 %collective-permute-start.3 = (bf16[224,512]{1,0:T(8,128)(2,1)S(1)}, bf16[224,512]{1,0:T(8,128)(2,1)S(1)}, u32[]{:S(2)}, u32[]{:S(2)}) collective-permute-start(bf16[224,512]{1,0:T(8,128)(2,1)S(1)} %slice.13), channel_id=1, source_target_pairs={{0,1},{1,0},{2,3},{3,2},{4,5},{5,4},{6,7},{7,6},{8,9},{9,8},{10,11... | collective-permute-start | bytes 688136 | tf_op jit(solution)/shard_map/ppermute | solution.py:39
  24.4 22.1 %copy-start.5 = (s32[256]{0:T(256)S(1)}, s32[256]{0:T(256)}, u32[]{:S(2)}) copy-start(s32[256]{0:T(256)} %param.16) | copy-start | bytes 3076
  24.4 22.2 %copy-start.6 = (s32[256]{0:T(256)S(1)}, s32[256]{0:T(256)}, u32[]{:S(2)}) copy-start(s32[256]{0:T(256)} %param.17) | copy-start | bytes 3076
  24.4 22.4 %copy-start.7 = (s32[256]{0:T(256)S(1)}, s32[256]{0:T(256)}, u32[]{:S(2)}) copy-start(s32[256]{0:T(256)} %param.15) | copy-start | bytes 3076
  29.2 6.5 %collective-permute-start.4 = (f32[64,512]{1,0:T(8,128)S(1)}, f32[64,512]{1,0:T(8,128)S(1)}, u32[]{:S(2)}, u32[]{:S(2)}) collective-permute-start(f32[64,512]{1,0:T(8,128)S(1)} %get-tuple-element.36), channel_id=1, source_target_pairs={{0,3},{1,2},{2,1},{3,0},{4,7},{5,6},{6,5},{7,4},{8,11},{9,10},{10,... | collective-permute-start | bytes 393224 | tf_op jit(solution)/shard_map/ppermute | solution.py:39
  31.3 5.8 %collective-permute-start.5 = (f32[64,512]{1,0:T(8,128)S(1)}, f32[64,512]{1,0:T(8,128)S(1)}, u32[]{:S(2)}, u32[]{:S(2)}) collective-permute-start(f32[64,512]{1,0:T(8,128)S(1)} %get-tuple-element.37), channel_id=1, source_target_pairs={{0,2},{1,3},{2,0},{3,1},{4,6},{5,7},{6,4},{7,5},{8,10},{9,11},{10,... | collective-permute-start | bytes 393224 | tf_op jit(solution)/shard_map/ppermute | solution.py:39
  31.8 5.3 %collective-permute-start.6 = (f32[64,512]{1,0:T(8,128)S(1)}, f32[64,512]{1,0:T(8,128)S(1)}, u32[]{:S(2)}, u32[]{:S(2)}) collective-permute-start(f32[64,512]{1,0:T(8,128)S(1)} %get-tuple-element.38), channel_id=1, source_target_pairs={{0,1},{1,0},{2,3},{3,2},{4,5},{5,4},{6,7},{7,6},{8,9},{9,8},{10,11... | collective-permute-start | bytes 393224 | tf_op jit(solution)/shard_map/ppermute | solution.py:39
  37.6 15.6 %collective-permute-start.17 = (bf16[512,2048]{1,0:T(8,128)(2,1)}, bf16[512,2048]{1,0:T(8,128)(2,1)}, u32[]{:S(2)}, u32[]{:S(2)}) collective-permute-start(bf16[512,2048]{1,0:T(8,128)(2,1)} %get-tuple-element.44), channel_id=1, source_target_pairs={{0,4},{4,0},{8,12},{12,8},{16,20},{20,16},{24,28},{28,24},{1,5},{5... | collective-permute-start | bytes 6291464 | tf_op jit(solution)/shard_map/ppermute | solution.py:39
  37.7 4.2 %collective-permute-start.7 = (f32[32,128]{1,0:T(8,128)S(1)}, f32[32,128]{1,0:T(8,128)S(1)}, u32[]{:S(2)}, u32[]{:S(2)}) collective-permute-start(f32[32,128]{1,0:T(8,128)S(1)} %get-tuple-element.42.refs_0_), channel_id=1, source_target_pairs={{0,8},{4,12},{8,0},{12,4},{16,24},{20,28},{24,16},{28,20},{1,9},{5... | collective-permute-start | bytes 49160 | tf_op jit(solution)/shard_map/ppermute | solution.py:39
  39.3 5.5 %collective-permute-start.8 = (f32[32,128]{1,0:T(8,128)S(1)}, f32[32,128]{1,0:T(8,128)S(1)}, u32[]{:S(2)}, u32[]{:S(2)}) collective-permute-start(f32[32,128]{1,0:T(8,128)S(1)} %get-tuple-element.42.refs_0_), channel_id=1, source_target_pairs={{0,24},{4,28},{8,16},{12,20},{16,8},{20,12},{24,0},{28,4},{1,25},{... | collective-permute-start | bytes 49160 | tf_op jit(solution)/shard_map/ppermute | solution.py:39
  41.8 4.6 %collective-permute-start.9 = (f32[32,128]{1,0:T(8,128)S(1)}, f32[32,128]{1,0:T(8,128)S(1)}, u32[]{:S(2)}, u32[]{:S(2)}) collective-permute-start(f32[32,128]{1,0:T(8,128)S(1)} %get-tuple-element.42.refs_0_), channel_id=1, source_target_pairs={{0,16},{4,20},{8,24},{12,28},{16,0},{20,4},{24,8},{28,12},{1,17},{... | collective-permute-start | bytes 49160 | tf_op jit(solution)/shard_map/ppermute | solution.py:39
  41.9 5.0 %collective-permute-start.10 = (f32[32,128]{1,0:T(8,128)S(1)}, f32[32,128]{1,0:T(8,128)S(1)}, u32[]{:S(2)}, u32[]{:S(2)}) collective-permute-start(f32[32,128]{1,0:T(8,128)S(1)} %get-tuple-element.42.refs_0_), channel_id=1, source_target_pairs={{0,4},{4,0},{8,12},{12,8},{16,20},{20,16},{24,28},{28,24},{1,5},{5... | collective-permute-start | bytes 49160 | tf_op jit(solution)/shard_map/ppermute | solution.py:39
  41.9 5.0 %collective-permute-start.11 = (f32[32,128]{1,0:T(8,128)S(1)}, f32[32,128]{1,0:T(8,128)S(1)}, u32[]{:S(2)}, u32[]{:S(2)}) collective-permute-start(f32[32,128]{1,0:T(8,128)S(1)} %collective-permute-done.7.refs_1_), channel_id=1, source_target_pairs={{0,4},{4,0},{8,12},{12,8},{16,20},{20,16},{24,28},{28,24},{1,5},{5... | collective-permute-start | bytes 49160 | tf_op jit(solution)/shard_map/ppermute | solution.py:39
  44.9 2.1 %collective-permute-start.12 = (f32[32,128]{1,0:T(8,128)S(1)}, f32[32,128]{1,0:T(8,128)S(1)}, u32[]{:S(2)}, u32[]{:S(2)}) collective-permute-start(f32[32,128]{1,0:T(8,128)S(1)} %collective-permute-done.8.refs_2_), channel_id=1, source_target_pairs={{0,4},{4,0},{8,12},{12,8},{16,20},{20,16},{24,28},{28,24},{1,5},{5... | collective-permute-start | bytes 49160 | tf_op jit(solution)/shard_map/ppermute | solution.py:39
  46.5 1.2 %collective-permute-start.13 = (f32[32,128]{1,0:T(8,128)S(1)}, f32[32,128]{1,0:T(8,128)S(1)}, u32[]{:S(2)}, u32[]{:S(2)}) collective-permute-start(f32[32,128]{1,0:T(8,128)S(1)} %collective-permute-done.9.refs_3_), channel_id=1, source_target_pairs={{0,4},{4,0},{8,12},{12,8},{16,20},{20,16},{24,28},{28,24},{1,5},{5... | collective-permute-start | bytes 49160 | tf_op jit(solution)/shard_map/ppermute | solution.py:39
  48.2 4.3 %collective-permute-start.14 = (bf16[64,512]{1,0:T(8,128)(2,1)S(1)}, bf16[64,512]{1,0:T(8,128)(2,1)S(1)}, u32[]{:S(2)}, u32[]{:S(2)}) collective-permute-start(bf16[64,512]{1,0:T(8,128)(2,1)S(1)} %get-tuple-element.43.refs_0_), channel_id=1, source_target_pairs={{0,1},{1,0},{2,3},{3,2},{4,5},{5,4},{6,7},{7,6},{8,9},{9,8},{10,11... | collective-permute-start | bytes 196616 | tf_op jit(solution)/shard_map/ppermute | solution.py:39
  49.0 4.3 %collective-permute-start.15 = (bf16[64,512]{1,0:T(8,128)(2,1)S(1)}, bf16[64,512]{1,0:T(8,128)(2,1)S(1)}, u32[]{:S(2)}, u32[]{:S(2)}) collective-permute-start(bf16[64,512]{1,0:T(8,128)(2,1)S(1)} %get-tuple-element.43.refs_0_), channel_id=1, source_target_pairs={{0,2},{1,3},{2,0},{3,1},{4,6},{5,7},{6,4},{7,5},{8,10},{9,11},{10,... | collective-permute-start | bytes 196616 | tf_op jit(solution)/shard_map/ppermute | solution.py:39
  50.4 5.2 %collective-permute-start.16 = (bf16[64,512]{1,0:T(8,128)(2,1)S(1)}, bf16[64,512]{1,0:T(8,128)(2,1)S(1)}, u32[]{:S(2)}, u32[]{:S(2)}) collective-permute-start(bf16[64,512]{1,0:T(8,128)(2,1)S(1)} %get-tuple-element.43.refs_0_), channel_id=1, source_target_pairs={{0,3},{1,2},{2,1},{3,0},{4,7},{5,6},{6,5},{7,4},{8,11},{9,10},{10,... | collective-permute-start | bytes 196616 | tf_op jit(solution)/shard_map/ppermute | solution.py:39
  51.8 4.8 %collective-permute-start.18 = (bf16[64,512]{1,0:T(8,128)(2,1)S(1)}, bf16[64,512]{1,0:T(8,128)(2,1)S(1)}, u32[]{:S(2)}, u32[]{:S(2)}) collective-permute-start(bf16[64,512]{1,0:T(8,128)(2,1)S(1)} %get-tuple-element.43.refs_0_), channel_id=1, source_target_pairs={{0,4},{4,0},{8,12},{12,8},{16,20},{20,16},{24,28},{28,24},{1,5},{5... | collective-permute-start | bytes 196616 | tf_op jit(solution)/shard_map/ppermute | solution.py:39
  52.6 4.1 %collective-permute-start.19 = (bf16[64,512]{1,0:T(8,128)(2,1)S(1)}, bf16[64,512]{1,0:T(8,128)(2,1)S(1)}, u32[]{:S(2)}, u32[]{:S(2)}) collective-permute-start(bf16[64,512]{1,0:T(8,128)(2,1)S(1)} %collective-permute-done.14.refs_1_), channel_id=1, source_target_pairs={{0,4},{4,0},{8,12},{12,8},{16,20},{20,16},{24,28},{28,24},{1,5},{5... | collective-permute-start | bytes 196616 | tf_op jit(solution)/shard_map/ppermute | solution.py:39
  53.2 3.4 %collective-permute-start.20 = (bf16[64,512]{1,0:T(8,128)(2,1)S(1)}, bf16[64,512]{1,0:T(8,128)(2,1)S(1)}, u32[]{:S(2)}, u32[]{:S(2)}) collective-permute-start(bf16[64,512]{1,0:T(8,128)(2,1)S(1)} %collective-permute-done.15.refs_2_), channel_id=1, source_target_pairs={{0,4},{4,0},{8,12},{12,8},{16,20},{20,16},{24,28},{28,24},{1,5},{5... | collective-permute-start | bytes 196616 | tf_op jit(solution)/shard_map/ppermute | solution.py:39
  55.5 1.3 %collective-permute-start.21 = (bf16[64,512]{1,0:T(8,128)(2,1)S(1)}, bf16[64,512]{1,0:T(8,128)(2,1)S(1)}, u32[]{:S(2)}, u32[]{:S(2)}) collective-permute-start(bf16[64,512]{1,0:T(8,128)(2,1)S(1)} %collective-permute-done.16.refs_3_), channel_id=1, source_target_pairs={{0,4},{4,0},{8,12},{12,8},{16,20},{20,16},{24,28},{28,24},{1,5},{5... | collective-permute-start | bytes 196616 | tf_op jit(solution)/shard_map/ppermute | solution.py:39
  58.0 6.6 %collective-permute-start.27 = (s16[32,2176]{1,0:T(8,128)(2,1)S(1)}, s16[32,2176]{1,0:T(8,128)(2,1)S(1)}, u32[]{:S(2)}, u32[]{:S(2)}) collective-permute-start(s16[32,2176]{1,0:T(8,128)(2,1)S(1)} %get-tuple-element.57), channel_id=1, source_target_pairs={{0,8},{4,12},{8,0},{12,4},{16,24},{20,28},{24,16},{28,20},{1,9},{5... | collective-permute-start | bytes 417800 | tf_op jit(solution)/shard_map/ppermute | solution.py:39
  58.8 8.7 %collective-permute-start.23 = (s16[32,2176]{1,0:T(8,128)(2,1)S(1)}, s16[32,2176]{1,0:T(8,128)(2,1)S(1)}, u32[]{:S(2)}, u32[]{:S(2)}) collective-permute-start(s16[32,2176]{1,0:T(8,128)(2,1)S(1)} %get-tuple-element.53), channel_id=1, source_target_pairs={{0,8},{4,12},{8,0},{12,4},{16,24},{20,28},{24,16},{28,20},{1,9},{5... | collective-permute-start | bytes 417800 | tf_op jit(solution)/shard_map/ppermute | solution.py:39
  61.8 16.8 %collective-permute-start.25 = (f32[32,2176]{1,0:T(8,128)S(1)}, f32[32,2176]{1,0:T(8,128)S(1)}, u32[]{:S(2)}, u32[]{:S(2)}) collective-permute-start(f32[32,2176]{1,0:T(8,128)S(1)} %get-tuple-element.55), channel_id=1, source_target_pairs={{0,4},{4,0},{8,12},{12,8},{16,20},{20,16},{24,28},{28,24},{1,5},{5... | collective-permute-start | bytes 835592 | tf_op jit(solution)/shard_map/ppermute | solution.py:39
  61.9 8.6 %collective-permute-start.22 = (s16[32,2176]{1,0:T(8,128)(2,1)S(1)}, s16[32,2176]{1,0:T(8,128)(2,1)S(1)}, u32[]{:S(2)}, u32[]{:S(2)}) collective-permute-start(s16[32,2176]{1,0:T(8,128)(2,1)S(1)} %get-tuple-element.52), channel_id=1, source_target_pairs={{0,8},{4,12},{8,0},{12,4},{16,24},{20,28},{24,16},{28,20},{1,9},{5... | collective-permute-start | bytes 417800 | tf_op jit(solution)/shard_map/ppermute | solution.py:39
  62.7 10.0 %collective-permute-start.26 = (s16[32,2176]{1,0:T(8,128)(2,1)S(1)}, s16[32,2176]{1,0:T(8,128)(2,1)S(1)}, u32[]{:S(2)}, u32[]{:S(2)}) collective-permute-start(s16[32,2176]{1,0:T(8,128)(2,1)S(1)} %get-tuple-element.56), channel_id=1, source_target_pairs={{0,12},{4,8},{8,4},{12,0},{16,28},{20,24},{24,20},{28,16},{1,13},{... | collective-permute-start | bytes 417800 | tf_op jit(solution)/shard_map/ppermute | solution.py:39
  64.8 10.3 %collective-permute-start.28 = (s16[32,2176]{1,0:T(8,128)(2,1)S(1)}, s16[32,2176]{1,0:T(8,128)(2,1)S(1)}, u32[]{:S(2)}, u32[]{:S(2)}) collective-permute-start(s16[32,2176]{1,0:T(8,128)(2,1)S(1)} %relay.3), channel_id=1, source_target_pairs={{0,28},{4,24},{8,20},{12,16},{16,12},{20,8},{24,4},{28,0},{1,29},{... | collective-permute-start | bytes 417800 | tf_op jit(solution)/shard_map/ppermute | solution.py:39
  67.8 10.9 %collective-permute-start.24 = (s16[32,2176]{1,0:T(8,128)(2,1)S(1)}, s16[32,2176]{1,0:T(8,128)(2,1)S(1)}, u32[]{:S(2)}, u32[]{:S(2)}) collective-permute-start(s16[32,2176]{1,0:T(8,128)(2,1)S(1)} %relay.2), channel_id=1, source_target_pairs={{0,24},{4,28},{8,16},{12,20},{16,8},{20,12},{24,0},{28,4},{1,25},{... | collective-permute-start | bytes 417800 | tf_op jit(solution)/shard_map/ppermute | solution.py:39
  (5 other events, 17.2 us)
